TPU v7x, 32 devices: a whole 2x2x4 slice. The times are simulated.
32 devices in a mesh: sp: 8 (over z, x), hd: 4 (over y, core).
Axes of the slice: x: 2, y: 2, z: 4, core: 2. Of those that a mesh axis runs over, the one named last changes fastest.
Arguments:
- tokens: bfloat16 [4096, 2304], P(('sp', 'hd')), may hold values from -6 to 6
- gains: float32 [4, 2304], replicated, may hold values from -0.5 to 0.5
- w_qkv: bfloat16 [2304, 4096], P(('sp', 'hd')), may hold values from -0.1875 to 0.1875
- w_out: bfloat16 [2304, 2048], P(('sp', 'hd')), may hold values from -0.125 to 0.125
- w_in: bfloat16 [2304, 18432], P(('sp', 'hd')), may hold values from -0.125 to 0.125
- w_down: bfloat16 [2304, 9216], P(('sp', 'hd')), may hold values from -0.0625 to 0.0625
- lengths: int32 [16], replicated, may hold values from 1 to 2048, 4096 in all
- cotangent: bfloat16 [4096, 2304], P(('sp', 'hd')), may hold values from -6 to 6
Outputs:
- result: bfloat16 [4096, 2304], P(('sp', 'hd'))
- grad_tokens: float32 [4096, 2304], P(('sp', 'hd'))
- grad_qkv: float32 [2304, 4096], P(('sp', 'hd'))
- grad_out: float32 [2304, 2048], P(('sp', 'hd'))
- grad_in: float32 [2304, 18432], P(('sp', 'hd'))
- grad_down: float32 [2304, 9216], P(('sp', 'hd'))
- grad_gains: float32 [4, 2304], replicated
- column_scales: float32 [22528], replicated
- row_scales: float32 [2, 2304], P(None, ('sp', 'hd'))
Inputs may be any that keep to these rules, and one draw needn't show every extreme that they name: `lengths`: they sum to 4096 and the longest is exactly 2048.
All inputs are finite; a program needn't handle non-finite values.
Results may differ from a plain program's by a relative error of at most 0.02.
Values may be sent and summed in bfloat16 or wider, within the bound.
No kernel may reach another device: no remote copies, remote signals or barrier semaphores. Data moves between devices by JAX's collectives and lax.ppermute only.
A program may use at most 640 MiB of HBM per device.

v0:
```python
import math

import jax
import jax.numpy as jnp
from jax import lax
from jax.sharding import PartitionSpec as P

FF = 9216
QH = 8
KVH = 4
HD = 256
WINDOW = 4096


EPSILON = 1e-06
SOFTCAP = 50.0
LEVEL_PULL = 0.75
TWO_PI = 2.0 * math.pi


def rms_scale(vector_in, gain_row):
    mean_sq = jnp.mean(vector_in * vector_in, axis=-1, keepdims=True)
    return vector_in * lax.rsqrt(mean_sq + EPSILON) * (1.0 + gain_row)


def soft_level(value):
    return value - LEVEL_PULL * jnp.sin(TWO_PI * value) / TWO_PI


def nested(weight, channel_scale):
    scaled_w = weight / channel_scale
    level_eight = soft_level(127.0 * scaled_w)
    level_four = 16.0 * soft_level(level_eight / 16.0)
    level_two = 64.0 * soft_level(level_eight / 64.0)
    return channel_scale * (level_eight + level_four + level_two) / 381.0


def rotate(vector_in, cosine, sine_tab):
    half_dim = vector_in.shape[-1] // 2
    first_half = vector_in[..., :half_dim]
    second_half = vector_in[..., half_dim:]
    return jnp.concatenate(
        [
            first_half * cosine - second_half * sine_tab,
            second_half * cosine + first_half * sine_tab,
        ],
        axis=-1,
    )


def rope_tables(position, head_dim):
    half_dim = head_dim // 2
    frequency = jnp.exp(
        jnp.arange(half_dim, dtype=jnp.float32) * (-2.0 * math.log(10000.0) / head_dim)
    )
    angle = position.astype(jnp.float32)[:, None] * frequency[None, :]
    return (jnp.cos(angle)[:, None, :], jnp.sin(angle)[:, None, :])


def doc_info(lengths, places):
    stop_at = jnp.cumsum(lengths, dtype=jnp.int32)
    starts = stop_at - lengths
    inside = starts[None, :] <= places[:, None]
    doc_index = jnp.sum(inside.astype(jnp.int32), axis=1) - 1
    doc_start = jnp.max(jnp.where(inside, starts[None, :], 0), axis=1)
    return (doc_index, places - doc_start)


def glu(gate_in, up_in):
    return jax.nn.gelu(gate_in, approximate=True) * up_in


def contract_rows(left, right):
    return lax.dot_general(
        left, right, (((1,), (1,)), ((), ())), preferred_element_type=jnp.float32
    )


def contract_first(left, right):
    return lax.dot_general(
        left, right, (((0,), (0,)), ((), ())), preferred_element_type=jnp.float32
    )


def capped_scores(query_loc, key_rows, allowed):
    root = math.sqrt(query_loc.shape[-1])
    raw_scores = (
        jnp.einsum("bgd,cd->gbc", query_loc, key_rows, preferred_element_type=jnp.float32) / root
    )
    tanh_part = jnp.tanh(raw_scores / SOFTCAP)
    capped = jnp.where(allowed[None], SOFTCAP * tanh_part, -1e30)
    return (capped, tanh_part)


def on_device(tokens, gains, w_qkv, w_out, w_in, w_down, lengths, cotangent):
    sp_count = lax.axis_size("sp")
    hd_count = lax.axis_size("hd")
    sp_index = lax.axis_index("sp")
    hd_index = lax.axis_index("hd")
    tok_rows = tokens.shape[0]
    shard_rows = tok_rows * hd_count
    head_dim = HD
    groups = QH // KVH
    root = math.sqrt(head_dim)
    qkv_max = jnp.max(jnp.abs(w_qkv.astype(jnp.float32)), axis=0)
    in_max = jnp.max(jnp.abs(w_in.astype(jnp.float32)), axis=0)
    qkv_max, in_max = (
        lax.pmax(qkv_max.astype(jnp.bfloat16), ("sp", "hd")).astype(qkv_max.dtype),
        lax.pmax(in_max.astype(jnp.bfloat16), ("sp", "hd")).astype(in_max.dtype),
    )
    qkv_scale = qkv_max + EPSILON
    in_scale = in_max + EPSILON
    out_scale = jnp.max(jnp.abs(w_out.astype(jnp.float32)), axis=1) + EPSILON
    down_scale = jnp.max(jnp.abs(w_down.astype(jnp.float32)), axis=1) + EPSILON
    eff_qkv = nested(w_qkv.astype(jnp.float32), qkv_scale[None, :]).astype(jnp.bfloat16)
    eff_out = nested(w_out.astype(jnp.float32), out_scale[:, None]).astype(jnp.bfloat16)
    eff_in = nested(w_in.astype(jnp.float32), in_scale[None, :]).astype(jnp.bfloat16)
    eff_down = nested(w_down.astype(jnp.float32), down_scale[:, None]).astype(jnp.bfloat16)
    full_qkv, full_out, full_in, full_down = (
        lax.all_gather(eff_qkv, ("sp", "hd"), axis=0, tiled=True),
        lax.all_gather(eff_out, ("sp", "hd"), axis=0, tiled=True),
        lax.all_gather(eff_in, ("sp", "hd"), axis=0, tiled=True),
        lax.all_gather(eff_down, ("sp", "hd"), axis=0, tiled=True),
    )
    places = (sp_index * hd_count + hd_index) * tok_rows + jnp.arange(tok_rows, dtype=jnp.int32)
    position = doc_info(lengths, places)[1]
    cosine, sine_tab = rope_tables(position, head_dim)
    inputs = tokens.astype(jnp.float32)
    normed = rms_scale(inputs, gains[0]).astype(jnp.bfloat16)
    mixed_qkv = jnp.dot(normed, full_qkv, preferred_element_type=jnp.float32)
    grouped = mixed_qkv.reshape(tok_rows, KVH, groups + 2, head_dim)
    query_rot = rotate(grouped[:, :, :groups].reshape(tok_rows, QH, head_dim), cosine, sine_tab)
    key_rot = rotate(grouped[:, :, groups], cosine, sine_tab)
    rounded = jnp.concatenate(
        [
            query_rot.reshape(tok_rows, KVH, groups, head_dim),
            key_rot[:, :, None],
            grouped[:, :, groups + 1 :],
        ],
        axis=2,
    )
    rounded = rounded.astype(jnp.bfloat16).reshape(tok_rows, KVH * (groups + 2) * head_dim)
    local_qkv = lax.all_to_all(rounded, "hd", split_axis=1, concat_axis=0, tiled=True).reshape(
        shard_rows, groups + 2, head_dim
    )
    query_loc = local_qkv[:, :groups]
    kv_own = local_qkv[:, groups:].reshape(shard_rows, 2 * head_dim)
    every_kv = lax.all_gather(kv_own, "sp", axis=0, tiled=True)
    padded = jnp.concatenate([jnp.zeros((WINDOW, 2 * head_dim), jnp.bfloat16), every_kv], axis=0)
    window_kv = lax.dynamic_slice_in_dim(padded, sp_index * shard_rows, WINDOW + shard_rows, 0)
    key_rows = window_kv[:, :head_dim]
    value_rows = window_kv[:, head_dim:]
    q_places = sp_index * shard_rows + jnp.arange(shard_rows, dtype=jnp.int32)
    k_places = sp_index * shard_rows - WINDOW + jnp.arange(WINDOW + shard_rows, dtype=jnp.int32)
    q_doc = doc_info(lengths, q_places)[0]
    k_doc = doc_info(lengths, k_places)[0]
    distance = q_places[:, None] - k_places[None, :]
    allowed = (q_doc[:, None] == k_doc[None, :]) & (distance >= 0) & (distance < WINDOW)
    capped, tanh_part = capped_scores(query_loc, key_rows, allowed)
    row_max = jnp.max(capped, axis=2, keepdims=True)
    exp_scores = jnp.exp(capped - row_max)
    row_total = jnp.sum(exp_scores, axis=2, keepdims=True)
    attn_probs = (exp_scores / row_total).astype(jnp.bfloat16)
    log_total = row_max + jnp.log(row_total)
    heads_loc = jnp.einsum(
        "gbc,cd->bgd", attn_probs, value_rows, preferred_element_type=jnp.float32
    )
    heads_loc = heads_loc.astype(jnp.bfloat16).reshape(shard_rows, groups * head_dim)
    heads_tok = lax.all_to_all(heads_loc, "hd", split_axis=0, concat_axis=1, tiled=True)
    branch = contract_rows(heads_tok, full_out)
    middle = inputs + rms_scale(branch, gains[1])
    pre_mlp = rms_scale(middle, gains[2]).astype(jnp.bfloat16)
    gate_up = jnp.dot(pre_mlp, full_in, preferred_element_type=jnp.float32)
    gate_part = gate_up[:, :FF]
    up_part = gate_up[:, FF:]
    hidden = glu(gate_part, up_part).astype(jnp.bfloat16)
    down_out = contract_rows(hidden, full_down)
    result = (middle + rms_scale(down_out, gains[3])).astype(jnp.bfloat16)
    back_qkv, back_out, back_in, back_down = (full_qkv, full_out, full_in, full_down)
    grad_result = cotangent.astype(jnp.float32)
    norm_four = jax.vjp(rms_scale, down_out, gains[3])[1]
    d_down, gain_four = norm_four(grad_result)
    d_down = d_down.astype(jnp.bfloat16)
    d_hidden = jnp.dot(d_down, back_down, preferred_element_type=jnp.float32)
    glu_back = jax.vjp(glu, gate_part, up_part)[1]
    d_gate, d_up = glu_back(d_hidden)
    d_both = jnp.concatenate([d_gate, d_up], axis=1).astype(jnp.bfloat16)
    d_pre = contract_rows(d_both, back_in)
    norm_three = jax.vjp(rms_scale, middle, gains[2])[1]
    d_mid_part, gain_three = norm_three(d_pre)
    d_middle = grad_result + d_mid_part
    norm_two = jax.vjp(rms_scale, branch, gains[1])[1]
    d_branch, gain_two = norm_two(d_middle)
    d_branch = d_branch.astype(jnp.bfloat16)
    d_heads_tok = jnp.dot(d_branch, back_out, preferred_element_type=jnp.float32).astype(
        jnp.bfloat16
    )
    d_heads_loc = lax.all_to_all(
        d_heads_tok, "hd", split_axis=1, concat_axis=0, tiled=True
    ).reshape(shard_rows, groups, head_dim)
    capped, tanh_part = capped_scores(query_loc, key_rows, allowed)
    probs_full = jnp.exp(capped - log_total)
    probs_low = probs_full.astype(jnp.bfloat16)
    d_prob = jnp.einsum("bgd,cd->gbc", d_heads_loc, value_rows, preferred_element_type=jnp.float32)
    delta = jnp.sum(probs_full * d_prob, axis=2, keepdims=True)
    d_raw = (probs_full * (d_prob - delta) * (1.0 - tanh_part * tanh_part)).astype(jnp.bfloat16)
    d_query = (
        jnp.einsum("gbc,cd->bgd", d_raw, key_rows, preferred_element_type=jnp.float32) / root
    ).astype(jnp.bfloat16)
    d_keys = jnp.einsum("gbc,bgd->cd", d_raw, query_loc, preferred_element_type=jnp.float32) / root
    d_values = jnp.einsum("gbc,bgd->cd", probs_low, d_heads_loc, preferred_element_type=jnp.float32)
    d_window = jnp.concatenate([d_keys, d_values], axis=1)
    spread = jnp.zeros((WINDOW + sp_count * shard_rows, 2 * head_dim), jnp.float32)
    spread = lax.dynamic_update_slice_in_dim(spread, d_window, sp_index * shard_rows, 0)
    d_kv = lax.psum_scatter(
        spread[WINDOW:].astype(jnp.bfloat16), "sp", scatter_dimension=0, tiled=True
    )
    d_local = jnp.concatenate([d_query, d_kv.reshape(shard_rows, 2, head_dim)], axis=1)
    d_local = d_local.reshape(shard_rows, (groups + 2) * head_dim)
    d_grouped = lax.all_to_all(d_local, "hd", split_axis=0, concat_axis=1, tiled=True).astype(
        jnp.float32
    )
    d_grouped = d_grouped.reshape(tok_rows, KVH, groups + 2, head_dim)
    d_query_lin = rotate(
        d_grouped[:, :, :groups].reshape(tok_rows, QH, head_dim), cosine, -sine_tab
    )
    d_key_lin = rotate(d_grouped[:, :, groups], cosine, -sine_tab)
    d_mixed = jnp.concatenate(
        [
            d_query_lin.reshape(tok_rows, KVH, groups, head_dim),
            d_key_lin[:, :, None],
            d_grouped[:, :, groups + 1 :],
        ],
        axis=2,
    )
    d_mixed = d_mixed.astype(jnp.bfloat16).reshape(tok_rows, KVH * (groups + 2) * head_dim)
    d_normed = contract_rows(d_mixed, back_qkv)
    norm_one = jax.vjp(rms_scale, inputs, gains[0])[1]
    d_input_part, gain_one = norm_one(d_normed)
    grad_tokens = d_middle + d_input_part
    grad_gains = lax.psum(
        jnp.stack([gain_one, gain_two, gain_three, gain_four], axis=0), ("sp", "hd")
    )
    own_rows = w_qkv.shape[0]
    group_all = (
        lax.all_gather(normed, "hd", axis=0, tiled=True),
        lax.all_gather(d_branch, "hd", axis=0, tiled=True),
        lax.all_gather(pre_mlp, "hd", axis=0, tiled=True),
        lax.all_gather(d_down, "hd", axis=0, tiled=True),
        lax.all_gather(d_mixed, "hd", axis=0, tiled=True),
        lax.all_gather(heads_tok, "hd", axis=0, tiled=True),
        lax.all_gather(d_both, "hd", axis=0, tiled=True),
        lax.all_gather(hidden, "hd", axis=0, tiled=True),
    )

    def pick_rows(matrix):
        split_cols = matrix.reshape(matrix.shape[0], sp_count, hd_count, own_rows)
        chosen = lax.dynamic_index_in_dim(split_cols, hd_index, 2, keepdims=False)
        return chosen.reshape(matrix.shape[0], sp_count * own_rows)

    term_qkv = contract_first(pick_rows(group_all[0]), group_all[4])
    term_out = contract_first(pick_rows(group_all[1]), group_all[5])
    term_in = contract_first(pick_rows(group_all[2]), group_all[6])
    term_down = contract_first(pick_rows(group_all[3]), group_all[7])
    grad_qkv, grad_out, grad_in, grad_down = (
        lax.psum_scatter(
            term_qkv.astype(jnp.bfloat16), "sp", scatter_dimension=0, tiled=True
        ).astype(jnp.float32),
        lax.psum_scatter(
            term_out.astype(jnp.bfloat16), "sp", scatter_dimension=0, tiled=True
        ).astype(jnp.float32),
        lax.psum_scatter(
            term_in.astype(jnp.bfloat16), "sp", scatter_dimension=0, tiled=True
        ).astype(jnp.float32),
        lax.psum_scatter(
            term_down.astype(jnp.bfloat16), "sp", scatter_dimension=0, tiled=True
        ).astype(jnp.float32),
    )
    column_scales = jnp.concatenate([qkv_scale, in_scale], axis=0)
    row_scales = jnp.stack([out_scale, down_scale], axis=0)
    return (
        result,
        grad_tokens,
        grad_qkv,
        grad_out,
        grad_in,
        grad_down,
        grad_gains,
        column_scales,
        row_scales,
    )


def solution(mesh):
    in_specs = (
        P(("sp", "hd"), None),
        P(),
        P(("sp", "hd"), None),
        P(("sp", "hd"), None),
        P(("sp", "hd"), None),
        P(("sp", "hd"), None),
        P(),
        P(("sp", "hd"), None),
    )
    out_specs = (
        P(("sp", "hd"), None),
        P(("sp", "hd"), None),
        P(("sp", "hd"), None),
        P(("sp", "hd"), None),
        P(("sp", "hd"), None),
        P(("sp", "hd"), None),
        P(),
        P(),
        P(None, ("sp", "hd")),
    )
    return jax.shard_map(
        on_device, mesh=mesh, in_specs=in_specs, out_specs=out_specs, check_vma=False
    )
```

profile of v0, /device:TPU:0, one launch (start us, length us, event | category | flops | bytes accessed | tf_op | source)
XLA Modules:
  0.0 2419.4 jit_solution(7015169284987151966)
XLA Ops:
  10.7 42.6 %all-reduce.2 = (bf16[4096]{0:T(1024)(128)(2,1)S(1)}, bf16[18432]{0:T(1024)(128)(2,1)S(1)}) all-reduce(bf16[4096]{0:T(1024)(128)(2,1)S(1)} %fusion.56, bf16[18432]{0:T(1024)(128)(2,1)S(1)} %fusion.16), channel_id=1, replica_groups=mesh['sp'=8,'hd'=4] {'sp','hd'}, use_global_device_ids=true, to_apply=%region_2.0 | all-reduce | flops 22528 | bytes 90112 | tf_op jit(solution)/shard_map/pmax | solution.py:108
  53.9 14.1 multiply_convert_fusion.5
  70.7 121.9 %all-gather.14.cloned.1.call-done = bf16[2304,4096]{1,0:T(8,128)(2,1)} async-done(((bf16[72,4096]{1,0:T(8,128)(2,1)}), bf16[2304,4096]{1,0:T(8,128)(2,1)}) %all-gather.14.cloned.1.call-update) | async-done | bytes 18874384 | tf_op jit(solution)/shard_map/all_gather | solution.py:120
  192.6 10.3 fusion.91
  212.5 17.6 all_to_all.61
  235.9 7.0 multiply_convert_fusion.6
  243.0 57.8 %multiply_convert_fusion = bf16[72,18432]{1,0:T(8,128)(2,1)} fusion(bf16[72,18432]{1,0:T(8,128)(2,1)} %param.12, f32[18432]{0:T(1024)S(1)} %convert_add_fusion.2), kind=kLoop, calls=%fused_computation.36 | loop fusion | flops 27869184 | bytes 5382144 | tf_op jit(solution)/shard_map/convert_element_type | solution.py:117
  301.0 28.6 %multiply_convert_fusion.3 = bf16[72,9216]{1,0:T(8,128)(2,1)} fusion(bf16[72,9216]{1,0:T(8,128)(2,1)S(1)} %copy-done.20, f32[72]{0:T(128)S(1)} %get-tuple-element.55), kind=kLoop, calls=%fused_computation.52 | loop fusion | flops 13934592 | bytes 2654496 | tf_op jit(solution)/shard_map/convert_element_type | solution.py:118
  329.9 5.3 fusion.10
  335.2 6.9 fusion.66
  342.2 6.3 fusion.3
  348.6 10.4 fusion.50
  363.9 30.4 %all-gather.18.cloned.1.call-done = bf16[2304,2048]{1,0:T(8,128)(2,1)} async-done(((bf16[72,2048]{1,0:T(8,128)(2,1)}), bf16[2304,2048]{1,0:T(8,128)(2,1)}) %all-gather.18.cloned.1.call-update) | async-done | bytes 9437200 | tf_op jit(solution)/shard_map/all_gather | solution.py:121
  394.3 7.2 multiply_reduce_fusion.6
  403.1 434.9 %all-gather.20.cloned.1.call-done = bf16[2304,18432]{1,0:T(8,128)(2,1)} async-done(((bf16[72,18432]{1,0:T(8,128)(2,1)}), bf16[2304,18432]{1,0:T(8,128)(2,1)}) %all-gather.20.cloned.1.call-update) | async-done | bytes 84934672 | tf_op jit(solution)/shard_map/all_gather | solution.py:122
  838.0 34.4 %fusion.92 = f32[128,18432]{1,0:T(8,128)} fusion(bf16[128,2304]{1,0:T(8,128)(2,1)S(1)} %multiply_convert_fusion.4, bf16[2304,18432]{1,0:T(8,128)(2,1)} %all-gather.20.cloned.1.call-done), kind=kOutput, calls=%fused_computation.188 | convolution fusion | flops 10871635968 | bytes 94961664 | tf_op jit(solution)/shard_map/dot_general | solution.py:173
  872.4 4.6 multiply_convert_fusion.2
  877.0 199.6 %all-gather.22.cloned.1.call-done = bf16[2304,9216]{1,0:T(8,128)(2,1)} async-done(((bf16[72,9216]{1,0:T(8,128)(2,1)}), bf16[2304,9216]{1,0:T(8,128)(2,1)}) %all-gather.22.cloned.1.call-update) | async-done | bytes 42467344 | tf_op jit(solution)/shard_map/all_gather | solution.py:123
  1076.7 21.3 multiply_reduce_fusion.4
  1104.4 21.9 fusion.23
  1126.4 37.5 %multiply_reduce_fusion = (f32[2304]{0:T(1024)}, f32[128]{0:T(128)S(1)}, f32[128,2304]{1,0:T(8,128)}) fusion(f32[128,2304]{1,0:T(8,128)S(1)} %get-tuple-element.25, f32[128]{0:T(128)} %copy-done.47, f32[2304]{0:T(1024)} %copy-done.33, bf16[2304,18432]{1,0:T(8,128)(2,1)} %all-gather.20.cloned.1.call-done, bf16[128,9216]{1,0:T(8,128)(2,1)} %get-tuple-element.27, ...), kind=kOutput, calls=%fused_computation.92 | convolution fusion | flops 10882840576 | bytes 92032000 | tf_op jit(solution)/shard_map/dot_general | solution.py:74
  1167.7 5.3 convolution_convert_fusion.4
  1177.6 8.7 all-to-all-done.2
  1187.4 12.4 fusion.12
  1199.8 8.5 fusion.31
  1208.3 30.6 %fusion.1 = bf16[2,512,4608]{1,2,0:T(8,128)(2,1)} fusion(f32[4608,512,2]{1,0,2:T(8,128)} %fusion.31, f32[4608,512,2]{1,0,2:T(8,128)} %copy-done.1, f32[2,512]{1,0:T(2,128)S(1)} %log_add_fusion, pred[512,4608]{0,1:T(8,128)(4,1)S(1)} %copy-done.10), kind=kOutput, calls=%fused_computation.3 | output fusion | flops 70784512 | bytes 49549312 | tf_op jit(solution)/shard_map/sub | solution.py:206
  1238.9 10.5 fusion.15
  1256.2 6.8 fusion.47
  1262.9 77.8 %reduce-scatter.8.cloned.1.call-done = bf16[512,512]{0,1:T(8,128)(2,1)} async-done(((bf16[4096,512]{0,1:T(8,128)(2,1)}), bf16[512,512]{0,1:T(8,128)(2,1)}) %reduce-scatter.8.cloned.1.call-update) | async-done | bytes 524304 | tf_op jit(solution)/shard_map/reduce_scatter | solution.py:215
  1347.0 23.2 all-to-all-done.3
  1384.6 14.2 all-gather.30.cloned.1.call-done
  1398.8 4.4 convolution_convert_fusion.3
  1403.3 21.3 all-gather.24.cloned.1.call-done
  1427.4 34.2 %all-gather.26.cloned.1.call-done = bf16[512,4096]{0,1:T(8,128)(2,1)} async-done(((bf16[128,4096]{0,1:T(8,128)(2,1)}), bf16[512,4096]{0,1:T(8,128)(2,1)}) %all-gather.26.cloned.1.call-update) | async-done | bytes 4194320 | tf_op jit(solution)/shard_map/all_gather | solution.py:250
  1461.6 6.4 convolution_convert_fusion.2
  1468.1 19.2 all-gather.36.cloned.1.call-done
  1490.3 62.9 %all-gather.38.cloned.1.call-done = bf16[512,9216]{1,0:T(8,128)(2,1)} async-done(((bf16[128,9216]{1,0:T(8,128)(2,1)}), bf16[512,9216]{1,0:T(8,128)(2,1)}) %all-gather.38.cloned.1.call-update) | async-done | bytes 9437200 | tf_op jit(solution)/shard_map/all_gather | solution.py:253
  1553.1 11.9 convolution_convert_fusion.1
  1565.1 13.8 all-gather.32.cloned.1.call-done
  1582.0 118.5 %all-gather.34.cloned.1.call-done = bf16[512,18432]{1,0:T(8,128)(2,1)} async-done(((bf16[128,18432]{1,0:T(8,128)(2,1)}), bf16[512,18432]{1,0:T(8,128)(2,1)}) %all-gather.34.cloned.1.call-update) | async-done | bytes 18874384 | tf_op jit(solution)/shard_map/all_gather | solution.py:252
  1700.4 20.8 convolution_convert_fusion
  1723.2 50.8 %reduce-scatter.12.cloned.1.call-done = bf16[72,2048]{1,0:T(8,128)(2,1)} async-done(((bf16[576,2048]{1,0:T(8,128)(2,1)}), bf16[72,2048]{1,0:T(8,128)(2,1)}) %reduce-scatter.12.cloned.1.call-update) | async-done | bytes 294928 | tf_op jit(solution)/shard_map/reduce_scatter | solution.py:269
  1775.9 13.9 fusion.54
  1789.9 42.4 %psum.7 = f32[4,2304]{1,0:T(4,128)} all-reduce(f32[4,2304]{1,0:T(4,128)S(1)} %pad_maximum_fusion.6), channel_id=1, replica_groups=mesh['sp'=8,'hd'=4] {'sp','hd'}, use_global_device_ids=true, to_apply=%region_30.31 | all-reduce | flops 9216 | bytes 73728 | tf_op jit(solution)/shard_map/psum | solution.py:241
  1834.9 39.7 %reduce-scatter.10.cloned.1.call-done = bf16[72,4096]{1,0:T(8,128)(2,1)} async-done(((bf16[576,4096]{1,0:T(8,128)(2,1)}), bf16[72,4096]{1,0:T(8,128)(2,1)}) %reduce-scatter.10.cloned.1.call-update) | async-done | bytes 589840 | tf_op jit(solution)/shard_map/reduce_scatter | solution.py:266
  1876.8 181.5 %reduce-scatter.14.cloned.1.call-done = bf16[72,9216]{1,0:T(8,128)(2,1)} async-done(((bf16[576,9216]{1,0:T(8,128)(2,1)}), bf16[72,9216]{1,0:T(8,128)(2,1)}) %reduce-scatter.14.cloned.1.call-update) | async-done | bytes 1327120 | tf_op jit(solution)/shard_map/reduce_scatter | solution.py:275
  2061.3 346.6 %reduce-scatter.16.cloned.1.call-done = bf16[72,18432]{1,0:T(8,128)(2,1)} async-done(((bf16[576,18432]{1,0:T(8,128)(2,1)}), bf16[72,18432]{1,0:T(8,128)(2,1)}) %reduce-scatter.16.cloned.1.call-update) | async-done | bytes 2654224
  2407.9 4.5 convert_element_type.189
  (262 shorter events, 92.7 us)
Async XLA Ops:
  7.2 60.8 %copy-start.53 = (s32[16]{0:T(128)S(1)}, s32[16]{0:T(128)}, u32[]{:S(2)}) copy-start(s32[16]{0:T(128)} %param.14) | copy-start | bytes 196
  7.2 62.4 %copy-start.40 = (f32[4,2304]{1,0:T(4,128)S(1)}, f32[4,2304]{1,0:T(4,128)}, u32[]{:S(2)}) copy-start(f32[4,2304]{1,0:T(4,128)} %param.9) | copy-start | bytes 110596
  7.2 63.0 %copy-start.5 = (bf16[128,2304]{1,0:T(8,128)(2,1)S(1)}, bf16[128,2304]{1,0:T(8,128)(2,1)}, u32[]{:S(2)}) copy-start(bf16[128,2304]{1,0:T(8,128)(2,1)} %param.8) | copy-start | bytes 1769476
  7.2 185.4 %all-gather.14.cloned.1.call-start = ((), (), s32[]{:S(2)}) async-start(), calls=%async_computation.9 | async-start | bytes 19464192 | tf_op jit(solution)/shard_map/all_gather | solution.py:120
  67.9 267.3 %all-gather.16.cloned.1.call-start = ((), (), s32[]{:S(2)}) async-start(), calls=%async_computation.10 | async-start | bytes 4718592 | tf_op jit(solution)/shard_map/all_gather | solution.py:148
  69.3 142.0 %copy-start.21 = (f32[128,128]{0,1:T(8,128)}, f32[128,128]{0,1:T(8,128)S(1)}, u32[]{:S(2)}) copy-start(f32[128,128]{0,1:T(8,128)S(1)} %get-tuple-element.42) | copy-start | bytes 196612
  69.6 142.5 %copy-start.24 = (f32[128,128]{1,0:T(8,128)}, f32[128,128]{1,0:T(8,128)S(1)}, u32[]{:S(2)}) copy-start(f32[128,128]{1,0:T(8,128)S(1)} %copy.124) | copy-start | bytes 196612
  70.2 132.7 %copy-start.31 = (f32[2304]{0:T(1024)}, f32[2304]{0:T(1024)S(1)}, u32[]{:S(2)}) copy-start(f32[2304]{0:T(1024)S(1)} %get-tuple-element.19) | copy-start | bytes 27652
  70.2 332.7 %copy-start.33 = (f32[2304]{0:T(1024)}, f32[2304]{0:T(1024)S(1)}, u32[]{:S(2)}) copy-start(f32[2304]{0:T(1024)S(1)} %get-tuple-element.20) | copy-start | bytes 27652
  70.4 132.5 %copy-start.54 = (f32[128]{0:T(128)}, f32[128]{0:T(128)S(1)}, u32[]{:S(2)}) copy-start(f32[128]{0:T(128)S(1)} %fusion.61) | copy-start | bytes 1540
  70.4 132.4 %copy-start.43 = (f32[128]{0:T(128)}, f32[128]{0:T(128)S(1)}, u32[]{:S(2)}) copy-start(f32[128]{0:T(128)S(1)} %fusion.70) | copy-start | bytes 1540
  70.7 132.2 %copy-start.14 = (bf16[128,2304]{1,0:T(8,128)(2,1)}, bf16[128,2304]{1,0:T(8,128)(2,1)S(1)}, u32[]{:S(2)}) copy-start(bf16[128,2304]{1,0:T(8,128)(2,1)S(1)} %fusion.53) | copy-start | bytes 1769476
  231.6 103.6 %copy-start.26 = (bf16[512,2,256]{2,1,0:T(2,128)(2,1)}, bf16[512,2,256]{2,1,0:T(2,128)(2,1)S(1)}, u32[]{:S(2)}) copy-start(bf16[512,2,256]{2,1,0:T(2,128)(2,1)S(1)} %get-tuple-element.34) | copy-start | bytes 1572868
  233.4 160.9 %all-gather.18.cloned.1.call-start = ((), (), s32[]{:S(2)}) async-start(), calls=%async_computation.11 | async-start | bytes 9732096 | tf_op jit(solution)/shard_map/all_gather | solution.py:121
  242.9 595.1 %all-gather.20.cloned.1.call-start = ((), (), s32[]{:S(2)}) async-start(), calls=%async_computation.12 | async-start | bytes 87588864 | tf_op jit(solution)/shard_map/all_gather | solution.py:122
  242.9 57.8 %copy-start.29 = (f32[18432]{0:T(1024)}, f32[18432]{0:T(1024)S(1)}, u32[]{:S(2)}) copy-start(f32[18432]{0:T(1024)S(1)} %convert_add_fusion.2) | copy-start | bytes 221188
  242.9 58.0 %copy-start.20 = (bf16[72,9216]{1,0:T(8,128)(2,1)S(1)}, bf16[72,9216]{1,0:T(8,128)(2,1)}, u32[]{:S(2)}) copy-start(bf16[72,9216]{1,0:T(8,128)(2,1)} %param.13) | copy-start | bytes 3981316
  300.8 775.9 %all-gather.22.cloned.1.call-start = ((), (), s32[]{:S(2)}) async-start(), calls=%async_computation.13 | async-start | bytes 43794432 | tf_op jit(solution)/shard_map/all_gather | solution.py:123
  360.0 34.2 %all-to-all-start.1 = ((bf16[4,128,512]{1,2,0:T(8,128)(2,1)}), bf16[4,128,512]{1,2,0:T(8,128)(2,1)S(1)}, u32[]{:S(2)}, u32[]{:S(2)}) async-start(bf16[4,128,512]{1,2,0:T(8,128)(2,1)} %copy.135), calls=%async_computation.1 | async-start | bytes 1048576 | tf_op jit(solution)/shard_map/all_to_all | solution.py:169
  401.5 436.5 %copy-start.45 = (f32[128]{0:T(128)}, f32[128]{0:T(128)S(1)}, u32[]{:S(2)}) copy-start(f32[128]{0:T(128)S(1)} %fusion.71) | copy-start | bytes 1540
  402.9 435.1 %copy-start.56 = (f32[128]{0:T(128)}, f32[128]{0:T(128)S(1)}, u32[]{:S(2)}) copy-start(f32[128]{0:T(128)S(1)} %get-tuple-element.24) | copy-start | bytes 1540
  402.9 435.1 %copy-start.47 = (f32[128]{0:T(128)}, f32[128]{0:T(128)S(1)}, u32[]{:S(2)}) copy-start(f32[128]{0:T(128)S(1)} %fusion.72) | copy-start | bytes 1540
  403.1 434.9 %copy-start.15 = (bf16[128,2304]{1,0:T(8,128)(2,1)}, bf16[128,2304]{1,0:T(8,128)(2,1)S(1)}, u32[]{:S(2)}) copy-start(bf16[128,2304]{1,0:T(8,128)(2,1)S(1)} %multiply_convert_fusion.4) | copy-start | bytes 1769476
  877.0 221.0 %copy-start = (bf16[128,9216]{1,0:T(8,128)(2,1)}, bf16[128,9216]{1,0:T(8,128)(2,1)S(1)}, u32[]{:S(2)}) copy-start(bf16[128,9216]{1,0:T(8,128)(2,1)S(1)} %multiply_convert_fusion.2) | copy-start | bytes 7077892
  1126.3 37.5 %copy-start.3 = (f32[128,2304]{1,0:T(8,128)S(1)}, f32[128,2304]{1,0:T(8,128)}, u32[]{:S(2)}) copy-start(f32[128,2304]{1,0:T(8,128)} %copy-done.2) | copy-start | bytes 3538948
  1126.3 37.5 %copy-start.16 = (bf16[128,2304]{1,0:T(8,128)(2,1)S(1)}, bf16[128,2304]{1,0:T(8,128)(2,1)}, u32[]{:S(2)}) copy-start(bf16[128,2304]{1,0:T(8,128)(2,1)} %param.15) | copy-start | bytes 1769476
  1126.3 37.5 %copy-start.34 = (f32[2304]{0:T(1024)S(1)}, f32[2304]{0:T(1024)}, u32[]{:S(2)}) copy-start(f32[2304]{0:T(1024)} %copy-done.33) | copy-start | bytes 27652
  1173.9 12.4 all-to-all-start.2
  1177.5 163.2 %reduce-scatter.8.cloned.1.call-start = ((), (), s32[]{:S(2)}) async-start(), calls=%async_computation.14 | async-start | bytes 4718592 | tf_op jit(solution)/shard_map/reduce_scatter | solution.py:215
  1253.9 127.6 %all-gather.28.cloned.1.call-start = ((), (), s32[]{:S(2)}) async-start(), calls=%async_computation.18 | async-start | bytes 2949120 | tf_op jit(solution)/shard_map/all_gather | solution.py:247
  1254.7 144.1 %all-gather.30.cloned.1.call-start = ((), (), s32[]{:S(2)}) async-start(), calls=%async_computation.19 | async-start | bytes 2621440 | tf_op jit(solution)/shard_map/all_gather | solution.py:251
  1255.4 169.1 %all-gather.24.cloned.1.call-start = ((), (), s32[]{:S(2)}) async-start(), calls=%async_computation.15 | async-start | bytes 2949120 | tf_op jit(solution)/shard_map/all_gather | solution.py:246
  1343.3 26.9 %all-to-all-start.3 = ((bf16[4,128,1024]{1,2,0:T(8,128)(2,1)}), bf16[4,128,1024]{1,2,0:T(8,128)(2,1)S(1)}, u32[]{:S(2)}, u32[]{:S(2)}) async-start(bf16[4,128,1024]{1,2,0:T(8,128)(2,1)} %copy.144), calls=%async_computation.4 | async-start | bytes 2097152 | tf_op jit(solution)/shard_map/all_to_all | solution.py:220
  1346.8 114.8 %all-gather.26.cloned.1.call-start = ((), (), s32[]{:S(2)}) async-start(), calls=%async_computation.16 | async-start | bytes 5242880 | tf_op jit(solution)/shard_map/all_gather | solution.py:250
  1375.0 112.3 %all-gather.36.cloned.1.call-start = ((), (), s32[]{:S(2)}) async-start(), calls=%async_computation.23 | async-start | bytes 2949120 | tf_op jit(solution)/shard_map/all_gather | solution.py:249
  1375.8 177.4 %all-gather.38.cloned.1.call-start = ((), (), s32[]{:S(2)}) async-start(), calls=%async_computation.24 | async-start | bytes 11796480 | tf_op jit(solution)/shard_map/all_gather | solution.py:253
  1376.4 202.5 %all-gather.32.cloned.1.call-start = ((), (), s32[]{:S(2)}) async-start(), calls=%async_computation.21 | async-start | bytes 2949120 | tf_op jit(solution)/shard_map/all_gather | solution.py:248
  1377.1 323.3 %all-gather.34.cloned.1.call-start = ((), (), s32[]{:S(2)}) async-start(), calls=%async_computation.22 | async-start | bytes 23592960 | tf_op jit(solution)/shard_map/all_gather | solution.py:252
  1381.4 392.6 %reduce-scatter.12.cloned.1.call-start = ((), (), s32[]{:S(2)}) async-start(), calls=%async_computation.20 | async-start | bytes 2654208 | tf_op jit(solution)/shard_map/reduce_scatter | solution.py:269
  1403.2 471.4 %reduce-scatter.10.cloned.1.call-start = ((), (), s32[]{:S(2)}) async-start(), calls=%async_computation.17 | async-start | bytes 5308416 | tf_op jit(solution)/shard_map/reduce_scatter | solution.py:266
  1468.1 590.1 %reduce-scatter.14.cloned.1.call-start = ((), (), s32[]{:S(2)}) async-start(), calls=%async_computation.25 | async-start | bytes 11943936 | tf_op jit(solution)/shard_map/reduce_scatter | solution.py:275
  1565.0 842.8 %reduce-scatter.16.cloned.1.call-start = ((), (), s32[]{:S(2)}) async-start(), calls=%async_computation.26 | async-start | bytes 23887872
  1721.3 54.6 %copy-start.6 = (bf16[128,2304]{1,0:T(8,128)(2,1)S(1)}, bf16[128,2304]{1,0:T(8,128)(2,1)}, u32[]{:S(2)}) copy-start(bf16[128,2304]{1,0:T(8,128)(2,1)} %param.8) | copy-start | bytes 1769476
  1721.3 54.6 %copy-start.12 = (bf16[128,4,4,256]{0,3,2,1:T(8,128)(2,1)S(1)}, bf16[128,4,4,256]{0,3,2,1:T(8,128)(2,1)}, u32[]{:S(2)}) copy-start(bf16[128,4,4,256]{0,3,2,1:T(8,128)(2,1)} %pad_maximum_fusion.2) | copy-start | bytes 3145732
  1721.3 54.6 %copy-start.32 = (f32[2304]{0:T(1024)S(1)}, f32[2304]{0:T(1024)}, u32[]{:S(2)}) copy-start(f32[2304]{0:T(1024)} %copy-done.31) | copy-start | bytes 27652
  1721.3 54.6 %copy-start.44 = (f32[128]{0:T(128)S(1)}, f32[128]{0:T(128)}, u32[]{:S(2)}) copy-start(f32[128]{0:T(128)} %copy-done.43) | copy-start | bytes 1540
  1775.9 56.4 %copy-start.55 = (f32[128]{0:T(128)S(1)}, f32[128]{0:T(128)}, u32[]{:S(2)}) copy-start(f32[128]{0:T(128)} %copy-done.54) | copy-start | bytes 1540
  1775.9 56.4 %copy-start.8 = (f32[128,2304]{1,0:T(8,128)S(1)}, f32[128,2304]{1,0:T(8,128)}, u32[]{:S(2)}) copy-start(f32[128,2304]{1,0:T(8,128)} %copy-done.7) | copy-start | bytes 3538948
  (32 other events, 318.8 us)
Sparse Core Ops, SparseCore 0:
  68.1 124.4 all-gather.13
  233.6 71.6 all-gather.15
  308.7 85.5 all-gather.17
  397.6 440.2 all-gather.19
  840.7 235.8 all-gather.21
  1254.0 86.6 reduce-scatter.7
  1342.9 32.4 all-gather.27
  1377.0 21.6 all-gather.29
  1400.4 24.0 all-gather.23
  1426.6 35.0 all-gather.25
  1463.3 24.0 all-gather.35
  1488.9 64.2 all-gather.37
  1554.8 24.0 all-gather.31
  1580.4 119.9 all-gather.33
  1704.8 69.2 reduce-scatter.11
  1778.6 95.9 reduce-scatter.9
  1878.5 179.7 reduce-scatter.13
  2062.0 345.8 reduce-scatter.15
where the time goes:
time: 2430 us; the launch traced here: 2420 us
  waiting for transfers between devices  1800 us (74%)
  matrix products  251 us (10%)
  other arithmetic  197 us (8%)
  blocking collectives  103 us (4%)
  local copies, waits for them, and re-layouts  38.1 us (2%)
    all_gather x1, waiting for transfers between devices, on_device(): lax.all_gather(eff_in, ('sp', 'hd'), axis=0, tiled=True)  435 us
    unnamed x19, waiting for transfers between devices  351 us
    all_gather x1, waiting for transfers between devices, on_device(): lax.all_gather(eff_down, ('sp', 'hd'), axis=0, tiled=True)  200 us
    reduce_scatter x1, waiting for transfers between devices, on_device(): lax.psum_scatter(term_down.astype(jnp.bfloat16), 'sp', scatter_dimension=...  181 us
    all_gather x1, waiting for transfers between devices, on_device(): lax.all_gather(eff_qkv, ('sp', 'hd'), axis=0, tiled=True)  122 us
    all_gather x1, waiting for transfers between devices, on_device(): lax.all_gather(d_both, 'hd', axis=0, tiled=True)  118 us
    dot_general x4, matrix products, contract_rows(): lax.dot_general(left, right, (((1,), (1,)), ((), ())), preferred_element_...  79.8 us
    reduce_scatter x1, waiting for transfers between devices, on_device(): lax.psum_scatter(spread[WINDOW:].astype(jnp.bfloat16), 'sp', scatter_dime...  77.8 us
  transfers between devices with their start and end apart: 21, of which 18 were waited for; matrix products, arithmetic and copies ran while one was open for 11% of the time, Pallas kernels for 0%

commit v1 on v0

v1 whole, which is shorter than its diff:
```python
import math

import jax
import jax.numpy as jnp
import numpy as np
from jax import lax
from jax.sharding import Mesh
from jax.sharding import PartitionSpec as P

FF = 9216
QH = 8
KVH = 4
HD = 256
WINDOW = 4096

EPSILON = 1e-06
SOFTCAP = 50.0
LEVEL_PULL = 0.75
TWO_PI = 2.0 * math.pi

FINE = ("zh", "zl", "x", "y", "c")
LINE = ("zh", "zl")
PLANE = ("x", "y", "c")
CUBE = ("zl", "x", "y")
SWAP = ((0, 1), (1, 0))

SINE = (
    25.13274115538592,
    -64.83582285607088,
    67.07662736368954,
    -38.49587868201696,
    14.049662842567686,
    -3.16160028673954,
)

f32 = jnp.float32
bf16 = jnp.bfloat16


def sin_turns(turns):
    part = turns - jnp.round(turns)
    square = part * part
    poly = SINE[5]
    for factor in SINE[4::-1]:
        poly = poly * square + factor
    return part * (0.25 - square) * poly


def rms_scale(vector_in, gain_row):
    mean_sq = jnp.mean(vector_in * vector_in, axis=-1, keepdims=True)
    return vector_in * lax.rsqrt(mean_sq + EPSILON) * (1.0 + gain_row)


def nested(weight, channel_scale):
    level = weight * (127.0 / channel_scale)
    level = level - (LEVEL_PULL / TWO_PI) * sin_turns(level)
    four = sin_turns(level * (1.0 / 16.0))
    two = sin_turns(level * (1.0 / 64.0))
    total = 3.0 * level - (16.0 * LEVEL_PULL / TWO_PI) * four - (64.0 * LEVEL_PULL / TWO_PI) * two
    return (channel_scale / 381.0) * total


def rotate(vector_in, cosine, sine_tab):
    half_dim = vector_in.shape[-1] // 2
    first_half = vector_in[..., :half_dim]
    second_half = vector_in[..., half_dim:]
    return jnp.concatenate(
        [
            first_half * cosine - second_half * sine_tab,
            second_half * cosine + first_half * sine_tab,
        ],
        axis=-1,
    )


def rope_tables(position, head_dim):
    half_dim = head_dim // 2
    frequency = np.exp(np.arange(half_dim) * (-2.0 * math.log(10000.0) / head_dim)) / TWO_PI
    coarse = frequency.astype(jnp.bfloat16).astype(np.float32)
    fine = (frequency - coarse).astype(np.float32)
    place = position.astype(f32)[:, None]
    turns = place * coarse[None, :]
    turns = (turns - jnp.round(turns)) + place * fine[None, :]
    return (sin_turns(turns + 0.25), sin_turns(turns))


def doc_info(lengths, places):
    stop_at = jnp.cumsum(lengths, dtype=jnp.int32)
    starts = stop_at - lengths
    inside = starts[None, :] <= places[:, None]
    doc_index = jnp.sum(inside.astype(jnp.int32), axis=1) - 1
    doc_start = jnp.max(jnp.where(inside, starts[None, :], 0), axis=1)
    return (doc_index, places - doc_start)


def glu(gate_in, up_in):
    return jax.nn.gelu(gate_in, approximate=True) * up_in


def dot(left, right, dims, out=f32):
    return lax.dot_general(left, right, (dims, ((), ())), preferred_element_type=out)


ROWS = ((1,), (1,))
COLS = ((1,), (0,))
FIRST = ((0,), (0,))


def swap(value, axis):
    return lax.ppermute(value, axis, SWAP)


def gather_blocks(block, axes, orders):
    rows, width = block.shape
    part = width // len(orders)
    parts = []
    for i, order in enumerate(orders):
        held = block[:, i * part : (i + 1) * part].reshape((1,) * len(axes) + (rows, part))
        for axis in order:
            held = jnp.concatenate([held, swap(held, axis)], axis=axes.index(axis))
        parts.append(held)
    return jnp.concatenate(parts, axis=-1).reshape(-1, width)


def scatter_blocks(partial, axes, orders):
    width = partial.shape[-1]
    part = width // len(orders)
    blocks = partial.reshape((2,) * len(axes) + (-1, width))
    parts = []
    for i, order in enumerate(orders):
        held = blocks[..., i * part : (i + 1) * part]
        for axis in order:
            at = axes.index(axis)
            keep = lax.slice_in_dim(held, 0, 1, axis=at)
            send = lax.slice_in_dim(held, 1, 2, axis=at).astype(bf16)
            held = keep.astype(f32) + swap(send, axis).astype(f32)
        parts.append(held.reshape(-1, part))
    return jnp.concatenate(parts, axis=-1)


TOKEN_AXES = ("c", "x", "y")
PLANE_GATHER = (("x", "y", "c"), ("y", "x", "c"))
PLANE_SCATTER = (("c", "y", "x"), ("c", "x", "y"))
CUBE_GATHER = (("zl", "x", "y"), ("x", "y", "zl"), ("y", "zl", "x"))
CUBE_SCATTER = (("y", "x", "zl"), ("zl", "y", "x"), ("x", "zl", "y"))


def both(value, axis):
    if lax.axis_size(axis) != 2:
        return lax.all_gather(value, axis, axis=0)
    other = swap(value, axis)
    first = lax.axis_index(axis) == 0
    return jnp.stack([jnp.where(first, value, other), jnp.where(first, other, value)], axis=0)


def sum_both(value, axis, dim):
    if lax.axis_size(axis) != 2:
        moved = jnp.moveaxis(value, dim, 0)
        return lax.psum_scatter(moved.astype(bf16), axis, scatter_dimension=0, tiled=False)
    me = lax.axis_index(axis)
    send = lax.dynamic_index_in_dim(value, 1 - me, dim, keepdims=False).astype(bf16)
    keep = lax.dynamic_index_in_dim(value, me, dim, keepdims=False)
    return (keep.astype(f32) + swap(send, axis).astype(f32)).astype(bf16)


def max_both(value, axis):
    if lax.axis_size(axis) != 2:
        return lax.pmax(value, axis)
    return jnp.maximum(value, swap(value, axis))


def widen(part):
    cube, own, width = part.shape
    line = both(part, "zh")
    full = both(line, "c")
    return full.transpose(1, 2, 0, 3, 4).reshape(-1, width)


def narrow(grad, own):
    width = grad.shape[-1]
    split = grad.reshape(lax.axis_size("zh"), 8, 2, own, width)
    mine = sum_both(split, "c", 2)
    return sum_both(mine, "zh", 0)


def exchange(value, axes):
    return lax.all_to_all(value, axes, split_axis=0, concat_axis=0, tiled=True)


def on_device(tokens, gains, w_qkv, w_out, w_in, w_down, lengths, cotangent):
    line_count = lax.axis_size(LINE)
    line_index = lax.axis_index(LINE)
    core = lax.axis_index("c")
    x_index = lax.axis_index("x")
    y_index = lax.axis_index("y")
    tok_rows, model = tokens.shape
    own = w_qkv.shape[0]
    block_rows = 8 * tok_rows
    total_rows = line_count * block_rows
    root = math.sqrt(HD)
    slice_ff = FF // 8

    qkv_out = w_qkv.reshape(own, KVH, 2, 2, HD).transpose(1, 3, 0, 2, 4).reshape(8, own, 2 * HD)
    qkv_out = jnp.broadcast_to(qkv_out[None], (line_count, 8, own, 2 * HD))
    qkv_lat = exchange(qkv_out.reshape(line_count * 8, own, 2 * HD), FINE).reshape(model, 2 * HD)

    inputs = tokens.astype(f32)
    normed = rms_scale(inputs, gains[0]).astype(bf16)
    normed_all = gather_blocks(normed, TOKEN_AXES, PLANE_GATHER)

    in_lat = exchange(
        w_in.reshape(own, 2, 8, slice_ff).transpose(2, 0, 1, 3).reshape(8, own, 2 * slice_ff), CUBE
    )

    out_scale = jnp.max(jnp.abs(w_out.astype(f32)), axis=1) + EPSILON
    down_scale = jnp.max(jnp.abs(w_down.astype(f32)), axis=1) + EPSILON
    eff_out = nested(w_out.astype(f32), out_scale[:, None]).astype(bf16)
    eff_out = eff_out.reshape(own, 8, HD).transpose(1, 0, 2)
    eff_out = jnp.broadcast_to(eff_out[None], (line_count, 8, own, HD))
    head_out = exchange(eff_out.reshape(line_count * 8, own, HD), FINE).reshape(model, HD)

    eff_down = nested(w_down.astype(f32), down_scale[:, None]).astype(bf16)
    eff_down = exchange(eff_down.reshape(own, 8, slice_ff).transpose(1, 0, 2), CUBE)

    qkv_max = jnp.max(jnp.abs(qkv_lat), axis=0)
    qkv_scale = qkv_max.astype(f32) + EPSILON
    head_qkv = nested(qkv_lat.astype(f32), qkv_scale[None, :]).astype(bf16)

    in_max = max_both(max_both(jnp.max(jnp.abs(in_lat), axis=(0, 1)), "c"), "zh")
    in_scale = in_max.astype(f32) + EPSILON
    cols_in = widen(nested(in_lat.astype(f32), in_scale[None, None, :]).astype(bf16))
    cols_down = widen(eff_down)

    dev = jnp.arange(8, dtype=jnp.int32)
    dev = (
        ((dev // 2 % 2) ^ x_index) * 4 + ((dev % 2) ^ y_index) * 2 + ((dev // 4) ^ core)
    ).astype(jnp.int32)
    inner = (dev[:, None] * tok_rows + jnp.arange(tok_rows, dtype=jnp.int32)[None, :]).reshape(-1)
    q_places = line_index * block_rows + inner
    q_doc, position = doc_info(lengths, q_places)
    cosine, sine_tab = rope_tables(position, HD)

    mixed = dot(normed_all, head_qkv, COLS)
    query = rotate(mixed[:, :HD], cosine, sine_tab).astype(bf16)
    second = mixed[:, HD:]
    kv_own = jnp.where(core == 0, rotate(second, cosine, sine_tab), second).astype(bf16)

    reach = min(WINDOW, total_rows // 2)
    back = min(line_count - 1, -(-(reach - 1) // block_rows))
    shifted = [kv_own]
    for n in range(1, back + 1):
        shifted.append(
            lax.ppermute(kv_own, LINE, [(i, i + n) for i in range(line_count - n)])
        )
    kv_mine = jnp.stack(shifted[::-1], axis=0)
    kv_flip = swap(kv_mine, "c")
    half_block = block_rows // 2
    kv_flip = jnp.concatenate([kv_flip[:, half_block:], kv_flip[:, :half_block]], axis=1)
    key_rows = jnp.where(core == 0, kv_mine, kv_flip).reshape(-1, HD)
    value_rows = jnp.where(core == 0, kv_flip, kv_mine).reshape(-1, HD)
    k_places = jnp.concatenate(
        [q_places - n * block_rows for n in range(back, -1, -1)], axis=0
    )
    k_doc = doc_info(lengths, k_places)[0]
    distance = q_places[:, None] - k_places[None, :]
    allowed = (q_doc[:, None] == k_doc[None, :]) & (distance >= 0) & (distance < WINDOW)

    tanh_part = jnp.tanh(dot(query, key_rows, ROWS) * (1.0 / (root * SOFTCAP)))
    capped = jnp.where(allowed, SOFTCAP * tanh_part, -1e30)
    row_max = jnp.max(capped, axis=1, keepdims=True)
    exp_scores = jnp.exp(capped - row_max)
    row_total = jnp.sum(exp_scores, axis=1, keepdims=True)
    probs = exp_scores / row_total
    probs_low = probs.astype(bf16)
    heads = dot(probs_low, value_rows, COLS).astype(bf16)

    branch = scatter_blocks(dot(heads, head_out, ROWS, bf16), TOKEN_AXES, PLANE_SCATTER)
    middle = inputs + rms_scale(branch, gains[1])
    pre_mlp = rms_scale(middle, gains[2]).astype(bf16)

    pre_all = gather_blocks(pre_mlp, CUBE, CUBE_GATHER)
    gate_up = dot(pre_all, cols_in, COLS)
    gate_part = gate_up[:, :slice_ff]
    up_part = gate_up[:, slice_ff:]
    hidden = glu(gate_part, up_part).astype(bf16)
    down_out = scatter_blocks(dot(hidden, cols_down, ROWS, bf16), CUBE, CUBE_SCATTER)
    result = (middle + rms_scale(down_out, gains[3])).astype(bf16)

    grad_result = cotangent.astype(f32)
    d_down, gain_four = jax.vjp(rms_scale, down_out, gains[3])[1](grad_result)
    d_down = d_down.astype(bf16)
    d_down_all = gather_blocks(d_down, CUBE, CUBE_GATHER)
    part_down = dot(d_down_all, hidden, FIRST, bf16)
    d_hidden = dot(d_down_all, cols_down, COLS)
    d_gate, d_up = jax.vjp(glu, gate_part, up_part)[1](d_hidden)
    d_both = jnp.concatenate([d_gate, d_up], axis=1).astype(bf16)
    d_pre = scatter_blocks(dot(d_both, cols_in, ROWS, bf16), CUBE, CUBE_SCATTER)
    part_in = dot(pre_all, d_both, FIRST, bf16)

    grad_down = exchange(narrow(part_down, own), CUBE)
    grad_down = grad_down.transpose(1, 0, 2).reshape(own, FF).astype(f32)
    grad_in = exchange(narrow(part_in, own), CUBE)
    grad_in = grad_in.reshape(8, own, 2, slice_ff).transpose(1, 2, 0, 3)
    grad_in = grad_in.reshape(own, 2 * FF).astype(f32)

    d_mid_part, gain_three = jax.vjp(rms_scale, middle, gains[2])[1](d_pre)
    d_middle = grad_result + d_mid_part
    d_branch, gain_two = jax.vjp(rms_scale, branch, gains[1])[1](d_middle)
    d_branch_all = gather_blocks(d_branch.astype(bf16), TOKEN_AXES, PLANE_GATHER)
    d_heads = dot(d_branch_all, head_out, COLS).astype(bf16)
    part_out = dot(d_branch_all, heads, FIRST, bf16)
    grad_out = exchange(part_out.reshape(line_count * 8, own, HD), FINE)
    grad_out = jnp.sum(grad_out.reshape(line_count, 8, own, HD).astype(f32), axis=0)
    grad_out = grad_out.transpose(1, 0, 2).reshape(own, QH * HD)

    d_prob = dot(d_heads, value_rows, ROWS)
    delta = jnp.sum(probs * d_prob, axis=1, keepdims=True)
    d_raw = (probs * (d_prob - delta) * (1.0 - tanh_part * tanh_part)).astype(bf16)
    d_query = (dot(d_raw, key_rows, COLS) * (1.0 / root)).astype(bf16)
    d_keys = dot(d_raw, query, FIRST) * (1.0 / root)
    d_values = dot(probs_low, d_heads, FIRST)
    d_keys = d_keys.reshape(back + 1, block_rows, HD)
    d_values = d_values.reshape(back + 1, block_rows, HD)
    send = jnp.where(core == 0, d_values, d_keys).astype(bf16)
    send = jnp.concatenate([send[:, half_block:], send[:, :half_block]], axis=1)
    d_window = jnp.where(core == 0, d_keys, d_values) + swap(send, "c").astype(f32)
    d_kv = d_window[back]
    for n in range(1, back + 1):
        d_kv = d_kv + lax.ppermute(
            d_window[back - n].astype(bf16), LINE, [(i + n, i) for i in range(line_count - n)]
        ).astype(f32)
    d_kv = d_kv.astype(bf16).astype(f32)
    d_query_lin = rotate(d_query.astype(f32), cosine, -sine_tab)
    d_second = jnp.where(core == 0, rotate(d_kv, cosine, -sine_tab), d_kv)
    d_mixed = jnp.concatenate([d_query_lin, d_second], axis=1).astype(bf16)

    d_normed = scatter_blocks(dot(d_mixed, head_qkv, ROWS, bf16), TOKEN_AXES, PLANE_SCATTER)
    d_input_part, gain_one = jax.vjp(rms_scale, inputs, gains[0])[1](d_normed)
    grad_tokens = d_middle + d_input_part
    part_qkv = dot(normed_all, d_mixed, FIRST, bf16)
    grad_qkv = exchange(part_qkv.reshape(line_count * 8, own, 2 * HD), FINE)
    grad_qkv = jnp.sum(grad_qkv.reshape(line_count, 8, own, 2 * HD).astype(f32), axis=0)
    grad_qkv = grad_qkv.reshape(KVH, 2, own, 2, HD).transpose(2, 0, 3, 1, 4)
    grad_qkv = grad_qkv.reshape(own, KVH * 4 * HD)

    grad_gains = lax.psum(jnp.stack([gain_one, gain_two, gain_three, gain_four], axis=0), FINE)
    qkv_scales = lax.all_gather(qkv_scale, PLANE, axis=0).reshape(KVH, 2, 2, HD)
    qkv_scales = qkv_scales.transpose(0, 2, 1, 3).reshape(-1)
    in_scales = lax.all_gather(in_scale, CUBE, axis=0).reshape(8, 2, slice_ff)
    in_scales = in_scales.transpose(1, 0, 2).reshape(-1)
    column_scales = jnp.concatenate([qkv_scales, in_scales], axis=0)
    row_scales = jnp.stack([out_scale, down_scale], axis=0)
    return (
        result,
        grad_tokens,
        grad_qkv,
        grad_out,
        grad_in,
        grad_down,
        grad_gains,
        column_scales,
        row_scales,
    )


def solution(mesh):
    fine = Mesh(
        mesh.devices.reshape(mesh.shape["sp"] // 4, 2, 2, mesh.shape["hd"] // 2, 2), FINE
    )
    split = P(FINE, None)
    in_specs = (split, P(), split, split, split, split, P(), split)
    out_specs = (split, split, split, split, split, split, P(), P(), P(None, FINE))
    return jax.shard_map(
        on_device, mesh=fine, in_specs=in_specs, out_specs=out_specs, check_vma=False
    )
```

time: 2430 us -> 1140 us (0.47)
  waiting for transfers between devices: 1800 us -> 327 us
  starting transfers between devices: 11.9 us -> 253 us
  matrix products: 251 us -> 123 us
  local copies, waits for them, and re-layouts: 38.1 us -> 109 us
    all_gather x13 -> x0, waiting for transfers between devices: 1070 us -> none  [the longest x1 435 us: on_device(): lax.all_gather(eff_in, ('sp', 'hd'), axis=0, tiled=True)]
    unnamed x19 -> x0, waiting for transfers between devices: 351 us -> none
    reduce_scatter x4 -> x0, waiting for transfers between devices: 350 us -> none  [the longest x1 181 us: on_device(): lax.psum_scatter(term_down.astype(jnp.bfloat16), 'sp', scatter_dimension=...]
    ppermute x0 -> x76, waiting for transfers between devices: none -> 277 us  [the longest x72 277 us: swap(): return lax.ppermute(value, axis, SWAP)]
    ppermute x0 -> x76, starting transfers between devices: none -> 155 us  [the longest x72 144 us: swap(): return lax.ppermute(value, axis, SWAP)]
    dot_general x18, matrix products: 251 us -> 123 us  [dot(): lax.dot_general(left, right, (dims, ((), ())), preferred_element_type=out)]
    all_to_all x3 -> x8, starting transfers between devices: 11 us -> 97.4 us  [exchange(): return lax.all_to_all(value, axes, split_axis=0, concat_axis=0, tiled=True)]
    all_gather x0 -> x2, blocking collectives: none -> 76.8 us  [the longest x1 67.6 us: on_device(): in_scales = lax.all_gather(in_scale, CUBE, axis=0).reshape(8, 2, slice_ff)]
  transfers between devices with their start and end apart: 21 -> 84, of which waited for: 18 -> 41; matrix products, arithmetic and copies ran while one was open for 11% -> 29% of each run, Pallas kernels for 0% -> 0%
where the time goes in v1:
time: 1140 us; the launch traced here: 1130 us
  waiting for transfers between devices  327 us (29%)
  starting transfers between devices  253 us (22%)
  other arithmetic  199 us (17%)
  matrix products  123 us (11%)
  blocking collectives  119 us (10%)
  local copies, waits for them, and re-layouts  109 us (10%)
    ppermute x72, waiting for transfers between devices, swap(): return lax.ppermute(value, axis, SWAP)  277 us
    ppermute x72, starting transfers between devices, swap(): return lax.ppermute(value, axis, SWAP)  144 us
    dot_general x18, matrix products, dot(): lax.dot_general(left, right, (dims, ((), ())), preferred_element_type=out)  123 us
    all_to_all x8, starting transfers between devices, exchange(): return lax.all_to_all(value, axes, split_axis=0, concat_axis=0, tiled=True)  97.4 us
    all_gather x1, blocking collectives, on_device(): in_scales = lax.all_gather(in_scale, CUBE, axis=0).reshape(8, 2, slice_ff)  67.6 us
    all_to_all x8, waiting for transfers between devices, exchange(): return lax.all_to_all(value, axes, split_axis=0, concat_axis=0, tiled=True)  49.8 us
    psum x1, blocking collectives, on_device(): lax.psum(jnp.stack([gain_one, gain_two, gain_three, gain_four], axis=0),...  42.6 us
    another operation x8, other arithmetic, both(): jnp.stack([jnp.where(first, value, other), jnp.where(first, other, value)...  31.6 us
  transfers between devices with their start and end apart: 84, of which 41 were waited for; matrix products, arithmetic and copies ran while one was open for 29% of the time, Pallas kernels for 0%

profile of v1, /device:TPU:0, one launch (start us, length us, event | category | flops | bytes accessed | tf_op | source)
XLA Modules:
  0.0 1133.1 jit_solution(18279161102895099541)
XLA Ops:
  5.3 7.3 all-to-all-start
  21.6 7.0 reshape.499
  31.9 5.8 collective-permute-done.3
  43.6 23.5 %all-to-all-done = bf16[32,72,512]{2,1,0:T(8,128)(2,1)S(1)} async-done(((bf16[32,72,512]{2,1,0:T(8,128)(2,1)}), bf16[32,72,512]{2,1,0:T(8,128)(2,1)S(1)}, u32[]{:S(2)}, u32[]{:S(2)}) %all-to-all-start) | async-done | bytes 2359328 | tf_op jit(solution)/shard_map/all_to_all | solution.py:187
  72.3 7.2 multiply_convert_fusion.6
  90.3 25.4 %collective-permute-done.1 = bf16[1,2,1,128,1152]{4,3,2,1,0:T(8,128)(2,1)S(1)} collective-permute-done((bf16[1,2,1,128,1152]{4,3,2,1,0:T(8,128)(2,1)S(1)}, bf16[1,2,1,128,1152]{4,3,2,1,0:T(8,128)(2,1)S(1)}, u32[]{:S(2)}, u32[]{:S(2)}) %collective-permute-start.1) | collective-permute-done | bytes 589856 | tf_op jit(solution)/shard_map/ppermute | solution.py:110
  128.1 5.1 maximum_maximum_fusion
  138.4 10.6 multiply_convert_fusion.5
  153.9 4.6 collective-permute-start.7
  175.0 80.3 %collective-permute-done.25 = bf16[2304]{0:T(1024)(128)(2,1)S(1)} collective-permute-done((bf16[2304]{0:T(1024)(128)(2,1)S(1)}, bf16[2304]{0:T(1024)(128)(2,1)S(1)}, u32[]{:S(2)}, u32[]{:S(2)}) %collective-permute-start.25) | collective-permute-done | bytes 4640 | tf_op jit(solution)/shard_map/ppermute | solution.py:110
  257.5 11.3 multiply_convert_fusion.1
  271.0 7.9 fusion.138
  310.1 20.0 %collective-permute-done.26 = bf16[8,72,2304]{2,1,0:T(8,128)(2,1)} collective-permute-done((bf16[8,72,2304]{2,1,0:T(8,128)(2,1)}, bf16[8,72,2304]{2,1,0:T(8,128)(2,1)}, u32[]{:S(2)}, u32[]{:S(2)}) %collective-permute-start.26) | collective-permute-done | bytes 2654240 | tf_op jit(solution)/shard_map/ppermute | solution.py:110
  330.1 12.2 %select_bitcast_fusion.5 = (bf16[1,8,72,2304]{3,2,1,0:T(8,128)(2,1)S(1)}, bf16[1,8,72,2304]{3,2,1,0:T(8,128)(2,1)S(1)}) fusion(bf16[8,72,2304]{2,1,0:T(8,128)(2,1)} %collective-permute-done.26, pred[]{:T(512)S(6)} %eq.17, f32[2304]{0:T(1024)S(1)} %get-tuple-element.78, bf16[8,72,2304]{2,1,0:T(8,128)(2,1)S(1)} %all-to-all-done.2, f32[2304]{0:T(1024)S(1)} %get-tuple-element.77), kind=kLoop, calls=%fused_computation.100 | loop fusion | flops 83607552 | bytes 10635265 | tf_op jit(solution)/shard_map/stack | solution.py:153
  346.4 12.3 %collective-permute-done.10 = bf16[1,2,1,128,1152]{4,3,2,1,0:T(8,128)(2,1)S(1)} collective-permute-done((bf16[1,2,1,128,1152]{4,3,2,1,0:T(8,128)(2,1)S(1)}, bf16[1,2,1,128,1152]{4,3,2,1,0:T(8,128)(2,1)S(1)}, u32[]{:S(2)}, u32[]{:S(2)}) %collective-permute-start.10) | collective-permute-done | bytes 589856 | tf_op jit(solution)/shard_map/ppermute | solution.py:110
  369.5 78.3 %collective-permute-start.15 = (bf16[1,1,1,128,768]{4,3,2,1,0:T(8,128)(2,1)S(1)}, bf16[1,1,1,128,768]{4,3,2,1,0:T(8,128)(2,1)S(1)}, u32[]{:S(2)}, u32[]{:S(2)}) collective-permute-start(bf16[1,1,1,128,768]{4,3,2,1,0:T(8,128)(2,1)S(1)} %get-tuple-element.71), channel_id=1, source_target_pairs={{0,8},{8,0},{1,9},{9,1},{2,10},{10,2},{3,11},{11,3},{4,12},{12,4},... | collective-permute-start | bytes 589832 | tf_op jit(solution)/shard_map/ppermute | solution.py:110
  471.1 7.3 collective-permute-done.23
  482.9 4.9 select_bitcast_fusion.1
  487.9 4.9 pad_maximum_fusion
  492.7 13.8 %fusion.145 = f32[1024,2304]{1,0:T(8,128)S(1)} fusion(bf16[1024,2304]{1,0:T(8,128)(2,1)S(1)} %bitcast.257, bf16[2304,2304]{1,0:T(8,128)(2,1)} %bitcast.265), kind=kOutput, calls=%fused_computation.394 | convolution fusion | flops 10871635968 | bytes 24772608 | tf_op jit(solution)/shard_map/dot_general | solution.py:101
  510.2 6.5 fusion.146
  519.1 12.9 %collective-permute-done.36 = bf16[2,1,2,128,768]{4,3,2,1,0:T(8,128)(2,1)S(1)} collective-permute-done((bf16[2,1,2,128,768]{4,3,2,1,0:T(8,128)(2,1)S(1)}, bf16[2,1,2,128,768]{4,3,2,1,0:T(8,128)(2,1)S(1)}, u32[]{:S(2)}, u32[]{:S(2)}) %collective-permute-start.36) | collective-permute-done | bytes 786464 | tf_op jit(solution)/shard_map/ppermute | solution.py:110
  558.5 5.0 collective-permute-done.45
  567.2 7.4 collective-permute-done.46
  581.2 6.6 copy.103
  596.8 14.4 %fusion.13 = (bf16[1024,1152]{1,0:T(8,128)(2,1)S(1)}, bf16[1024,1152]{1,0:T(8,128)(2,1)S(1)}) fusion(f32[1024,2304]{1,0:T(8,128)} %copy-done.17, bf16[1024,2304]{1,0:T(8,128)(2,1)S(1)} %bitcast.261, bf16[2304,1152]{1,0:T(8,128)(2,1)} %bitcast.273), kind=kOutput, calls=%fused_computation.41 | convolution fusion | flops 5464129536 | bytes 24182784 | tf_op jit(solution)/shard_map/dot_general | solution.py:101
  611.3 11.4 %fusion.14 = bf16[2,2,2,128,2304]{4,3,2,1,0:T(8,128)(2,1)S(1)} fusion(bf16[2304,2304,1,1,1]{1,0,4,3,2:T(8,128)(2,1)S(1)} %bitcast.268, bf16[2,2,2,128,1152]{4,3,2,1,0:T(8,128)(2,1)S(1)} %bitcast.308, bf16[2,2,2,128,1152]{4,3,2,1,0:T(8,128)(2,1)S(1)} %bitcast.307), kind=kOutput, calls=%fused_computation.45 | convolution fusion | flops 10881073152 | bytes 20054016 | tf_op jit(solution)/shard_map/dot_general | solution.py:101
  629.6 6.7 copy.105
  636.3 9.5 fusion.43
  682.9 14.5 %fusion.18 = bf16[2,8,2,72,2304]{4,3,2,1,0:T(8,128)(2,1)S(1)} fusion(bf16[2,8,2,72,1024]{4,3,2,1,0:T(8,128)(2,1)} %bitcast.279, bf16[1024,1152]{1,0:T(8,128)(2,1)} %copy-done.94, bf16[1024,1152]{1,0:T(8,128)(2,1)} %copy-done.93), kind=kOutput, calls=%fused_computation.51 | convolution fusion | flops 10881073152 | bytes 20054016 | tf_op jit(solution)/shard_map/dot_general | solution.py:101
  716.4 6.6 multiply_reduce_fusion
  723.0 14.3 %multiply_convert_fusion = bf16[1024,3072]{1,0:T(8,128)(2,1)S(1)} fusion(f32[1024,3072]{1,0:T(8,128)} %get-tuple-element.93, f32[1024,3072]{1,0:T(8,128)} %get-tuple-element.91, f32[1024]{0:T(1024)S(1)} %get-tuple-element.92, f32[1024]{0:T(1024)S(1)} %copy-done.63, f32[1024,3072]{1,0:T(8,128)} %copy-done.1, f32[1024]{0:T(1024)S(1)} %copy-done.61), kind=kLoop, calls=%fused_computation.2 | loop fusion | flops 28311552 | bytes 44052480 | tf_op jit(solution)/shard_map/convert_element_type | solution.py:318
  745.7 6.7 copy.101
  752.5 4.8 fusion.103
  757.2 4.8 all-to-all-start.5
  762.6 6.7 copy.99
  769.3 5.0 fusion.55
  784.2 22.3 %all-to-all-done.5 = bf16[32,72,256]{2,1,0:T(8,128)(2,1)} async-done(((bf16[32,72,256]{2,1,0:T(8,128)(2,1)}), bf16[32,72,256]{2,1,0:T(8,128)(2,1)}, u32[]{:S(2)}, u32[]{:S(2)}) %all-to-all-start.5) | async-done | bytes 1179680 | tf_op jit(solution)/shard_map/all_to_all | solution.py:187
  810.7 5.3 fusion.4
  821.1 6.4 fusion.75
  831.5 65.8 %all-to-all-start.4 = ((bf16[32,72,512]{2,1,0:T(8,128)(2,1)}), bf16[32,72,512]{2,1,0:T(8,128)(2,1)}, u32[]{:S(2)}, u32[]{:S(2)}) async-start(bf16[32,72,512]{2,1,0:T(8,128)(2,1)} %fusion.75), calls=%async_computation.4 | async-start | bytes 4718592 | tf_op jit(solution)/shard_map/all_to_all | solution.py:187
  897.4 10.2 multiply_convert_fusion.2
  907.6 9.2 all-gather.2
  916.9 67.6 %all-gather.3 = f32[8,1,2304]{2,1,0:T(1,128)S(1)} all-gather(f32[1,1,2304]{2,1,0:T(1,128)S(1)} %reshape.545), channel_id=3, replica_groups=mesh['zh'=2,'zl'=2,'x'=2,'y'=2,'c'=2] {'zl','x','y'}, dimensions={0}, use_global_device_ids=true | all-gather | bytes 82944 | tf_op jit(solution)/shard_map/all_gather | solution.py:349
  984.8 4.9 fusion.45
  1014.5 37.9 %collective-permute-done.70 = bf16[1,1,2,128,1152]{4,3,2,1,0:T(8,128)(2,1)S(1)} collective-permute-done((bf16[1,1,2,128,1152]{4,3,2,1,0:T(8,128)(2,1)S(1)}, bf16[1,1,2,128,1152]{4,3,2,1,0:T(8,128)(2,1)S(1)}, u32[]{:S(2)}, u32[]{:S(2)}) %collective-permute-start.70) | collective-permute-done | bytes 589856 | tf_op jit(solution)/shard_map/ppermute | solution.py:110
  1052.9 7.8 collective-permute-done.71
  1062.5 42.6 %psum.7 = f32[4,2304]{1,0:T(4,128)} all-reduce(f32[4,2304]{1,0:T(4,128)S(1)} %pad_maximum_fusion.35), channel_id=1, replica_groups=mesh['zh'=2,'zl'=2,'x'=2,'y'=2,'c'=2] {'zh','zl','x','y','c'}, use_global_device_ids=true, to_apply=%region_25.26 | all-reduce | flops 9216 | bytes 73728 | tf_op jit(solution)/shard_map/psum | solution.py:346
  (563 shorter events, 356.6 us)
Async XLA Ops:
  5.3 61.7 %all-to-all-start = ((bf16[32,72,512]{2,1,0:T(8,128)(2,1)}), bf16[32,72,512]{2,1,0:T(8,128)(2,1)S(1)}, u32[]{:S(2)}, u32[]{:S(2)}) async-start(bf16[32,72,512]{2,1,0:T(8,128)(2,1)} %bitcast.270), calls=%async_computation | async-start | bytes 4718592 | tf_op jit(solution)/shard_map/all_to_all | solution.py:187
  14.3 23.4 %collective-permute-start.3 = (bf16[1,1,1,128,1152]{4,3,2,1,0:T(8,128)(2,1)S(1)}, bf16[1,1,1,128,1152]{4,3,2,1,0:T(8,128)(2,1)}, u32[]{:S(2)}, u32[]{:S(2)}) collective-permute-start(bf16[1,1,1,128,1152]{4,3,2,1,0:T(8,128)(2,1)S(1)} %get-tuple-element.75), channel_id=1, source_target_pairs={{0,2},{2,0},{1,3},{3,1},{4,6},{6,4},{5,7},{7,5},{8,10},{10,8},{9,1... | collective-permute-start | bytes 884744 | tf_op jit(solution)/shard_map/ppermute | solution.py:110
  16.2 68.0 %collective-permute-start = (bf16[1,1,1,128,1152]{4,3,2,1,0:T(8,128)(2,1)S(1)}, bf16[1,1,1,128,1152]{4,3,2,1,0:T(8,128)(2,1)}, u32[]{:S(2)}, u32[]{:S(2)}) collective-permute-start(bf16[1,1,1,128,1152]{4,3,2,1,0:T(8,128)(2,1)S(1)} %get-tuple-element.74), channel_id=1, source_target_pairs={{0,4},{4,0},{1,5},{5,1},{2,6},{6,2},{3,7},{7,3},{8,12},{12,8},{9,1... | collective-permute-start | bytes 884744 | tf_op jit(solution)/shard_map/ppermute | solution.py:110
  39.6 48.3 %collective-permute-start.4 = (bf16[1,1,2,128,1152]{4,3,2,1,0:T(8,128)(2,1)}, bf16[1,1,2,128,1152]{4,3,2,1,0:T(8,128)(2,1)}, u32[]{:S(2)}, u32[]{:S(2)}) collective-permute-start(bf16[1,1,2,128,1152]{4,3,2,1,0:T(8,128)(2,1)} %pad_maximum_fusion.22), channel_id=1, source_target_pairs={{0,4},{4,0},{1,5},{5,1},{2,6},{6,2},{3,7},{7,3},{8,12},{12,8},{9,1... | collective-permute-start | bytes 1769480 | tf_op jit(solution)/shard_map/ppermute | solution.py:110
  68.5 65.6 %all-to-all-start.2 = ((bf16[8,72,2304]{2,1,0:T(8,128)(2,1)}), bf16[8,72,2304]{2,1,0:T(8,128)(2,1)S(1)}, u32[]{:S(2)}, u32[]{:S(2)}) async-start(bf16[8,72,2304]{2,1,0:T(8,128)(2,1)} %reshape.499), calls=%async_computation.2 | async-start | bytes 5308416 | tf_op jit(solution)/shard_map/all_to_all | solution.py:187
  85.2 30.5 %collective-permute-start.1 = (bf16[1,2,1,128,1152]{4,3,2,1,0:T(8,128)(2,1)S(1)}, bf16[1,2,1,128,1152]{4,3,2,1,0:T(8,128)(2,1)S(1)}, u32[]{:S(2)}, u32[]{:S(2)}) collective-permute-start(bf16[1,2,1,128,1152]{4,3,2,1,0:T(8,128)(2,1)S(1)} %pad_maximum_fusion.21), channel_id=1, source_target_pairs={{0,2},{2,0},{1,3},{3,1},{4,6},{6,4},{5,7},{7,5},{8,10},{10,8},{9,1... | collective-permute-start | bytes 1769480 | tf_op jit(solution)/shard_map/ppermute | solution.py:110
  90.3 37.8 %collective-permute-start.5 = (bf16[1,2,2,128,1152]{4,3,2,1,0:T(8,128)(2,1)}, bf16[1,2,2,128,1152]{4,3,2,1,0:T(8,128)(2,1)}, u32[]{:S(2)}, u32[]{:S(2)}) collective-permute-start(bf16[1,2,2,128,1152]{4,3,2,1,0:T(8,128)(2,1)} %pad_maximum_fusion.8), channel_id=1, source_target_pairs={{0,1},{1,0},{2,3},{3,2},{4,5},{5,4},{6,7},{7,6},{8,9},{9,8},{10,11... | collective-permute-start | bytes 3538952 | tf_op jit(solution)/shard_map/ppermute | solution.py:110
  134.1 30.4 %all-to-all-start.3 = ((bf16[8,72,1152]{2,1,0:T(8,128)(2,1)}), bf16[8,72,1152]{2,1,0:T(8,128)(2,1)}, u32[]{:S(2)}, u32[]{:S(2)}) async-start(bf16[8,72,1152]{2,1,0:T(8,128)(2,1)} %bitcast.278), calls=%async_computation.3 | async-start | bytes 2654208 | tf_op jit(solution)/shard_map/all_to_all | solution.py:187
  153.9 102.0 %collective-permute-start.7 = (bf16[1024,256]{1,0:T(8,128)(2,1)}, bf16[1024,256]{1,0:T(8,128)(2,1)}, u32[]{:S(2)}, u32[]{:S(2)}) collective-permute-start(bf16[1024,256]{1,0:T(8,128)(2,1)} %fusion.68), channel_id=1, source_target_pairs={{0,8},{8,16},{16,24},{1,9},{9,17},{17,25},{2,10},{10,18},{18,26},{... | collective-permute-start | bytes 1572872 | tf_op jit(solution)/shard_map/ppermute | solution.py:253
  158.5 97.4 %collective-permute-start.6 = (bf16[1024,256]{1,0:T(8,128)(2,1)}, bf16[1024,256]{1,0:T(8,128)(2,1)}, u32[]{:S(2)}, u32[]{:S(2)}) collective-permute-start(bf16[1024,256]{1,0:T(8,128)(2,1)} %fusion.68), channel_id=1, source_target_pairs={{0,16},{8,24},{1,17},{9,25},{2,18},{10,26},{3,19},{11,27},{4,20},{... | collective-permute-start | bytes 1572872 | tf_op jit(solution)/shard_map/ppermute | solution.py:253
  165.6 128.3 %all-to-all-start.1 = ((bf16[32,72,256]{2,1,0:T(8,128)(2,1)}), bf16[32,72,256]{2,1,0:T(8,128)(2,1)}, u32[]{:S(2)}, u32[]{:S(2)}) async-start(bf16[32,72,256]{2,1,0:T(8,128)(2,1)} %bitcast.283), calls=%async_computation.1 | async-start | bytes 2359296 | tf_op jit(solution)/shard_map/all_to_all | solution.py:187
  169.2 132.0 %collective-permute-start.28 = (bf16[8,72,1152]{2,1,0:T(8,128)(2,1)}, bf16[8,72,1152]{2,1,0:T(8,128)(2,1)}, u32[]{:S(2)}, u32[]{:S(2)}) collective-permute-start(bf16[8,72,1152]{2,1,0:T(8,128)(2,1)} %all-to-all-done.3), channel_id=1, source_target_pairs={{0,16},{16,0},{1,17},{17,1},{2,18},{18,2},{3,19},{19,3},{4,20},{20... | collective-permute-start | bytes 3981320 | tf_op jit(solution)/shard_map/ppermute | solution.py:110
  172.7 82.6 %collective-permute-start.25 = (bf16[2304]{0:T(1024)(128)(2,1)S(1)}, bf16[2304]{0:T(1024)(128)(2,1)S(1)}, u32[]{:S(2)}, u32[]{:S(2)}) collective-permute-start(bf16[2304]{0:T(1024)(128)(2,1)S(1)} %max.6), channel_id=1, source_target_pairs={{0,16},{16,0},{1,17},{17,1},{2,18},{18,2},{3,19},{19,3},{4,20},{20... | collective-permute-start | bytes 13832 | tf_op jit(solution)/shard_map/ppermute | solution.py:110
  268.8 61.2 %collective-permute-start.26 = (bf16[8,72,2304]{2,1,0:T(8,128)(2,1)}, bf16[8,72,2304]{2,1,0:T(8,128)(2,1)}, u32[]{:S(2)}, u32[]{:S(2)}) collective-permute-start(bf16[8,72,2304]{2,1,0:T(8,128)(2,1)} %multiply_convert_fusion.1), channel_id=1, source_target_pairs={{0,16},{16,0},{1,17},{17,1},{2,18},{18,2},{3,19},{19,3},{4,20},{20... | collective-permute-start | bytes 7962632 | tf_op jit(solution)/shard_map/ppermute | solution.py:110
  304.9 160.8 %collective-permute-start.29 = (bf16[2,8,72,1152]{3,2,1,0:T(8,128)(2,1)}, bf16[2,8,72,1152]{3,2,1,0:T(8,128)(2,1)}, u32[]{:S(2)}, u32[]{:S(2)}) collective-permute-start(bf16[2,8,72,1152]{3,2,1,0:T(8,128)(2,1)} %pad_maximum_fusion.3), channel_id=1, source_target_pairs={{0,1},{1,0},{2,3},{3,2},{4,5},{5,4},{6,7},{7,6},{8,9},{9,8},{10,11... | collective-permute-start | bytes 7962632 | tf_op jit(solution)/shard_map/ppermute | solution.py:110
  308.5 36.0 %collective-permute-start.13 = (bf16[1,1,2,128,1152]{4,3,2,1,0:T(8,128)(2,1)S(1)}, bf16[1,1,2,128,1152]{4,3,2,1,0:T(8,128)(2,1)}, u32[]{:S(2)}, u32[]{:S(2)}) collective-permute-start(bf16[1,1,2,128,1152]{4,3,2,1,0:T(8,128)(2,1)S(1)} %slice.646), channel_id=1, source_target_pairs={{0,4},{4,0},{1,5},{5,1},{2,6},{6,2},{3,7},{7,3},{8,12},{12,8},{9,1... | collective-permute-start | bytes 1769480 | tf_op jit(solution)/shard_map/ppermute | solution.py:110
  342.4 16.3 %collective-permute-start.10 = (bf16[1,2,1,128,1152]{4,3,2,1,0:T(8,128)(2,1)S(1)}, bf16[1,2,1,128,1152]{4,3,2,1,0:T(8,128)(2,1)S(1)}, u32[]{:S(2)}, u32[]{:S(2)}) collective-permute-start(bf16[1,2,1,128,1152]{4,3,2,1,0:T(8,128)(2,1)S(1)} %slice.647), channel_id=1, source_target_pairs={{0,2},{2,0},{1,3},{3,1},{4,6},{6,4},{5,7},{7,5},{8,10},{10,8},{9,1... | collective-permute-start | bytes 1769480 | tf_op jit(solution)/shard_map/ppermute | solution.py:110
  344.4 138.5 %collective-permute-start.27 = (bf16[2,8,72,2304]{3,2,1,0:T(8,128)(2,1)S(1)}, bf16[2,8,72,2304]{3,2,1,0:T(8,128)(2,1)}, u32[]{:S(2)}, u32[]{:S(2)}) collective-permute-start(bf16[2,8,72,2304]{3,2,1,0:T(8,128)(2,1)S(1)} %pad_maximum_fusion.1), channel_id=1, source_target_pairs={{0,1},{1,0},{2,3},{3,2},{4,5},{5,4},{6,7},{7,6},{8,9},{9,8},{10,11... | collective-permute-start | bytes 15925256 | tf_op jit(solution)/shard_map/ppermute | solution.py:110
  345.8 17.9 %collective-permute-start.14 = (bf16[1,1,1,128,1152]{4,3,2,1,0:T(8,128)(2,1)S(1)}, bf16[1,1,1,128,1152]{4,3,2,1,0:T(8,128)(2,1)S(1)}, u32[]{:S(2)}, u32[]{:S(2)}) collective-permute-start(bf16[1,1,1,128,1152]{4,3,2,1,0:T(8,128)(2,1)S(1)} %slice.656), channel_id=1, source_target_pairs={{0,2},{2,0},{1,3},{3,1},{4,6},{6,4},{5,7},{7,5},{8,10},{10,8},{9,1... | collective-permute-start | bytes 884744 | tf_op jit(solution)/shard_map/ppermute | solution.py:110
  366.5 81.3 %collective-permute-start.21 = (bf16[1,1,1,128,768]{4,3,2,1,0:T(8,128)(2,1)S(1)}, bf16[1,1,1,128,768]{4,3,2,1,0:T(8,128)(2,1)S(1)}, u32[]{:S(2)}, u32[]{:S(2)}) collective-permute-start(bf16[1,1,1,128,768]{4,3,2,1,0:T(8,128)(2,1)S(1)} %get-tuple-element.72), channel_id=1, source_target_pairs={{0,2},{2,0},{1,3},{3,1},{4,6},{6,4},{5,7},{7,5},{8,10},{10,8},{9,1... | collective-permute-start | bytes 589832 | tf_op jit(solution)/shard_map/ppermute | solution.py:110
  368.1 82.6 %collective-permute-start.18 = (bf16[1,1,1,128,768]{4,3,2,1,0:T(8,128)(2,1)S(1)}, bf16[1,1,1,128,768]{4,3,2,1,0:T(8,128)(2,1)S(1)}, u32[]{:S(2)}, u32[]{:S(2)}) collective-permute-start(bf16[1,1,1,128,768]{4,3,2,1,0:T(8,128)(2,1)S(1)} %get-tuple-element.73), channel_id=1, source_target_pairs={{0,4},{4,0},{1,5},{5,1},{2,6},{6,2},{3,7},{7,3},{8,12},{12,8},{9,1... | collective-permute-start | bytes 589832 | tf_op jit(solution)/shard_map/ppermute | solution.py:110
  369.5 84.1 %collective-permute-start.15 = (bf16[1,1,1,128,768]{4,3,2,1,0:T(8,128)(2,1)S(1)}, bf16[1,1,1,128,768]{4,3,2,1,0:T(8,128)(2,1)S(1)}, u32[]{:S(2)}, u32[]{:S(2)}) collective-permute-start(bf16[1,1,1,128,768]{4,3,2,1,0:T(8,128)(2,1)S(1)} %get-tuple-element.71), channel_id=1, source_target_pairs={{0,8},{8,0},{1,9},{9,1},{2,10},{10,2},{3,11},{11,3},{4,12},{12,4},... | collective-permute-start | bytes 589832 | tf_op jit(solution)/shard_map/ppermute | solution.py:110
  459.0 19.4 %collective-permute-start.23 = (bf16[2,1,2,128,768]{4,3,2,1,0:T(8,128)(2,1)}, bf16[2,1,2,128,768]{4,3,2,1,0:T(8,128)(2,1)S(1)}, u32[]{:S(2)}, u32[]{:S(2)}) collective-permute-start(bf16[2,1,2,128,768]{4,3,2,1,0:T(8,128)(2,1)} %pad_maximum_fusion.17), channel_id=1, source_target_pairs={{0,4},{4,0},{1,5},{5,1},{2,6},{6,2},{3,7},{7,3},{8,12},{12,8},{9,1... | collective-permute-start | bytes 2359304 | tf_op jit(solution)/shard_map/ppermute | solution.py:110
  461.6 16.8 %collective-permute-start.20 = (bf16[1,2,2,128,768]{4,3,2,1,0:T(8,128)(2,1)}, bf16[1,2,2,128,768]{4,3,2,1,0:T(8,128)(2,1)}, u32[]{:S(2)}, u32[]{:S(2)}) collective-permute-start(bf16[1,2,2,128,768]{4,3,2,1,0:T(8,128)(2,1)} %pad_maximum_fusion.16), channel_id=1, source_target_pairs={{0,8},{8,0},{1,9},{9,1},{2,10},{10,2},{3,11},{11,3},{4,12},{12,4},... | collective-permute-start | bytes 2359304 | tf_op jit(solution)/shard_map/ppermute | solution.py:110
  465.1 15.3 %collective-permute-start.17 = (bf16[2,2,1,128,768]{4,3,2,1,0:T(8,128)(2,1)}, bf16[2,2,1,128,768]{4,3,2,1,0:T(8,128)(2,1)}, u32[]{:S(2)}, u32[]{:S(2)}) collective-permute-start(bf16[2,2,1,128,768]{4,3,2,1,0:T(8,128)(2,1)} %pad_maximum_fusion.15), channel_id=1, source_target_pairs={{0,2},{2,0},{1,3},{3,1},{4,6},{6,4},{5,7},{7,5},{8,10},{10,8},{9,1... | collective-permute-start | bytes 2359304 | tf_op jit(solution)/shard_map/ppermute | solution.py:110
  516.8 15.2 %collective-permute-start.36 = (bf16[2,1,2,128,768]{4,3,2,1,0:T(8,128)(2,1)S(1)}, bf16[2,1,2,128,768]{4,3,2,1,0:T(8,128)(2,1)S(1)}, u32[]{:S(2)}, u32[]{:S(2)}) collective-permute-start(bf16[2,1,2,128,768]{4,3,2,1,0:T(8,128)(2,1)S(1)} %slice.468), channel_id=1, source_target_pairs={{0,4},{4,0},{1,5},{5,1},{2,6},{6,2},{3,7},{7,3},{8,12},{12,8},{9,1... | collective-permute-start | bytes 2359304 | tf_op jit(solution)/shard_map/ppermute | solution.py:110
  517.2 19.0 %collective-permute-start.33 = (bf16[1,2,2,128,768]{4,3,2,1,0:T(8,128)(2,1)S(1)}, bf16[1,2,2,128,768]{4,3,2,1,0:T(8,128)(2,1)S(1)}, u32[]{:S(2)}, u32[]{:S(2)}) collective-permute-start(bf16[1,2,2,128,768]{4,3,2,1,0:T(8,128)(2,1)S(1)} %slice.462), channel_id=1, source_target_pairs={{0,8},{8,0},{1,9},{9,1},{2,10},{10,2},{3,11},{11,3},{4,12},{12,4},... | collective-permute-start | bytes 2359304 | tf_op jit(solution)/shard_map/ppermute | solution.py:110
  517.9 19.1 %collective-permute-start.30 = (bf16[2,2,1,128,768]{4,3,2,1,0:T(8,128)(2,1)S(1)}, bf16[2,2,1,128,768]{4,3,2,1,0:T(8,128)(2,1)S(1)}, u32[]{:S(2)}, u32[]{:S(2)}) collective-permute-start(bf16[2,2,1,128,768]{4,3,2,1,0:T(8,128)(2,1)S(1)} %slice.456), channel_id=1, source_target_pairs={{0,2},{2,0},{1,3},{3,1},{4,6},{6,4},{5,7},{7,5},{8,10},{10,8},{9,1... | collective-permute-start | bytes 2359304 | tf_op jit(solution)/shard_map/ppermute | solution.py:110
  566.4 13.7 %collective-permute-start.40 = (bf16[2,1,1,128,768]{4,3,2,1,0:T(8,128)(2,1)S(1)}, bf16[2,1,1,128,768]{4,3,2,1,0:T(8,128)(2,1)S(1)}, u32[]{:S(2)}, u32[]{:S(2)}) collective-permute-start(bf16[2,1,1,128,768]{4,3,2,1,0:T(8,128)(2,1)S(1)} %pad_maximum_fusion.29), channel_id=1, source_target_pairs={{0,4},{4,0},{1,5},{5,1},{2,6},{6,2},{3,7},{7,3},{8,12},{12,8},{9,1... | collective-permute-start | bytes 1179656 | tf_op jit(solution)/shard_map/ppermute | solution.py:110
  626.3 19.5 %collective-permute-start.54 = (bf16[2,1,2,128,768]{4,3,2,1,0:T(8,128)(2,1)}, bf16[2,1,2,128,768]{4,3,2,1,0:T(8,128)(2,1)}, u32[]{:S(2)}, u32[]{:S(2)}) collective-permute-start(bf16[2,1,2,128,768]{4,3,2,1,0:T(8,128)(2,1)} %slice.489), channel_id=1, source_target_pairs={{0,4},{4,0},{1,5},{5,1},{2,6},{6,2},{3,7},{7,3},{8,12},{12,8},{9,1... | collective-permute-start | bytes 2359304 | tf_op jit(solution)/shard_map/ppermute | solution.py:110
  626.3 22.1 %collective-permute-start.51 = (bf16[1,2,2,128,768]{4,3,2,1,0:T(8,128)(2,1)}, bf16[1,2,2,128,768]{4,3,2,1,0:T(8,128)(2,1)}, u32[]{:S(2)}, u32[]{:S(2)}) collective-permute-start(bf16[1,2,2,128,768]{4,3,2,1,0:T(8,128)(2,1)} %slice.483), channel_id=1, source_target_pairs={{0,8},{8,0},{1,9},{9,1},{2,10},{10,2},{3,11},{11,3},{4,12},{12,4},... | collective-permute-start | bytes 2359304 | tf_op jit(solution)/shard_map/ppermute | solution.py:110
  627.5 22.4 %collective-permute-start.48 = (bf16[2,2,1,128,768]{4,3,2,1,0:T(8,128)(2,1)}, bf16[2,2,1,128,768]{4,3,2,1,0:T(8,128)(2,1)}, u32[]{:S(2)}, u32[]{:S(2)}) collective-permute-start(bf16[2,2,1,128,768]{4,3,2,1,0:T(8,128)(2,1)} %slice.477), channel_id=1, source_target_pairs={{0,2},{2,0},{1,3},{3,1},{4,6},{6,4},{5,7},{7,5},{8,10},{10,8},{9,1... | collective-permute-start | bytes 2359304 | tf_op jit(solution)/shard_map/ppermute | solution.py:110
  672.8 30.9 %collective-permute-start.74 = (bf16[2,8,72,1152]{3,2,1,0:T(8,128)(2,1)S(1)}, bf16[2,8,72,1152]{3,2,1,0:T(8,128)(2,1)}, u32[]{:S(2)}, u32[]{:S(2)}) collective-permute-start(bf16[2,8,72,1152]{3,2,1,0:T(8,128)(2,1)S(1)} %dynamic-slice_bitcast_fusion.1), channel_id=1, source_target_pairs={{0,1},{1,0},{2,3},{3,2},{4,5},{5,4},{6,7},{7,6},{8,9},{9,8},{10,11... | collective-permute-start | bytes 7962632 | tf_op jit(solution)/shard_map/ppermute | solution.py:110
  677.2 20.3 %collective-permute-start.61 = (bf16[1,1,2,128,1152]{4,3,2,1,0:T(8,128)(2,1)S(1)}, bf16[1,1,2,128,1152]{4,3,2,1,0:T(8,128)(2,1)S(1)}, u32[]{:S(2)}, u32[]{:S(2)}) collective-permute-start(bf16[1,1,2,128,1152]{4,3,2,1,0:T(8,128)(2,1)S(1)} %pad_maximum_fusion.24), channel_id=1, source_target_pairs={{0,4},{4,0},{1,5},{5,1},{2,6},{6,2},{3,7},{7,3},{8,12},{12,8},{9,1... | collective-permute-start | bytes 1769480 | tf_op jit(solution)/shard_map/ppermute | solution.py:110
  682.9 14.8 %collective-permute-start.58 = (bf16[1,2,1,128,1152]{4,3,2,1,0:T(8,128)(2,1)}, bf16[1,2,1,128,1152]{4,3,2,1,0:T(8,128)(2,1)S(1)}, u32[]{:S(2)}, u32[]{:S(2)}) collective-permute-start(bf16[1,2,1,128,1152]{4,3,2,1,0:T(8,128)(2,1)} %pad_maximum_fusion.23), channel_id=1, source_target_pairs={{0,2},{2,0},{1,3},{3,1},{4,6},{6,4},{5,7},{7,5},{8,10},{10,8},{9,1... | collective-permute-start | bytes 1769480 | tf_op jit(solution)/shard_map/ppermute | solution.py:110
  697.6 12.5 %collective-permute-start.62 = (bf16[1,2,2,128,1152]{4,3,2,1,0:T(8,128)(2,1)S(1)}, bf16[1,2,2,128,1152]{4,3,2,1,0:T(8,128)(2,1)S(1)}, u32[]{:S(2)}, u32[]{:S(2)}) collective-permute-start(bf16[1,2,2,128,1152]{4,3,2,1,0:T(8,128)(2,1)S(1)} %pad_maximum_fusion.13), channel_id=1, source_target_pairs={{0,1},{1,0},{2,3},{3,2},{4,5},{5,4},{6,7},{7,6},{8,9},{9,8},{10,11... | collective-permute-start | bytes 3538952 | tf_op jit(solution)/shard_map/ppermute | solution.py:110
  703.7 107.0 %collective-permute-start.72 = (bf16[2,8,72,2304]{3,2,1,0:T(8,128)(2,1)}, bf16[2,8,72,2304]{3,2,1,0:T(8,128)(2,1)}, u32[]{:S(2)}, u32[]{:S(2)}) collective-permute-start(bf16[2,8,72,2304]{3,2,1,0:T(8,128)(2,1)} %dynamic-slice_bitcast_fusion), channel_id=1, source_target_pairs={{0,1},{1,0},{2,3},{3,2},{4,5},{5,4},{6,7},{7,6},{8,9},{9,8},{10,11... | collective-permute-start | bytes 15925256 | tf_op jit(solution)/shard_map/ppermute | solution.py:110
  708.3 67.7 %collective-permute-start.75 = (bf16[8,72,1152]{2,1,0:T(8,128)(2,1)}, bf16[8,72,1152]{2,1,0:T(8,128)(2,1)}, u32[]{:S(2)}, u32[]{:S(2)}) collective-permute-start(bf16[8,72,1152]{2,1,0:T(8,128)(2,1)} %dynamic-slice_bitcast_fusion.3), channel_id=1, source_target_pairs={{0,16},{16,0},{1,17},{17,1},{2,18},{18,2},{3,19},{19,3},{4,20},{20... | collective-permute-start | bytes 3981320 | tf_op jit(solution)/shard_map/ppermute | solution.py:110
  745.5 33.2 %collective-permute-start.63 = (bf16[3,1024,256]{2,1,0:T(8,128)(2,1)}, bf16[3,1024,256]{2,1,0:T(8,128)(2,1)}, u32[]{:S(2)}, u32[]{:S(2)}) collective-permute-start(bf16[3,1024,256]{2,1,0:T(8,128)(2,1)} %pad_maximum_fusion.6), channel_id=1, source_target_pairs={{0,1},{1,0},{2,3},{3,2},{4,5},{5,4},{6,7},{7,6},{8,9},{9,8},{10,11... | collective-permute-start | bytes 4718600 | tf_op jit(solution)/shard_map/ppermute | solution.py:110
  757.2 49.2 %all-to-all-start.5 = ((bf16[32,72,256]{2,1,0:T(8,128)(2,1)}), bf16[32,72,256]{2,1,0:T(8,128)(2,1)}, u32[]{:S(2)}, u32[]{:S(2)}) async-start(bf16[32,72,256]{2,1,0:T(8,128)(2,1)} %fusion.103), calls=%async_computation.5 | async-start | bytes 2359296 | tf_op jit(solution)/shard_map/all_to_all | solution.py:187
  781.6 36.3 %collective-permute-start.65 = (bf16[1024,256]{1,0:T(8,128)(2,1)}, bf16[1024,256]{1,0:T(8,128)(2,1)}, u32[]{:S(2)}, u32[]{:S(2)}) collective-permute-start(bf16[1024,256]{1,0:T(8,128)(2,1)} %get-tuple-element.55), channel_id=1, source_target_pairs={{16,0},{24,8},{17,1},{25,9},{18,2},{26,10},{19,3},{27,11},{20,4},{... | collective-permute-start | bytes 1572872 | tf_op jit(solution)/shard_map/ppermute | solution.py:329
  782.9 35.0 %collective-permute-start.64 = (bf16[1024,256]{1,0:T(8,128)(2,1)}, bf16[1024,256]{1,0:T(8,128)(2,1)}, u32[]{:S(2)}, u32[]{:S(2)}) collective-permute-start(bf16[1024,256]{1,0:T(8,128)(2,1)} %get-tuple-element.54), channel_id=1, source_target_pairs={{8,0},{16,8},{24,16},{9,1},{17,9},{25,17},{10,2},{18,10},{26,18},{... | collective-permute-start | bytes 1572872 | tf_op jit(solution)/shard_map/ppermute | solution.py:329
  806.4 25.1 %all-to-all-start.7 = ((bf16[8,72,1152]{2,1,0:T(8,128)(2,1)}), bf16[8,72,1152]{2,1,0:T(8,128)(2,1)}, u32[]{:S(2)}, u32[]{:S(2)}) async-start(bf16[8,72,1152]{2,1,0:T(8,128)(2,1)} %fusion.42), calls=%async_computation.7 | async-start | bytes 2654208 | tf_op jit(solution)/shard_map/all_to_all | solution.py:187
  817.9 179.2 %collective-permute-start.73 = (bf16[8,72,2304]{2,1,0:T(8,128)(2,1)}, bf16[8,72,2304]{2,1,0:T(8,128)(2,1)}, u32[]{:S(2)}, u32[]{:S(2)}) collective-permute-start(bf16[8,72,2304]{2,1,0:T(8,128)(2,1)} %dynamic-slice_bitcast_fusion.2), channel_id=1, source_target_pairs={{0,16},{16,0},{1,17},{17,1},{2,18},{18,2},{3,19},{19,3},{4,20},{20... | collective-permute-start | bytes 7962632 | tf_op jit(solution)/shard_map/ppermute | solution.py:110
  831.5 169.6 %all-to-all-start.4 = ((bf16[32,72,512]{2,1,0:T(8,128)(2,1)}), bf16[32,72,512]{2,1,0:T(8,128)(2,1)}, u32[]{:S(2)}, u32[]{:S(2)}) async-start(bf16[32,72,512]{2,1,0:T(8,128)(2,1)} %fusion.75), calls=%async_computation.4 | async-start | bytes 4718592 | tf_op jit(solution)/shard_map/all_to_all | solution.py:187
  1001.1 119.3 %all-to-all-start.6 = ((bf16[8,72,2304]{2,1,0:T(8,128)(2,1)}), bf16[8,72,2304]{2,1,0:T(8,128)(2,1)S(1)}, u32[]{:S(2)}, u32[]{:S(2)}) async-start(bf16[8,72,2304]{2,1,0:T(8,128)(2,1)} %fusion.6), calls=%async_computation.6 | async-start | bytes 5308416 | tf_op jit(solution)/shard_map/all_to_all | solution.py:187
  1007.7 44.7 %collective-permute-start.70 = (bf16[1,1,2,128,1152]{4,3,2,1,0:T(8,128)(2,1)S(1)}, bf16[1,1,2,128,1152]{4,3,2,1,0:T(8,128)(2,1)S(1)}, u32[]{:S(2)}, u32[]{:S(2)}) collective-permute-start(bf16[1,1,2,128,1152]{4,3,2,1,0:T(8,128)(2,1)S(1)} %slice.644), channel_id=1, source_target_pairs={{0,4},{4,0},{1,5},{5,1},{2,6},{6,2},{3,7},{7,3},{8,12},{12,8},{9,1... | collective-permute-start | bytes 1769480 | tf_op jit(solution)/shard_map/ppermute | solution.py:110
  1009.7 42.9 %collective-permute-start.67 = (bf16[1,2,1,128,1152]{4,3,2,1,0:T(8,128)(2,1)S(1)}, bf16[1,2,1,128,1152]{4,3,2,1,0:T(8,128)(2,1)S(1)}, u32[]{:S(2)}, u32[]{:S(2)}) collective-permute-start(bf16[1,2,1,128,1152]{4,3,2,1,0:T(8,128)(2,1)S(1)} %slice.645), channel_id=1, source_target_pairs={{0,2},{2,0},{1,3},{3,1},{4,6},{6,4},{5,7},{7,5},{8,10},{10,8},{9,1... | collective-permute-start | bytes 1769480 | tf_op jit(solution)/shard_map/ppermute | solution.py:110
  (141 other events, 2295.5 us)

commit v2 on v1

v2 whole, which is shorter than its diff:
```python
import math

import jax
import jax.numpy as jnp
import numpy as np
from jax import lax
from jax.experimental import pallas as pl
from jax.experimental.pallas import tpu as pltpu
from jax.sharding import Mesh
from jax.sharding import PartitionSpec as P

FF = 9216
QH = 8
KVH = 4
HD = 256
WINDOW = 4096

EPSILON = 1e-06
SOFTCAP = 50.0
LEVEL_PULL = 0.75
TWO_PI = 2.0 * math.pi

FINE = ("zh", "zl", "x", "y", "c")
LINE = ("zh", "zl")
PLANE = ("x", "y", "c")
CUBE = ("zl", "x", "y")
SWAP = ((0, 1), (1, 0))

SINE = (
    25.13274115538592,
    -64.83582285607088,
    67.07662736368954,
    -38.49587868201696,
    14.049662842567686,
    -3.16160028673954,
)

f32 = jnp.float32
bf16 = jnp.bfloat16


def sin_turns(turns):
    part = turns - jnp.round(turns)
    square = part * part
    poly = SINE[5]
    for factor in SINE[4::-1]:
        poly = poly * square + factor
    return part * (0.25 - square) * poly


def rms_scale(vector_in, gain_row):
    mean_sq = jnp.mean(vector_in * vector_in, axis=-1, keepdims=True)
    return vector_in * lax.rsqrt(mean_sq + EPSILON) * (1.0 + gain_row)


def nested(weight, channel_scale):
    level = weight * (127.0 / channel_scale)
    level = level - (LEVEL_PULL / TWO_PI) * sin_turns(level)
    four = sin_turns(level * (1.0 / 16.0))
    two = sin_turns(level * (1.0 / 64.0))
    total = 3.0 * level - (16.0 * LEVEL_PULL / TWO_PI) * four - (64.0 * LEVEL_PULL / TWO_PI) * two
    return (channel_scale / 381.0) * total


def rotate(vector_in, cosine, sine_tab):
    half_dim = vector_in.shape[-1] // 2
    first_half = vector_in[..., :half_dim]
    second_half = vector_in[..., half_dim:]
    return jnp.concatenate(
        [
            first_half * cosine - second_half * sine_tab,
            second_half * cosine + first_half * sine_tab,
        ],
        axis=-1,
    )


def rope_tables(position, head_dim):
    half_dim = head_dim // 2
    frequency = np.exp(np.arange(half_dim) * (-2.0 * math.log(10000.0) / head_dim)) / TWO_PI
    coarse = frequency.astype(jnp.bfloat16).astype(np.float32)
    fine = (frequency - coarse).astype(np.float32)
    place = position.astype(f32)[:, None]
    turns = place * coarse[None, :]
    turns = (turns - jnp.round(turns)) + place * fine[None, :]
    return (sin_turns(turns + 0.25), sin_turns(turns))


def doc_info(lengths, places):
    stop_at = jnp.cumsum(lengths, dtype=jnp.int32)
    starts = stop_at - lengths
    inside = starts[None, :] <= places[:, None]
    doc_index = jnp.sum(inside.astype(jnp.int32), axis=1) - 1
    doc_start = jnp.max(jnp.where(inside, starts[None, :], 0), axis=1)
    return (doc_index, places - doc_start)


def glu(gate_in, up_in):
    return jax.nn.gelu(gate_in, approximate=True) * up_in


def dot(left, right, dims, out=f32):
    return lax.dot_general(left, right, (dims, ((), ())), preferred_element_type=out)


ROWS = ((1,), (1,))
COLS = ((1,), (0,))
FIRST = ((0,), (0,))


def swap(value, axis):
    return lax.ppermute(value, axis, SWAP)


def gather_blocks(block, axes, orders):
    rows, width = block.shape
    part = width // len(orders)
    parts = []
    for i, order in enumerate(orders):
        held = block[:, i * part : (i + 1) * part].reshape((1,) * len(axes) + (rows, part))
        for axis in order:
            held = jnp.concatenate([held, swap(held, axis)], axis=axes.index(axis))
        parts.append(held)
    return jnp.concatenate(parts, axis=-1).reshape(-1, width)


def scatter_blocks(partial, axes, orders):
    width = partial.shape[-1]
    part = width // len(orders)
    blocks = partial.reshape((2,) * len(axes) + (-1, width))
    parts = []
    for i, order in enumerate(orders):
        held = blocks[..., i * part : (i + 1) * part]
        for axis in order:
            at = axes.index(axis)
            keep = lax.slice_in_dim(held, 0, 1, axis=at)
            send = lax.slice_in_dim(held, 1, 2, axis=at).astype(bf16)
            held = keep.astype(f32) + swap(send, axis).astype(f32)
        parts.append(held.reshape(-1, part))
    return jnp.concatenate(parts, axis=-1)


TOKEN_AXES = ("c", "x", "y")
PLANE_GATHER = (("x", "y", "c"), ("y", "x", "c"))
PLANE_SCATTER = (("c", "y", "x"), ("c", "x", "y"))
CUBE_GATHER = (("zl", "x", "y"), ("x", "y", "zl"), ("y", "zl", "x"))
CUBE_SCATTER = (("y", "x", "zl"), ("zl", "y", "x"), ("x", "zl", "y"))


def after(value, *events):
    return lax.optimization_barrier((value,) + events)[0]


def both(value, axis):
    other = swap(value, axis)
    first = lax.axis_index(axis) == 0
    return jnp.stack([jnp.where(first, value, other), jnp.where(first, other, value)], axis=0)


def core_sum(grad, own):
    split = grad.reshape(lax.axis_size("zh"), 8, 2, own, grad.shape[-1])
    me = lax.axis_index("c")
    send = lax.dynamic_index_in_dim(split, 1 - me, 2, keepdims=False)
    keep = lax.dynamic_index_in_dim(split, me, 2, keepdims=False)
    return (keep.astype(f32) + swap(send, "c").astype(f32)).astype(bf16)


def line_sum(part):
    flat = part.reshape(-1, part.shape[-1])
    return lax.psum_scatter(flat, "zh", scatter_dimension=0, tiled=True).reshape(part.shape[1:])


def max_both(value, axis):
    return jnp.maximum(value, swap(value, axis))


def sum_all(value):
    for axis in ("c", "x", "y", "zl", "zh"):
        if lax.axis_size(axis) == 2:
            value = value + swap(value, axis)
        else:
            value = lax.psum(value, axis)
    return value


def shift(value, step):
    count = lax.axis_size(LINE)
    return lax.ppermute(value, LINE, [(i, i + step) for i in range(count) if 0 <= i + step < count])


def by_core(part):
    other = swap(part, "c")
    full = jnp.broadcast_to(part[:, :, None], part.shape[:2] + (2,) + part.shape[2:])
    full = lax.dynamic_update_slice_in_dim(full, other[:, :, None], 1 - lax.axis_index("c"), 2)
    return full.reshape(-1, part.shape[-1])


Q_ROWS = 128


def scores(q_ref, k_ref, low_ref, place_ref, k_place_ref):
    raw = dot(q_ref[...], k_ref[...], ROWS) * (1.0 / (math.sqrt(HD) * SOFTCAP))
    places = k_place_ref[...]
    allowed = (places >= low_ref[...]) & (places <= place_ref[...])
    return jnp.tanh(raw), allowed


def attend_kernel(q_ref, k_ref, v_ref, low_ref, place_ref, k_place_ref, out_ref, lse_ref):
    tanh_part, allowed = scores(q_ref, k_ref, low_ref, place_ref, k_place_ref)
    capped = jnp.where(allowed, SOFTCAP * tanh_part, -1e30)
    row_max = jnp.max(capped, axis=1, keepdims=True)
    exp_scores = jnp.exp(capped - row_max)
    row_total = jnp.sum(exp_scores, axis=1, keepdims=True)
    probs = (exp_scores * (1.0 / row_total)).astype(bf16)
    out_ref[...] = dot(probs, v_ref[...], COLS).astype(bf16)
    lse_ref[...] = row_max + jnp.log(row_total)


def attend_back_kernel(
    q_ref, k_ref, v_ref, low_ref, place_ref, k_place_ref, lse_ref, d_ref, dq_ref, dk_ref, dv_ref
):
    @pl.when(pl.program_id(0) == 0)
    def _():
        dk_ref[...] = jnp.zeros_like(dk_ref)
        dv_ref[...] = jnp.zeros_like(dv_ref)

    scale = 1.0 / math.sqrt(HD)
    tanh_part, allowed = scores(q_ref, k_ref, low_ref, place_ref, k_place_ref)
    probs = jnp.where(allowed, jnp.exp(SOFTCAP * tanh_part - lse_ref[...]), 0.0)
    dv_ref[...] += dot(probs.astype(bf16), d_ref[...], FIRST)
    d_prob = dot(d_ref[...], v_ref[...], ROWS)
    delta = jnp.sum(probs * d_prob, axis=1, keepdims=True)
    d_raw = (probs * (d_prob - delta) * (1.0 - tanh_part * tanh_part)).astype(bf16)
    dq_ref[...] = (dot(d_raw, k_ref[...], COLS) * scale).astype(bf16)
    dk_ref[...] += dot(d_raw, q_ref[...], FIRST) * scale


def attention_specs(rows, keys):
    q_spec = pl.BlockSpec((Q_ROWS, HD), lambda i: (i, 0))
    k_spec = pl.BlockSpec((keys, HD), lambda i: (0, 0))
    row_spec = pl.BlockSpec((Q_ROWS, 1), lambda i: (i, 0))
    place_spec = pl.BlockSpec((1, keys), lambda i: (0, 0))
    common = dict(
        grid=(rows // Q_ROWS,),
        compiler_params=pltpu.CompilerParams(
            dimension_semantics=("arbitrary",), vmem_limit_bytes=56 * 2**20
        ),
        cost_estimate=pl.CostEstimate(flops=1, bytes_accessed=1, transcendentals=0),
    )
    return q_spec, k_spec, row_spec, place_spec, common


def attend(query, key_rows, value_rows, low, place, k_place):
    rows, keys = query.shape[0], key_rows.shape[0]
    q_spec, k_spec, row_spec, place_spec, common = attention_specs(rows, keys)
    return pl.pallas_call(
        attend_kernel,
        out_shape=(
            jax.ShapeDtypeStruct((rows, HD), bf16),
            jax.ShapeDtypeStruct((rows, 1), f32),
        ),
        in_specs=[q_spec, k_spec, k_spec, row_spec, row_spec, place_spec],
        out_specs=(q_spec, row_spec),
        **common,
    )(query, key_rows, value_rows, low, place, k_place)


def attend_back(query, key_rows, value_rows, low, place, k_place, lse, d_heads):
    rows, keys = query.shape[0], key_rows.shape[0]
    q_spec, k_spec, row_spec, place_spec, common = attention_specs(rows, keys)
    return pl.pallas_call(
        attend_back_kernel,
        out_shape=(
            jax.ShapeDtypeStruct((rows, HD), bf16),
            jax.ShapeDtypeStruct((keys, HD), f32),
            jax.ShapeDtypeStruct((keys, HD), f32),
        ),
        in_specs=[q_spec, k_spec, k_spec, row_spec, row_spec, place_spec, row_spec, q_spec],
        out_specs=(q_spec, k_spec, k_spec),
        **common,
    )(query, key_rows, value_rows, low, place, k_place, lse, d_heads)


def exchange(value, axes):
    return lax.all_to_all(value, axes, split_axis=0, concat_axis=0, tiled=True)


def columns(weight, count):
    own, width = weight.shape
    return weight.reshape(own, count, width // count).transpose(1, 0, 2)


def uncolumns(parts):
    count, own, width = parts.shape
    return parts.transpose(1, 0, 2).reshape(own, count * width)


def on_device(tokens, gains, w_qkv, w_out, w_in, w_down, lengths, cotangent):
    line_count = lax.axis_size(LINE)
    line_index = lax.axis_index(LINE)
    core = lax.axis_index("c")
    x_index = lax.axis_index("x")
    y_index = lax.axis_index("y")
    tok_rows, model = tokens.shape
    own = w_qkv.shape[0]
    block_rows = 8 * tok_rows
    total_rows = line_count * block_rows
    slice_ff = FF // 8

    units = lax.optimization_barrier(columns(w_qkv, 16)).reshape(KVH, 2, 2, own, HD)
    qkv_out = units.transpose(0, 2, 1, 3, 4).reshape(8, 2, own, HD)
    qkv_out = jnp.broadcast_to(qkv_out[None], (line_count, 8, 2, own, HD))
    qkv_lat = exchange(qkv_out.reshape(line_count * 8, 2, own, HD), FINE)
    qkv_lat = qkv_lat.reshape(line_count, 8, 2, own, HD)

    inputs = tokens.astype(f32)
    normed = rms_scale(inputs, gains[0]).astype(bf16)
    normed_all = gather_blocks(normed, TOKEN_AXES, PLANE_GATHER)

    out_scale = jnp.max(jnp.abs(w_out.astype(f32)), axis=1) + EPSILON
    down_scale = jnp.max(jnp.abs(w_down.astype(f32)), axis=1) + EPSILON
    eff_out = nested(w_out.astype(f32), out_scale[:, None]).astype(bf16)
    eff_down = nested(w_down.astype(f32), down_scale[:, None]).astype(bf16)
    in_out = lax.optimization_barrier(columns(w_in, 16)).reshape(2, 8, own, slice_ff)
    in_own = exchange(after(in_out.transpose(1, 0, 2, 3), qkv_lat), CUBE)
    in_lat = lax.all_gather(in_own.transpose(1, 0, 2, 3), "zh", axis=0)
    down_own = exchange(after(columns(eff_down, 8), in_own), CUBE)
    down_lat = lax.all_gather(after(down_own, in_lat), "zh", axis=0)
    eff_out = jnp.broadcast_to(columns(eff_out, 8)[None], (line_count, 8, own, HD))
    head_out = exchange(after(eff_out.reshape(line_count * 8, own, HD), down_own), FINE)
    head_out = head_out.reshape(model, HD)

    qkv_max = jnp.max(jnp.abs(qkv_lat), axis=(0, 1, 3))
    qkv_scale = qkv_max.astype(f32) + EPSILON
    head_qkv = nested(qkv_lat.astype(f32), qkv_scale[None, None, :, None, :]).astype(bf16)
    head_q = head_qkv[:, :, 0].reshape(model, HD)
    head_kv = head_qkv[:, :, 1].reshape(model, HD)

    dev = jnp.arange(8, dtype=jnp.int32)
    dev = (
        ((dev // 2 % 2) ^ x_index) * 4 + ((dev % 2) ^ y_index) * 2 + ((dev // 4) ^ core)
    ).astype(jnp.int32)
    inner = (dev[:, None] * tok_rows + jnp.arange(tok_rows, dtype=jnp.int32)[None, :]).reshape(-1)
    q_places = line_index * block_rows + inner
    position = doc_info(lengths, q_places)[1]
    cosine, sine_tab = rope_tables(position, HD)

    second = dot(normed_all, head_kv, COLS)
    kv_own = jnp.where(core == 0, rotate(second, cosine, sine_tab), second).astype(bf16)

    reach = min(WINDOW, total_rows // 2)
    back = min(line_count - 1, -(-(reach - 1) // block_rows))
    shifted = [kv_own]
    for _ in range(back):
        shifted.append(shift(shifted[-1], 1))
    query = rotate(dot(normed_all, head_q, COLS), cosine, sine_tab).astype(bf16)

    def effective(lat):
        top = max_both(jnp.max(jnp.abs(lat), axis=(0, 1, 2)), "c")
        scale = top.astype(f32) + EPSILON
        return top, by_core(nested(lat.astype(f32), scale).astype(bf16))

    gate_top, cols_gate = effective(in_lat[:, 0])
    up_top, cols_up = effective(in_lat[:, 1])
    cols_down = by_core(down_lat)

    kv_mine = jnp.stack(shifted[::-1], axis=0)
    kv_flip = swap(kv_mine, "c")
    half_block = block_rows // 2
    kv_flip = jnp.concatenate([kv_flip[:, half_block:], kv_flip[:, :half_block]], axis=1)
    key_rows = jnp.where(core == 0, kv_mine, kv_flip).reshape(-1, HD)
    value_rows = jnp.where(core == 0, kv_flip, kv_mine).reshape(-1, HD)
    k_places = jnp.concatenate(
        [q_places - n * block_rows for n in range(back, -1, -1)], axis=0
    )
    place = q_places[:, None]
    low = jnp.maximum(q_places - position, q_places - (WINDOW - 1))[:, None]
    heads, lse = attend(query, key_rows, value_rows, low, place, k_places[None])

    branch = dot(after(heads, in_lat), head_out, ROWS, bf16)
    branch = scatter_blocks(branch, TOKEN_AXES, PLANE_SCATTER)
    middle = inputs + rms_scale(branch, gains[1])
    pre_mlp = rms_scale(middle, gains[2]).astype(bf16)

    pre_all = gather_blocks(pre_mlp, CUBE, CUBE_GATHER)
    gate_part = dot(pre_all, cols_gate, COLS)
    up_part = dot(pre_all, cols_up, COLS)
    hidden = glu(gate_part, up_part).astype(bf16)
    down_out = scatter_blocks(dot(hidden, cols_down, ROWS, bf16), CUBE, CUBE_SCATTER)
    result = (middle + rms_scale(down_out, gains[3])).astype(bf16)

    grad_result = cotangent.astype(f32)
    d_down, gain_four = jax.vjp(rms_scale, down_out, gains[3])[1](grad_result)
    d_down = d_down.astype(bf16)
    tops = [both(qkv_max.reshape(-1), "c").reshape(-1), gate_top, up_top]
    tops = after(jnp.concatenate(tops, axis=0), d_down)
    tops = both(both(both(tops, "y"), "x"), "zl")
    d_down_all = gather_blocks(d_down, CUBE, CUBE_GATHER)
    d_hidden = dot(after(d_down_all, tops), cols_down, COLS)
    d_gate, d_up = jax.vjp(glu, gate_part, up_part)[1](d_hidden)
    d_gate = d_gate.astype(bf16)
    d_up = d_up.astype(bf16)
    d_pre = (dot(d_gate, cols_gate, ROWS) + dot(d_up, cols_up, ROWS)).astype(bf16)
    part_down = core_sum(dot(d_down_all, hidden, FIRST, bf16), own)
    d_pre = after(d_pre, part_down)
    grad_down = exchange(line_sum(part_down), CUBE)
    part_gate = core_sum(dot(pre_all, after(d_gate, d_pre), FIRST, bf16), own)
    part_up = core_sum(dot(pre_all, after(d_up, d_pre), FIRST, bf16), own)
    part_in = jnp.stack([part_gate, part_up], axis=1)
    d_pre = after(scatter_blocks(d_pre, CUBE, CUBE_SCATTER), part_in)
    part_in = line_sum(part_in).transpose(1, 0, 2, 3)

    d_mid_part, gain_three = jax.vjp(rms_scale, middle, gains[2])[1](d_pre)
    d_middle = grad_result + d_mid_part
    d_branch, gain_two = jax.vjp(rms_scale, branch, gains[1])[1](d_middle)
    d_branch_all = gather_blocks(d_branch.astype(bf16), TOKEN_AXES, PLANE_GATHER)
    d_heads = dot(d_branch_all, head_out, COLS).astype(bf16)

    d_query, d_keys, d_values = attend_back(
        query, key_rows, value_rows, low, place, k_places[None], lse, d_heads
    )
    d_keys = d_keys.reshape(back + 1, block_rows, HD)
    d_values = d_values.reshape(back + 1, block_rows, HD)
    send = jnp.where(core == 0, d_values, d_keys).astype(bf16)
    send = jnp.concatenate([send[:, half_block:], send[:, :half_block]], axis=1)
    d_window = jnp.where(core == 0, d_keys, d_values) + swap(send, "c").astype(f32)
    d_kv = d_window[0]
    for n in range(1, back + 1):
        d_kv = d_window[n] + shift(d_kv.astype(bf16), -1).astype(f32)
    d_kv = d_kv.astype(bf16).astype(f32)
    d_query_lin = rotate(d_query.astype(f32), cosine, -sine_tab).astype(bf16)
    d_second = jnp.where(core == 0, rotate(d_kv, cosine, -sine_tab), d_kv).astype(bf16)

    d_mixed = (dot(d_query_lin, head_q, ROWS) + dot(d_second, head_kv, ROWS)).astype(bf16)
    d_normed = scatter_blocks(d_mixed, TOKEN_AXES, PLANE_SCATTER)
    d_input_part, gain_one = jax.vjp(rms_scale, inputs, gains[0])[1](d_normed)
    grad_tokens = d_middle + d_input_part

    grad_down = uncolumns(grad_down).astype(f32)
    part_out = dot(d_branch_all, heads, FIRST, bf16).reshape(line_count * 8, own, HD)
    grad_out = exchange(after(part_out, grad_down), FINE)
    part_q = dot(normed_all, d_query_lin, FIRST, bf16)
    part_kv = dot(normed_all, d_second, FIRST, bf16)
    part_qkv = jnp.stack(
        [part_q.reshape(line_count * 8, own, HD), part_kv.reshape(line_count * 8, own, HD)], axis=1
    )
    grad_qkv = exchange(after(part_qkv, grad_out), FINE)
    in_back = exchange(after(part_in, grad_qkv), CUBE)
    grad_out = jnp.sum(grad_out.reshape(line_count, 8, own, HD).astype(f32), axis=0)
    grad_out = uncolumns(grad_out)

    qkv_sum = jnp.sum(grad_qkv.reshape(line_count, 16, own, HD).astype(f32), axis=0)
    grad_qkv = qkv_sum.reshape(KVH, 2, 2, own, HD).transpose(0, 2, 1, 3, 4)
    grad_qkv = uncolumns(lax.optimization_barrier(grad_qkv).reshape(16, own, HD))
    grad_in = in_back.transpose(1, 0, 2, 3)
    grad_in = lax.optimization_barrier(grad_in).reshape(16, own, slice_ff)
    grad_in = uncolumns(grad_in).astype(f32)

    grad_gains = sum_all(jnp.stack([gain_one, gain_two, gain_three, gain_four], axis=0))

    tops = tops.astype(f32) + EPSILON
    qkv_tops = tops[0, :, :, : 4 * HD].reshape(KVH, 2, 2, HD).transpose(0, 2, 1, 3).reshape(-1)
    in_tops = tops[..., 4 * HD :].reshape(8, 2, slice_ff).transpose(1, 0, 2).reshape(-1)
    column_scales = jnp.concatenate([qkv_tops, in_tops], axis=0)
    row_scales = jnp.stack([out_scale, down_scale], axis=0)
    return (
        result,
        grad_tokens,
        grad_qkv,
        grad_out,
        grad_in,
        grad_down,
        grad_gains,
        column_scales,
        row_scales,
    )


def solution(mesh):
    fine = Mesh(
        mesh.devices.reshape(mesh.shape["sp"] // 4, 2, 2, mesh.shape["hd"] // 2, 2), FINE
    )
    split = P(FINE, None)
    in_specs = (split, P(), split, split, split, split, P(), split)
    out_specs = (split, split, split, split, split, split, P(), P(), P(None, FINE))
    return jax.shard_map(
        on_device, mesh=fine, in_specs=in_specs, out_specs=out_specs, check_vma=False
    )
```

time: 1140 us -> 1020 us (0.89)
  blocking collectives: 119 us -> 0 us
  waiting for transfers between devices: 327 us -> 445 us
  starting transfers between devices: 253 us -> 166 us
  other arithmetic: 199 us -> 124 us
  Pallas kernels: 0 us -> 42.2 us
  between operations: 2.91 us -> 16.7 us
    ppermute x4, waiting for transfers between devices: 0.01 us -> 153 us  [shift(): lax.ppermute(value, LINE, [(i, i + step) for i in range(count) if 0 <= i...]
    all_gather x2 -> x0, blocking collectives: 76.8 us -> none  [the longest x1 67.6 us: on_device(): in_scales = lax.all_gather(in_scale, CUBE, axis=0).reshape(8, 2, slice_ff)]
    ppermute x72 -> x79, starting transfers between devices: 144 us -> 92.8 us  [swap(): return lax.ppermute(value, axis, SWAP)]
    psum x1 -> x0, blocking collectives: 42.6 us -> none  [on_device(): lax.psum(jnp.stack([gain_one, gain_two, gain_three, gain_four], axis=0),...]
    pallas_call x0 -> x2, Pallas kernels: none -> 42.2 us  [the longest x1 25.8 us: attend_back(): pl.pallas_call(attend_back_kernel, out_shape=(jax.ShapeDtypeStruct((rows,...]
    all_to_all x8, starting transfers between devices: 97.4 us -> 56.5 us  [exchange(): return lax.all_to_all(value, axes, split_axis=0, concat_axis=0, tiled=True)]
    ppermute x72 -> x79, waiting for transfers between devices: 277 us -> 240 us  [swap(): return lax.ppermute(value, axis, SWAP)]
    another operation x8 -> x4, other arithmetic: 31.6 us -> 0.92 us  [both(): jnp.stack([jnp.where(first, value, other), jnp.where(first, other, value)...]
  transfers between devices with their start and end apart: 84 -> 95, of which waited for: 41 -> 51; matrix products, arithmetic and copies ran while one was open for 29% -> 27% of each run, Pallas kernels for 0% -> 4%
where the time goes in v2:
time: 1020 us; the launch traced here: 1010 us
  waiting for transfers between devices  445 us (44%)
  starting transfers between devices  166 us (16%)
  other arithmetic  124 us (12%)
  matrix products  112 us (11%)
  local copies, waits for them, and re-layouts  102 us (10%)
  Pallas kernels  42.2 us (4%)
  between operations  16.7 us (2%)
    ppermute x79, waiting for transfers between devices, swap(): return lax.ppermute(value, axis, SWAP)  240 us
    ppermute x4, waiting for transfers between devices, shift(): lax.ppermute(value, LINE, [(i, i + step) for i in range(count) if 0 <= i...  153 us
    dot_general x18, matrix products, dot(): lax.dot_general(left, right, (dims, ((), ())), preferred_element_type=out)  112 us
    ppermute x79, starting transfers between devices, swap(): return lax.ppermute(value, axis, SWAP)  92.8 us
    all_to_all x8, starting transfers between devices, exchange(): return lax.all_to_all(value, axes, split_axis=0, concat_axis=0, tiled=True)  56.5 us
    all_to_all x8, waiting for transfers between devices, exchange(): return lax.all_to_all(value, axes, split_axis=0, concat_axis=0, tiled=True)  51.3 us
    dot_general x4, local copies, waits for them, and re-layouts, dot(): lax.dot_general(left, right, (dims, ((), ())), preferred_element_type=out)  26.7 us
    pallas_call x1, Pallas kernels, attend_back(): pl.pallas_call(attend_back_kernel, out_shape=(jax.ShapeDtypeStruct((rows,...  25.8 us
  transfers between devices with their start and end apart: 95, of which 51 were waited for; matrix products, arithmetic and copies ran while one was open for 27% of the time, Pallas kernels for 4%

profile of v2, /device:TPU:0, one launch (start us, length us, event | category | flops | bytes accessed | tf_op | source)
XLA Modules:
  0.0 1008.1 jit_solution(5652532071048666767)
XLA Ops:
  10.2 7.3 all-to-all-start
  25.3 21.7 %collective-permute-done = bf16[1,1,1,128,1152]{4,3,2,1,0:T(8,128)(2,1)S(1)} collective-permute-done((bf16[1,1,1,128,1152]{4,3,2,1,0:T(8,128)(2,1)S(1)}, bf16[1,1,1,128,1152]{4,3,2,1,0:T(8,128)(2,1)S(1)}, u32[]{:S(2)}, u32[]{:S(2)}) %collective-permute-start) | collective-permute-done | bytes 294944 | tf_op jit(solution)/shard_map/ppermute | solution.py:112
  51.3 13.5 %collective-permute-done.1 = bf16[1,2,1,128,1152]{4,3,2,1,0:T(8,128)(2,1)S(1)} collective-permute-done((bf16[1,2,1,128,1152]{4,3,2,1,0:T(8,128)(2,1)S(1)}, bf16[1,2,1,128,1152]{4,3,2,1,0:T(8,128)(2,1)S(1)}, u32[]{:S(2)}, u32[]{:S(2)}) %collective-permute-start.1) | collective-permute-done | bytes 589856 | tf_op jit(solution)/shard_map/ppermute | solution.py:112
  66.0 6.0 all-to-all-done
  82.2 6.2 multiply_convert_fusion.5
  99.1 15.0 %all-to-all-done.1 = bf16[8,2,72,1152]{3,2,1,0:T(8,128)(2,1)} async-done(((bf16[8,2,72,1152]{3,2,1,0:T(8,128)(2,1)}), bf16[8,2,72,1152]{3,2,1,0:T(8,128)(2,1)}, u32[]{:S(2)}, u32[]{:S(2)}) %all-to-all-start.1) | async-done | bytes 2654240 | tf_op jit(solution)/shard_map/all_to_all | solution.py:285
  117.6 9.4 multiply_convert_fusion.4
  143.6 42.8 %collective-permute-done.6 = bf16[1024,256]{1,0:T(8,128)(2,1)S(1)} collective-permute-done((bf16[1024,256]{1,0:T(8,128)(2,1)S(1)}, bf16[1024,256]{1,0:T(8,128)(2,1)S(1)}, u32[]{:S(2)}, u32[]{:S(2)}) %collective-permute-start.6) | collective-permute-done | bytes 524320 | tf_op jit(solution)/shard_map/ppermute | solution.py:188
  186.4 9.2 collective-permute-start.7
  195.6 21.0 %collective-permute-done.7 = bf16[1024,256]{1,0:T(8,128)(2,1)S(1)} collective-permute-done((bf16[1024,256]{1,0:T(8,128)(2,1)S(1)}, bf16[1024,256]{1,0:T(8,128)(2,1)S(1)}, u32[]{:S(2)}, u32[]{:S(2)}) %collective-permute-start.7) | collective-permute-done | bytes 524320 | tf_op jit(solution)/shard_map/ppermute | solution.py:188
  222.3 25.0 %all-to-all-start.3 = ((bf16[32,72,256]{2,1,0:T(8,128)(2,1)}), bf16[32,72,256]{2,1,0:T(8,128)(2,1)}, u32[]{:S(2)}, u32[]{:S(2)}) async-start(bf16[32,72,256]{2,1,0:T(8,128)(2,1)} %bitcast.368), calls=%async_computation.3 | async-start | bytes 2359296 | tf_op jit(solution)/shard_map/all_to_all | solution.py:285
  259.0 16.4 %shard_map.169 = (bf16[1024,256]{1,0:T(8,128)(2,1)}, f32[1024,1]{1,0:T(8,128)}) custom-call(bf16[1024,256]{1,0:T(8,128)(2,1)} %pad_maximum_fusion.23.q_ref, bf16[3072,256]{1,0:T(8,128)(2,1)} %bitcast.322, bf16[3072,256]{1,0:T(8,128)(2,1)} %bitcast.320, s32[1024,1]{1,0:T(8,128)} %add_maximum_fusion.low_ref, s32[1024,1]{1,0:T(8,128)} %copy-done.13, ...), custom_call_target="tpu_custom_call" | custom-call | flops 1 | bytes 1 | tf_op jit(solution)/shard_map/pallas_call | solution.py:256
  294.8 21.9 %multiply_convert_fusion.1 = (bf16[2,8,72,1152]{3,2,1,0:T(8,128)(2,1)}, bf16[2,8,72,1152]{3,2,1,0:T(8,128)(2,1)}) fusion(f32[1152]{0:T(1024)S(1)} %fusion.128, f32[1152]{0:T(1024)S(1)} %get-tuple-element.60, bf16[2,2,8,72,1152]{4,3,2,1,0:T(8,128)(2,1)S(1)} %bitcast.304, f32[1152]{0:T(1024)S(1)} %fusion.126, f32[1152]{0:T(1024)S(1)} %get-tuple-element.62), kind=kLoop, calls=%fused_computation.56 | loop fusion | flops 161906688 | bytes 10635264 | tf_op jit(solution)/shard_map/convert_element_type | solution.py:361
  318.6 7.8 collective-permute-done.14
  328.4 15.9 %collective-permute-start.15 = (bf16[1,1,1,128,768]{4,3,2,1,0:T(8,128)(2,1)S(1)}, bf16[1,1,1,128,768]{4,3,2,1,0:T(8,128)(2,1)S(1)}, u32[]{:S(2)}, u32[]{:S(2)}) collective-permute-start(bf16[1,1,1,128,768]{4,3,2,1,0:T(8,128)(2,1)S(1)} %get-tuple-element.101), channel_id=1, source_target_pairs={{0,8},{8,0},{1,9},{9,1},{2,10},{10,2},{3,11},{11,3},{4,12},{12,4},... | collective-permute-start | bytes 589832 | tf_op jit(solution)/shard_map/ppermute | solution.py:112
  346.4 28.5 %collective-permute-done.15 = bf16[1,1,1,128,768]{4,3,2,1,0:T(8,128)(2,1)S(1)} collective-permute-done((bf16[1,1,1,128,768]{4,3,2,1,0:T(8,128)(2,1)S(1)}, bf16[1,1,1,128,768]{4,3,2,1,0:T(8,128)(2,1)S(1)}, u32[]{:S(2)}, u32[]{:S(2)}) %collective-permute-start.15) | collective-permute-done | bytes 196640 | tf_op jit(solution)/shard_map/ppermute | solution.py:112
  380.2 6.8 collective-permute-done.16
  410.1 6.3 fusion.159
  416.4 8.5 multiply_convert_fusion.3
  426.3 6.5 fusion.160
  436.2 14.2 %collective-permute-done.29 = bf16[2,2,1,128,768]{4,3,2,1,0:T(8,128)(2,1)S(1)} collective-permute-done((bf16[2,2,1,128,768]{4,3,2,1,0:T(8,128)(2,1)S(1)}, bf16[2,2,1,128,768]{4,3,2,1,0:T(8,128)(2,1)S(1)}, u32[]{:S(2)}, u32[]{:S(2)}) %collective-permute-start.29) | collective-permute-done | bytes 786464 | tf_op jit(solution)/shard_map/ppermute | solution.py:112
  485.4 5.8 collective-permute-done.39
  501.0 6.6 copy.288
  516.0 6.7 copy.287
  522.7 9.5 fusion.66
  536.3 14.7 %fusion.41 = (bf16[1024,1152]{1,0:T(8,128)(2,1)}, bf16[1024,1152]{1,0:T(8,128)(2,1)S(1)}) fusion(f32[1024,1152]{1,0:T(8,128)} %copy-done.96, f32[1024,1152]{1,0:T(8,128)} %get-tuple-element.128, bf16[1024,2304]{1,0:T(8,128)(2,1)S(1)} %bitcast.317, bf16[2304,1152]{1,0:T(8,128)(2,1)} %bitcast.342), kind=kOutput, calls=%fused_computation.63 | convolution fusion | flops 5464129536 | bytes 24182784 | tf_op jit(solution)/shard_map/dot_general | solution.py:103
  551.1 8.6 fusion.161
  559.8 10.9 %add_convert_fusion.1 = bf16[1024,2304]{1,0:T(8,128)(2,1)} fusion(f32[1024,2304]{1,0:T(8,128)} %fusion.161, bf16[1024,1152]{1,0:T(8,128)(2,1)} %get-tuple-element.37, bf16[2304,1152]{1,0:T(8,128)(2,1)S(1)} %bitcast.336), kind=kOutput, calls=%fused_computation.1 | convolution fusion | flops 5440536576 | bytes 21823488 | tf_op jit(solution)/shard_map/dot_general | solution.py:103
  578.8 6.8 fusion.64
  585.5 6.6 fusion.62
  599.1 5.7 collective-permute-done.53
  622.9 5.6 collective-permute-done.63
  633.8 8.4 collective-permute-done.64
  652.0 25.8 %shard_map.170 = (bf16[1024,256]{1,0:T(8,128)(2,1)}, f32[3072,256]{1,0:T(8,128)}, f32[3072,256]{1,0:T(8,128)}) custom-call(bf16[1024,256]{1,0:T(8,128)(2,1)} %pad_maximum_fusion.23.q_ref, bf16[3072,256]{1,0:T(8,128)(2,1)} %bitcast.323, bf16[3072,256]{1,0:T(8,128)(2,1)} %bitcast.321, s32[1024,1]{1,0:T(8,128)} %add_maximum_fusion.low_ref, ...), custom_call_target="tpu_custom_call" | custom-call | flops 1 | bytes 1 | tf_op jit(solution)/shard_map/pallas_call | solution.py:271
  682.6 6.7 copy.291
  689.5 5.2 copy.298
  712.2 6.7 copy.292
  718.9 5.0 fusion.111
  723.8 18.5 %collective-permute-done.70 = bf16[1024,256]{1,0:T(8,128)(2,1)} collective-permute-done((bf16[1024,256]{1,0:T(8,128)(2,1)}, bf16[1024,256]{1,0:T(8,128)(2,1)}, u32[]{:S(2)}, u32[]{:S(2)}) %collective-permute-start.70) | collective-permute-done | bytes 524320 | tf_op jit(solution)/shard_map/ppermute | solution.py:188
  746.0 5.0 fusion.121
  751.0 70.5 %collective-permute-done.71 = bf16[1024,256]{1,0:T(8,128)(2,1)S(1)} collective-permute-done((bf16[1024,256]{1,0:T(8,128)(2,1)S(1)}, bf16[1024,256]{1,0:T(8,128)(2,1)S(1)}, u32[]{:S(2)}, u32[]{:S(2)}) %collective-permute-start.71) | collective-permute-done | bytes 524320 | tf_op jit(solution)/shard_map/ppermute | solution.py:188
  830.6 5.8 add_convert_fusion
  843.3 28.0 %all-to-all-done.5 = bf16[32,72,256]{2,1,0:T(8,128)(2,1)S(1)} async-done(((bf16[32,72,256]{2,1,0:T(8,128)(2,1)}), bf16[32,72,256]{2,1,0:T(8,128)(2,1)S(1)}, u32[]{:S(2)}, u32[]{:S(2)}) %all-to-all-start.5) | async-done | bytes 1179680 | tf_op jit(solution)/shard_map/all_to_all | solution.py:285
  884.2 14.3 %collective-permute-done.49 = bf16[2,3328]{1,0:T(2,128)(2,1)S(1)} collective-permute-done((bf16[2,3328]{1,0:T(2,128)(2,1)S(1)}, bf16[2,3328]{1,0:T(2,128)(2,1)S(1)}, u32[]{:S(2)}, u32[]{:S(2)}) %collective-permute-start.49) | collective-permute-done | bytes 13344 | tf_op jit(solution)/shard_map/ppermute | solution.py:112
  898.9 18.6 %collective-permute-done.76 = bf16[1,1,2,128,1152]{4,3,2,1,0:T(8,128)(2,1)S(1)} collective-permute-done((bf16[1,1,2,128,1152]{4,3,2,1,0:T(8,128)(2,1)S(1)}, bf16[1,1,2,128,1152]{4,3,2,1,0:T(8,128)(2,1)S(1)}, u32[]{:S(2)}, u32[]{:S(2)}) %collective-permute-start.76) | collective-permute-done | bytes 589856 | tf_op jit(solution)/shard_map/ppermute | solution.py:112
  920.2 10.1 %collective-permute-done.77 = bf16[1,1,1,128,1152]{4,3,2,1,0:T(8,128)(2,1)S(1)} collective-permute-done((bf16[1,1,1,128,1152]{4,3,2,1,0:T(8,128)(2,1)S(1)}, bf16[1,1,1,128,1152]{4,3,2,1,0:T(8,128)(2,1)S(1)}, u32[]{:S(2)}, u32[]{:S(2)}) %collective-permute-start.77) | collective-permute-done | bytes 294944 | tf_op jit(solution)/shard_map/ppermute | solution.py:112
  936.6 4.8 all-to-all-start.7
  945.2 31.2 %collective-permute-done.79 = f32[4,2304]{1,0:T(4,128)S(1)} collective-permute-done((f32[4,2304]{1,0:T(4,128)S(1)}, f32[4,2304]{1,0:T(4,128)S(1)}, u32[]{:S(2)}, u32[]{:S(2)}) %collective-permute-start.79) | collective-permute-done | bytes 36896 | tf_op jit(solution)/shard_map/ppermute | solution.py:112
  (639 shorter events, 329.4 us)
Async XLA Ops:
  10.2 61.8 %all-to-all-start = ((bf16[32,2,72,256]{3,2,1,0:T(8,128)(2,1)}), bf16[32,2,72,256]{3,2,1,0:T(8,128)(2,1)S(1)}, u32[]{:S(2)}, u32[]{:S(2)}) async-start(bf16[32,2,72,256]{3,2,1,0:T(8,128)(2,1)} %bitcast.329), calls=%async_computation | async-start | bytes 4718592 | tf_op jit(solution)/shard_map/all_to_all | solution.py:285
  19.3 27.7 %collective-permute-start = (bf16[1,1,1,128,1152]{4,3,2,1,0:T(8,128)(2,1)S(1)}, bf16[1,1,1,128,1152]{4,3,2,1,0:T(8,128)(2,1)S(1)}, u32[]{:S(2)}, u32[]{:S(2)}) collective-permute-start(bf16[1,1,1,128,1152]{4,3,2,1,0:T(8,128)(2,1)S(1)} %get-tuple-element.104), channel_id=1, source_target_pairs={{0,4},{4,0},{1,5},{5,1},{2,6},{6,2},{3,7},{7,3},{8,12},{12,8},{9,1... | collective-permute-start | bytes 884744 | tf_op jit(solution)/shard_map/ppermute | solution.py:112
  21.1 26.0 %collective-permute-start.3 = (bf16[1,1,1,128,1152]{4,3,2,1,0:T(8,128)(2,1)S(1)}, bf16[1,1,1,128,1152]{4,3,2,1,0:T(8,128)(2,1)S(1)}, u32[]{:S(2)}, u32[]{:S(2)}) collective-permute-start(bf16[1,1,1,128,1152]{4,3,2,1,0:T(8,128)(2,1)S(1)} %get-tuple-element.105), channel_id=1, source_target_pairs={{0,2},{2,0},{1,3},{3,1},{4,6},{6,4},{5,7},{7,5},{8,10},{10,8},{9,1... | collective-permute-start | bytes 884744 | tf_op jit(solution)/shard_map/ppermute | solution.py:112
  48.1 31.8 %collective-permute-start.4 = (bf16[1,1,2,128,1152]{4,3,2,1,0:T(8,128)(2,1)}, bf16[1,1,2,128,1152]{4,3,2,1,0:T(8,128)(2,1)}, u32[]{:S(2)}, u32[]{:S(2)}) collective-permute-start(bf16[1,1,2,128,1152]{4,3,2,1,0:T(8,128)(2,1)} %pad_maximum_fusion.20), channel_id=1, source_target_pairs={{0,4},{4,0},{1,5},{5,1},{2,6},{6,2},{3,7},{7,3},{8,12},{12,8},{9,1... | collective-permute-start | bytes 1769480 | tf_op jit(solution)/shard_map/ppermute | solution.py:112
  66.0 28.0 %collective-permute-start.2 = (bf16[1,2,2,128,1152]{4,3,2,1,0:T(8,128)(2,1)}, bf16[1,2,2,128,1152]{4,3,2,1,0:T(8,128)(2,1)}, u32[]{:S(2)}, u32[]{:S(2)}) collective-permute-start(bf16[1,2,2,128,1152]{4,3,2,1,0:T(8,128)(2,1)} %pad_maximum_fusion.5), channel_id=1, source_target_pairs={{0,1},{1,0},{2,3},{3,2},{4,5},{5,4},{6,7},{7,6},{8,9},{9,8},{10,11... | collective-permute-start | bytes 3538952 | tf_op jit(solution)/shard_map/ppermute | solution.py:112
  75.4 38.7 %all-to-all-start.1 = ((bf16[8,2,72,1152]{3,2,1,0:T(8,128)(2,1)}), bf16[8,2,72,1152]{3,2,1,0:T(8,128)(2,1)}, u32[]{:S(2)}, u32[]{:S(2)}) async-start(bf16[8,2,72,1152]{3,2,1,0:T(8,128)(2,1)} %copy.279), calls=%async_computation.1 | async-start | bytes 5308416 | tf_op jit(solution)/shard_map/all_to_all | solution.py:285
  79.8 195.6 %all-gather.5.cloned.1.call-start = ((), (), s32[]{:S(2)}) async-start(), calls=%async_computation.12 | async-start | bytes 7962624 | tf_op jit(solution)/shard_map/all_gather | solution.py:326
  130.1 89.9 %all-to-all-start.2 = ((bf16[8,72,1152]{2,1,0:T(8,128)(2,1)}), bf16[8,72,1152]{2,1,0:T(8,128)(2,1)S(1)}, u32[]{:S(2)}, u32[]{:S(2)}) async-start(bf16[8,72,1152]{2,1,0:T(8,128)(2,1)} %copy.282), calls=%async_computation.2 | async-start | bytes 2654208 | tf_op jit(solution)/shard_map/all_to_all | solution.py:285
  139.4 47.0 %collective-permute-start.6 = (bf16[1024,256]{1,0:T(8,128)(2,1)S(1)}, bf16[1024,256]{1,0:T(8,128)(2,1)S(1)}, u32[]{:S(2)}, u32[]{:S(2)}) collective-permute-start(bf16[1024,256]{1,0:T(8,128)(2,1)S(1)} %fusion.85), channel_id=1, source_target_pairs={{0,8},{8,16},{16,24},{1,9},{9,17},{17,25},{2,10},{10,18},{18,26},{... | collective-permute-start | bytes 1572872 | tf_op jit(solution)/shard_map/ppermute | solution.py:188
  186.4 30.2 %collective-permute-start.7 = (bf16[1024,256]{1,0:T(8,128)(2,1)S(1)}, bf16[1024,256]{1,0:T(8,128)(2,1)S(1)}, u32[]{:S(2)}, u32[]{:S(2)}) collective-permute-start(bf16[1024,256]{1,0:T(8,128)(2,1)S(1)} %collective-permute-done.6), channel_id=1, source_target_pairs={{0,8},{8,16},{16,24},{1,9},{9,17},{17,25},{2,10},{10,18},{18,26},{... | collective-permute-start | bytes 1572872 | tf_op jit(solution)/shard_map/ppermute | solution.py:188
  217.9 37.4 %collective-permute-start.8 = (bf16[3,1024,256]{2,1,0:T(8,128)(2,1)}, bf16[3,1024,256]{2,1,0:T(8,128)(2,1)}, u32[]{:S(2)}, u32[]{:S(2)}) collective-permute-start(bf16[3,1024,256]{2,1,0:T(8,128)(2,1)} %pad_maximum_fusion.2), channel_id=1, source_target_pairs={{0,1},{1,0},{2,3},{3,2},{4,5},{5,4},{6,7},{7,6},{8,9},{9,8},{10,11... | collective-permute-start | bytes 4718600 | tf_op jit(solution)/shard_map/ppermute | solution.py:112
  222.3 55.5 %all-to-all-start.3 = ((bf16[32,72,256]{2,1,0:T(8,128)(2,1)}), bf16[32,72,256]{2,1,0:T(8,128)(2,1)}, u32[]{:S(2)}, u32[]{:S(2)}) async-start(bf16[32,72,256]{2,1,0:T(8,128)(2,1)} %bitcast.368), calls=%async_computation.3 | async-start | bytes 2359296 | tf_op jit(solution)/shard_map/all_to_all | solution.py:285
  247.4 132.8 %all-gather.7.cloned.1.call-start = ((), (), s32[]{:S(2)}) async-start(), calls=%async_computation.13 | async-start | bytes 3981312 | tf_op jit(solution)/shard_map/all_gather | solution.py:328
  285.5 414.5 %reduce-scatter.3.cloned.1.call-start = ((), (), s32[]{:S(2)}) async-start(), calls=%async_computation.10 | async-start | bytes 3981312 | tf_op jit(solution)/shard_map/reduce_scatter | solution.py:170
  291.6 25.6 %collective-permute-start.13 = (bf16[1,1,2,128,1152]{4,3,2,1,0:T(8,128)(2,1)S(1)}, bf16[1,1,2,128,1152]{4,3,2,1,0:T(8,128)(2,1)S(1)}, u32[]{:S(2)}, u32[]{:S(2)}) collective-permute-start(bf16[1,1,2,128,1152]{4,3,2,1,0:T(8,128)(2,1)S(1)} %slice.647), channel_id=1, source_target_pairs={{0,4},{4,0},{1,5},{5,1},{2,6},{6,2},{3,7},{7,3},{8,12},{12,8},{9,1... | collective-permute-start | bytes 1769480 | tf_op jit(solution)/shard_map/ppermute | solution.py:112
  293.4 24.7 %collective-permute-start.10 = (bf16[1,2,1,128,1152]{4,3,2,1,0:T(8,128)(2,1)S(1)}, bf16[1,2,1,128,1152]{4,3,2,1,0:T(8,128)(2,1)S(1)}, u32[]{:S(2)}, u32[]{:S(2)}) collective-permute-start(bf16[1,2,1,128,1152]{4,3,2,1,0:T(8,128)(2,1)S(1)} %slice.648), channel_id=1, source_target_pairs={{0,2},{2,0},{1,3},{3,1},{4,6},{6,4},{5,7},{7,5},{8,10},{10,8},{9,1... | collective-permute-start | bytes 1769480 | tf_op jit(solution)/shard_map/ppermute | solution.py:112
  316.7 74.5 %collective-permute-start.25 = (bf16[2,8,72,1152]{3,2,1,0:T(8,128)(2,1)}, bf16[2,8,72,1152]{3,2,1,0:T(8,128)(2,1)}, u32[]{:S(2)}, u32[]{:S(2)}) collective-permute-start(bf16[2,8,72,1152]{3,2,1,0:T(8,128)(2,1)} %get-tuple-element.68), channel_id=1, source_target_pairs={{0,1},{1,0},{2,3},{3,2},{4,5},{5,4},{6,7},{7,6},{8,9},{9,8},{10,11... | collective-permute-start | bytes 7962632 | tf_op jit(solution)/shard_map/ppermute | solution.py:112
  316.7 80.2 %collective-permute-start.27 = (bf16[2,8,72,1152]{3,2,1,0:T(8,128)(2,1)}, bf16[2,8,72,1152]{3,2,1,0:T(8,128)(2,1)}, u32[]{:S(2)}, u32[]{:S(2)}) collective-permute-start(bf16[2,8,72,1152]{3,2,1,0:T(8,128)(2,1)} %get-tuple-element.69), channel_id=1, source_target_pairs={{0,1},{1,0},{2,3},{3,2},{4,5},{5,4},{6,7},{7,6},{8,9},{9,8},{10,11... | collective-permute-start | bytes 7962632 | tf_op jit(solution)/shard_map/ppermute | solution.py:112
  328.4 46.5 %collective-permute-start.15 = (bf16[1,1,1,128,768]{4,3,2,1,0:T(8,128)(2,1)S(1)}, bf16[1,1,1,128,768]{4,3,2,1,0:T(8,128)(2,1)S(1)}, u32[]{:S(2)}, u32[]{:S(2)}) collective-permute-start(bf16[1,1,1,128,768]{4,3,2,1,0:T(8,128)(2,1)S(1)} %get-tuple-element.101), channel_id=1, source_target_pairs={{0,8},{8,0},{1,9},{9,1},{2,10},{10,2},{3,11},{11,3},{4,12},{12,4},... | collective-permute-start | bytes 589832 | tf_op jit(solution)/shard_map/ppermute | solution.py:112
  344.3 32.8 %collective-permute-start.21 = (bf16[1,1,1,128,768]{4,3,2,1,0:T(8,128)(2,1)S(1)}, bf16[1,1,1,128,768]{4,3,2,1,0:T(8,128)(2,1)S(1)}, u32[]{:S(2)}, u32[]{:S(2)}) collective-permute-start(bf16[1,1,1,128,768]{4,3,2,1,0:T(8,128)(2,1)S(1)} %get-tuple-element.102), channel_id=1, source_target_pairs={{0,2},{2,0},{1,3},{3,1},{4,6},{6,4},{5,7},{7,5},{8,10},{10,8},{9,1... | collective-permute-start | bytes 589832 | tf_op jit(solution)/shard_map/ppermute | solution.py:112
  345.8 32.1 %collective-permute-start.18 = (bf16[1,1,1,128,768]{4,3,2,1,0:T(8,128)(2,1)S(1)}, bf16[1,1,1,128,768]{4,3,2,1,0:T(8,128)(2,1)S(1)}, u32[]{:S(2)}, u32[]{:S(2)}) collective-permute-start(bf16[1,1,1,128,768]{4,3,2,1,0:T(8,128)(2,1)S(1)} %get-tuple-element.103), channel_id=1, source_target_pairs={{0,4},{4,0},{1,5},{5,1},{2,6},{6,2},{3,7},{7,3},{8,12},{12,8},{9,1... | collective-permute-start | bytes 589832 | tf_op jit(solution)/shard_map/ppermute | solution.py:112
  386.9 38.0 %collective-permute-start.28 = (bf16[2,8,72,1152]{3,2,1,0:T(8,128)(2,1)}, bf16[2,8,72,1152]{3,2,1,0:T(8,128)(2,1)S(1)}, u32[]{:S(2)}, u32[]{:S(2)}) collective-permute-start(bf16[2,8,72,1152]{3,2,1,0:T(8,128)(2,1)} %bitcast.375), channel_id=1, source_target_pairs={{0,1},{1,0},{2,3},{3,2},{4,5},{5,4},{6,7},{7,6},{8,9},{9,8},{10,11... | collective-permute-start | bytes 7962632 | tf_op jit(solution)/shard_map/ppermute | solution.py:112
  388.8 18.3 %collective-permute-start.17 = (bf16[2,2,1,128,768]{4,3,2,1,0:T(8,128)(2,1)S(1)}, bf16[2,2,1,128,768]{4,3,2,1,0:T(8,128)(2,1)S(1)}, u32[]{:S(2)}, u32[]{:S(2)}) collective-permute-start(bf16[2,2,1,128,768]{4,3,2,1,0:T(8,128)(2,1)S(1)} %pad_maximum_fusion.13), channel_id=1, source_target_pairs={{0,2},{2,0},{1,3},{3,1},{4,6},{6,4},{5,7},{7,5},{8,10},{10,8},{9,1... | collective-permute-start | bytes 2359304 | tf_op jit(solution)/shard_map/ppermute | solution.py:112
  390.4 18.0 %collective-permute-start.23 = (bf16[2,1,2,128,768]{4,3,2,1,0:T(8,128)(2,1)S(1)}, bf16[2,1,2,128,768]{4,3,2,1,0:T(8,128)(2,1)S(1)}, u32[]{:S(2)}, u32[]{:S(2)}) collective-permute-start(bf16[2,1,2,128,768]{4,3,2,1,0:T(8,128)(2,1)S(1)} %pad_maximum_fusion.15), channel_id=1, source_target_pairs={{0,4},{4,0},{1,5},{5,1},{2,6},{6,2},{3,7},{7,3},{8,12},{12,8},{9,1... | collective-permute-start | bytes 2359304 | tf_op jit(solution)/shard_map/ppermute | solution.py:112
  391.2 18.5 %collective-permute-start.20 = (bf16[1,2,2,128,768]{4,3,2,1,0:T(8,128)(2,1)S(1)}, bf16[1,2,2,128,768]{4,3,2,1,0:T(8,128)(2,1)S(1)}, u32[]{:S(2)}, u32[]{:S(2)}) collective-permute-start(bf16[1,2,2,128,768]{4,3,2,1,0:T(8,128)(2,1)S(1)} %pad_maximum_fusion.14), channel_id=1, source_target_pairs={{0,8},{8,0},{1,9},{9,1},{2,10},{10,2},{3,11},{11,3},{4,12},{12,4},... | collective-permute-start | bytes 2359304 | tf_op jit(solution)/shard_map/ppermute | solution.py:112
  434.8 17.8 %collective-permute-start.35 = (bf16[2,1,2,128,768]{4,3,2,1,0:T(8,128)(2,1)S(1)}, bf16[2,1,2,128,768]{4,3,2,1,0:T(8,128)(2,1)S(1)}, u32[]{:S(2)}, u32[]{:S(2)}) collective-permute-start(bf16[2,1,2,128,768]{4,3,2,1,0:T(8,128)(2,1)S(1)} %slice.475), channel_id=1, source_target_pairs={{0,4},{4,0},{1,5},{5,1},{2,6},{6,2},{3,7},{7,3},{8,12},{12,8},{9,1... | collective-permute-start | bytes 2359304 | tf_op jit(solution)/shard_map/ppermute | solution.py:112
  536.3 34.4 %collective-permute-start.51 = (bf16[2,8,72,1152]{3,2,1,0:T(8,128)(2,1)}, bf16[2,8,72,1152]{3,2,1,0:T(8,128)(2,1)}, u32[]{:S(2)}, u32[]{:S(2)}) collective-permute-start(bf16[2,8,72,1152]{3,2,1,0:T(8,128)(2,1)} %dynamic-slice_bitcast_fusion.2), channel_id=1, source_target_pairs={{0,1},{1,0},{2,3},{3,2},{4,5},{5,4},{6,7},{7,6},{8,9},{9,8},{10,11... | collective-permute-start | bytes 7962632 | tf_op jit(solution)/shard_map/ppermute | solution.py:112
  575.0 19.4 %collective-permute-start.52 = (bf16[2,2,1,128,768]{4,3,2,1,0:T(8,128)(2,1)S(1)}, bf16[2,2,1,128,768]{4,3,2,1,0:T(8,128)(2,1)S(1)}, u32[]{:S(2)}, u32[]{:S(2)}) collective-permute-start(bf16[2,2,1,128,768]{4,3,2,1,0:T(8,128)(2,1)S(1)} %slice.484), channel_id=1, source_target_pairs={{0,2},{2,0},{1,3},{3,1},{4,6},{6,4},{5,7},{7,5},{8,10},{10,8},{9,1... | collective-permute-start | bytes 2359304 | tf_op jit(solution)/shard_map/ppermute | solution.py:112
  575.6 20.6 %collective-permute-start.55 = (bf16[1,2,2,128,768]{4,3,2,1,0:T(8,128)(2,1)S(1)}, bf16[1,2,2,128,768]{4,3,2,1,0:T(8,128)(2,1)S(1)}, u32[]{:S(2)}, u32[]{:S(2)}) collective-permute-start(bf16[1,2,2,128,768]{4,3,2,1,0:T(8,128)(2,1)S(1)} %slice.490), channel_id=1, source_target_pairs={{0,8},{8,0},{1,9},{9,1},{2,10},{10,2},{3,11},{11,3},{4,12},{12,4},... | collective-permute-start | bytes 2359304 | tf_op jit(solution)/shard_map/ppermute | solution.py:112
  577.6 19.2 %collective-permute-start.58 = (bf16[2,1,2,128,768]{4,3,2,1,0:T(8,128)(2,1)S(1)}, bf16[2,1,2,128,768]{4,3,2,1,0:T(8,128)(2,1)S(1)}, u32[]{:S(2)}, u32[]{:S(2)}) collective-permute-start(bf16[2,1,2,128,768]{4,3,2,1,0:T(8,128)(2,1)S(1)} %slice.496), channel_id=1, source_target_pairs={{0,4},{4,0},{1,5},{5,1},{2,6},{6,2},{3,7},{7,3},{8,12},{12,8},{9,1... | collective-permute-start | bytes 2359304 | tf_op jit(solution)/shard_map/ppermute | solution.py:112
  592.4 22.2 %collective-permute-start.61 = (bf16[2,8,72,1152]{3,2,1,0:T(8,128)(2,1)S(1)}, bf16[2,8,72,1152]{3,2,1,0:T(8,128)(2,1)S(1)}, u32[]{:S(2)}, u32[]{:S(2)}) collective-permute-start(bf16[2,8,72,1152]{3,2,1,0:T(8,128)(2,1)S(1)} %dynamic-slice_bitcast_fusion.1), channel_id=1, source_target_pairs={{0,1},{1,0},{2,3},{3,2},{4,5},{5,4},{6,7},{7,6},{8,9},{9,8},{10,11... | collective-permute-start | bytes 7962632 | tf_op jit(solution)/shard_map/ppermute | solution.py:112
  592.7 22.6 %collective-permute-start.62 = (bf16[2,8,72,1152]{3,2,1,0:T(8,128)(2,1)S(1)}, bf16[2,8,72,1152]{3,2,1,0:T(8,128)(2,1)S(1)}, u32[]{:S(2)}, u32[]{:S(2)}) collective-permute-start(bf16[2,8,72,1152]{3,2,1,0:T(8,128)(2,1)S(1)} %dynamic-slice_bitcast_fusion), channel_id=1, source_target_pairs={{0,1},{1,0},{2,3},{3,2},{4,5},{5,4},{6,7},{7,6},{8,9},{9,8},{10,11... | collective-permute-start | bytes 7962632 | tf_op jit(solution)/shard_map/ppermute | solution.py:112
  633.8 297.1 %reduce-scatter.5.cloned.1.call-start = ((), (), s32[]{:S(2)}) async-start(), calls=%async_computation.11 | async-start | bytes 7962624 | tf_op jit(solution)/shard_map/reduce_scatter | solution.py:170
  681.5 22.7 %collective-permute-start.69 = (bf16[3,1024,256]{2,1,0:T(8,128)(2,1)}, bf16[3,1024,256]{2,1,0:T(8,128)(2,1)}, u32[]{:S(2)}, u32[]{:S(2)}) collective-permute-start(bf16[3,1024,256]{2,1,0:T(8,128)(2,1)} %pad_maximum_fusion.4), channel_id=1, source_target_pairs={{0,1},{1,0},{2,3},{3,2},{4,5},{5,4},{6,7},{7,6},{8,9},{9,8},{10,11... | collective-permute-start | bytes 4718600 | tf_op jit(solution)/shard_map/ppermute | solution.py:112
  689.5 21.4 %collective-permute-start.48 = (bf16[3328]{0:T(1024)(128)(2,1)S(1)}, bf16[3328]{0:T(1024)(128)(2,1)S(1)}, u32[]{:S(2)}, u32[]{:S(2)}) collective-permute-start(bf16[3328]{0:T(1024)(128)(2,1)S(1)} %pad_maximum_fusion.38), channel_id=1, source_target_pairs={{0,2},{2,0},{1,3},{3,1},{4,6},{6,4},{5,7},{7,5},{8,10},{10,8},{9,1... | collective-permute-start | bytes 19976 | tf_op jit(solution)/shard_map/ppermute | solution.py:112
  699.9 123.4 %all-to-all-start.4 = ((bf16[8,72,1152]{2,1,0:T(8,128)(2,1)}), bf16[8,72,1152]{2,1,0:T(8,128)(2,1)}, u32[]{:S(2)}, u32[]{:S(2)}) async-start(bf16[8,72,1152]{2,1,0:T(8,128)(2,1)} %bitcast.385), calls=%async_computation.5 | async-start | bytes 2654208 | tf_op jit(solution)/shard_map/all_to_all | solution.py:285
  709.5 32.8 %collective-permute-start.70 = (bf16[1024,256]{1,0:T(8,128)(2,1)}, bf16[1024,256]{1,0:T(8,128)(2,1)}, u32[]{:S(2)}, u32[]{:S(2)}) collective-permute-start(bf16[1024,256]{1,0:T(8,128)(2,1)} %fusion.110), channel_id=1, source_target_pairs={{8,0},{16,8},{24,16},{9,1},{17,9},{25,17},{10,2},{18,10},{26,18},{... | collective-permute-start | bytes 1572872 | tf_op jit(solution)/shard_map/ppermute | solution.py:188
  743.5 78.1 %collective-permute-start.71 = (bf16[1024,256]{1,0:T(8,128)(2,1)S(1)}, bf16[1024,256]{1,0:T(8,128)(2,1)S(1)}, u32[]{:S(2)}, u32[]{:S(2)}) collective-permute-start(bf16[1024,256]{1,0:T(8,128)(2,1)S(1)} %fusion.82), channel_id=1, source_target_pairs={{8,0},{16,8},{24,16},{9,1},{17,9},{25,17},{10,2},{18,10},{26,18},{... | collective-permute-start | bytes 1572872 | tf_op jit(solution)/shard_map/ppermute | solution.py:188
  826.5 44.8 %all-to-all-start.5 = ((bf16[32,72,256]{2,1,0:T(8,128)(2,1)}), bf16[32,72,256]{2,1,0:T(8,128)(2,1)S(1)}, u32[]{:S(2)}, u32[]{:S(2)}) async-start(bf16[32,72,256]{2,1,0:T(8,128)(2,1)} %fusion.111), calls=%async_computation.6 | async-start | bytes 2359296 | tf_op jit(solution)/shard_map/all_to_all | solution.py:285
  838.0 43.1 %collective-permute-start.72 = (bf16[1,2,2,128,1152]{4,3,2,1,0:T(8,128)(2,1)}, bf16[1,2,2,128,1152]{4,3,2,1,0:T(8,128)(2,1)S(1)}, u32[]{:S(2)}, u32[]{:S(2)}) collective-permute-start(bf16[1,2,2,128,1152]{4,3,2,1,0:T(8,128)(2,1)} %get-tuple-element.72), channel_id=1, source_target_pairs={{0,1},{1,0},{2,3},{3,2},{4,5},{5,4},{6,7},{7,6},{8,9},{9,8},{10,11... | collective-permute-start | bytes 3538952 | tf_op jit(solution)/shard_map/ppermute | solution.py:112
  838.3 42.8 %collective-permute-start.75 = (bf16[1,2,2,128,1152]{4,3,2,1,0:T(8,128)(2,1)}, bf16[1,2,2,128,1152]{4,3,2,1,0:T(8,128)(2,1)}, u32[]{:S(2)}, u32[]{:S(2)}) collective-permute-start(bf16[1,2,2,128,1152]{4,3,2,1,0:T(8,128)(2,1)} %get-tuple-element.73), channel_id=1, source_target_pairs={{0,1},{1,0},{2,3},{3,2},{4,5},{5,4},{6,7},{7,6},{8,9},{9,8},{10,11... | collective-permute-start | bytes 3538952 | tf_op jit(solution)/shard_map/ppermute | solution.py:112
  875.1 58.0 %all-to-all-start.6 = ((bf16[32,2,72,256]{3,2,1,0:T(8,128)(2,1)}), bf16[32,2,72,256]{3,2,1,0:T(8,128)(2,1)}, u32[]{:S(2)}, u32[]{:S(2)}) async-start(bf16[32,2,72,256]{3,2,1,0:T(8,128)(2,1)} %copy.294), calls=%async_computation.7 | async-start | bytes 4718592 | tf_op jit(solution)/shard_map/all_to_all | solution.py:285
  879.5 19.0 %collective-permute-start.49 = (bf16[2,3328]{1,0:T(2,128)(2,1)S(1)}, bf16[2,3328]{1,0:T(2,128)(2,1)S(1)}, u32[]{:S(2)}, u32[]{:S(2)}) collective-permute-start(bf16[2,3328]{1,0:T(2,128)(2,1)S(1)} %pad_maximum_fusion.37), channel_id=1, source_target_pairs={{0,4},{4,0},{1,5},{5,1},{2,6},{6,2},{3,7},{7,3},{8,12},{12,8},{9,1... | collective-permute-start | bytes 39944 | tf_op jit(solution)/shard_map/ppermute | solution.py:112
  883.6 33.9 %collective-permute-start.76 = (bf16[1,1,2,128,1152]{4,3,2,1,0:T(8,128)(2,1)S(1)}, bf16[1,1,2,128,1152]{4,3,2,1,0:T(8,128)(2,1)S(1)}, u32[]{:S(2)}, u32[]{:S(2)}) collective-permute-start(bf16[1,1,2,128,1152]{4,3,2,1,0:T(8,128)(2,1)S(1)} %slice.645), channel_id=1, source_target_pairs={{0,4},{4,0},{1,5},{5,1},{2,6},{6,2},{3,7},{7,3},{8,12},{12,8},{9,1... | collective-permute-start | bytes 1769480 | tf_op jit(solution)/shard_map/ppermute | solution.py:112
  898.6 19.8 %collective-permute-start.73 = (bf16[1,2,1,128,1152]{4,3,2,1,0:T(8,128)(2,1)S(1)}, bf16[1,2,1,128,1152]{4,3,2,1,0:T(8,128)(2,1)S(1)}, u32[]{:S(2)}, u32[]{:S(2)}) collective-permute-start(bf16[1,2,1,128,1152]{4,3,2,1,0:T(8,128)(2,1)S(1)} %slice.646), channel_id=1, source_target_pairs={{0,2},{2,0},{1,3},{3,1},{4,6},{6,4},{5,7},{7,5},{8,10},{10,8},{9,1... | collective-permute-start | bytes 1769480 | tf_op jit(solution)/shard_map/ppermute | solution.py:112
  898.7 42.8 %collective-permute-start.50 = (bf16[2,2,3328]{2,1,0:T(2,128)(2,1)S(1)}, bf16[2,2,3328]{2,1,0:T(2,128)(2,1)S(1)}, u32[]{:S(2)}, u32[]{:S(2)}) collective-permute-start(bf16[2,2,3328]{2,1,0:T(2,128)(2,1)S(1)} %pad_maximum_fusion.36), channel_id=1, source_target_pairs={{0,8},{8,0},{1,9},{9,1},{2,10},{10,2},{3,11},{11,3},{4,12},{12,4},... | collective-permute-start | bytes 79880 | tf_op jit(solution)/shard_map/ppermute | solution.py:112
  936.6 59.1 %all-to-all-start.7 = ((bf16[8,2,72,1152]{3,2,1,0:T(8,128)(2,1)}), bf16[8,2,72,1152]{3,2,1,0:T(8,128)(2,1)}, u32[]{:S(2)}, u32[]{:S(2)}) async-start(bf16[8,2,72,1152]{3,2,1,0:T(8,128)(2,1)} %copy.299), calls=%async_computation.9 | async-start | bytes 5308416 | tf_op jit(solution)/shard_map/all_to_all | solution.py:285
  942.8 33.5 %collective-permute-start.79 = (f32[4,2304]{1,0:T(4,128)S(1)}, f32[4,2304]{1,0:T(4,128)S(1)}, u32[]{:S(2)}, u32[]{:S(2)}) collective-permute-start(f32[4,2304]{1,0:T(4,128)S(1)} %fusion.150), channel_id=1, source_target_pairs={{0,4},{4,0},{1,5},{5,1},{2,6},{6,2},{3,7},{7,3},{8,12},{12,8},{9,1... | collective-permute-start | bytes 110600 | tf_op jit(solution)/shard_map/ppermute | solution.py:112
  (163 other events, 1971.8 us)
Sparse Core Ops, SparseCore 0:
  117.7 127.4 all-gather.4
  285.6 85.4 all-gather.6
  633.9 65.9 reduce-scatter.2
  702.1 171.0 reduce-scatter.4

commit v3 on v2

--- a/solution.py
+++ b/solution.py
@@ -151,6 +151,15 @@
     return lax.optimization_barrier((value,) + events)[0]
 
 
+def apart(run, step, *args):
+    like = jax.eval_shape(step, *args)
+
+    def nothing(*_):
+        return jax.tree.map(lambda leaf: jnp.zeros(leaf.shape, leaf.dtype), like)
+
+    return lax.cond(run, step, nothing, *args)
+
+
 def both(value, axis):
     other = swap(value, axis)
     first = lax.axis_index(axis) == 0
@@ -306,6 +315,7 @@
     block_rows = 8 * tok_rows
     total_rows = line_count * block_rows
     slice_ff = FF // 8
+    run = lengths[0] > 0
 
     units = lax.optimization_barrier(columns(w_qkv, 16)).reshape(KVH, 2, 2, own, HD)
     qkv_out = units.transpose(0, 2, 1, 3, 4).reshape(8, 2, own, HD)
@@ -315,19 +325,33 @@
 
     inputs = tokens.astype(f32)
     normed = rms_scale(inputs, gains[0]).astype(bf16)
-    normed_all = gather_blocks(normed, TOKEN_AXES, PLANE_GATHER)
+    def gather_plane(block):
+        return gather_blocks(block, TOKEN_AXES, PLANE_GATHER)
+
+    def scatter_plane(partial):
+        return scatter_blocks(partial, TOKEN_AXES, PLANE_SCATTER)
+
+    def gather_cube(block):
+        return gather_blocks(block, CUBE, CUBE_GATHER)
+
+    def scatter_cube(partial):
+        return scatter_blocks(partial, CUBE, CUBE_SCATTER)
+
+    normed_all = apart(run, gather_plane, normed)
 
     out_scale = jnp.max(jnp.abs(w_out.astype(f32)), axis=1) + EPSILON
     down_scale = jnp.max(jnp.abs(w_down.astype(f32)), axis=1) + EPSILON
     eff_out = nested(w_out.astype(f32), out_scale[:, None]).astype(bf16)
     eff_down = nested(w_down.astype(f32), down_scale[:, None]).astype(bf16)
-    in_out = lax.optimization_barrier(columns(w_in, 16)).reshape(2, 8, own, slice_ff)
-    in_own = exchange(after(in_out.transpose(1, 0, 2, 3), qkv_lat), CUBE)
-    in_lat = lax.all_gather(in_own.transpose(1, 0, 2, 3), "zh", axis=0)
-    down_own = exchange(after(columns(eff_down, 8), in_own), CUBE)
-    down_lat = lax.all_gather(after(down_own, in_lat), "zh", axis=0)
     eff_out = jnp.broadcast_to(columns(eff_out, 8)[None], (line_count, 8, own, HD))
-    head_out = exchange(after(eff_out.reshape(line_count * 8, own, HD), down_own), FINE)
+    head_out = after(eff_out.reshape(line_count * 8, own, HD), qkv_lat, normed_all)
+    head_out = exchange(head_out, FINE)
+
+    def spread(weight, *events):
+        cols = jnp.broadcast_to(weight[None], (lax.axis_size("zh"),) + weight.shape)
+        cols = after(cols.reshape(-1, own, slice_ff), *events)
+        return exchange(cols, LINE + ("x", "y")).reshape(-1, 8, own, slice_ff)
+
     head_out = head_out.reshape(model, HD)
 
     qkv_max = jnp.max(jnp.abs(qkv_lat), axis=(0, 1, 3))
@@ -350,26 +374,29 @@
 
     reach = min(WINDOW, total_rows // 2)
     back = min(line_count - 1, -(-(reach - 1) // block_rows))
-    shifted = [kv_own]
-    for _ in range(back):
-        shifted.append(shift(shifted[-1], 1))
+    half_block = block_rows // 2
+
+    def flip(value):
+        return jnp.concatenate([value[:, half_block:], value[:, :half_block]], axis=1)
+
+    def pass_up(own_rows):
+        shifted = [own_rows]
+        for _ in range(back):
+            shifted.append(shift(shifted[-1], 1))
+        mine = jnp.stack(shifted[::-1], axis=0)
+        other = flip(swap(mine, "c"))
+        keys = jnp.where(core == 0, mine, other).reshape(-1, HD)
+        values = jnp.where(core == 0, other, mine).reshape(-1, HD)
+        return keys, values
+
+    key_rows, value_rows = apart(run, pass_up, kv_own)
     query = rotate(dot(normed_all, head_q, COLS), cosine, sine_tab).astype(bf16)
 
+    gate_lat = spread(columns(w_in[:, :FF], 8), head_out, key_rows)
     def effective(lat):
         top = max_both(jnp.max(jnp.abs(lat), axis=(0, 1, 2)), "c")
-        scale = top.astype(f32) + EPSILON
-        return top, by_core(nested(lat.astype(f32), scale).astype(bf16))
-
-    gate_top, cols_gate = effective(in_lat[:, 0])
-    up_top, cols_up = effective(in_lat[:, 1])
-    cols_down = by_core(down_lat)
-
-    kv_mine = jnp.stack(shifted[::-1], axis=0)
-    kv_flip = swap(kv_mine, "c")
-    half_block = block_rows // 2
-    kv_flip = jnp.concatenate([kv_flip[:, half_block:], kv_flip[:, :half_block]], axis=1)
-    key_rows = jnp.where(core == 0, kv_mine, kv_flip).reshape(-1, HD)
-    value_rows = jnp.where(core == 0, kv_flip, kv_mine).reshape(-1, HD)
+        return top, by_core(nested(lat.astype(f32), top.astype(f32) + EPSILON).astype(bf16))
+
     k_places = jnp.concatenate(
         [q_places - n * block_rows for n in range(back, -1, -1)], axis=0
     )
@@ -377,86 +404,106 @@
     low = jnp.maximum(q_places - position, q_places - (WINDOW - 1))[:, None]
     heads, lse = attend(query, key_rows, value_rows, low, place, k_places[None])
 
-    branch = dot(after(heads, in_lat), head_out, ROWS, bf16)
-    branch = scatter_blocks(branch, TOKEN_AXES, PLANE_SCATTER)
+    branch = dot(heads, head_out, ROWS, bf16)
+
+    branch = apart(run, scatter_plane, branch)
+    up_lat = spread(columns(w_in[:, FF:], 8), gate_lat, branch)
     middle = inputs + rms_scale(branch, gains[1])
     pre_mlp = rms_scale(middle, gains[2]).astype(bf16)
-
-    pre_all = gather_blocks(pre_mlp, CUBE, CUBE_GATHER)
+    pre_all = apart(run, gather_cube, pre_mlp)
+    gate_top, cols_gate = apart(run, effective, after(gate_lat, pre_all))
+    down_lat = spread(columns(eff_down, 8), up_lat, cols_gate)
+    up_top, cols_up = apart(run, effective, after(up_lat, cols_gate))
+    pre_turned = lax.optimization_barrier(pre_all.T)
     gate_part = dot(pre_all, cols_gate, COLS)
     up_part = dot(pre_all, cols_up, COLS)
     hidden = glu(gate_part, up_part).astype(bf16)
-    down_out = scatter_blocks(dot(hidden, cols_down, ROWS, bf16), CUBE, CUBE_SCATTER)
+    cols_down = apart(run, by_core, after(down_lat, gate_part, up_part))
+    down_out = apart(run, scatter_cube, dot(hidden, cols_down, ROWS, bf16))
     result = (middle + rms_scale(down_out, gains[3])).astype(bf16)
 
     grad_result = cotangent.astype(f32)
     d_down, gain_four = jax.vjp(rms_scale, down_out, gains[3])[1](grad_result)
     d_down = d_down.astype(bf16)
-    tops = [both(qkv_max.reshape(-1), "c").reshape(-1), gate_top, up_top]
-    tops = after(jnp.concatenate(tops, axis=0), d_down)
-    tops = both(both(both(tops, "y"), "x"), "zl")
-    d_down_all = gather_blocks(d_down, CUBE, CUBE_GATHER)
-    d_hidden = dot(after(d_down_all, tops), cols_down, COLS)
-    d_gate, d_up = jax.vjp(glu, gate_part, up_part)[1](d_hidden)
-    d_gate = d_gate.astype(bf16)
-    d_up = d_up.astype(bf16)
+
+    def gather_down(block, qkv_row, in_row):
+        tops = jnp.concatenate([both(qkv_row, "c").reshape(-1), in_row], axis=0)
+        return gather_cube(block), both(both(both(tops, "y"), "x"), "zl")
+
+    d_down_all, tops = apart(
+        run, gather_down, d_down, qkv_max.reshape(-1), jnp.concatenate([gate_top, up_top])
+    )
+
+    def hidden_back(d_down_all, hidden, gate_part, up_part, cols_down):
+        part = dot(d_down_all, hidden, FIRST, bf16)
+        d_hidden = dot(after(d_down_all, part), cols_down, COLS)
+        d_gate, d_up = jax.vjp(glu, gate_part, up_part)[1](d_hidden)
+        return core_sum(part, own), d_gate.astype(bf16), d_up.astype(bf16)
+
+    part_down, d_gate, d_up = apart(
+        run, hidden_back, d_down_all, hidden, gate_part, up_part, cols_down
+    )
+
+    def collect(part, *events):
+        flat = after(part.reshape(-1, own, slice_ff), *events)
+        return exchange(flat, LINE + ("x", "y")).reshape(-1, 8, own, slice_ff)
+
+    down_back = collect(part_down)
     d_pre = (dot(d_gate, cols_gate, ROWS) + dot(d_up, cols_up, ROWS)).astype(bf16)
-    part_down = core_sum(dot(d_down_all, hidden, FIRST, bf16), own)
-    d_pre = after(d_pre, part_down)
-    grad_down = exchange(line_sum(part_down), CUBE)
-    part_gate = core_sum(dot(pre_all, after(d_gate, d_pre), FIRST, bf16), own)
-    part_up = core_sum(dot(pre_all, after(d_up, d_pre), FIRST, bf16), own)
-    part_in = jnp.stack([part_gate, part_up], axis=1)
-    d_pre = after(scatter_blocks(d_pre, CUBE, CUBE_SCATTER), part_in)
-    part_in = line_sum(part_in).transpose(1, 0, 2, 3)
-
+
+    def scatter_pre(partial, gate, up):
+        return scatter_cube(partial), core_sum(gate, own), core_sum(up, own)
+
+    d_pre, part_gate, part_up = apart(
+        run, scatter_pre, d_pre, dot(pre_turned, d_gate, COLS, bf16), dot(pre_turned, d_up, COLS, bf16)
+    )
+    gate_back = collect(part_gate, down_back)
     d_mid_part, gain_three = jax.vjp(rms_scale, middle, gains[2])[1](d_pre)
     d_middle = grad_result + d_mid_part
     d_branch, gain_two = jax.vjp(rms_scale, branch, gains[1])[1](d_middle)
-    d_branch_all = gather_blocks(d_branch.astype(bf16), TOKEN_AXES, PLANE_GATHER)
+    d_branch_all = apart(run, gather_plane, d_branch.astype(bf16))
+    up_back = collect(part_up, gate_back, d_branch_all)
     d_heads = dot(d_branch_all, head_out, COLS).astype(bf16)
 
     d_query, d_keys, d_values = attend_back(
         query, key_rows, value_rows, low, place, k_places[None], lse, d_heads
     )
-    d_keys = d_keys.reshape(back + 1, block_rows, HD)
-    d_values = d_values.reshape(back + 1, block_rows, HD)
-    send = jnp.where(core == 0, d_values, d_keys).astype(bf16)
-    send = jnp.concatenate([send[:, half_block:], send[:, :half_block]], axis=1)
-    d_window = jnp.where(core == 0, d_keys, d_values) + swap(send, "c").astype(f32)
-    d_kv = d_window[0]
-    for n in range(1, back + 1):
-        d_kv = d_window[n] + shift(d_kv.astype(bf16), -1).astype(f32)
-    d_kv = d_kv.astype(bf16).astype(f32)
+
+    def pass_down(d_keys, d_values):
+        d_keys = d_keys.reshape(back + 1, block_rows, HD)
+        d_values = d_values.reshape(back + 1, block_rows, HD)
+        send = flip(jnp.where(core == 0, d_values, d_keys).astype(bf16))
+        window = jnp.where(core == 0, d_keys, d_values) + swap(send, "c").astype(f32)
+        total = window[0]
+        for n in range(1, back + 1):
+            total = window[n] + shift(total.astype(bf16), -1).astype(f32)
+        return total.astype(bf16)
+
+    d_kv = apart(run, pass_down, d_keys, d_values).astype(f32)
     d_query_lin = rotate(d_query.astype(f32), cosine, -sine_tab).astype(bf16)
     d_second = jnp.where(core == 0, rotate(d_kv, cosine, -sine_tab), d_kv).astype(bf16)
 
     d_mixed = (dot(d_query_lin, head_q, ROWS) + dot(d_second, head_kv, ROWS)).astype(bf16)
-    d_normed = scatter_blocks(d_mixed, TOKEN_AXES, PLANE_SCATTER)
+    d_normed = apart(run, scatter_plane, d_mixed)
     d_input_part, gain_one = jax.vjp(rms_scale, inputs, gains[0])[1](d_normed)
     grad_tokens = d_middle + d_input_part
 
-    grad_down = uncolumns(grad_down).astype(f32)
-    part_out = dot(d_branch_all, heads, FIRST, bf16).reshape(line_count * 8, own, HD)
-    grad_out = exchange(after(part_out, grad_down), FINE)
-    part_q = dot(normed_all, d_query_lin, FIRST, bf16)
-    part_kv = dot(normed_all, d_second, FIRST, bf16)
-    part_qkv = jnp.stack(
-        [part_q.reshape(line_count * 8, own, HD), part_kv.reshape(line_count * 8, own, HD)], axis=1
-    )
-    grad_qkv = exchange(after(part_qkv, grad_out), FINE)
-    in_back = exchange(after(part_in, grad_qkv), CUBE)
-    grad_out = jnp.sum(grad_out.reshape(line_count, 8, own, HD).astype(f32), axis=0)
-    grad_out = uncolumns(grad_out)
-
-    qkv_sum = jnp.sum(grad_qkv.reshape(line_count, 16, own, HD).astype(f32), axis=0)
-    grad_qkv = qkv_sum.reshape(KVH, 2, 2, own, HD).transpose(0, 2, 1, 3, 4)
+    parts = [dot(normed_all, d_query_lin, FIRST, bf16), dot(normed_all, d_second, FIRST, bf16)]
+    parts.append(dot(d_branch_all, heads, FIRST, bf16))
+    parts = jnp.stack([part.reshape(line_count * 8, own, HD) for part in parts], axis=1)
+    sums = exchange(after(parts, up_back), FINE).reshape(line_count, 8, 3, own, HD)
+    sums = jnp.sum(sums.astype(f32), axis=0)
+    grad_out = uncolumns(sums[:, 2])
+    grad_qkv = sums[:, :2].reshape(KVH, 2, 2, own, HD).transpose(0, 2, 1, 3, 4)
     grad_qkv = uncolumns(lax.optimization_barrier(grad_qkv).reshape(16, own, HD))
-    grad_in = in_back.transpose(1, 0, 2, 3)
-    grad_in = lax.optimization_barrier(grad_in).reshape(16, own, slice_ff)
-    grad_in = uncolumns(grad_in).astype(f32)
-
-    grad_gains = sum_all(jnp.stack([gain_one, gain_two, gain_three, gain_four], axis=0))
+
+    def owned(back):
+        return uncolumns(jnp.sum(back.astype(f32), axis=0))
+
+    grad_in = jnp.concatenate([owned(gate_back), owned(up_back)], axis=1)
+    grad_down = owned(down_back)
+
+    grad_gains = apart(run, sum_all, jnp.stack([gain_one, gain_two, gain_three, gain_four], axis=0))
 
     tops = tops.astype(f32) + EPSILON
     qkv_tops = tops[0, :, :, : 4 * HD].reshape(KVH, 2, 2, HD).transpose(0, 2, 1, 3).reshape(-1)

time: 1020 us -> 970 us (0.951)
  waiting for transfers between devices: 445 us -> 403 us
  local copies, waits for them, and re-layouts: 102 us -> 78.2 us
  matrix products: 112 us -> 130 us
  between operations: 16.7 us -> 2.27 us
  other arithmetic: 124 us -> 136 us
    ppermute x79, waiting for transfers between devices: 240 us -> 333 us  [swap(): return lax.ppermute(value, axis, SWAP)]
    ppermute x4, waiting for transfers between devices: 153 us -> 70.1 us  [shift(): lax.ppermute(value, LINE, [(i, i + step) for i in range(count) if 0 <= i...]
    all_to_all x8 -> x9, waiting for transfers between devices: 51.3 us -> 0.5 us  [exchange(): return lax.all_to_all(value, axes, split_axis=0, concat_axis=0, tiled=True)]
    dot_general x4 -> x0, local copies, waits for them, and re-layouts: 26.7 us -> none  [dot(): lax.dot_general(left, right, (dims, ((), ())), preferred_element_type=out)]
    dot_general x18, matrix products: 112 us -> 130 us  [dot(): lax.dot_general(left, right, (dims, ((), ())), preferred_element_type=out)]
    optimization_barrier x6 -> x0, local copies, waits for them, and re-layouts: 14 us -> none  [the longest x4 11.9 us: after(): return lax.optimization_barrier((value,) + events)[0]]
    concatenate x20, other arithmetic: 12.2 us -> 1.53 us  [gather_blocks(): held = jnp.concatenate([held, swap(held, axis)], axis=axes.index(axis))]
    convert_element_type x5 -> x7, other arithmetic: 25.8 us -> 28.5 us  [the longest x2 24.7 us: effective(): nested(lat.astype(f32), top.astype(f32) + EPSILON).astype(bf16)]
  transfers between devices with their start and end apart: 95 -> 92, of which waited for: 51 -> 67; matrix products, arithmetic and copies ran while one was open for 27% -> 27% of each run, Pallas kernels for 4% -> 4%
where the time goes in v3:
time: 970 us; the launch traced here: 959 us
  waiting for transfers between devices  403 us (42%)
  starting transfers between devices  166 us (17%)
  other arithmetic  136 us (14%)
  matrix products  130 us (13%)
  local copies, waits for them, and re-layouts  78.2 us (8%)
  Pallas kernels  40.7 us (4%)
    ppermute x79, waiting for transfers between devices, swap(): return lax.ppermute(value, axis, SWAP)  333 us
    dot_general x18, matrix products, dot(): lax.dot_general(left, right, (dims, ((), ())), preferred_element_type=out)  130 us
    ppermute x79, starting transfers between devices, swap(): return lax.ppermute(value, axis, SWAP)  92.1 us
    ppermute x4, waiting for transfers between devices, shift(): lax.ppermute(value, LINE, [(i, i + step) for i in range(count) if 0 <= i...  70.1 us
    all_to_all x9, starting transfers between devices, exchange(): return lax.all_to_all(value, axes, split_axis=0, concat_axis=0, tiled=True)  58.1 us
    convert_element_type x2, other arithmetic, effective(): nested(lat.astype(f32), top.astype(f32) + EPSILON).astype(bf16)  24.7 us
    pallas_call x1, Pallas kernels, attend_back(): pl.pallas_call(attend_back_kernel, out_shape=(jax.ShapeDtypeStruct((rows,...  24.6 us
  transfers between devices with their start and end apart: 92, of which 67 were waited for; matrix products, arithmetic and copies ran while one was open for 27% of the time, Pallas kernels for 4%

profile of v3, /device:TPU:0, one launch (start us, length us, event | category | flops | bytes accessed | tf_op | source)
XLA Modules:
  0.0 959.0 jit_solution(14182154538066031800)
XLA Ops:
  22.1 47.4 %conditional.15 = (bf16[1024,2304]{1,0:T(8,128)(2,1)}) conditional(s32[]{:T(128)} %bitcast.63, () %tuple.136, bf16[128,2304]{1,0:T(8,128)(2,1)S(1)} %fusion.64), branch_computations={%region_1.0_spmd, %region_2.0_spmd} | conditional | flops 40697856 | bytes 34210040 | solution.py:160
  25.5 16.0 %collective-permute-done.8 = bf16[1,1,1,128,1152]{4,3,2,1,0:T(8,128)(2,1)S(1)} collective-permute-done((bf16[1,1,1,128,1152]{4,3,2,1,0:T(8,128)(2,1)S(1)}, bf16[1,1,1,128,1152]{4,3,2,1,0:T(8,128)(2,1)S(1)}, u32[]{:S(2)}, u32[]{:S(2)}) %collective-permute-start.8) | collective-permute-done | bytes 294944 | tf_op jit(solution)/shard_map/cond/branch_1_fun/ppermute | solution.py:112
  43.5 16.6 %collective-permute-done.9 = bf16[1,1,2,128,1152]{4,3,2,1,0:T(8,128)(2,1)S(1)} collective-permute-done((bf16[1,1,2,128,1152]{4,3,2,1,0:T(8,128)(2,1)S(1)}, bf16[1,1,2,128,1152]{4,3,2,1,0:T(8,128)(2,1)S(1)}, u32[]{:S(2)}, u32[]{:S(2)}) %collective-permute-start.9) | collective-permute-done | bytes 589856 | tf_op jit(solution)/shard_map/cond/branch_1_fun/ppermute | solution.py:112
  76.9 9.4 multiply_convert_fusion.3
  92.8 43.8 %conditional.16 = (bf16[3072,256]{1,0:T(8,128)(2,1)S(1)}, bf16[3072,256]{1,0:T(8,128)(2,1)}) conditional(s32[]{:T(128)} %bitcast.63, () %tuple.137, (s32[]{:T(128)}, bf16[1024,256]{1,0:T(8,128)(2,1)S(1)}) %tuple.138), branch_computations={%region_6.7_spmd, %region_7.8_spmd} | conditional | flops 11010049 | bytes 27263176 | solution.py:160
  96.5 11.4 %collective-permute-done.64 = bf16[1024,256]{1,0:T(8,128)(2,1)S(1)} collective-permute-done((bf16[1024,256]{1,0:T(8,128)(2,1)S(1)}, bf16[1024,256]{1,0:T(8,128)(2,1)S(1)}, u32[]{:S(2)}, u32[]{:S(2)}) %collective-permute-start.64) | collective-permute-done | bytes 524320 | tf_op jit(solution)/shard_map/cond/branch_1_fun/ppermute | solution.py:197
  107.9 9.6 %collective-permute-start.65 = (bf16[1024,256]{1,0:T(8,128)(2,1)S(1)}, bf16[1024,256]{1,0:T(8,128)(2,1)S(1)}, u32[]{:S(2)}, u32[]{:S(2)}) collective-permute-start(bf16[1024,256]{1,0:T(8,128)(2,1)S(1)} %collective-permute-done.64), channel_id=1, source_target_pairs={{0,8},{8,16},{16,24},{1,9},{9,17},{17,25},{2,10},{10,18},{18,26},{... | collective-permute-start | bytes 1572872 | tf_op jit(solution)/shard_map/cond/branch_1_fun/ppermute | solution.py:197
  117.6 11.3 %collective-permute-done.65 = bf16[1024,256]{1,0:T(8,128)(2,1)S(1)} collective-permute-done((bf16[1024,256]{1,0:T(8,128)(2,1)S(1)}, bf16[1024,256]{1,0:T(8,128)(2,1)S(1)}, u32[]{:S(2)}, u32[]{:S(2)}) %collective-permute-start.65) | collective-permute-done | bytes 524320 | tf_op jit(solution)/shard_map/cond/branch_1_fun/ppermute | solution.py:197
  158.4 16.1 %shard_map.169 = (bf16[1024,256]{1,0:T(8,128)(2,1)}, f32[1024,1]{1,0:T(8,128)}) custom-call(bf16[1024,256]{1,0:T(8,128)(2,1)} %pad_maximum_fusion.31.q_ref, bf16[3072,256]{1,0:T(8,128)(2,1)S(1)} %get-tuple-element.138.k_ref, bf16[3072,256]{1,0:T(8,128)(2,1)} %get-tuple-element.139.v_ref, s32[1024,1]{1,0:T(8,128)} %add_maximum_fusion.low_ref, ...), custom_call_target="tpu_custom_call" | custom-call | flops 1 | bytes 1 | tf_op jit(solution)/shard_map/pallas_call | solution.py:265
  179.6 40.1 %conditional.17 = (f32[128,2304]{1,0:T(8,128)S(1)}) conditional(s32[]{:T(128)} %bitcast.63, () %tuple.135, bf16[1024,2304]{1,0:T(8,128)(2,1)} %fusion.127), branch_computations={%region_9.10_spmd, %region_10.11_spmd} | conditional | flops 5603328 | bytes 64291092 | solution.py:160
  190.3 19.1 %collective-permute-done.71 = bf16[1,1,2,128,1152]{4,3,2,1,0:T(8,128)(2,1)S(1)} collective-permute-done((bf16[1,1,2,128,1152]{4,3,2,1,0:T(8,128)(2,1)S(1)}, bf16[1,1,2,128,1152]{4,3,2,1,0:T(8,128)(2,1)S(1)}, u32[]{:S(2)}, u32[]{:S(2)}) %collective-permute-start.71) | collective-permute-done | bytes 589856 | tf_op jit(solution)/shard_map/cond/branch_1_fun/ppermute | solution.py:112
  223.2 9.5 all-to-all-start.3
  242.0 73.4 %conditional.18 = (bf16[1024,2304]{1,0:T(8,128)(2,1)}) conditional(s32[]{:T(128)} %bitcast.63, () %tuple.141, bf16[128,2304]{1,0:T(8,128)(2,1)S(1)} %multiply_convert_fusion.5), branch_computations={%region_13.14_spmd, %region_14.15_spmd} | conditional | flops 59572224 | bytes 34210160 | solution.py:160
  257.6 23.3 %collective-permute-done.11 = bf16[1,1,1,128,768]{4,3,2,1,0:T(8,128)(2,1)S(1)} collective-permute-done((bf16[1,1,1,128,768]{4,3,2,1,0:T(8,128)(2,1)S(1)}, bf16[1,1,1,128,768]{4,3,2,1,0:T(8,128)(2,1)S(1)}, u32[]{:S(2)}, u32[]{:S(2)}) %collective-permute-start.11) | collective-permute-done | bytes 196640 | tf_op jit(solution)/shard_map/cond/branch_1_fun/ppermute | solution.py:112
  293.9 15.5 %collective-permute-done.19 = bf16[2,1,2,128,768]{4,3,2,1,0:T(8,128)(2,1)S(1)} collective-permute-done((bf16[2,1,2,128,768]{4,3,2,1,0:T(8,128)(2,1)S(1)}, bf16[2,1,2,128,768]{4,3,2,1,0:T(8,128)(2,1)S(1)}, u32[]{:S(2)}, u32[]{:S(2)}) %collective-permute-start.19) | collective-permute-done | bytes 786464 | tf_op jit(solution)/shard_map/cond/branch_1_fun/ppermute | solution.py:112
  315.4 30.3 %conditional.19 = (bf16[1152]{0:T(1024)(128)(2,1)}, bf16[2304,1152]{1,0:T(8,128)(2,1)}) conditional(s32[]{:T(128)} %bitcast.63, () %tuple.142, bf16[2,8,72,1152]{3,2,1,0:T(8,128)(2,1)} %bitcast.82), branch_computations={%region_15.16_spmd, %region_16.18_spmd} | conditional | flops 83614464 | bytes 31889830 | solution.py:160
  320.1 12.3 %multiply_convert_fusion = bf16[2,8,72,1152]{3,2,1,0:T(8,128)(2,1)} fusion(bf16[2,8,72,1152]{3,2,1,0:T(8,128)(2,1)} %param.9, f32[1152]{0:T(1024)S(1)} %fusion.2, f32[1152]{0:T(1024)S(1)} %get-tuple-element.185), kind=kLoop, calls=%fused_computation.37 | loop fusion | flops 80953344 | bytes 5317632 | tf_op jit(solution)/shard_map/cond/branch_1_fun/convert_element_type | solution.py:398
  352.8 11.0 %fusion.128 = f32[1024,1152]{1,0:T(8,128)} fusion(bf16[1024,2304]{1,0:T(8,128)(2,1)} %get-tuple-element.304, bf16[2304,1152]{1,0:T(8,128)(2,1)} %get-tuple-element.144), kind=kOutput, calls=%fused_computation.373 | convolution fusion | flops 5435817984 | bytes 14745600 | tf_op jit(solution)/shard_map/dot_general | solution.py:103
  363.8 30.4 %conditional.20 = (bf16[1152]{0:T(1024)(128)(2,1)}, bf16[2304,1152]{1,0:T(8,128)(2,1)}) conditional(s32[]{:T(128)} %bitcast.63, () %tuple.145, bf16[2,8,72,1152]{3,2,1,0:T(8,128)(2,1)} %bitcast.85), branch_computations={%region_18.19_spmd, %region_19.21_spmd} | conditional | flops 83614464 | bytes 31889830 | solution.py:160
  368.4 12.4 %multiply_convert_fusion.1 = bf16[2,8,72,1152]{3,2,1,0:T(8,128)(2,1)} fusion(bf16[2,8,72,1152]{3,2,1,0:T(8,128)(2,1)} %param.11, f32[1152]{0:T(1024)S(1)} %fusion.4, f32[1152]{0:T(1024)S(1)} %get-tuple-element.187), kind=kLoop, calls=%fused_computation.46 | loop fusion | flops 80953344 | bytes 5317632 | tf_op jit(solution)/shard_map/cond/branch_1_fun/convert_element_type | solution.py:398
  394.3 12.1 %fusion.42 = (bf16[1024,1152]{1,0:T(8,128)(2,1)S(1)}, f32[1024,1152]{1,0:T(8,128)}) fusion(f32[1024,1152]{1,0:T(8,128)} %fusion.128, bf16[1024,2304]{1,0:T(8,128)(2,1)} %get-tuple-element.304, bf16[2304,1152]{1,0:T(8,128)(2,1)} %get-tuple-element.147), kind=kOutput, calls=%fused_computation.190 | convolution fusion | flops 5447614464 | bytes 21823488 | tf_op jit(solution)/shard_map/dot_general | solution.py:103
  406.9 13.3 %conditional.21 = (bf16[2304,1152]{1,0:T(8,128)(2,1)}) conditional(s32[]{:T(128)} %bitcast.63, () %tuple.148, bf16[2,8,72,1152]{3,2,1,0:T(8,128)(2,1)} %bitcast.88), branch_computations={%region_22.23_spmd, %region_23.24_spmd} | conditional | flops 6 | bytes 23887990 | solution.py:160
  420.2 9.0 fusion.129
  429.2 51.0 %conditional.22 = (f32[128,2304]{1,0:T(8,128)S(1)}, f32[128]{0:T(128)}, f32[128,1]{0,1:T(1,128)S(1)}) conditional(s32[]{:T(128)} %bitcast.63, () %tuple.140, bf16[1024,2304]{1,0:T(8,128)(2,1)S(1)} %fusion.129), branch_computations={%region_24.25_spmd, %region_25.27_spmd} | conditional | flops 6487936 | bytes 45418368 | solution.py:160
  443.1 9.3 collective-permute-done.61
  483.2 48.1 %conditional.23 = (bf16[1024,2304]{1,0:T(8,128)(2,1)}, f32[2,2,2,3328]{3,2,1,0:T(2,128)S(1)}) conditional(s32[]{:T(128)} %bitcast.63, () %tuple.153, (bf16[128,2304]{1,0:T(8,128)(2,1)S(1)}, bf16[2,256]{1,0:T(2,128)(2,1)S(1)}, bf16[1152]{0:T(1024)(128)(2,1)}, bf16[1152]{0:T(1024)(128)(2,1)}) %tuple.154), branch_computations={%region_28.29_spmd, %region_29.30_spmd} | conditional | flops 59757056 | bytes 34885300 | solution.py:160
  510.4 14.4 %collective-permute-done.33 = bf16[2,1,2,128,768]{4,3,2,1,0:T(8,128)(2,1)S(1)} collective-permute-done((bf16[2,1,2,128,768]{4,3,2,1,0:T(8,128)(2,1)S(1)}, bf16[2,1,2,128,768]{4,3,2,1,0:T(8,128)(2,1)S(1)}, u32[]{:S(2)}, u32[]{:S(2)}) %collective-permute-start.33) | collective-permute-done | bytes 786464 | tf_op jit(solution)/shard_map/cond/branch_1_fun/ppermute | solution.py:112
  531.9 33.5 %conditional.24 = (bf16[2,8,72,1152]{3,2,1,0:T(8,128)(2,1)}, bf16[1024,1152]{1,0:T(8,128)(2,1)S(1)}, bf16[1024,1152]{1,0:T(8,128)(2,1)}) conditional(s32[]{:T(128)} %bitcast.63, () %tuple.152, (bf16[1024,2304]{1,0:T(8,128)(2,1)}, bf16[1024,1152]{1,0:T(8,128)(2,1)}, bf16[2304,1152]{1,0:T(8,128)(2,1)}, f32[1024,1152]{1,0:T(8,128)}, ...), branch_computations={%region_30.31_spmd, %region_31.32_spmd} | conditional | flops 10905255936 | bytes 81690824 | solution.py:160
  532.1 10.5 %fusion.124 = bf16[2304,1152]{1,0:T(8,128)(2,1)} fusion(bf16[1024,2304]{1,0:T(8,128)(2,1)} %get-tuple-element.84, bf16[1024,1152]{1,0:T(8,128)(2,1)} %get-tuple-element.83), kind=kOutput, calls=%fused_computation.369 | convolution fusion | flops 5435817984 | bytes 12386304 | tf_op jit(solution)/shard_map/cond/branch_1_fun/dot_general | solution.py:103
  546.0 15.4 %multiply_convert_fusion.2 = (bf16[1024,1152]{1,0:T(8,128)(2,1)}, bf16[1024,1152]{1,0:T(8,128)(2,1)S(1)}) fusion(f32[1024,1152]{1,0:T(8,128)} %get-tuple-element.87, f32[1024,1152]{1,0:T(8,128)} %get-tuple-element.86, bf16[1024,2304]{1,0:T(8,128)(2,1)} %get-tuple-element.84, bf16[2304,1152]{1,0:T(8,128)(2,1)} %get-tuple-element.85), kind=kOutput, calls=%fused_computation.111 | convolution fusion | flops 5464129536 | bytes 24182784 | tf_op jit(solution)/shard_map/cond/branch_1_fun/dot_general | solution.py:103
  565.4 11.2 %fusion.130 = f32[1024,2304]{1,0:T(8,128)} fusion(bf16[1024,1152]{1,0:T(8,128)(2,1)S(1)} %get-tuple-element.156, bf16[2304,1152]{1,0:T(8,128)(2,1)} %get-tuple-element.144), kind=kOutput, calls=%fused_computation.375 | convolution fusion | flops 5435817984 | bytes 17104896 | tf_op jit(solution)/shard_map/dot_general | solution.py:103
  581.4 10.8 %add_convert_fusion.1 = bf16[1024,2304]{1,0:T(8,128)(2,1)S(1)} fusion(f32[1024,2304]{1,0:T(8,128)} %fusion.130, bf16[1024,1152]{1,0:T(8,128)(2,1)} %get-tuple-element.157, bf16[2304,1152]{1,0:T(8,128)(2,1)} %get-tuple-element.147), kind=kOutput, calls=%fused_computation.172 | convolution fusion | flops 5440536576 | bytes 21823488 | tf_op jit(solution)/shard_map/dot_general | solution.py:103
  592.2 9.7 %fusion.131 = bf16[2304,1152]{1,0:T(8,128)(2,1)} fusion(bf16[2304,1024]{0,1:T(8,128)(2,1)} %bitcast.318, bf16[1024,1152]{1,0:T(8,128)(2,1)S(1)} %get-tuple-element.156), kind=kOutput, calls=%fused_computation.376 | convolution fusion | flops 5435817984 | bytes 12386304 | tf_op jit(solution)/shard_map/dot_general | solution.py:103
  601.9 10.5 %fusion.132 = bf16[2304,1152]{1,0:T(8,128)(2,1)} fusion(bf16[2304,1024]{0,1:T(8,128)(2,1)} %bitcast.319, bf16[1024,1152]{1,0:T(8,128)(2,1)} %get-tuple-element.157), kind=kOutput, calls=%fused_computation.377 | convolution fusion | flops 5435817984 | bytes 12386304 | tf_op jit(solution)/shard_map/dot_general | solution.py:103
  612.4 66.0 %conditional.25 = (f32[128,2304]{1,0:T(8,128)S(1)}, bf16[16,72,1152]{2,1,0:T(8,128)(2,1)}, bf16[16,72,1152]{2,1,0:T(8,128)(2,1)}) conditional(s32[]{:T(128)} %bitcast.63, () %tuple.151, (bf16[1024,2304]{1,0:T(8,128)(2,1)S(1)}, bf16[2304,1152]{1,0:T(8,128)(2,1)}, bf16[2304,1152]{1,0:T(8,128)(2,1)}) %tuple.156), branch_computations={%region_32.33_spmd, %region_33.34_spmd} | conditional | flops 16515081 | bytes 165151456 | solution.py:160
  623.7 16.7 %collective-permute-done.44 = bf16[2,1,2,128,768]{4,3,2,1,0:T(8,128)(2,1)} collective-permute-done((bf16[2,1,2,128,768]{4,3,2,1,0:T(8,128)(2,1)S(1)}, bf16[2,1,2,128,768]{4,3,2,1,0:T(8,128)(2,1)}, u32[]{:S(2)}, u32[]{:S(2)}) %collective-permute-start.44) | collective-permute-done | bytes 786464 | tf_op jit(solution)/shard_map/cond/branch_1_fun/ppermute | solution.py:112
  692.1 51.0 %conditional.26 = (bf16[1024,2304]{1,0:T(8,128)(2,1)}) conditional(s32[]{:T(128)} %bitcast.63, () %tuple.158, bf16[128,2304]{1,0:T(8,128)(2,1)S(1)} %fusion.69), branch_computations={%region_36.37_spmd, %region_37.38_spmd} | conditional | flops 40697856 | bytes 34210040 | solution.py:160
  695.6 10.4 %collective-permute-done.52 = bf16[1,1,1,128,1152]{4,3,2,1,0:T(8,128)(2,1)S(1)} collective-permute-done((bf16[1,1,1,128,1152]{4,3,2,1,0:T(8,128)(2,1)S(1)}, bf16[1,1,1,128,1152]{4,3,2,1,0:T(8,128)(2,1)S(1)}, u32[]{:S(2)}, u32[]{:S(2)}) %collective-permute-start.52) | collective-permute-done | bytes 294944 | tf_op jit(solution)/shard_map/cond/branch_1_fun/ppermute | solution.py:112
  706.1 8.7 collective-permute-done.49
  716.6 10.8 %collective-permute-done.53 = bf16[1,1,2,128,1152]{4,3,2,1,0:T(8,128)(2,1)S(1)} collective-permute-done((bf16[1,1,2,128,1152]{4,3,2,1,0:T(8,128)(2,1)S(1)}, bf16[1,1,2,128,1152]{4,3,2,1,0:T(8,128)(2,1)S(1)}, u32[]{:S(2)}, u32[]{:S(2)}) %collective-permute-start.53) | collective-permute-done | bytes 589856 | tf_op jit(solution)/shard_map/cond/branch_1_fun/ppermute | solution.py:112
  727.6 8.5 collective-permute-done.50
  754.8 24.6 %shard_map.170 = (bf16[1024,256]{1,0:T(8,128)(2,1)}, f32[3072,256]{1,0:T(8,128)S(1)}, f32[3072,256]{1,0:T(8,128)}) custom-call(bf16[1024,256]{1,0:T(8,128)(2,1)} %pad_maximum_fusion.31.q_ref, bf16[3072,256]{1,0:T(8,128)(2,1)S(1)} %copy-done.7, bf16[3072,256]{1,0:T(8,128)(2,1)} %get-tuple-element.139.v_ref, s32[1024,1]{1,0:T(8,128)} %add_maximum_fusion.low_ref, ...), custom_call_target="tpu_custom_call" | custom-call | flops 1 | bytes 1 | tf_op jit(solution)/shard_map/pallas_call | solution.py:280
  781.5 60.0 %conditional.27 = (f32[1024,256]{1,0:T(8,128)}, f32[1024,128]{1,0:T(8,128)}, f32[1024,128]{1,0:T(8,128)}) conditional(s32[]{:T(128)} %bitcast.63, () %tuple.159, (s32[]{:T(128)}, f32[3072,256]{1,0:T(8,128)S(1)}, f32[3072,256]{1,0:T(8,128)}) %tuple.160), branch_computations={%region_38.39_spmd, %region_39.40_spmd} | conditional | flops 8126465 | bytes 62390456 | solution.py:160
  789.1 22.0 %collective-permute-done.74 = bf16[1024,256]{1,0:T(8,128)(2,1)S(1)} collective-permute-done((bf16[1024,256]{1,0:T(8,128)(2,1)S(1)}, bf16[1024,256]{1,0:T(8,128)(2,1)S(1)}, u32[]{:S(2)}, u32[]{:S(2)}) %collective-permute-start.74) | collective-permute-done | bytes 524320 | tf_op jit(solution)/shard_map/cond/branch_1_fun/ppermute | solution.py:197
  812.5 25.4 %collective-permute-done.75 = bf16[1024,256]{1,0:T(8,128)(2,1)S(1)} collective-permute-done((bf16[1024,256]{1,0:T(8,128)(2,1)S(1)}, bf16[1024,256]{1,0:T(8,128)(2,1)S(1)}, u32[]{:S(2)}, u32[]{:S(2)}) %collective-permute-start.75) | collective-permute-done | bytes 524320 | tf_op jit(solution)/shard_map/cond/branch_1_fun/ppermute | solution.py:197
  863.7 54.6 %conditional.28 = (f32[128,2304]{1,0:T(8,128)S(1)}) conditional(s32[]{:T(128)} %bitcast.63, () %tuple.157, bf16[1024,2304]{1,0:T(8,128)(2,1)} %add_convert_fusion), branch_computations={%region_40.41_spmd, %region_41.42_spmd} | conditional | flops 5603328 | bytes 64291092 | solution.py:160
  874.1 29.8 %collective-permute-done.80 = bf16[1,1,2,128,1152]{4,3,2,1,0:T(8,128)(2,1)S(1)} collective-permute-done((bf16[1,1,2,128,1152]{4,3,2,1,0:T(8,128)(2,1)S(1)}, bf16[1,1,2,128,1152]{4,3,2,1,0:T(8,128)(2,1)S(1)}, u32[]{:S(2)}, u32[]{:S(2)}) %collective-permute-start.80) | collective-permute-done | bytes 589856 | tf_op jit(solution)/shard_map/cond/branch_1_fun/ppermute | solution.py:112
  919.1 20.1 %conditional.29 = (f32[4,2304]{1,0:T(4,128)S(1)}) conditional(s32[]{:T(128)} %bitcast.63, () %tuple.164, f32[4,2304]{1,0:T(4,128)S(1)} %pad_maximum_fusion.36), branch_computations={%region_51.52_spmd, %region_52.53_spmd} | conditional | flops 46080 | bytes 1290448 | solution.py:160
  (558 shorter events, 490.5 us)
Async XLA Ops:
  3.7 66.2 %all-to-all-start = ((bf16[32,2,72,256]{3,2,1,0:T(8,128)(2,1)}), bf16[32,2,72,256]{3,2,1,0:T(8,128)(2,1)S(1)}, u32[]{:S(2)}, u32[]{:S(2)}) async-start(bf16[32,2,72,256]{3,2,1,0:T(8,128)(2,1)} %bitcast.280), calls=%async_computation | async-start | bytes 4718592 | tf_op jit(solution)/shard_map/all_to_all | solution.py:294
  22.2 19.3 %collective-permute-start.8 = (bf16[1,1,1,128,1152]{4,3,2,1,0:T(8,128)(2,1)S(1)}, bf16[1,1,1,128,1152]{4,3,2,1,0:T(8,128)(2,1)S(1)}, u32[]{:S(2)}, u32[]{:S(2)}) collective-permute-start(bf16[1,1,1,128,1152]{4,3,2,1,0:T(8,128)(2,1)S(1)} %get-tuple-element.195), channel_id=1, source_target_pairs={{0,2},{2,0},{1,3},{3,1},{4,6},{6,4},{5,7},{7,5},{8,10},{10,8},{9,1... | collective-permute-start | bytes 884744 | tf_op jit(solution)/shard_map/cond/branch_1_fun/ppermute | solution.py:112
  24.0 19.3 %collective-permute-start.5 = (bf16[1,1,1,128,1152]{4,3,2,1,0:T(8,128)(2,1)S(1)}, bf16[1,1,1,128,1152]{4,3,2,1,0:T(8,128)(2,1)S(1)}, u32[]{:S(2)}, u32[]{:S(2)}) collective-permute-start(bf16[1,1,1,128,1152]{4,3,2,1,0:T(8,128)(2,1)S(1)} %get-tuple-element.194), channel_id=1, source_target_pairs={{0,4},{4,0},{1,5},{5,1},{2,6},{6,2},{3,7},{7,3},{8,12},{12,8},{9,1... | collective-permute-start | bytes 884744 | tf_op jit(solution)/shard_map/cond/branch_1_fun/ppermute | solution.py:112
  41.5 18.6 %collective-permute-start.9 = (bf16[1,1,2,128,1152]{4,3,2,1,0:T(8,128)(2,1)S(1)}, bf16[1,1,2,128,1152]{4,3,2,1,0:T(8,128)(2,1)S(1)}, u32[]{:S(2)}, u32[]{:S(2)}) collective-permute-start(bf16[1,1,2,128,1152]{4,3,2,1,0:T(8,128)(2,1)S(1)} %pad_maximum_fusion.3), channel_id=1, source_target_pairs={{0,4},{4,0},{1,5},{5,1},{2,6},{6,2},{3,7},{7,3},{8,12},{12,8},{9,1... | collective-permute-start | bytes 1769480 | tf_op jit(solution)/shard_map/cond/branch_1_fun/ppermute | solution.py:112
  43.4 19.0 %collective-permute-start.6 = (bf16[1,2,1,128,1152]{4,3,2,1,0:T(8,128)(2,1)S(1)}, bf16[1,2,1,128,1152]{4,3,2,1,0:T(8,128)(2,1)S(1)}, u32[]{:S(2)}, u32[]{:S(2)}) collective-permute-start(bf16[1,2,1,128,1152]{4,3,2,1,0:T(8,128)(2,1)S(1)} %pad_maximum_fusion.2), channel_id=1, source_target_pairs={{0,2},{2,0},{1,3},{3,1},{4,6},{6,4},{5,7},{7,5},{8,10},{10,8},{9,1... | collective-permute-start | bytes 1769480 | tf_op jit(solution)/shard_map/cond/branch_1_fun/ppermute | solution.py:112
  72.2 64.4 %all-to-all-start.1 = ((bf16[32,72,256]{2,1,0:T(8,128)(2,1)}), bf16[32,72,256]{2,1,0:T(8,128)(2,1)}, u32[]{:S(2)}, u32[]{:S(2)}) async-start(bf16[32,72,256]{2,1,0:T(8,128)(2,1)} %bitcast.323), calls=%async_computation.1 | async-start | bytes 2359296 | tf_op jit(solution)/shard_map/all_to_all | solution.py:294
  92.8 15.1 %collective-permute-start.64 = (bf16[1024,256]{1,0:T(8,128)(2,1)S(1)}, bf16[1024,256]{1,0:T(8,128)(2,1)S(1)}, u32[]{:S(2)}, u32[]{:S(2)}) collective-permute-start(bf16[1024,256]{1,0:T(8,128)(2,1)S(1)} %get-tuple-element.77), channel_id=1, source_target_pairs={{0,8},{8,16},{16,24},{1,9},{9,17},{17,25},{2,10},{10,18},{18,26},{... | collective-permute-start | bytes 1572872 | tf_op jit(solution)/shard_map/cond/branch_1_fun/ppermute | solution.py:197
  107.9 20.9 %collective-permute-start.65 = (bf16[1024,256]{1,0:T(8,128)(2,1)S(1)}, bf16[1024,256]{1,0:T(8,128)(2,1)S(1)}, u32[]{:S(2)}, u32[]{:S(2)}) collective-permute-start(bf16[1024,256]{1,0:T(8,128)(2,1)S(1)} %collective-permute-done.64), channel_id=1, source_target_pairs={{0,8},{8,16},{16,24},{1,9},{9,17},{17,25},{2,10},{10,18},{18,26},{... | collective-permute-start | bytes 1572872 | tf_op jit(solution)/shard_map/cond/branch_1_fun/ppermute | solution.py:197
  140.2 79.6 %all-to-all-start.2 = ((bf16[16,72,1152]{2,1,0:T(8,128)(2,1)}), bf16[16,72,1152]{2,1,0:T(8,128)(2,1)}, u32[]{:S(2)}, u32[]{:S(2)}) async-start(bf16[16,72,1152]{2,1,0:T(8,128)(2,1)} %bitcast.273), calls=%async_computation.2 | async-start | bytes 5308416 | tf_op jit(solution)/shard_map/all_to_all | solution.py:294
  186.7 22.7 %collective-permute-start.71 = (bf16[1,1,2,128,1152]{4,3,2,1,0:T(8,128)(2,1)S(1)}, bf16[1,1,2,128,1152]{4,3,2,1,0:T(8,128)(2,1)S(1)}, u32[]{:S(2)}, u32[]{:S(2)}) collective-permute-start(bf16[1,1,2,128,1152]{4,3,2,1,0:T(8,128)(2,1)S(1)} %slice.567), channel_id=1, source_target_pairs={{0,4},{4,0},{1,5},{5,1},{2,6},{6,2},{3,7},{7,3},{8,12},{12,8},{9,1... | collective-permute-start | bytes 1769480 | tf_op jit(solution)/shard_map/cond/branch_1_fun/ppermute | solution.py:112
  188.7 22.6 %collective-permute-start.68 = (bf16[1,2,1,128,1152]{4,3,2,1,0:T(8,128)(2,1)S(1)}, bf16[1,2,1,128,1152]{4,3,2,1,0:T(8,128)(2,1)S(1)}, u32[]{:S(2)}, u32[]{:S(2)}) collective-permute-start(bf16[1,2,1,128,1152]{4,3,2,1,0:T(8,128)(2,1)S(1)} %slice.568), channel_id=1, source_target_pairs={{0,2},{2,0},{1,3},{3,1},{4,6},{6,4},{5,7},{7,5},{8,10},{10,8},{9,1... | collective-permute-start | bytes 1769480 | tf_op jit(solution)/shard_map/cond/branch_1_fun/ppermute | solution.py:112
  223.2 122.5 %all-to-all-start.3 = ((bf16[16,72,1152]{2,1,0:T(8,128)(2,1)}), bf16[16,72,1152]{2,1,0:T(8,128)(2,1)}, u32[]{:S(2)}, u32[]{:S(2)}) async-start(bf16[16,72,1152]{2,1,0:T(8,128)(2,1)} %bitcast.272), calls=%async_computation.3 | async-start | bytes 5308416 | tf_op jit(solution)/shard_map/all_to_all | solution.py:294
  244.4 11.8 %collective-permute-start.14 = (bf16[1,1,1,128,768]{4,3,2,1,0:T(8,128)(2,1)S(1)}, bf16[1,1,1,128,768]{4,3,2,1,0:T(8,128)(2,1)S(1)}, u32[]{:S(2)}, u32[]{:S(2)}) collective-permute-start(bf16[1,1,1,128,768]{4,3,2,1,0:T(8,128)(2,1)S(1)} %get-tuple-element.206), channel_id=1, source_target_pairs={{0,4},{4,0},{1,5},{5,1},{2,6},{6,2},{3,7},{7,3},{8,12},{12,8},{9,1... | collective-permute-start | bytes 589832 | tf_op jit(solution)/shard_map/cond/branch_1_fun/ppermute | solution.py:112
  245.8 35.1 %collective-permute-start.11 = (bf16[1,1,1,128,768]{4,3,2,1,0:T(8,128)(2,1)S(1)}, bf16[1,1,1,128,768]{4,3,2,1,0:T(8,128)(2,1)S(1)}, u32[]{:S(2)}, u32[]{:S(2)}) collective-permute-start(bf16[1,1,1,128,768]{4,3,2,1,0:T(8,128)(2,1)S(1)} %get-tuple-element.204), channel_id=1, source_target_pairs={{0,8},{8,0},{1,9},{9,1},{2,10},{10,2},{3,11},{11,3},{4,12},{12,4},... | collective-permute-start | bytes 589832 | tf_op jit(solution)/shard_map/cond/branch_1_fun/ppermute | solution.py:112
  252.1 38.8 %collective-permute-start.18 = (bf16[1,1,2,128,768]{4,3,2,1,0:T(8,128)(2,1)S(1)}, bf16[1,1,2,128,768]{4,3,2,1,0:T(8,128)(2,1)S(1)}, u32[]{:S(2)}, u32[]{:S(2)}) collective-permute-start(bf16[1,1,2,128,768]{4,3,2,1,0:T(8,128)(2,1)S(1)} %pad_maximum_fusion.12), channel_id=1, source_target_pairs={{0,8},{8,0},{1,9},{9,1},{2,10},{10,2},{3,11},{11,3},{4,12},{12,4},... | collective-permute-start | bytes 1179656 | tf_op jit(solution)/shard_map/cond/branch_1_fun/ppermute | solution.py:112
  256.2 36.0 %collective-permute-start.15 = (bf16[1,2,1,128,768]{4,3,2,1,0:T(8,128)(2,1)S(1)}, bf16[1,2,1,128,768]{4,3,2,1,0:T(8,128)(2,1)S(1)}, u32[]{:S(2)}, u32[]{:S(2)}) collective-permute-start(bf16[1,2,1,128,768]{4,3,2,1,0:T(8,128)(2,1)S(1)} %pad_maximum_fusion.11), channel_id=1, source_target_pairs={{0,2},{2,0},{1,3},{3,1},{4,6},{6,4},{5,7},{7,5},{8,10},{10,8},{9,1... | collective-permute-start | bytes 1179656 | tf_op jit(solution)/shard_map/cond/branch_1_fun/ppermute | solution.py:112
  290.9 18.6 %collective-permute-start.19 = (bf16[2,1,2,128,768]{4,3,2,1,0:T(8,128)(2,1)S(1)}, bf16[2,1,2,128,768]{4,3,2,1,0:T(8,128)(2,1)S(1)}, u32[]{:S(2)}, u32[]{:S(2)}) collective-permute-start(bf16[2,1,2,128,768]{4,3,2,1,0:T(8,128)(2,1)S(1)} %pad_maximum_fusion.9), channel_id=1, source_target_pairs={{0,4},{4,0},{1,5},{5,1},{2,6},{6,2},{3,7},{7,3},{8,12},{12,8},{9,1... | collective-permute-start | bytes 2359304 | tf_op jit(solution)/shard_map/cond/branch_1_fun/ppermute | solution.py:112
  292.2 18.3 %collective-permute-start.16 = (bf16[1,2,2,128,768]{4,3,2,1,0:T(8,128)(2,1)S(1)}, bf16[1,2,2,128,768]{4,3,2,1,0:T(8,128)(2,1)S(1)}, u32[]{:S(2)}, u32[]{:S(2)}) collective-permute-start(bf16[1,2,2,128,768]{4,3,2,1,0:T(8,128)(2,1)S(1)} %pad_maximum_fusion.8), channel_id=1, source_target_pairs={{0,8},{8,0},{1,9},{9,1},{2,10},{10,2},{3,11},{11,3},{4,12},{12,4},... | collective-permute-start | bytes 2359304 | tf_op jit(solution)/shard_map/cond/branch_1_fun/ppermute | solution.py:112
  292.4 18.3 %collective-permute-start.13 = (bf16[2,2,1,128,768]{4,3,2,1,0:T(8,128)(2,1)S(1)}, bf16[2,2,1,128,768]{4,3,2,1,0:T(8,128)(2,1)S(1)}, u32[]{:S(2)}, u32[]{:S(2)}) collective-permute-start(bf16[2,2,1,128,768]{4,3,2,1,0:T(8,128)(2,1)S(1)} %pad_maximum_fusion.7), channel_id=1, source_target_pairs={{0,2},{2,0},{1,3},{3,1},{4,6},{6,4},{5,7},{7,5},{8,10},{10,8},{9,1... | collective-permute-start | bytes 2359304 | tf_op jit(solution)/shard_map/cond/branch_1_fun/ppermute | solution.py:112
  347.4 59.5 %all-to-all-start.4 = ((bf16[16,72,1152]{2,1,0:T(8,128)(2,1)}), bf16[16,72,1152]{2,1,0:T(8,128)(2,1)}, u32[]{:S(2)}, u32[]{:S(2)}) async-start(bf16[16,72,1152]{2,1,0:T(8,128)(2,1)} %bitcast.274), calls=%async_computation.4 | async-start | bytes 5308416 | tf_op jit(solution)/shard_map/all_to_all | solution.py:294
  429.3 23.1 %collective-permute-start.61 = (bf16[2,1,2,128,768]{4,3,2,1,0:T(8,128)(2,1)S(1)}, bf16[2,1,2,128,768]{4,3,2,1,0:T(8,128)(2,1)S(1)}, u32[]{:S(2)}, u32[]{:S(2)}) collective-permute-start(bf16[2,1,2,128,768]{4,3,2,1,0:T(8,128)(2,1)S(1)} %slice.401), channel_id=1, source_target_pairs={{0,4},{4,0},{1,5},{5,1},{2,6},{6,2},{3,7},{7,3},{8,12},{12,8},{9,1... | collective-permute-start | bytes 2359304 | tf_op jit(solution)/shard_map/cond/branch_1_fun/ppermute | solution.py:112
  434.6 25.9 %collective-permute-start.58 = (bf16[1,2,2,128,768]{4,3,2,1,0:T(8,128)(2,1)S(1)}, bf16[1,2,2,128,768]{4,3,2,1,0:T(8,128)(2,1)S(1)}, u32[]{:S(2)}, u32[]{:S(2)}) collective-permute-start(bf16[1,2,2,128,768]{4,3,2,1,0:T(8,128)(2,1)S(1)} %slice.395), channel_id=1, source_target_pairs={{0,8},{8,0},{1,9},{9,1},{2,10},{10,2},{3,11},{11,3},{4,12},{12,4},... | collective-permute-start | bytes 2359304 | tf_op jit(solution)/shard_map/cond/branch_1_fun/ppermute | solution.py:112
  442.5 19.1 %collective-permute-start.55 = (bf16[2,2,1,128,768]{4,3,2,1,0:T(8,128)(2,1)S(1)}, bf16[2,2,1,128,768]{4,3,2,1,0:T(8,128)(2,1)S(1)}, u32[]{:S(2)}, u32[]{:S(2)}) collective-permute-start(bf16[2,2,1,128,768]{4,3,2,1,0:T(8,128)(2,1)S(1)} %slice.389), channel_id=1, source_target_pairs={{0,2},{2,0},{1,3},{3,1},{4,6},{6,4},{5,7},{7,5},{8,10},{10,8},{9,1... | collective-permute-start | bytes 2359304 | tf_op jit(solution)/shard_map/cond/branch_1_fun/ppermute | solution.py:112
  452.6 16.8 %collective-permute-start.62 = (bf16[1,1,2,128,768]{4,3,2,1,0:T(8,128)(2,1)S(1)}, bf16[1,1,2,128,768]{4,3,2,1,0:T(8,128)(2,1)S(1)}, u32[]{:S(2)}, u32[]{:S(2)}) collective-permute-start(bf16[1,1,2,128,768]{4,3,2,1,0:T(8,128)(2,1)S(1)} %slice.571), channel_id=1, source_target_pairs={{0,8},{8,0},{1,9},{9,1},{2,10},{10,2},{3,11},{11,3},{4,12},{12,4},... | collective-permute-start | bytes 1179656 | tf_op jit(solution)/shard_map/cond/branch_1_fun/ppermute | solution.py:112
  507.1 17.7 %collective-permute-start.33 = (bf16[2,1,2,128,768]{4,3,2,1,0:T(8,128)(2,1)S(1)}, bf16[2,1,2,128,768]{4,3,2,1,0:T(8,128)(2,1)S(1)}, u32[]{:S(2)}, u32[]{:S(2)}) collective-permute-start(bf16[2,1,2,128,768]{4,3,2,1,0:T(8,128)(2,1)S(1)} %pad_maximum_fusion.16), channel_id=1, source_target_pairs={{0,4},{4,0},{1,5},{5,1},{2,6},{6,2},{3,7},{7,3},{8,12},{12,8},{9,1... | collective-permute-start | bytes 2359304 | tf_op jit(solution)/shard_map/cond/branch_1_fun/ppermute | solution.py:112
  508.6 17.3 %collective-permute-start.30 = (bf16[1,2,2,128,768]{4,3,2,1,0:T(8,128)(2,1)S(1)}, bf16[1,2,2,128,768]{4,3,2,1,0:T(8,128)(2,1)S(1)}, u32[]{:S(2)}, u32[]{:S(2)}) collective-permute-start(bf16[1,2,2,128,768]{4,3,2,1,0:T(8,128)(2,1)S(1)} %pad_maximum_fusion.15), channel_id=1, source_target_pairs={{0,8},{8,0},{1,9},{9,1},{2,10},{10,2},{3,11},{11,3},{4,12},{12,4},... | collective-permute-start | bytes 2359304 | tf_op jit(solution)/shard_map/cond/branch_1_fun/ppermute | solution.py:112
  509.5 17.0 %collective-permute-start.27 = (bf16[2,2,1,128,768]{4,3,2,1,0:T(8,128)(2,1)S(1)}, bf16[2,2,1,128,768]{4,3,2,1,0:T(8,128)(2,1)S(1)}, u32[]{:S(2)}, u32[]{:S(2)}) collective-permute-start(bf16[2,2,1,128,768]{4,3,2,1,0:T(8,128)(2,1)S(1)} %pad_maximum_fusion.14), channel_id=1, source_target_pairs={{0,2},{2,0},{1,3},{3,1},{4,6},{6,4},{5,7},{7,5},{8,10},{10,8},{9,1... | collective-permute-start | bytes 2359304 | tf_op jit(solution)/shard_map/cond/branch_1_fun/ppermute | solution.py:112
  546.0 15.4 %collective-permute-start.82 = (bf16[2,8,72,1152]{3,2,1,0:T(8,128)(2,1)}, bf16[2,8,72,1152]{3,2,1,0:T(8,128)(2,1)}, u32[]{:S(2)}, u32[]{:S(2)}) collective-permute-start(bf16[2,8,72,1152]{3,2,1,0:T(8,128)(2,1)} %dynamic-slice_bitcast_fusion), channel_id=1, source_target_pairs={{0,1},{1,0},{2,3},{3,2},{4,5},{5,4},{6,7},{7,6},{8,9},{9,8},{10,11... | collective-permute-start | bytes 7962632 | tf_op jit(solution)/shard_map/cond/branch_1_fun/ppermute | solution.py:112
  576.5 101.9 %all-to-all-start.5 = ((bf16[16,72,1152]{2,1,0:T(8,128)(2,1)}), bf16[16,72,1152]{2,1,0:T(8,128)(2,1)}, u32[]{:S(2)}, u32[]{:S(2)}) async-start(bf16[16,72,1152]{2,1,0:T(8,128)(2,1)} %bitcast.97), calls=%async_computation.5 | async-start | bytes 5308416 | tf_op jit(solution)/shard_map/all_to_all | solution.py:294
  612.7 27.7 %collective-permute-start.44 = (bf16[2,1,2,128,768]{4,3,2,1,0:T(8,128)(2,1)S(1)}, bf16[2,1,2,128,768]{4,3,2,1,0:T(8,128)(2,1)}, u32[]{:S(2)}, u32[]{:S(2)}) collective-permute-start(bf16[2,1,2,128,768]{4,3,2,1,0:T(8,128)(2,1)S(1)} %slice.419), channel_id=1, source_target_pairs={{0,4},{4,0},{1,5},{5,1},{2,6},{6,2},{3,7},{7,3},{8,12},{12,8},{9,1... | collective-permute-start | bytes 2359304 | tf_op jit(solution)/shard_map/cond/branch_1_fun/ppermute | solution.py:112
  614.7 33.1 %collective-permute-start.41 = (bf16[1,2,2,128,768]{4,3,2,1,0:T(8,128)(2,1)S(1)}, bf16[1,2,2,128,768]{4,3,2,1,0:T(8,128)(2,1)}, u32[]{:S(2)}, u32[]{:S(2)}) collective-permute-start(bf16[1,2,2,128,768]{4,3,2,1,0:T(8,128)(2,1)S(1)} %slice.413), channel_id=1, source_target_pairs={{0,8},{8,0},{1,9},{9,1},{2,10},{10,2},{3,11},{11,3},{4,12},{12,4},... | collective-permute-start | bytes 2359304 | tf_op jit(solution)/shard_map/cond/branch_1_fun/ppermute | solution.py:112
  616.3 34.6 %collective-permute-start.38 = (bf16[2,2,1,128,768]{4,3,2,1,0:T(8,128)(2,1)S(1)}, bf16[2,2,1,128,768]{4,3,2,1,0:T(8,128)(2,1)}, u32[]{:S(2)}, u32[]{:S(2)}) collective-permute-start(bf16[2,2,1,128,768]{4,3,2,1,0:T(8,128)(2,1)S(1)} %slice.407), channel_id=1, source_target_pairs={{0,2},{2,0},{1,3},{3,1},{4,6},{6,4},{5,7},{7,5},{8,10},{10,8},{9,1... | collective-permute-start | bytes 2359304 | tf_op jit(solution)/shard_map/cond/branch_1_fun/ppermute | solution.py:112
  621.5 48.8 %collective-permute-start.47 = (bf16[2,8,72,1152]{3,2,1,0:T(8,128)(2,1)}, bf16[2,8,72,1152]{3,2,1,0:T(8,128)(2,1)}, u32[]{:S(2)}, u32[]{:S(2)}) collective-permute-start(bf16[2,8,72,1152]{3,2,1,0:T(8,128)(2,1)} %dynamic-slice_bitcast_fusion.2), channel_id=1, source_target_pairs={{0,1},{1,0},{2,3},{3,2},{4,5},{5,4},{6,7},{7,6},{8,9},{9,8},{10,11... | collective-permute-start | bytes 7962632 | tf_op jit(solution)/shard_map/cond/branch_1_fun/ppermute | solution.py:112
  623.5 51.0 %collective-permute-start.48 = (bf16[2,8,72,1152]{3,2,1,0:T(8,128)(2,1)}, bf16[2,8,72,1152]{3,2,1,0:T(8,128)(2,1)}, u32[]{:S(2)}, u32[]{:S(2)}) collective-permute-start(bf16[2,8,72,1152]{3,2,1,0:T(8,128)(2,1)} %dynamic-slice_bitcast_fusion.1), channel_id=1, source_target_pairs={{0,1},{1,0},{2,3},{3,2},{4,5},{5,4},{6,7},{7,6},{8,9},{9,8},{10,11... | collective-permute-start | bytes 7962632 | tf_op jit(solution)/shard_map/cond/branch_1_fun/ppermute | solution.py:112
  642.0 13.8 %collective-permute-start.45 = (bf16[1,1,2,128,768]{4,3,2,1,0:T(8,128)(2,1)S(1)}, bf16[1,1,2,128,768]{4,3,2,1,0:T(8,128)(2,1)S(1)}, u32[]{:S(2)}, u32[]{:S(2)}) collective-permute-start(bf16[1,1,2,128,768]{4,3,2,1,0:T(8,128)(2,1)S(1)} %slice.577), channel_id=1, source_target_pairs={{0,8},{8,0},{1,9},{9,1},{2,10},{10,2},{3,11},{11,3},{4,12},{12,4},... | collective-permute-start | bytes 1179656 | tf_op jit(solution)/shard_map/cond/branch_1_fun/ppermute | solution.py:112
  649.4 12.0 %collective-permute-start.42 = (bf16[1,2,1,128,768]{4,3,2,1,0:T(8,128)(2,1)S(1)}, bf16[1,2,1,128,768]{4,3,2,1,0:T(8,128)(2,1)S(1)}, u32[]{:S(2)}, u32[]{:S(2)}) collective-permute-start(bf16[1,2,1,128,768]{4,3,2,1,0:T(8,128)(2,1)S(1)} %slice.578), channel_id=1, source_target_pairs={{0,2},{2,0},{1,3},{3,1},{4,6},{6,4},{5,7},{7,5},{8,10},{10,8},{9,1... | collective-permute-start | bytes 1179656 | tf_op jit(solution)/shard_map/cond/branch_1_fun/ppermute | solution.py:112
  678.5 64.7 %all-to-all-start.6 = ((bf16[16,72,1152]{2,1,0:T(8,128)(2,1)}), bf16[16,72,1152]{2,1,0:T(8,128)(2,1)}, u32[]{:S(2)}, u32[]{:S(2)}) async-start(bf16[16,72,1152]{2,1,0:T(8,128)(2,1)} %get-tuple-element.169), calls=%async_computation.6 | async-start | bytes 5308416 | tf_op jit(solution)/shard_map/all_to_all | solution.py:294
  692.2 13.8 %collective-permute-start.52 = (bf16[1,1,1,128,1152]{4,3,2,1,0:T(8,128)(2,1)S(1)}, bf16[1,1,1,128,1152]{4,3,2,1,0:T(8,128)(2,1)S(1)}, u32[]{:S(2)}, u32[]{:S(2)}) collective-permute-start(bf16[1,1,1,128,1152]{4,3,2,1,0:T(8,128)(2,1)S(1)} %get-tuple-element.221), channel_id=1, source_target_pairs={{0,2},{2,0},{1,3},{3,1},{4,6},{6,4},{5,7},{7,5},{8,10},{10,8},{9,1... | collective-permute-start | bytes 884744 | tf_op jit(solution)/shard_map/cond/branch_1_fun/ppermute | solution.py:112
  694.1 20.8 %collective-permute-start.49 = (bf16[1,1,1,128,1152]{4,3,2,1,0:T(8,128)(2,1)S(1)}, bf16[1,1,1,128,1152]{4,3,2,1,0:T(8,128)(2,1)S(1)}, u32[]{:S(2)}, u32[]{:S(2)}) collective-permute-start(bf16[1,1,1,128,1152]{4,3,2,1,0:T(8,128)(2,1)S(1)} %get-tuple-element.220), channel_id=1, source_target_pairs={{0,4},{4,0},{1,5},{5,1},{2,6},{6,2},{3,7},{7,3},{8,12},{12,8},{9,1... | collective-permute-start | bytes 884744 | tf_op jit(solution)/shard_map/cond/branch_1_fun/ppermute | solution.py:112
  706.1 21.3 %collective-permute-start.53 = (bf16[1,1,2,128,1152]{4,3,2,1,0:T(8,128)(2,1)S(1)}, bf16[1,1,2,128,1152]{4,3,2,1,0:T(8,128)(2,1)S(1)}, u32[]{:S(2)}, u32[]{:S(2)}) collective-permute-start(bf16[1,1,2,128,1152]{4,3,2,1,0:T(8,128)(2,1)S(1)} %pad_maximum_fusion.26), channel_id=1, source_target_pairs={{0,4},{4,0},{1,5},{5,1},{2,6},{6,2},{3,7},{7,3},{8,12},{12,8},{9,1... | collective-permute-start | bytes 1769480 | tf_op jit(solution)/shard_map/cond/branch_1_fun/ppermute | solution.py:112
  714.9 21.2 %collective-permute-start.50 = (bf16[1,2,1,128,1152]{4,3,2,1,0:T(8,128)(2,1)S(1)}, bf16[1,2,1,128,1152]{4,3,2,1,0:T(8,128)(2,1)S(1)}, u32[]{:S(2)}, u32[]{:S(2)}) collective-permute-start(bf16[1,2,1,128,1152]{4,3,2,1,0:T(8,128)(2,1)S(1)} %pad_maximum_fusion.25), channel_id=1, source_target_pairs={{0,2},{2,0},{1,3},{3,1},{4,6},{6,4},{5,7},{7,5},{8,10},{10,8},{9,1... | collective-permute-start | bytes 1769480 | tf_op jit(solution)/shard_map/cond/branch_1_fun/ppermute | solution.py:112
  743.1 110.8 %all-to-all-start.7 = ((bf16[16,72,1152]{2,1,0:T(8,128)(2,1)}), bf16[16,72,1152]{2,1,0:T(8,128)(2,1)}, u32[]{:S(2)}, u32[]{:S(2)}) async-start(bf16[16,72,1152]{2,1,0:T(8,128)(2,1)} %get-tuple-element.170), calls=%async_computation.7 | async-start | bytes 5308416 | tf_op jit(solution)/shard_map/all_to_all | solution.py:294
  787.8 23.3 %collective-permute-start.74 = (bf16[1024,256]{1,0:T(8,128)(2,1)S(1)}, bf16[1024,256]{1,0:T(8,128)(2,1)S(1)}, u32[]{:S(2)}, u32[]{:S(2)}) collective-permute-start(bf16[1024,256]{1,0:T(8,128)(2,1)S(1)} %fusion.31), channel_id=1, source_target_pairs={{8,0},{16,8},{24,16},{9,1},{17,9},{25,17},{10,2},{18,10},{26,18},{... | collective-permute-start | bytes 1572872 | tf_op jit(solution)/shard_map/cond/branch_1_fun/ppermute | solution.py:197
  811.2 26.7 %collective-permute-start.75 = (bf16[1024,256]{1,0:T(8,128)(2,1)S(1)}, bf16[1024,256]{1,0:T(8,128)(2,1)S(1)}, u32[]{:S(2)}, u32[]{:S(2)}) collective-permute-start(bf16[1024,256]{1,0:T(8,128)(2,1)S(1)} %fusion.27), channel_id=1, source_target_pairs={{8,0},{16,8},{24,16},{9,1},{17,9},{25,17},{10,2},{18,10},{26,18},{... | collective-permute-start | bytes 1572872 | tf_op jit(solution)/shard_map/cond/branch_1_fun/ppermute | solution.py:197
  854.0 99.5 %all-to-all-start.8 = ((bf16[32,3,72,256]{3,2,1,0:T(8,128)(2,1)}), bf16[32,3,72,256]{3,2,1,0:T(8,128)(2,1)}, u32[]{:S(2)}, u32[]{:S(2)}) async-start(bf16[32,3,72,256]{3,2,1,0:T(8,128)(2,1)} %pad_maximum_fusion.30), calls=%async_computation.8 | async-start | bytes 7077888 | tf_op jit(solution)/shard_map/all_to_all | solution.py:294
  870.8 33.1 %collective-permute-start.80 = (bf16[1,1,2,128,1152]{4,3,2,1,0:T(8,128)(2,1)S(1)}, bf16[1,1,2,128,1152]{4,3,2,1,0:T(8,128)(2,1)S(1)}, u32[]{:S(2)}, u32[]{:S(2)}) collective-permute-start(bf16[1,1,2,128,1152]{4,3,2,1,0:T(8,128)(2,1)S(1)} %slice.583), channel_id=1, source_target_pairs={{0,4},{4,0},{1,5},{5,1},{2,6},{6,2},{3,7},{7,3},{8,12},{12,8},{9,1... | collective-permute-start | bytes 1769480 | tf_op jit(solution)/shard_map/cond/branch_1_fun/ppermute | solution.py:112
  872.5 33.4 %collective-permute-start.77 = (bf16[1,2,1,128,1152]{4,3,2,1,0:T(8,128)(2,1)S(1)}, bf16[1,2,1,128,1152]{4,3,2,1,0:T(8,128)(2,1)S(1)}, u32[]{:S(2)}, u32[]{:S(2)}) collective-permute-start(bf16[1,2,1,128,1152]{4,3,2,1,0:T(8,128)(2,1)S(1)} %slice.584), channel_id=1, source_target_pairs={{0,2},{2,0},{1,3},{3,1},{4,6},{6,4},{5,7},{7,5},{8,10},{10,8},{9,1... | collective-permute-start | bytes 1769480 | tf_op jit(solution)/shard_map/cond/branch_1_fun/ppermute | solution.py:112
  906.1 11.8 %collective-permute-start.78 = (bf16[1,1,1,128,1152]{4,3,2,1,0:T(8,128)(2,1)S(1)}, bf16[1,1,1,128,1152]{4,3,2,1,0:T(8,128)(2,1)S(1)}, u32[]{:S(2)}, u32[]{:S(2)}) collective-permute-start(bf16[1,1,1,128,1152]{4,3,2,1,0:T(8,128)(2,1)S(1)} %slice.586), channel_id=1, source_target_pairs={{0,4},{4,0},{1,5},{5,1},{2,6},{6,2},{3,7},{7,3},{8,12},{12,8},{9,1... | collective-permute-start | bytes 884744 | tf_op jit(solution)/shard_map/cond/branch_1_fun/ppermute | solution.py:112
  (116 other events, 1507.0 us)

commit v4 on v3

--- a/solution.py
+++ b/solution.py
@@ -379,7 +379,8 @@
     def flip(value):
         return jnp.concatenate([value[:, half_block:], value[:, :half_block]], axis=1)
 
-    def pass_up(own_rows):
+    def pass_up(own_rows, normed_all, head_q, cosine, sine_tab):
+        query = rotate(dot(normed_all, head_q, COLS), cosine, sine_tab).astype(bf16)
         shifted = [own_rows]
         for _ in range(back):
             shifted.append(shift(shifted[-1], 1))
@@ -387,10 +388,11 @@
         other = flip(swap(mine, "c"))
         keys = jnp.where(core == 0, mine, other).reshape(-1, HD)
         values = jnp.where(core == 0, other, mine).reshape(-1, HD)
-        return keys, values
-
-    key_rows, value_rows = apart(run, pass_up, kv_own)
-    query = rotate(dot(normed_all, head_q, COLS), cosine, sine_tab).astype(bf16)
+        return keys, values, query
+
+    key_rows, value_rows, query = apart(
+        run, pass_up, kv_own, normed_all, head_q, cosine, sine_tab
+    )
 
     gate_lat = spread(columns(w_in[:, :FF], 8), head_out, key_rows)
     def effective(lat):
@@ -411,14 +413,19 @@
     middle = inputs + rms_scale(branch, gains[1])
     pre_mlp = rms_scale(middle, gains[2]).astype(bf16)
     pre_all = apart(run, gather_cube, pre_mlp)
-    gate_top, cols_gate = apart(run, effective, after(gate_lat, pre_all))
-    down_lat = spread(columns(eff_down, 8), up_lat, cols_gate)
-    up_top, cols_up = apart(run, effective, after(up_lat, cols_gate))
+    down_lat = spread(columns(eff_down, 8), up_lat, pre_all)
+
+    def both_effective(gate_lat, up_lat):
+        gate_top, cols_gate = effective(gate_lat)
+        up_top, cols_up = effective(up_lat)
+        return cols_gate, cols_up, jnp.concatenate([gate_top, up_top])
+
+    cols_gate, cols_up, in_tops = apart(run, both_effective, after(gate_lat, pre_all), up_lat)
     pre_turned = lax.optimization_barrier(pre_all.T)
     gate_part = dot(pre_all, cols_gate, COLS)
     up_part = dot(pre_all, cols_up, COLS)
+    cols_down = apart(run, by_core, after(down_lat, gate_part, up_part))
     hidden = glu(gate_part, up_part).astype(bf16)
-    cols_down = apart(run, by_core, after(down_lat, gate_part, up_part))
     down_out = apart(run, scatter_cube, dot(hidden, cols_down, ROWS, bf16))
     result = (middle + rms_scale(down_out, gains[3])).astype(bf16)
 
@@ -431,7 +438,7 @@
         return gather_cube(block), both(both(both(tops, "y"), "x"), "zl")
 
     d_down_all, tops = apart(
-        run, gather_down, d_down, qkv_max.reshape(-1), jnp.concatenate([gate_top, up_top])
+        run, gather_down, d_down, qkv_max.reshape(-1), in_tops
     )
 
     def hidden_back(d_down_all, hidden, gate_part, up_part, cols_down):

time: 970 us -> 956 us (0.986)
  waiting for transfers between devices: 403 us -> 390 us
    ppermute x79, waiting for transfers between devices: 333 us -> 320 us  [swap(): return lax.ppermute(value, axis, SWAP)]
  transfers between devices with their start and end apart: 92 -> 92, of which waited for: 67 -> 59; matrix products, arithmetic and copies ran while one was open for 27% -> 28% of each run, Pallas kernels for 4% -> 4%
where the time goes in v4:
time: 956 us; the launch traced here: 945 us
  waiting for transfers between devices  390 us (41%)
  starting transfers between devices  163 us (17%)
  other arithmetic  137 us (14%)
  matrix products  128 us (13%)
  local copies, waits for them, and re-layouts  81.6 us (9%)
  Pallas kernels  40.5 us (4%)
    ppermute x79, waiting for transfers between devices, swap(): return lax.ppermute(value, axis, SWAP)  320 us
    dot_general x18, matrix products, dot(): lax.dot_general(left, right, (dims, ((), ())), preferred_element_type=out)  128 us
    ppermute x79, starting transfers between devices, swap(): return lax.ppermute(value, axis, SWAP)  84.8 us
    ppermute x4, waiting for transfers between devices, shift(): lax.ppermute(value, LINE, [(i, i + step) for i in range(count) if 0 <= i...  69.8 us
    all_to_all x9, starting transfers between devices, exchange(): return lax.all_to_all(value, axes, split_axis=0, concat_axis=0, tiled=True)  61.6 us
    convert_element_type x2, other arithmetic, effective(): nested(lat.astype(f32), top.astype(f32) + EPSILON).astype(bf16)  24.8 us
    pallas_call x1, Pallas kernels, attend_back(): pl.pallas_call(attend_back_kernel, out_shape=(jax.ShapeDtypeStruct((rows,...  24.5 us
  transfers between devices with their start and end apart: 92, of which 59 were waited for; matrix products, arithmetic and copies ran while one was open for 28% of the time, Pallas kernels for 4%

profile of v4, /device:TPU:0, one launch (start us, length us, event | category | flops | bytes accessed | tf_op | source)
XLA Modules:
  0.0 945.2 jit_solution(901357319403351013)
XLA Ops:
  21.1 48.4 %conditional.14 = (bf16[1024,2304]{1,0:T(8,128)(2,1)}) conditional(s32[]{:T(128)} %bitcast.63, () %tuple.128, bf16[128,2304]{1,0:T(8,128)(2,1)S(1)} %fusion.64), branch_computations={%region_1.0_spmd, %region_2.0_spmd} | conditional | flops 40697856 | bytes 34210040 | solution.py:160
  24.4 17.0 %collective-permute-done.8 = bf16[1,1,1,128,1152]{4,3,2,1,0:T(8,128)(2,1)S(1)} collective-permute-done((bf16[1,1,1,128,1152]{4,3,2,1,0:T(8,128)(2,1)S(1)}, bf16[1,1,1,128,1152]{4,3,2,1,0:T(8,128)(2,1)S(1)}, u32[]{:S(2)}, u32[]{:S(2)}) %collective-permute-start.8) | collective-permute-done | bytes 294944 | tf_op jit(solution)/shard_map/cond/branch_1_fun/ppermute | solution.py:112
  43.5 16.6 %collective-permute-done.9 = bf16[1,1,2,128,1152]{4,3,2,1,0:T(8,128)(2,1)S(1)} collective-permute-done((bf16[1,1,2,128,1152]{4,3,2,1,0:T(8,128)(2,1)S(1)}, bf16[1,1,2,128,1152]{4,3,2,1,0:T(8,128)(2,1)S(1)}, u32[]{:S(2)}, u32[]{:S(2)}) %collective-permute-start.9) | collective-permute-done | bytes 589856 | tf_op jit(solution)/shard_map/cond/branch_1_fun/ppermute | solution.py:112
  78.9 9.4 multiply_convert_fusion.3
  94.8 50.0 %conditional.15 = (bf16[3072,256]{1,0:T(8,128)(2,1)S(1)}, bf16[3072,256]{1,0:T(8,128)(2,1)}, bf16[1024,256]{1,0:T(8,128)(2,1)S(1)}) conditional(s32[]{:T(128)} %bitcast.63, () %tuple.127, (s32[]{:T(128)}, bf16[1024,256]{1,0:T(8,128)(2,1)S(1)}, bf16[1024,2304]{1,0:T(8,128)(2,1)}, bf16[2304,256]{1,0:T(8,128)(2,1)}, f32[1024,128]{1,0:T(8,128)}, ...), branch_computations={%region_6.7_spmd, %region_7.8_spmd} | conditional | flops 1221066752 | bytes 47841544 | solution.py:160
  98.6 11.4 %collective-permute-done.79 = bf16[1024,256]{1,0:T(8,128)(2,1)S(1)} collective-permute-done((bf16[1024,256]{1,0:T(8,128)(2,1)S(1)}, bf16[1024,256]{1,0:T(8,128)(2,1)S(1)}, u32[]{:S(2)}, u32[]{:S(2)}) %collective-permute-start.79) | collective-permute-done | bytes 524320 | tf_op jit(solution)/shard_map/cond/branch_1_fun/ppermute | solution.py:197
  110.0 9.8 %collective-permute-start.80 = (bf16[1024,256]{1,0:T(8,128)(2,1)S(1)}, bf16[1024,256]{1,0:T(8,128)(2,1)S(1)}, u32[]{:S(2)}, u32[]{:S(2)}) collective-permute-start(bf16[1024,256]{1,0:T(8,128)(2,1)S(1)} %collective-permute-done.79), channel_id=1, source_target_pairs={{0,8},{8,16},{16,24},{1,9},{9,17},{17,25},{2,10},{10,18},{18,26},{... | collective-permute-start | bytes 1572872 | tf_op jit(solution)/shard_map/cond/branch_1_fun/ppermute | solution.py:197
  119.8 11.0 %collective-permute-done.80 = bf16[1024,256]{1,0:T(8,128)(2,1)S(1)} collective-permute-done((bf16[1024,256]{1,0:T(8,128)(2,1)S(1)}, bf16[1024,256]{1,0:T(8,128)(2,1)S(1)}, u32[]{:S(2)}, u32[]{:S(2)}) %collective-permute-start.80) | collective-permute-done | bytes 524320 | tf_op jit(solution)/shard_map/cond/branch_1_fun/ppermute | solution.py:197
  162.1 16.0 %shard_map.169 = (bf16[1024,256]{1,0:T(8,128)(2,1)}, f32[1024,1]{1,0:T(8,128)}) custom-call(bf16[1024,256]{1,0:T(8,128)(2,1)S(1)} %get-tuple-element.238.q_ref, bf16[3072,256]{1,0:T(8,128)(2,1)S(1)} %get-tuple-element.151.k_ref, bf16[3072,256]{1,0:T(8,128)(2,1)} %get-tuple-element.152.v_ref, s32[1024,1]{1,0:T(8,128)} %add_maximum_fusion.low_ref, ...), custom_call_target="tpu_custom_call" | custom-call | flops 1 | bytes 1 | tf_op jit(solution)/shard_map/pallas_call | solution.py:265
  183.2 44.3 %conditional.16 = (f32[128,2304]{1,0:T(8,128)S(1)}) conditional(s32[]{:T(128)} %bitcast.63, () %tuple.126, bf16[1024,2304]{1,0:T(8,128)(2,1)} %fusion.127), branch_computations={%region_9.10_spmd, %region_10.11_spmd} | conditional | flops 5603328 | bytes 64291092 | solution.py:160
  193.8 19.1 %collective-permute-done.68 = bf16[1,1,2,128,1152]{4,3,2,1,0:T(8,128)(2,1)S(1)} collective-permute-done((bf16[1,1,2,128,1152]{4,3,2,1,0:T(8,128)(2,1)S(1)}, bf16[1,1,2,128,1152]{4,3,2,1,0:T(8,128)(2,1)S(1)}, u32[]{:S(2)}, u32[]{:S(2)}) %collective-permute-start.68) | collective-permute-done | bytes 589856 | tf_op jit(solution)/shard_map/cond/branch_1_fun/ppermute | solution.py:112
  230.9 11.0 %all-to-all-start.3 = ((bf16[16,72,1152]{2,1,0:T(8,128)(2,1)}), bf16[16,72,1152]{2,1,0:T(8,128)(2,1)}, u32[]{:S(2)}, u32[]{:S(2)}) async-start(bf16[16,72,1152]{2,1,0:T(8,128)(2,1)} %bitcast.272), calls=%async_computation.3 | async-start | bytes 5308416 | tf_op jit(solution)/shard_map/all_to_all | solution.py:294
  251.2 73.4 %conditional.17 = (bf16[1024,2304]{1,0:T(8,128)(2,1)}) conditional(s32[]{:T(128)} %bitcast.63, () %tuple.132, bf16[128,2304]{1,0:T(8,128)(2,1)S(1)} %multiply_convert_fusion.5), branch_computations={%region_13.14_spmd, %region_14.15_spmd} | conditional | flops 59572224 | bytes 34210160 | solution.py:160
  266.8 23.3 %collective-permute-done.11 = bf16[1,1,1,128,768]{4,3,2,1,0:T(8,128)(2,1)S(1)} collective-permute-done((bf16[1,1,1,128,768]{4,3,2,1,0:T(8,128)(2,1)S(1)}, bf16[1,1,1,128,768]{4,3,2,1,0:T(8,128)(2,1)S(1)}, u32[]{:S(2)}, u32[]{:S(2)}) %collective-permute-start.11) | collective-permute-done | bytes 196640 | tf_op jit(solution)/shard_map/cond/branch_1_fun/ppermute | solution.py:112
  303.1 15.6 %collective-permute-done.19 = bf16[2,1,2,128,768]{4,3,2,1,0:T(8,128)(2,1)S(1)} collective-permute-done((bf16[2,1,2,128,768]{4,3,2,1,0:T(8,128)(2,1)S(1)}, bf16[2,1,2,128,768]{4,3,2,1,0:T(8,128)(2,1)S(1)}, u32[]{:S(2)}, u32[]{:S(2)}) %collective-permute-start.19) | collective-permute-done | bytes 786464 | tf_op jit(solution)/shard_map/cond/branch_1_fun/ppermute | solution.py:112
  331.7 46.2 %conditional.18 = (bf16[2304,1152]{1,0:T(8,128)(2,1)}, bf16[2304,1152]{1,0:T(8,128)(2,1)}, bf16[2304]{0:T(1024)(128)(2,1)S(1)}) conditional(s32[]{:T(128)} %bitcast.63, () %tuple.133, (bf16[2,8,72,1152]{3,2,1,0:T(8,128)(2,1)}, bf16[2,8,72,1152]{3,2,1,0:T(8,128)(2,1)}) %tuple.137), branch_computations={%region_15.16_spmd, %region_16.19_spmd} | conditional | flops 167238144 | bytes 63788804 | solution.py:160
  336.6 12.4 %multiply_convert_fusion.1 = bf16[2,8,72,1152]{3,2,1,0:T(8,128)(2,1)} fusion(bf16[2,8,72,1152]{3,2,1,0:T(8,128)(2,1)} %get-tuple-element.90, f32[1152]{0:T(1024)S(1)} %fusion.4, f32[1152]{0:T(1024)S(1)} %get-tuple-element.253), kind=kLoop, calls=%fused_computation.44 | loop fusion | flops 80953344 | bytes 5317632 | tf_op jit(solution)/shard_map/cond/branch_1_fun/convert_element_type | solution.py:400
  349.0 12.4 %multiply_convert_fusion = bf16[2,8,72,1152]{3,2,1,0:T(8,128)(2,1)} fusion(bf16[2,8,72,1152]{3,2,1,0:T(8,128)(2,1)} %get-tuple-element.91, f32[1152]{0:T(1024)S(1)} %fusion.2, f32[1152]{0:T(1024)S(1)} %get-tuple-element.251), kind=kLoop, calls=%fused_computation.43 | loop fusion | flops 80953344 | bytes 5317632 | tf_op jit(solution)/shard_map/cond/branch_1_fun/convert_element_type | solution.py:400
  377.9 9.7 %fusion.128 = f32[1024,1152]{1,0:T(8,128)S(1)} fusion(bf16[1024,2304]{1,0:T(8,128)(2,1)} %get-tuple-element.372, bf16[2304,1152]{1,0:T(8,128)(2,1)} %get-tuple-element.158), kind=kOutput, calls=%fused_computation.375 | convolution fusion | flops 5435817984 | bytes 14745600 | tf_op jit(solution)/shard_map/dot_general | solution.py:103
  389.7 11.4 %fusion.42 = (bf16[1024,1152]{1,0:T(8,128)(2,1)S(1)}, f32[1024,1152]{1,0:T(8,128)}) fusion(f32[1024,1152]{1,0:T(8,128)S(1)} %fusion.128, bf16[1024,2304]{1,0:T(8,128)(2,1)} %get-tuple-element.372, bf16[2304,1152]{1,0:T(8,128)(2,1)} %get-tuple-element.159), kind=kOutput, calls=%fused_computation.195 | convolution fusion | flops 5447614464 | bytes 21823488 | tf_op jit(solution)/shard_map/dot_general | solution.py:103
  401.1 13.4 %conditional.19 = (bf16[2304,1152]{1,0:T(8,128)(2,1)}) conditional(s32[]{:T(128)} %bitcast.63, () %tuple.138, bf16[2,8,72,1152]{3,2,1,0:T(8,128)(2,1)} %bitcast.88), branch_computations={%region_20.21_spmd, %region_21.22_spmd} | conditional | flops 6 | bytes 23887990 | solution.py:160
  414.6 9.0 fusion.129
  423.6 41.4 %conditional.20 = (f32[128,2304]{1,0:T(8,128)S(1)}, f32[128]{0:T(128)}, f32[128,1]{0,1:T(1,128)S(1)}) conditional(s32[]{:T(128)} %bitcast.63, () %tuple.131, bf16[1024,2304]{1,0:T(8,128)(2,1)S(1)} %fusion.129), branch_computations={%region_22.23_spmd, %region_23.25_spmd} | conditional | flops 6487936 | bytes 45418368 | solution.py:160
  428.8 14.7 %collective-permute-done.61 = bf16[2,1,2,128,768]{4,3,2,1,0:T(8,128)(2,1)S(1)} collective-permute-done((bf16[2,1,2,128,768]{4,3,2,1,0:T(8,128)(2,1)S(1)}, bf16[2,1,2,128,768]{4,3,2,1,0:T(8,128)(2,1)S(1)}, u32[]{:S(2)}, u32[]{:S(2)}) %collective-permute-start.61) | collective-permute-done | bytes 786464 | tf_op jit(solution)/shard_map/cond/branch_1_fun/ppermute | solution.py:112
  467.9 46.7 %conditional.21 = (bf16[1024,2304]{1,0:T(8,128)(2,1)}, f32[2,2,2,3328]{3,2,1,0:T(2,128)S(1)}) conditional(s32[]{:T(128)} %bitcast.63, () %tuple.143, (bf16[128,2304]{1,0:T(8,128)(2,1)S(1)}, bf16[2,256]{1,0:T(2,128)(2,1)S(1)}, bf16[2304]{0:T(1024)(128)(2,1)}) %tuple.247), branch_computations={%region_26.27_spmd, %region_27.28_spmd} | conditional | flops 59757056 | bytes 34886828 | solution.py:160
  494.7 14.7 %collective-permute-done.33 = bf16[2,1,2,128,768]{4,3,2,1,0:T(8,128)(2,1)S(1)} collective-permute-done((bf16[2,1,2,128,768]{4,3,2,1,0:T(8,128)(2,1)S(1)}, bf16[2,1,2,128,768]{4,3,2,1,0:T(8,128)(2,1)S(1)}, u32[]{:S(2)}, u32[]{:S(2)}) %collective-permute-start.33) | collective-permute-done | bytes 786464 | tf_op jit(solution)/shard_map/cond/branch_1_fun/ppermute | solution.py:112
  515.3 33.7 %conditional.22 = (bf16[2,8,72,1152]{3,2,1,0:T(8,128)(2,1)}, bf16[1024,1152]{1,0:T(8,128)(2,1)S(1)}, bf16[1024,1152]{1,0:T(8,128)(2,1)}) conditional(s32[]{:T(128)} %bitcast.63, () %tuple.142, (bf16[1024,2304]{1,0:T(8,128)(2,1)}, bf16[1024,1152]{1,0:T(8,128)(2,1)}, bf16[2304,1152]{1,0:T(8,128)(2,1)}, f32[1024,1152]{1,0:T(8,128)}, ...), branch_computations={%region_28.29_spmd, %region_29.30_spmd} | conditional | flops 10905255936 | bytes 81690824 | solution.py:160
  515.6 10.4 %fusion.124 = bf16[2304,1152]{1,0:T(8,128)(2,1)} fusion(bf16[1024,2304]{1,0:T(8,128)(2,1)} %get-tuple-element.97, bf16[1024,1152]{1,0:T(8,128)(2,1)} %get-tuple-element.96), kind=kOutput, calls=%fused_computation.371 | convolution fusion | flops 5435817984 | bytes 12386304 | tf_op jit(solution)/shard_map/cond/branch_1_fun/dot_general | solution.py:103
  529.5 15.4 %multiply_convert_fusion.2 = (bf16[1024,1152]{1,0:T(8,128)(2,1)}, bf16[1024,1152]{1,0:T(8,128)(2,1)S(1)}) fusion(f32[1024,1152]{1,0:T(8,128)} %get-tuple-element.100, f32[1024,1152]{1,0:T(8,128)} %get-tuple-element.99, bf16[1024,2304]{1,0:T(8,128)(2,1)} %get-tuple-element.97, bf16[2304,1152]{1,0:T(8,128)(2,1)} %get-tuple-element.98), kind=kOutput, calls=%fused_computation.116 | convolution fusion | flops 5464129536 | bytes 24182784 | tf_op jit(solution)/shard_map/cond/branch_1_fun/dot_general | solution.py:103
  548.9 11.2 %fusion.130 = f32[1024,2304]{1,0:T(8,128)} fusion(bf16[1024,1152]{1,0:T(8,128)(2,1)S(1)} %get-tuple-element.167, bf16[2304,1152]{1,0:T(8,128)(2,1)} %get-tuple-element.158), kind=kOutput, calls=%fused_computation.377 | convolution fusion | flops 5435817984 | bytes 17104896 | tf_op jit(solution)/shard_map/dot_general | solution.py:103
  566.1 10.8 %add_convert_fusion.2 = bf16[1024,2304]{1,0:T(8,128)(2,1)S(1)} fusion(f32[1024,2304]{1,0:T(8,128)} %fusion.130, bf16[1024,1152]{1,0:T(8,128)(2,1)} %get-tuple-element.168, bf16[2304,1152]{1,0:T(8,128)(2,1)} %get-tuple-element.159), kind=kOutput, calls=%fused_computation.177 | convolution fusion | flops 5440536576 | bytes 21823488 | tf_op jit(solution)/shard_map/dot_general | solution.py:103
  576.9 9.7 %fusion.131 = bf16[2304,1152]{1,0:T(8,128)(2,1)} fusion(bf16[2304,1024]{0,1:T(8,128)(2,1)} %bitcast.318, bf16[1024,1152]{1,0:T(8,128)(2,1)S(1)} %get-tuple-element.167), kind=kOutput, calls=%fused_computation.378 | convolution fusion | flops 5435817984 | bytes 12386304 | tf_op jit(solution)/shard_map/dot_general | solution.py:103
  586.7 10.5 %fusion.132 = bf16[2304,1152]{1,0:T(8,128)(2,1)} fusion(bf16[2304,1024]{0,1:T(8,128)(2,1)} %bitcast.319, bf16[1024,1152]{1,0:T(8,128)(2,1)} %get-tuple-element.168), kind=kOutput, calls=%fused_computation.379 | convolution fusion | flops 5435817984 | bytes 12386304 | tf_op jit(solution)/shard_map/dot_general | solution.py:103
  597.2 65.7 %conditional.23 = (f32[128,2304]{1,0:T(8,128)S(1)}, bf16[16,72,1152]{2,1,0:T(8,128)(2,1)}, bf16[16,72,1152]{2,1,0:T(8,128)(2,1)}) conditional(s32[]{:T(128)} %bitcast.63, () %tuple.141, (bf16[1024,2304]{1,0:T(8,128)(2,1)S(1)}, bf16[2304,1152]{1,0:T(8,128)(2,1)}, bf16[2304,1152]{1,0:T(8,128)(2,1)}) %tuple.146), branch_computations={%region_30.31_spmd, %region_31.32_spmd} | conditional | flops 16515081 | bytes 165151456 | solution.py:160
  608.5 16.2 %collective-permute-done.44 = bf16[2,1,2,128,768]{4,3,2,1,0:T(8,128)(2,1)} collective-permute-done((bf16[2,1,2,128,768]{4,3,2,1,0:T(8,128)(2,1)S(1)}, bf16[2,1,2,128,768]{4,3,2,1,0:T(8,128)(2,1)}, u32[]{:S(2)}, u32[]{:S(2)}) %collective-permute-start.44) | collective-permute-done | bytes 786464 | tf_op jit(solution)/shard_map/cond/branch_1_fun/ppermute | solution.py:112
  662.9 8.4 all-to-all-start.6
  676.9 51.7 %conditional.24 = (bf16[1024,2304]{1,0:T(8,128)(2,1)}) conditional(s32[]{:T(128)} %bitcast.63, () %tuple.148, bf16[128,2304]{1,0:T(8,128)(2,1)S(1)} %fusion.69), branch_computations={%region_34.35_spmd, %region_35.36_spmd} | conditional | flops 40697856 | bytes 34210040 | solution.py:160
  680.4 10.6 %collective-permute-done.52 = bf16[1,1,1,128,1152]{4,3,2,1,0:T(8,128)(2,1)S(1)} collective-permute-done((bf16[1,1,1,128,1152]{4,3,2,1,0:T(8,128)(2,1)S(1)}, bf16[1,1,1,128,1152]{4,3,2,1,0:T(8,128)(2,1)S(1)}, u32[]{:S(2)}, u32[]{:S(2)}) %collective-permute-start.52) | collective-permute-done | bytes 294944 | tf_op jit(solution)/shard_map/cond/branch_1_fun/ppermute | solution.py:112
  691.2 9.1 collective-permute-done.49
  701.9 11.0 %collective-permute-done.53 = bf16[1,1,2,128,1152]{4,3,2,1,0:T(8,128)(2,1)S(1)} collective-permute-done((bf16[1,1,2,128,1152]{4,3,2,1,0:T(8,128)(2,1)S(1)}, bf16[1,1,2,128,1152]{4,3,2,1,0:T(8,128)(2,1)S(1)}, u32[]{:S(2)}, u32[]{:S(2)}) %collective-permute-start.53) | collective-permute-done | bytes 589856 | tf_op jit(solution)/shard_map/cond/branch_1_fun/ppermute | solution.py:112
  713.0 8.7 collective-permute-done.50
  740.9 24.5 %shard_map.170 = (bf16[1024,256]{1,0:T(8,128)(2,1)}, f32[3072,256]{1,0:T(8,128)S(1)}, f32[3072,256]{1,0:T(8,128)}) custom-call(bf16[1024,256]{1,0:T(8,128)(2,1)S(1)} %copy-done.20, bf16[3072,256]{1,0:T(8,128)(2,1)S(1)} %copy-done.7, bf16[3072,256]{1,0:T(8,128)(2,1)} %get-tuple-element.152.v_ref, s32[1024,1]{1,0:T(8,128)} %add_maximum_fusion.low_ref, ...), custom_call_target="tpu_custom_call" | custom-call | flops 1 | bytes 1 | tf_op jit(solution)/shard_map/pallas_call | solution.py:280
  767.5 60.3 %conditional.25 = (f32[1024,256]{1,0:T(8,128)}, f32[1024,128]{1,0:T(8,128)}, f32[1024,128]{1,0:T(8,128)}) conditional(s32[]{:T(128)} %bitcast.63, () %tuple.149, (s32[]{:T(128)}, f32[3072,256]{1,0:T(8,128)S(1)}, f32[3072,256]{1,0:T(8,128)}) %tuple.150), branch_computations={%region_36.37_spmd, %region_37.38_spmd} | conditional | flops 8126465 | bytes 62390456 | solution.py:160
  775.1 22.0 %collective-permute-done.71 = bf16[1024,256]{1,0:T(8,128)(2,1)S(1)} collective-permute-done((bf16[1024,256]{1,0:T(8,128)(2,1)S(1)}, bf16[1024,256]{1,0:T(8,128)(2,1)S(1)}, u32[]{:S(2)}, u32[]{:S(2)}) %collective-permute-start.71) | collective-permute-done | bytes 524320 | tf_op jit(solution)/shard_map/cond/branch_1_fun/ppermute | solution.py:197
  798.6 25.4 %collective-permute-done.72 = bf16[1024,256]{1,0:T(8,128)(2,1)S(1)} collective-permute-done((bf16[1024,256]{1,0:T(8,128)(2,1)S(1)}, bf16[1024,256]{1,0:T(8,128)(2,1)S(1)}, u32[]{:S(2)}, u32[]{:S(2)}) %collective-permute-start.72) | collective-permute-done | bytes 524320 | tf_op jit(solution)/shard_map/cond/branch_1_fun/ppermute | solution.py:197
  850.1 54.5 %conditional.26 = (f32[128,2304]{1,0:T(8,128)S(1)}) conditional(s32[]{:T(128)} %bitcast.63, () %tuple.147, bf16[1024,2304]{1,0:T(8,128)(2,1)} %add_convert_fusion.1), branch_computations={%region_38.39_spmd, %region_39.40_spmd} | conditional | flops 5603328 | bytes 64291092 | solution.py:160
  860.5 29.8 %collective-permute-done.77 = bf16[1,1,2,128,1152]{4,3,2,1,0:T(8,128)(2,1)S(1)} collective-permute-done((bf16[1,1,2,128,1152]{4,3,2,1,0:T(8,128)(2,1)S(1)}, bf16[1,1,2,128,1152]{4,3,2,1,0:T(8,128)(2,1)S(1)}, u32[]{:S(2)}, u32[]{:S(2)}) %collective-permute-start.77) | collective-permute-done | bytes 589856 | tf_op jit(solution)/shard_map/cond/branch_1_fun/ppermute | solution.py:112
  905.4 20.2 %conditional.27 = (f32[4,2304]{1,0:T(4,128)S(1)}) conditional(s32[]{:T(128)} %bitcast.63, () %tuple.154, f32[4,2304]{1,0:T(4,128)S(1)} %pad_maximum_fusion.37), branch_computations={%region_49.50_spmd, %region_50.51_spmd} | conditional | flops 46080 | bytes 1290448 | solution.py:160
  (579 shorter events, 461.7 us)
Async XLA Ops:
  3.7 69.1 %all-to-all-start = ((bf16[32,2,72,256]{3,2,1,0:T(8,128)(2,1)}), bf16[32,2,72,256]{3,2,1,0:T(8,128)(2,1)S(1)}, u32[]{:S(2)}, u32[]{:S(2)}) async-start(bf16[32,2,72,256]{3,2,1,0:T(8,128)(2,1)} %bitcast.280), calls=%async_computation | async-start | bytes 4718592 | tf_op jit(solution)/shard_map/all_to_all | solution.py:294
  21.1 20.3 %collective-permute-start.8 = (bf16[1,1,1,128,1152]{4,3,2,1,0:T(8,128)(2,1)S(1)}, bf16[1,1,1,128,1152]{4,3,2,1,0:T(8,128)(2,1)S(1)}, u32[]{:S(2)}, u32[]{:S(2)}) collective-permute-start(bf16[1,1,1,128,1152]{4,3,2,1,0:T(8,128)(2,1)S(1)} %get-tuple-element.261), channel_id=1, source_target_pairs={{0,2},{2,0},{1,3},{3,1},{4,6},{6,4},{5,7},{7,5},{8,10},{10,8},{9,1... | collective-permute-start | bytes 884744 | tf_op jit(solution)/shard_map/cond/branch_1_fun/ppermute | solution.py:112
  23.0 20.4 %collective-permute-start.5 = (bf16[1,1,1,128,1152]{4,3,2,1,0:T(8,128)(2,1)S(1)}, bf16[1,1,1,128,1152]{4,3,2,1,0:T(8,128)(2,1)S(1)}, u32[]{:S(2)}, u32[]{:S(2)}) collective-permute-start(bf16[1,1,1,128,1152]{4,3,2,1,0:T(8,128)(2,1)S(1)} %get-tuple-element.260), channel_id=1, source_target_pairs={{0,4},{4,0},{1,5},{5,1},{2,6},{6,2},{3,7},{7,3},{8,12},{12,8},{9,1... | collective-permute-start | bytes 884744 | tf_op jit(solution)/shard_map/cond/branch_1_fun/ppermute | solution.py:112
  41.5 18.6 %collective-permute-start.9 = (bf16[1,1,2,128,1152]{4,3,2,1,0:T(8,128)(2,1)S(1)}, bf16[1,1,2,128,1152]{4,3,2,1,0:T(8,128)(2,1)S(1)}, u32[]{:S(2)}, u32[]{:S(2)}) collective-permute-start(bf16[1,1,2,128,1152]{4,3,2,1,0:T(8,128)(2,1)S(1)} %pad_maximum_fusion.3), channel_id=1, source_target_pairs={{0,4},{4,0},{1,5},{5,1},{2,6},{6,2},{3,7},{7,3},{8,12},{12,8},{9,1... | collective-permute-start | bytes 1769480 | tf_op jit(solution)/shard_map/cond/branch_1_fun/ppermute | solution.py:112
  43.4 19.0 %collective-permute-start.6 = (bf16[1,2,1,128,1152]{4,3,2,1,0:T(8,128)(2,1)S(1)}, bf16[1,2,1,128,1152]{4,3,2,1,0:T(8,128)(2,1)S(1)}, u32[]{:S(2)}, u32[]{:S(2)}) collective-permute-start(bf16[1,2,1,128,1152]{4,3,2,1,0:T(8,128)(2,1)S(1)} %pad_maximum_fusion.2), channel_id=1, source_target_pairs={{0,2},{2,0},{1,3},{3,1},{4,6},{6,4},{5,7},{7,5},{8,10},{10,8},{9,1... | collective-permute-start | bytes 1769480 | tf_op jit(solution)/shard_map/cond/branch_1_fun/ppermute | solution.py:112
  74.1 70.6 %all-to-all-start.1 = ((bf16[32,72,256]{2,1,0:T(8,128)(2,1)}), bf16[32,72,256]{2,1,0:T(8,128)(2,1)}, u32[]{:S(2)}, u32[]{:S(2)}) async-start(bf16[32,72,256]{2,1,0:T(8,128)(2,1)} %bitcast.323), calls=%async_computation.1 | async-start | bytes 2359296 | tf_op jit(solution)/shard_map/all_to_all | solution.py:294
  94.8 15.2 %collective-permute-start.79 = (bf16[1024,256]{1,0:T(8,128)(2,1)S(1)}, bf16[1024,256]{1,0:T(8,128)(2,1)S(1)}, u32[]{:S(2)}, u32[]{:S(2)}) collective-permute-start(bf16[1024,256]{1,0:T(8,128)(2,1)S(1)} %get-tuple-element.85), channel_id=1, source_target_pairs={{0,8},{8,16},{16,24},{1,9},{9,17},{17,25},{2,10},{10,18},{18,26},{... | collective-permute-start | bytes 1572872 | tf_op jit(solution)/shard_map/cond/branch_1_fun/ppermute | solution.py:197
  110.0 20.8 %collective-permute-start.80 = (bf16[1024,256]{1,0:T(8,128)(2,1)S(1)}, bf16[1024,256]{1,0:T(8,128)(2,1)S(1)}, u32[]{:S(2)}, u32[]{:S(2)}) collective-permute-start(bf16[1024,256]{1,0:T(8,128)(2,1)S(1)} %collective-permute-done.79), channel_id=1, source_target_pairs={{0,8},{8,16},{16,24},{1,9},{9,17},{17,25},{2,10},{10,18},{18,26},{... | collective-permute-start | bytes 1572872 | tf_op jit(solution)/shard_map/cond/branch_1_fun/ppermute | solution.py:197
  148.5 78.9 %all-to-all-start.2 = ((bf16[16,72,1152]{2,1,0:T(8,128)(2,1)}), bf16[16,72,1152]{2,1,0:T(8,128)(2,1)}, u32[]{:S(2)}, u32[]{:S(2)}) async-start(bf16[16,72,1152]{2,1,0:T(8,128)(2,1)} %bitcast.273), calls=%async_computation.2 | async-start | bytes 5308416 | tf_op jit(solution)/shard_map/all_to_all | solution.py:294
  190.3 22.7 %collective-permute-start.68 = (bf16[1,1,2,128,1152]{4,3,2,1,0:T(8,128)(2,1)S(1)}, bf16[1,1,2,128,1152]{4,3,2,1,0:T(8,128)(2,1)S(1)}, u32[]{:S(2)}, u32[]{:S(2)}) collective-permute-start(bf16[1,1,2,128,1152]{4,3,2,1,0:T(8,128)(2,1)S(1)} %slice.565), channel_id=1, source_target_pairs={{0,4},{4,0},{1,5},{5,1},{2,6},{6,2},{3,7},{7,3},{8,12},{12,8},{9,1... | collective-permute-start | bytes 1769480 | tf_op jit(solution)/shard_map/cond/branch_1_fun/ppermute | solution.py:112
  192.3 22.6 %collective-permute-start.65 = (bf16[1,2,1,128,1152]{4,3,2,1,0:T(8,128)(2,1)S(1)}, bf16[1,2,1,128,1152]{4,3,2,1,0:T(8,128)(2,1)S(1)}, u32[]{:S(2)}, u32[]{:S(2)}) collective-permute-start(bf16[1,2,1,128,1152]{4,3,2,1,0:T(8,128)(2,1)S(1)} %slice.566), channel_id=1, source_target_pairs={{0,2},{2,0},{1,3},{3,1},{4,6},{6,4},{5,7},{7,5},{8,10},{10,8},{9,1... | collective-permute-start | bytes 1769480 | tf_op jit(solution)/shard_map/cond/branch_1_fun/ppermute | solution.py:112
  215.1 12.2 %collective-permute-start.66 = (bf16[1,1,1,128,1152]{4,3,2,1,0:T(8,128)(2,1)S(1)}, bf16[1,1,1,128,1152]{4,3,2,1,0:T(8,128)(2,1)S(1)}, u32[]{:S(2)}, u32[]{:S(2)}) collective-permute-start(bf16[1,1,1,128,1152]{4,3,2,1,0:T(8,128)(2,1)S(1)} %slice.568), channel_id=1, source_target_pairs={{0,4},{4,0},{1,5},{5,1},{2,6},{6,2},{3,7},{7,3},{8,12},{12,8},{9,1... | collective-permute-start | bytes 884744 | tf_op jit(solution)/shard_map/cond/branch_1_fun/ppermute | solution.py:112
  230.9 93.7 %all-to-all-start.3 = ((bf16[16,72,1152]{2,1,0:T(8,128)(2,1)}), bf16[16,72,1152]{2,1,0:T(8,128)(2,1)}, u32[]{:S(2)}, u32[]{:S(2)}) async-start(bf16[16,72,1152]{2,1,0:T(8,128)(2,1)} %bitcast.272), calls=%async_computation.3 | async-start | bytes 5308416 | tf_op jit(solution)/shard_map/all_to_all | solution.py:294
  253.2 12.0 %collective-permute-start.14 = (bf16[1,1,1,128,768]{4,3,2,1,0:T(8,128)(2,1)S(1)}, bf16[1,1,1,128,768]{4,3,2,1,0:T(8,128)(2,1)S(1)}, u32[]{:S(2)}, u32[]{:S(2)}) collective-permute-start(bf16[1,1,1,128,768]{4,3,2,1,0:T(8,128)(2,1)S(1)} %get-tuple-element.274), channel_id=1, source_target_pairs={{0,4},{4,0},{1,5},{5,1},{2,6},{6,2},{3,7},{7,3},{8,12},{12,8},{9,1... | collective-permute-start | bytes 589832 | tf_op jit(solution)/shard_map/cond/branch_1_fun/ppermute | solution.py:112
  254.7 35.4 %collective-permute-start.11 = (bf16[1,1,1,128,768]{4,3,2,1,0:T(8,128)(2,1)S(1)}, bf16[1,1,1,128,768]{4,3,2,1,0:T(8,128)(2,1)S(1)}, u32[]{:S(2)}, u32[]{:S(2)}) collective-permute-start(bf16[1,1,1,128,768]{4,3,2,1,0:T(8,128)(2,1)S(1)} %get-tuple-element.272), channel_id=1, source_target_pairs={{0,8},{8,0},{1,9},{9,1},{2,10},{10,2},{3,11},{11,3},{4,12},{12,4},... | collective-permute-start | bytes 589832 | tf_op jit(solution)/shard_map/cond/branch_1_fun/ppermute | solution.py:112
  261.0 38.9 %collective-permute-start.18 = (bf16[1,1,2,128,768]{4,3,2,1,0:T(8,128)(2,1)S(1)}, bf16[1,1,2,128,768]{4,3,2,1,0:T(8,128)(2,1)S(1)}, u32[]{:S(2)}, u32[]{:S(2)}) collective-permute-start(bf16[1,1,2,128,768]{4,3,2,1,0:T(8,128)(2,1)S(1)} %pad_maximum_fusion.13), channel_id=1, source_target_pairs={{0,8},{8,0},{1,9},{9,1},{2,10},{10,2},{3,11},{11,3},{4,12},{12,4},... | collective-permute-start | bytes 1179656 | tf_op jit(solution)/shard_map/cond/branch_1_fun/ppermute | solution.py:112
  265.3 36.0 %collective-permute-start.15 = (bf16[1,2,1,128,768]{4,3,2,1,0:T(8,128)(2,1)S(1)}, bf16[1,2,1,128,768]{4,3,2,1,0:T(8,128)(2,1)S(1)}, u32[]{:S(2)}, u32[]{:S(2)}) collective-permute-start(bf16[1,2,1,128,768]{4,3,2,1,0:T(8,128)(2,1)S(1)} %pad_maximum_fusion.12), channel_id=1, source_target_pairs={{0,2},{2,0},{1,3},{3,1},{4,6},{6,4},{5,7},{7,5},{8,10},{10,8},{9,1... | collective-permute-start | bytes 1179656 | tf_op jit(solution)/shard_map/cond/branch_1_fun/ppermute | solution.py:112
  300.1 18.6 %collective-permute-start.19 = (bf16[2,1,2,128,768]{4,3,2,1,0:T(8,128)(2,1)S(1)}, bf16[2,1,2,128,768]{4,3,2,1,0:T(8,128)(2,1)S(1)}, u32[]{:S(2)}, u32[]{:S(2)}) collective-permute-start(bf16[2,1,2,128,768]{4,3,2,1,0:T(8,128)(2,1)S(1)} %pad_maximum_fusion.10), channel_id=1, source_target_pairs={{0,4},{4,0},{1,5},{5,1},{2,6},{6,2},{3,7},{7,3},{8,12},{12,8},{9,1... | collective-permute-start | bytes 2359304 | tf_op jit(solution)/shard_map/cond/branch_1_fun/ppermute | solution.py:112
  301.4 18.3 %collective-permute-start.16 = (bf16[1,2,2,128,768]{4,3,2,1,0:T(8,128)(2,1)S(1)}, bf16[1,2,2,128,768]{4,3,2,1,0:T(8,128)(2,1)S(1)}, u32[]{:S(2)}, u32[]{:S(2)}) collective-permute-start(bf16[1,2,2,128,768]{4,3,2,1,0:T(8,128)(2,1)S(1)} %pad_maximum_fusion.9), channel_id=1, source_target_pairs={{0,8},{8,0},{1,9},{9,1},{2,10},{10,2},{3,11},{11,3},{4,12},{12,4},... | collective-permute-start | bytes 2359304 | tf_op jit(solution)/shard_map/cond/branch_1_fun/ppermute | solution.py:112
  301.6 18.3 %collective-permute-start.13 = (bf16[2,2,1,128,768]{4,3,2,1,0:T(8,128)(2,1)S(1)}, bf16[2,2,1,128,768]{4,3,2,1,0:T(8,128)(2,1)S(1)}, u32[]{:S(2)}, u32[]{:S(2)}) collective-permute-start(bf16[2,2,1,128,768]{4,3,2,1,0:T(8,128)(2,1)S(1)} %pad_maximum_fusion.8), channel_id=1, source_target_pairs={{0,2},{2,0},{1,3},{3,1},{4,6},{6,4},{5,7},{7,5},{8,10},{10,8},{9,1... | collective-permute-start | bytes 2359304 | tf_op jit(solution)/shard_map/cond/branch_1_fun/ppermute | solution.py:112
  326.3 74.8 %all-to-all-start.4 = ((bf16[16,72,1152]{2,1,0:T(8,128)(2,1)}), bf16[16,72,1152]{2,1,0:T(8,128)(2,1)}, u32[]{:S(2)}, u32[]{:S(2)}) async-start(bf16[16,72,1152]{2,1,0:T(8,128)(2,1)} %bitcast.274), calls=%async_computation.4 | async-start | bytes 5308416 | tf_op jit(solution)/shard_map/all_to_all | solution.py:294
  336.0 13.0 %collective-permute-start.22 = (bf16[1152]{0:T(1024)(128)(2,1)S(1)}, bf16[1152]{0:T(1024)(128)(2,1)S(1)}, u32[]{:S(2)}, u32[]{:S(2)}) collective-permute-start(bf16[1152]{0:T(1024)(128)(2,1)S(1)} %abs_reduce_fusion), channel_id=1, source_target_pairs={{0,1},{1,0},{2,3},{3,2},{4,5},{5,4},{6,7},{7,6},{8,9},{9,8},{10,11... | collective-permute-start | bytes 6920 | tf_op jit(solution)/shard_map/cond/branch_1_fun/ppermute | solution.py:112
  349.0 12.9 %collective-permute-start.21 = (bf16[2,8,72,1152]{3,2,1,0:T(8,128)(2,1)}, bf16[2,8,72,1152]{3,2,1,0:T(8,128)(2,1)}, u32[]{:S(2)}, u32[]{:S(2)}) collective-permute-start(bf16[2,8,72,1152]{3,2,1,0:T(8,128)(2,1)} %multiply_convert_fusion.1), channel_id=1, source_target_pairs={{0,1},{1,0},{2,3},{3,2},{4,5},{5,4},{6,7},{7,6},{8,9},{9,8},{10,11... | collective-permute-start | bytes 7962632 | tf_op jit(solution)/shard_map/cond/branch_1_fun/ppermute | solution.py:112
  423.7 19.8 %collective-permute-start.61 = (bf16[2,1,2,128,768]{4,3,2,1,0:T(8,128)(2,1)S(1)}, bf16[2,1,2,128,768]{4,3,2,1,0:T(8,128)(2,1)S(1)}, u32[]{:S(2)}, u32[]{:S(2)}) collective-permute-start(bf16[2,1,2,128,768]{4,3,2,1,0:T(8,128)(2,1)S(1)} %slice.401), channel_id=1, source_target_pairs={{0,4},{4,0},{1,5},{5,1},{2,6},{6,2},{3,7},{7,3},{8,12},{12,8},{9,1... | collective-permute-start | bytes 2359304 | tf_op jit(solution)/shard_map/cond/branch_1_fun/ppermute | solution.py:112
  425.7 19.8 %collective-permute-start.58 = (bf16[1,2,2,128,768]{4,3,2,1,0:T(8,128)(2,1)S(1)}, bf16[1,2,2,128,768]{4,3,2,1,0:T(8,128)(2,1)S(1)}, u32[]{:S(2)}, u32[]{:S(2)}) collective-permute-start(bf16[1,2,2,128,768]{4,3,2,1,0:T(8,128)(2,1)S(1)} %slice.395), channel_id=1, source_target_pairs={{0,8},{8,0},{1,9},{9,1},{2,10},{10,2},{3,11},{11,3},{4,12},{12,4},... | collective-permute-start | bytes 2359304 | tf_op jit(solution)/shard_map/cond/branch_1_fun/ppermute | solution.py:112
  427.2 20.0 %collective-permute-start.55 = (bf16[2,2,1,128,768]{4,3,2,1,0:T(8,128)(2,1)S(1)}, bf16[2,2,1,128,768]{4,3,2,1,0:T(8,128)(2,1)S(1)}, u32[]{:S(2)}, u32[]{:S(2)}) collective-permute-start(bf16[2,2,1,128,768]{4,3,2,1,0:T(8,128)(2,1)S(1)} %slice.389), channel_id=1, source_target_pairs={{0,2},{2,0},{1,3},{3,1},{4,6},{6,4},{5,7},{7,5},{8,10},{10,8},{9,1... | collective-permute-start | bytes 2359304 | tf_op jit(solution)/shard_map/cond/branch_1_fun/ppermute | solution.py:112
  491.6 17.7 %collective-permute-start.33 = (bf16[2,1,2,128,768]{4,3,2,1,0:T(8,128)(2,1)S(1)}, bf16[2,1,2,128,768]{4,3,2,1,0:T(8,128)(2,1)S(1)}, u32[]{:S(2)}, u32[]{:S(2)}) collective-permute-start(bf16[2,1,2,128,768]{4,3,2,1,0:T(8,128)(2,1)S(1)} %pad_maximum_fusion.18), channel_id=1, source_target_pairs={{0,4},{4,0},{1,5},{5,1},{2,6},{6,2},{3,7},{7,3},{8,12},{12,8},{9,1... | collective-permute-start | bytes 2359304 | tf_op jit(solution)/shard_map/cond/branch_1_fun/ppermute | solution.py:112
  492.4 17.3 %collective-permute-start.30 = (bf16[1,2,2,128,768]{4,3,2,1,0:T(8,128)(2,1)S(1)}, bf16[1,2,2,128,768]{4,3,2,1,0:T(8,128)(2,1)S(1)}, u32[]{:S(2)}, u32[]{:S(2)}) collective-permute-start(bf16[1,2,2,128,768]{4,3,2,1,0:T(8,128)(2,1)S(1)} %pad_maximum_fusion.17), channel_id=1, source_target_pairs={{0,8},{8,0},{1,9},{9,1},{2,10},{10,2},{3,11},{11,3},{4,12},{12,4},... | collective-permute-start | bytes 2359304 | tf_op jit(solution)/shard_map/cond/branch_1_fun/ppermute | solution.py:112
  493.2 16.6 %collective-permute-start.27 = (bf16[2,2,1,128,768]{4,3,2,1,0:T(8,128)(2,1)S(1)}, bf16[2,2,1,128,768]{4,3,2,1,0:T(8,128)(2,1)S(1)}, u32[]{:S(2)}, u32[]{:S(2)}) collective-permute-start(bf16[2,2,1,128,768]{4,3,2,1,0:T(8,128)(2,1)S(1)} %pad_maximum_fusion.16), channel_id=1, source_target_pairs={{0,2},{2,0},{1,3},{3,1},{4,6},{6,4},{5,7},{7,5},{8,10},{10,8},{9,1... | collective-permute-start | bytes 2359304 | tf_op jit(solution)/shard_map/cond/branch_1_fun/ppermute | solution.py:112
  529.5 15.4 %collective-permute-start.82 = (bf16[2,8,72,1152]{3,2,1,0:T(8,128)(2,1)}, bf16[2,8,72,1152]{3,2,1,0:T(8,128)(2,1)}, u32[]{:S(2)}, u32[]{:S(2)}) collective-permute-start(bf16[2,8,72,1152]{3,2,1,0:T(8,128)(2,1)} %dynamic-slice_bitcast_fusion), channel_id=1, source_target_pairs={{0,1},{1,0},{2,3},{3,2},{4,5},{5,4},{6,7},{7,6},{8,9},{9,8},{10,11... | collective-permute-start | bytes 7962632 | tf_op jit(solution)/shard_map/cond/branch_1_fun/ppermute | solution.py:112
  560.1 102.7 %all-to-all-start.5 = ((bf16[16,72,1152]{2,1,0:T(8,128)(2,1)}), bf16[16,72,1152]{2,1,0:T(8,128)(2,1)}, u32[]{:S(2)}, u32[]{:S(2)}) async-start(bf16[16,72,1152]{2,1,0:T(8,128)(2,1)} %bitcast.97), calls=%async_computation.5 | async-start | bytes 5308416 | tf_op jit(solution)/shard_map/all_to_all | solution.py:294
  597.4 27.3 %collective-permute-start.44 = (bf16[2,1,2,128,768]{4,3,2,1,0:T(8,128)(2,1)S(1)}, bf16[2,1,2,128,768]{4,3,2,1,0:T(8,128)(2,1)}, u32[]{:S(2)}, u32[]{:S(2)}) collective-permute-start(bf16[2,1,2,128,768]{4,3,2,1,0:T(8,128)(2,1)S(1)} %slice.419), channel_id=1, source_target_pairs={{0,4},{4,0},{1,5},{5,1},{2,6},{6,2},{3,7},{7,3},{8,12},{12,8},{9,1... | collective-permute-start | bytes 2359304 | tf_op jit(solution)/shard_map/cond/branch_1_fun/ppermute | solution.py:112
  599.6 32.7 %collective-permute-start.41 = (bf16[1,2,2,128,768]{4,3,2,1,0:T(8,128)(2,1)S(1)}, bf16[1,2,2,128,768]{4,3,2,1,0:T(8,128)(2,1)}, u32[]{:S(2)}, u32[]{:S(2)}) collective-permute-start(bf16[1,2,2,128,768]{4,3,2,1,0:T(8,128)(2,1)S(1)} %slice.413), channel_id=1, source_target_pairs={{0,8},{8,0},{1,9},{9,1},{2,10},{10,2},{3,11},{11,3},{4,12},{12,4},... | collective-permute-start | bytes 2359304 | tf_op jit(solution)/shard_map/cond/branch_1_fun/ppermute | solution.py:112
  601.2 34.2 %collective-permute-start.38 = (bf16[2,2,1,128,768]{4,3,2,1,0:T(8,128)(2,1)S(1)}, bf16[2,2,1,128,768]{4,3,2,1,0:T(8,128)(2,1)}, u32[]{:S(2)}, u32[]{:S(2)}) collective-permute-start(bf16[2,2,1,128,768]{4,3,2,1,0:T(8,128)(2,1)S(1)} %slice.407), channel_id=1, source_target_pairs={{0,2},{2,0},{1,3},{3,1},{4,6},{6,4},{5,7},{7,5},{8,10},{10,8},{9,1... | collective-permute-start | bytes 2359304 | tf_op jit(solution)/shard_map/cond/branch_1_fun/ppermute | solution.py:112
  606.3 48.4 %collective-permute-start.47 = (bf16[2,8,72,1152]{3,2,1,0:T(8,128)(2,1)}, bf16[2,8,72,1152]{3,2,1,0:T(8,128)(2,1)}, u32[]{:S(2)}, u32[]{:S(2)}) collective-permute-start(bf16[2,8,72,1152]{3,2,1,0:T(8,128)(2,1)} %dynamic-slice_bitcast_fusion.2), channel_id=1, source_target_pairs={{0,1},{1,0},{2,3},{3,2},{4,5},{5,4},{6,7},{7,6},{8,9},{9,8},{10,11... | collective-permute-start | bytes 7962632 | tf_op jit(solution)/shard_map/cond/branch_1_fun/ppermute | solution.py:112
  608.3 50.6 %collective-permute-start.48 = (bf16[2,8,72,1152]{3,2,1,0:T(8,128)(2,1)}, bf16[2,8,72,1152]{3,2,1,0:T(8,128)(2,1)}, u32[]{:S(2)}, u32[]{:S(2)}) collective-permute-start(bf16[2,8,72,1152]{3,2,1,0:T(8,128)(2,1)} %dynamic-slice_bitcast_fusion.1), channel_id=1, source_target_pairs={{0,1},{1,0},{2,3},{3,2},{4,5},{5,4},{6,7},{7,6},{8,9},{9,8},{10,11... | collective-permute-start | bytes 7962632 | tf_op jit(solution)/shard_map/cond/branch_1_fun/ppermute | solution.py:112
  626.3 13.6 %collective-permute-start.45 = (bf16[1,1,2,128,768]{4,3,2,1,0:T(8,128)(2,1)S(1)}, bf16[1,1,2,128,768]{4,3,2,1,0:T(8,128)(2,1)S(1)}, u32[]{:S(2)}, u32[]{:S(2)}) collective-permute-start(bf16[1,1,2,128,768]{4,3,2,1,0:T(8,128)(2,1)S(1)} %slice.575), channel_id=1, source_target_pairs={{0,8},{8,0},{1,9},{9,1},{2,10},{10,2},{3,11},{11,3},{4,12},{12,4},... | collective-permute-start | bytes 1179656 | tf_op jit(solution)/shard_map/cond/branch_1_fun/ppermute | solution.py:112
  662.9 65.8 %all-to-all-start.6 = ((bf16[16,72,1152]{2,1,0:T(8,128)(2,1)}), bf16[16,72,1152]{2,1,0:T(8,128)(2,1)}, u32[]{:S(2)}, u32[]{:S(2)}) async-start(bf16[16,72,1152]{2,1,0:T(8,128)(2,1)} %get-tuple-element.180), calls=%async_computation.6 | async-start | bytes 5308416 | tf_op jit(solution)/shard_map/all_to_all | solution.py:294
  677.0 14.0 %collective-permute-start.52 = (bf16[1,1,1,128,1152]{4,3,2,1,0:T(8,128)(2,1)S(1)}, bf16[1,1,1,128,1152]{4,3,2,1,0:T(8,128)(2,1)S(1)}, u32[]{:S(2)}, u32[]{:S(2)}) collective-permute-start(bf16[1,1,1,128,1152]{4,3,2,1,0:T(8,128)(2,1)S(1)} %get-tuple-element.289), channel_id=1, source_target_pairs={{0,2},{2,0},{1,3},{3,1},{4,6},{6,4},{5,7},{7,5},{8,10},{10,8},{9,1... | collective-permute-start | bytes 884744 | tf_op jit(solution)/shard_map/cond/branch_1_fun/ppermute | solution.py:112
  678.9 21.3 %collective-permute-start.49 = (bf16[1,1,1,128,1152]{4,3,2,1,0:T(8,128)(2,1)S(1)}, bf16[1,1,1,128,1152]{4,3,2,1,0:T(8,128)(2,1)S(1)}, u32[]{:S(2)}, u32[]{:S(2)}) collective-permute-start(bf16[1,1,1,128,1152]{4,3,2,1,0:T(8,128)(2,1)S(1)} %get-tuple-element.288), channel_id=1, source_target_pairs={{0,4},{4,0},{1,5},{5,1},{2,6},{6,2},{3,7},{7,3},{8,12},{12,8},{9,1... | collective-permute-start | bytes 884744 | tf_op jit(solution)/shard_map/cond/branch_1_fun/ppermute | solution.py:112
  691.1 21.7 %collective-permute-start.53 = (bf16[1,1,2,128,1152]{4,3,2,1,0:T(8,128)(2,1)S(1)}, bf16[1,1,2,128,1152]{4,3,2,1,0:T(8,128)(2,1)S(1)}, u32[]{:S(2)}, u32[]{:S(2)}) collective-permute-start(bf16[1,1,2,128,1152]{4,3,2,1,0:T(8,128)(2,1)S(1)} %pad_maximum_fusion.28), channel_id=1, source_target_pairs={{0,4},{4,0},{1,5},{5,1},{2,6},{6,2},{3,7},{7,3},{8,12},{12,8},{9,1... | collective-permute-start | bytes 1769480 | tf_op jit(solution)/shard_map/cond/branch_1_fun/ppermute | solution.py:112
  700.4 21.3 %collective-permute-start.50 = (bf16[1,2,1,128,1152]{4,3,2,1,0:T(8,128)(2,1)S(1)}, bf16[1,2,1,128,1152]{4,3,2,1,0:T(8,128)(2,1)S(1)}, u32[]{:S(2)}, u32[]{:S(2)}) collective-permute-start(bf16[1,2,1,128,1152]{4,3,2,1,0:T(8,128)(2,1)S(1)} %pad_maximum_fusion.27), channel_id=1, source_target_pairs={{0,2},{2,0},{1,3},{3,1},{4,6},{6,4},{5,7},{7,5},{8,10},{10,8},{9,1... | collective-permute-start | bytes 1769480 | tf_op jit(solution)/shard_map/cond/branch_1_fun/ppermute | solution.py:112
  728.7 111.8 %all-to-all-start.7 = ((bf16[16,72,1152]{2,1,0:T(8,128)(2,1)}), bf16[16,72,1152]{2,1,0:T(8,128)(2,1)}, u32[]{:S(2)}, u32[]{:S(2)}) async-start(bf16[16,72,1152]{2,1,0:T(8,128)(2,1)} %get-tuple-element.181), calls=%async_computation.7 | async-start | bytes 5308416 | tf_op jit(solution)/shard_map/all_to_all | solution.py:294
  773.8 23.3 %collective-permute-start.71 = (bf16[1024,256]{1,0:T(8,128)(2,1)S(1)}, bf16[1024,256]{1,0:T(8,128)(2,1)S(1)}, u32[]{:S(2)}, u32[]{:S(2)}) collective-permute-start(bf16[1024,256]{1,0:T(8,128)(2,1)S(1)} %fusion.31), channel_id=1, source_target_pairs={{8,0},{16,8},{24,16},{9,1},{17,9},{25,17},{10,2},{18,10},{26,18},{... | collective-permute-start | bytes 1572872 | tf_op jit(solution)/shard_map/cond/branch_1_fun/ppermute | solution.py:197
  797.3 26.7 %collective-permute-start.72 = (bf16[1024,256]{1,0:T(8,128)(2,1)S(1)}, bf16[1024,256]{1,0:T(8,128)(2,1)S(1)}, u32[]{:S(2)}, u32[]{:S(2)}) collective-permute-start(bf16[1024,256]{1,0:T(8,128)(2,1)S(1)} %fusion.27), channel_id=1, source_target_pairs={{8,0},{16,8},{24,16},{9,1},{17,9},{25,17},{10,2},{18,10},{26,18},{... | collective-permute-start | bytes 1572872 | tf_op jit(solution)/shard_map/cond/branch_1_fun/ppermute | solution.py:197
  840.5 99.5 %all-to-all-start.8 = ((bf16[32,3,72,256]{3,2,1,0:T(8,128)(2,1)}), bf16[32,3,72,256]{3,2,1,0:T(8,128)(2,1)}, u32[]{:S(2)}, u32[]{:S(2)}) async-start(bf16[32,3,72,256]{3,2,1,0:T(8,128)(2,1)} %pad_maximum_fusion.32), calls=%async_computation.8 | async-start | bytes 7077888 | tf_op jit(solution)/shard_map/all_to_all | solution.py:294
  857.3 33.1 %collective-permute-start.77 = (bf16[1,1,2,128,1152]{4,3,2,1,0:T(8,128)(2,1)S(1)}, bf16[1,1,2,128,1152]{4,3,2,1,0:T(8,128)(2,1)S(1)}, u32[]{:S(2)}, u32[]{:S(2)}) collective-permute-start(bf16[1,1,2,128,1152]{4,3,2,1,0:T(8,128)(2,1)S(1)} %slice.581), channel_id=1, source_target_pairs={{0,4},{4,0},{1,5},{5,1},{2,6},{6,2},{3,7},{7,3},{8,12},{12,8},{9,1... | collective-permute-start | bytes 1769480 | tf_op jit(solution)/shard_map/cond/branch_1_fun/ppermute | solution.py:112
  859.0 33.4 %collective-permute-start.74 = (bf16[1,2,1,128,1152]{4,3,2,1,0:T(8,128)(2,1)S(1)}, bf16[1,2,1,128,1152]{4,3,2,1,0:T(8,128)(2,1)S(1)}, u32[]{:S(2)}, u32[]{:S(2)}) collective-permute-start(bf16[1,2,1,128,1152]{4,3,2,1,0:T(8,128)(2,1)S(1)} %slice.582), channel_id=1, source_target_pairs={{0,2},{2,0},{1,3},{3,1},{4,6},{6,4},{5,7},{7,5},{8,10},{10,8},{9,1... | collective-permute-start | bytes 1769480 | tf_op jit(solution)/shard_map/cond/branch_1_fun/ppermute | solution.py:112
  (125 other events, 1661.1 us)

commit v5 on v4

--- a/solution.py
+++ b/solution.py
@@ -112,7 +112,7 @@
     return lax.ppermute(value, axis, SWAP)
 
 
-def gather_blocks(block, axes, orders):
+def gather_blocks(block, axes, orders, beside=()):
     rows, width = block.shape
     part = width // len(orders)
     parts = []
@@ -120,11 +120,13 @@
         held = block[:, i * part : (i + 1) * part].reshape((1,) * len(axes) + (rows, part))
         for axis in order:
             held = jnp.concatenate([held, swap(held, axis)], axis=axes.index(axis))
+            if axis == order[0]:
+                held = after(held, *beside)
         parts.append(held)
     return jnp.concatenate(parts, axis=-1).reshape(-1, width)
 
 
-def scatter_blocks(partial, axes, orders):
+def scatter_blocks(partial, axes, orders, beside=()):
     width = partial.shape[-1]
     part = width // len(orders)
     blocks = partial.reshape((2,) * len(axes) + (-1, width))
@@ -135,7 +137,10 @@
             at = axes.index(axis)
             keep = lax.slice_in_dim(held, 0, 1, axis=at)
             send = lax.slice_in_dim(held, 1, 2, axis=at).astype(bf16)
-            held = keep.astype(f32) + swap(send, axis).astype(f32)
+            come = swap(send, axis)
+            if axis == order[0]:
+                come = after(come, *beside)
+            held = keep.astype(f32) + come.astype(f32)
         parts.append(held.reshape(-1, part))
     return jnp.concatenate(parts, axis=-1)
 
@@ -342,15 +347,16 @@
     out_scale = jnp.max(jnp.abs(w_out.astype(f32)), axis=1) + EPSILON
     down_scale = jnp.max(jnp.abs(w_down.astype(f32)), axis=1) + EPSILON
     eff_out = nested(w_out.astype(f32), out_scale[:, None]).astype(bf16)
-    eff_down = nested(w_down.astype(f32), down_scale[:, None]).astype(bf16)
     eff_out = jnp.broadcast_to(columns(eff_out, 8)[None], (line_count, 8, own, HD))
     head_out = after(eff_out.reshape(line_count * 8, own, HD), qkv_lat, normed_all)
     head_out = exchange(head_out, FINE)
 
-    def spread(weight, *events):
+    def spread(weight):
         cols = jnp.broadcast_to(weight[None], (lax.axis_size("zh"),) + weight.shape)
-        cols = after(cols.reshape(-1, own, slice_ff), *events)
-        return exchange(cols, LINE + ("x", "y")).reshape(-1, 8, own, slice_ff)
+        return cols.reshape(-1, own, slice_ff)
+
+    def rows_of(sent, *events):
+        return exchange(after(sent, *events), LINE + ("x", "y")).reshape(-1, 8, own, slice_ff)
 
     head_out = head_out.reshape(model, HD)
 
@@ -379,25 +385,26 @@
     def flip(value):
         return jnp.concatenate([value[:, half_block:], value[:, :half_block]], axis=1)
 
-    def pass_up(own_rows, normed_all, head_q, cosine, sine_tab):
+    def pass_up(own_rows, normed_all, head_q, cosine, sine_tab, w_in):
         query = rotate(dot(normed_all, head_q, COLS), cosine, sine_tab).astype(bf16)
+        sent = spread(columns(w_in[:, :FF], 8))
         shifted = [own_rows]
         for _ in range(back):
-            shifted.append(shift(shifted[-1], 1))
+            shifted.append(after(shift(shifted[-1], 1), query, sent))
         mine = jnp.stack(shifted[::-1], axis=0)
         other = flip(swap(mine, "c"))
         keys = jnp.where(core == 0, mine, other).reshape(-1, HD)
         values = jnp.where(core == 0, other, mine).reshape(-1, HD)
-        return keys, values, query
-
-    key_rows, value_rows, query = apart(
-        run, pass_up, kv_own, normed_all, head_q, cosine, sine_tab
-    )
-
-    gate_lat = spread(columns(w_in[:, :FF], 8), head_out, key_rows)
-    def effective(lat):
+        return keys, values, query, sent
+
+    key_rows, value_rows, query, gate_sent = apart(
+        run, pass_up, kv_own, normed_all, head_q, cosine, sine_tab, w_in
+    )
+
+    gate_lat = rows_of(gate_sent, head_out, key_rows)
+    def quantize(lat):
         top = max_both(jnp.max(jnp.abs(lat), axis=(0, 1, 2)), "c")
-        return top, by_core(nested(lat.astype(f32), top.astype(f32) + EPSILON).astype(bf16))
+        return top, nested(lat.astype(f32), top.astype(f32) + EPSILON).astype(bf16)
 
     k_places = jnp.concatenate(
         [q_places - n * block_rows for n in range(back, -1, -1)], axis=0
@@ -408,19 +415,34 @@
 
     branch = dot(heads, head_out, ROWS, bf16)
 
-    branch = apart(run, scatter_plane, branch)
-    up_lat = spread(columns(w_in[:, FF:], 8), gate_lat, branch)
+
+    def scatter_branch(partial, w_in):
+        sent = spread(columns(w_in[:, FF:], 8))
+        return scatter_blocks(partial, TOKEN_AXES, PLANE_SCATTER, (sent,)), sent
+
+    branch, up_sent = apart(run, scatter_branch, branch, w_in)
+    up_lat = rows_of(up_sent, gate_lat, branch)
     middle = inputs + rms_scale(branch, gains[1])
     pre_mlp = rms_scale(middle, gains[2]).astype(bf16)
-    pre_all = apart(run, gather_cube, pre_mlp)
-    down_lat = spread(columns(eff_down, 8), up_lat, pre_all)
-
-    def both_effective(gate_lat, up_lat):
-        gate_top, cols_gate = effective(gate_lat)
-        up_top, cols_up = effective(up_lat)
-        return cols_gate, cols_up, jnp.concatenate([gate_top, up_top])
-
-    cols_gate, cols_up, in_tops = apart(run, both_effective, after(gate_lat, pre_all), up_lat)
+
+    def gather_pre(block, lat, w_down, down_scale):
+        top, low = quantize(lat)
+        eff_down = nested(w_down.astype(f32), down_scale[:, None]).astype(bf16)
+        down_sent = spread(columns(eff_down, 8))
+        tokens_all = gather_blocks(block, CUBE, CUBE_GATHER, (low, down_sent))
+        return tokens_all, top, by_core(low), down_sent
+
+    pre_all, gate_top, cols_gate, down_sent = apart(
+        run, gather_pre, pre_mlp, gate_lat, w_down, down_scale
+    )
+    down_lat = rows_of(down_sent, up_lat, pre_all)
+
+    def effective(lat):
+        top, low = quantize(lat)
+        return top, by_core(low)
+
+    up_top, cols_up = apart(run, effective, after(up_lat, cols_gate))
+    in_tops = jnp.concatenate([gate_top, up_top])
     pre_turned = lax.optimization_barrier(pre_all.T)
     gate_part = dot(pre_all, cols_gate, COLS)
     up_part = dot(pre_all, cols_up, COLS)
@@ -458,12 +480,13 @@
     down_back = collect(part_down)
     d_pre = (dot(d_gate, cols_gate, ROWS) + dot(d_up, cols_up, ROWS)).astype(bf16)
 
-    def scatter_pre(partial, gate, up):
-        return scatter_cube(partial), core_sum(gate, own), core_sum(up, own)
-
-    d_pre, part_gate, part_up = apart(
-        run, scatter_pre, d_pre, dot(pre_turned, d_gate, COLS, bf16), dot(pre_turned, d_up, COLS, bf16)
-    )
+    def scatter_pre(partial, pre_turned, d_gate, d_up):
+        gate = dot(pre_turned, d_gate, COLS, bf16)
+        up = dot(pre_turned, d_up, COLS, bf16)
+        total = scatter_blocks(partial, CUBE, CUBE_SCATTER, (gate, up))
+        return total, core_sum(gate, own), core_sum(up, own)
+
+    d_pre, part_gate, part_up = apart(run, scatter_pre, d_pre, pre_turned, d_gate, d_up)
     gate_back = collect(part_gate, down_back)
     d_mid_part, gain_three = jax.vjp(rms_scale, middle, gains[2])[1](d_pre)
     d_middle = grad_result + d_mid_part
@@ -476,17 +499,23 @@
         query, key_rows, value_rows, low, place, k_places[None], lse, d_heads
     )
 
-    def pass_down(d_keys, d_values):
+    def pass_down(d_keys, d_values, d_branch_all, heads, normed_all):
+        part_out = dot(d_branch_all, heads, FIRST, bf16)
+        normed_turned = lax.optimization_barrier(normed_all.T)
         d_keys = d_keys.reshape(back + 1, block_rows, HD)
         d_values = d_values.reshape(back + 1, block_rows, HD)
         send = flip(jnp.where(core == 0, d_values, d_keys).astype(bf16))
         window = jnp.where(core == 0, d_keys, d_values) + swap(send, "c").astype(f32)
         total = window[0]
         for n in range(1, back + 1):
-            total = window[n] + shift(total.astype(bf16), -1).astype(f32)
-        return total.astype(bf16)
-
-    d_kv = apart(run, pass_down, d_keys, d_values).astype(f32)
+            come = shift(total.astype(bf16), -1)
+            total = window[n] + after(come, part_out, normed_turned).astype(f32)
+        return total.astype(bf16), part_out, normed_turned
+
+    d_kv, part_out, normed_turned = apart(
+        run, pass_down, d_keys, d_values, d_branch_all, heads, normed_all
+    )
+    d_kv = d_kv.astype(f32)
     d_query_lin = rotate(d_query.astype(f32), cosine, -sine_tab).astype(bf16)
     d_second = jnp.where(core == 0, rotate(d_kv, cosine, -sine_tab), d_kv).astype(bf16)
 
@@ -495,8 +524,8 @@
     d_input_part, gain_one = jax.vjp(rms_scale, inputs, gains[0])[1](d_normed)
     grad_tokens = d_middle + d_input_part
 
-    parts = [dot(normed_all, d_query_lin, FIRST, bf16), dot(normed_all, d_second, FIRST, bf16)]
-    parts.append(dot(d_branch_all, heads, FIRST, bf16))
+    parts = [dot(normed_turned, d_query_lin, COLS, bf16), dot(normed_turned, d_second, COLS, bf16)]
+    parts.append(part_out)
     parts = jnp.stack([part.reshape(line_count * 8, own, HD) for part in parts], axis=1)
     sums = exchange(after(parts, up_back), FINE).reshape(line_count, 8, 3, own, HD)
     sums = jnp.sum(sums.astype(f32), axis=0)

time: 956 us -> 929 us (0.972)
  waiting for transfers between devices: 390 us -> 352 us
    ppermute x79, waiting for transfers between devices: 320 us -> 297 us  [swap(): return lax.ppermute(value, axis, SWAP)]
    ppermute x4, waiting for transfers between devices: 69.8 us -> 55.1 us  [shift(): lax.ppermute(value, LINE, [(i, i + step) for i in range(count) if 0 <= i...]
    ppermute x79, starting transfers between devices: 84.8 us -> 95.5 us  [swap(): return lax.ppermute(value, axis, SWAP)]
  transfers between devices with their start and end apart: 92 -> 92, of which waited for: 59 -> 61; matrix products, arithmetic and copies ran while one was open for 28% -> 32% of each run, Pallas kernels for 4% -> 4%
where the time goes in v5:
time: 929 us; the launch traced here: 919 us
  waiting for transfers between devices  352 us (38%)
  starting transfers between devices  168 us (18%)
  other arithmetic  141 us (15%)
  matrix products  127 us (14%)
  local copies, waits for them, and re-layouts  84.3 us (9%)
  Pallas kernels  41 us (4%)
    ppermute x79, waiting for transfers between devices, swap(): return lax.ppermute(value, axis, SWAP)  297 us
    dot_general x18, matrix products, dot(): lax.dot_general(left, right, (dims, ((), ())), preferred_element_type=out)  127 us
    ppermute x79, starting transfers between devices, swap(): return lax.ppermute(value, axis, SWAP)  95.5 us
    all_to_all x9, starting transfers between devices, exchange(): return lax.all_to_all(value, axes, split_axis=0, concat_axis=0, tiled=True)  56.7 us
    ppermute x4, waiting for transfers between devices, shift(): lax.ppermute(value, LINE, [(i, i + step) for i in range(count) if 0 <= i...  55.1 us
    pallas_call x1, Pallas kernels, attend_back(): pl.pallas_call(attend_back_kernel, out_shape=(jax.ShapeDtypeStruct((rows,...  25.1 us
    convert_element_type x2, other arithmetic, quantize(): nested(lat.astype(f32), top.astype(f32) + EPSILON).astype(bf16)  23.7 us
  transfers between devices with their start and end apart: 92, of which 61 were waited for; matrix products, arithmetic and copies ran while one was open for 32% of the time, Pallas kernels for 4%

profile of v5, /device:TPU:0, one launch (start us, length us, event | category | flops | bytes accessed | tf_op | source)
XLA Modules:
  0.0 919.1 jit_solution(14508518259362608625)
XLA Ops:
  16.7 52.8 %conditional.14 = (bf16[1024,2304]{1,0:T(8,128)(2,1)}) conditional(s32[]{:T(128)} %bitcast.71, () %tuple.146, bf16[128,2304]{1,0:T(8,128)(2,1)} %fusion.47), branch_computations={%region_1.0_spmd, %region_2.0_spmd} | conditional | flops 30081024 | bytes 34210040 | solution.py:165
  21.1 20.3 %collective-permute-done.8 = bf16[1,1,1,128,1152]{4,3,2,1,0:T(8,128)(2,1)S(1)} collective-permute-done((bf16[1,1,1,128,1152]{4,3,2,1,0:T(8,128)(2,1)S(1)}, bf16[1,1,1,128,1152]{4,3,2,1,0:T(8,128)(2,1)S(1)}, u32[]{:S(2)}, u32[]{:S(2)}) %collective-permute-start.8) | collective-permute-done | bytes 294944 | tf_op jit(solution)/shard_map/cond/branch_1_fun/ppermute | solution.py:112
  43.5 16.6 %collective-permute-done.9 = bf16[1,1,2,128,1152]{4,3,2,1,0:T(8,128)(2,1)S(1)} collective-permute-done((bf16[1,1,2,128,1152]{4,3,2,1,0:T(8,128)(2,1)S(1)}, bf16[1,1,2,128,1152]{4,3,2,1,0:T(8,128)(2,1)S(1)}, u32[]{:S(2)}, u32[]{:S(2)}) %collective-permute-start.9) | collective-permute-done | bytes 589856 | tf_op jit(solution)/shard_map/cond/branch_1_fun/ppermute | solution.py:112
  79.5 9.4 %multiply_convert_fusion.4 = bf16[4,8,2,72,256]{4,3,2,1,0:T(8,128)(2,1)S(1)} fusion(bf16[4,8,2,72,256]{4,3,2,1,0:T(8,128)(2,1)S(1)} %bitcast.264, f32[2,256]{1,0:T(2,128)S(1)} %get-tuple-element.379, f32[2,256]{1,0:T(2,128)S(1)} %get-tuple-element.378), kind=kLoop, calls=%fused_computation.204 | loop fusion | flops 71958528 | bytes 4722688 | tf_op jit(solution)/shard_map/convert_element_type | solution.py:365
  95.8 48.5 %conditional.15 = (bf16[3072,256]{1,0:T(8,128)(2,1)}, bf16[3072,256]{1,0:T(8,128)(2,1)}, bf16[16,72,1152]{2,1,0:T(8,128)(2,1)S(1)}, bf16[1024,256]{1,0:T(8,128)(2,1)}) conditional(s32[]{:T(128)} %bitcast.71, () %tuple.145, (s32[]{:T(128)}, bf16[1024,256]{1,0:T(8,128)(2,1)}, bf16[1024,2304]{1,0:T(8,128)(2,1)S(1)}, bf16[2304,256]{1,0:T(8,128)(2,1)S(1)}, ...), branch_computations={%region_6.7_spmd, %region_7.8_spmd} | conditional | flops 1221066752 | bytes 71975240 | solution.py:165
  111.4 9.0 collective-permute-start.66
  120.5 11.6 %collective-permute-done.66 = bf16[1024,256]{1,0:T(8,128)(2,1)S(1)} collective-permute-done((bf16[1024,256]{1,0:T(8,128)(2,1)}, bf16[1024,256]{1,0:T(8,128)(2,1)S(1)}, u32[]{:S(2)}, u32[]{:S(2)}) %collective-permute-start.66) | collective-permute-done | bytes 524320 | tf_op jit(solution)/shard_map/cond/branch_1_fun/ppermute | solution.py:202
  145.8 7.9 all-to-all-start.2
  158.4 15.9 %shard_map.169 = (bf16[1024,256]{1,0:T(8,128)(2,1)S(1)}, f32[1024,1]{1,0:T(8,128)}) custom-call(bf16[1024,256]{1,0:T(8,128)(2,1)} %get-tuple-element.302.q_ref, bf16[3072,256]{1,0:T(8,128)(2,1)} %get-tuple-element.197.k_ref, bf16[3072,256]{1,0:T(8,128)(2,1)} %get-tuple-element.198.v_ref, s32[1024,1]{1,0:T(8,128)} %add_maximum_fusion.low_ref, ...), custom_call_target="tpu_custom_call" | custom-call | flops 1 | bytes 1 | tf_op jit(solution)/shard_map/pallas_call | solution.py:270
  177.3 47.9 %conditional.16 = (f32[128,2304]{1,0:T(8,128)}, bf16[16,72,1152]{2,1,0:T(8,128)(2,1)}, f32[128]{0:T(128)S(1)}) conditional(s32[]{:T(128)} %bitcast.71, () %tuple.144, (bf16[1024,2304]{1,0:T(8,128)(2,1)S(1)}, bf16[72,18432]{1,0:T(8,128)(2,1)S(1)}) %tuple.270), branch_computations={%region_9.10_spmd, %region_10.11_spmd} | conditional | flops 6193024 | bytes 57361160 | solution.py:165
  186.2 19.6 %collective-permute-done.63 = bf16[1,1,2,128,1152]{4,3,2,1,0:T(8,128)(2,1)S(1)} collective-permute-done((bf16[1,1,2,128,1152]{4,3,2,1,0:T(8,128)(2,1)S(1)}, bf16[1,1,2,128,1152]{4,3,2,1,0:T(8,128)(2,1)S(1)}, u32[]{:S(2)}, u32[]{:S(2)}) %collective-permute-start.63) | collective-permute-done | bytes 589856 | tf_op jit(solution)/shard_map/cond/branch_1_fun/ppermute | solution.py:112
  225.1 8.7 all-to-all-start.3
  238.1 85.3 %conditional.17 = (bf16[1024,2304]{1,0:T(8,128)(2,1)}, bf16[1152]{0:T(1024)(128)(2,1)S(1)}, bf16[2304,1152]{1,0:T(8,128)(2,1)}, bf16[16,72,1152]{2,1,0:T(8,128)(2,1)}) conditional(s32[]{:T(128)} %bitcast.71, () %tuple.151, (bf16[128,2304]{1,0:T(8,128)(2,1)S(1)}, bf16[2,8,72,1152]{3,2,1,0:T(8,128)(2,1)S(1)}, f32[72]{0:T(128)S(1)}, ...), branch_computations={%region_14.15_spmd, %region_15.17_spmd} | conditional | flops 152992736 | bytes 78063856 | solution.py:165
  249.7 11.3 %multiply_convert_fusion = bf16[2,8,72,1152]{3,2,1,0:T(8,128)(2,1)} fusion(bf16[2,8,72,1152]{3,2,1,0:T(8,128)(2,1)S(1)} %get-tuple-element.114, f32[1152]{0:T(1024)S(1)} %fusion.2, f32[1152]{0:T(1024)S(1)} %get-tuple-element.317), kind=kLoop, calls=%fused_computation.31 | loop fusion | flops 80953344 | bytes 5317632 | tf_op jit(solution)/shard_map/cond/branch_1_fun/convert_element_type | solution.py:407
  264.1 18.0 %collective-permute-done.11 = bf16[1,1,1,128,768]{4,3,2,1,0:T(8,128)(2,1)S(1)} collective-permute-done((bf16[1,1,1,128,768]{4,3,2,1,0:T(8,128)(2,1)S(1)}, bf16[1,1,1,128,768]{4,3,2,1,0:T(8,128)(2,1)S(1)}, u32[]{:S(2)}, u32[]{:S(2)}) %collective-permute-start.11) | collective-permute-done | bytes 196640 | tf_op jit(solution)/shard_map/cond/branch_1_fun/ppermute | solution.py:112
  284.2 7.8 collective-permute-done.19
  294.9 15.7 %collective-permute-done.20 = bf16[2,1,2,128,768]{4,3,2,1,0:T(8,128)(2,1)} collective-permute-done((bf16[2,1,2,128,768]{4,3,2,1,0:T(8,128)(2,1)S(1)}, bf16[2,1,2,128,768]{4,3,2,1,0:T(8,128)(2,1)}, u32[]{:S(2)}, u32[]{:S(2)}) %collective-permute-start.20) | collective-permute-done | bytes 786464 | tf_op jit(solution)/shard_map/cond/branch_1_fun/ppermute | solution.py:112
  330.2 11.1 %fusion.112 = f32[1024,1152]{1,0:T(8,128)} fusion(bf16[1024,2304]{1,0:T(8,128)(2,1)} %get-tuple-element.204, bf16[2304,1152]{1,0:T(8,128)(2,1)} %get-tuple-element.205), kind=kOutput, calls=%fused_computation.359 | convolution fusion | flops 5435817984 | bytes 14745600 | tf_op jit(solution)/shard_map/dot_general | solution.py:103
  341.3 30.4 %conditional.18 = (bf16[1152]{0:T(1024)(128)(2,1)}, bf16[2304,1152]{1,0:T(8,128)(2,1)}) conditional(s32[]{:T(128)} %bitcast.71, () %tuple.154, bf16[2,8,72,1152]{3,2,1,0:T(8,128)(2,1)} %bitcast.89), branch_computations={%region_17.18_spmd, %region_18.20_spmd} | conditional | flops 83614464 | bytes 31889830 | solution.py:165
  346.0 12.3 %multiply_convert_fusion.2 = bf16[2,8,72,1152]{3,2,1,0:T(8,128)(2,1)} fusion(bf16[2,8,72,1152]{3,2,1,0:T(8,128)(2,1)} %param.9, f32[1152]{0:T(1024)S(1)} %fusion.4, f32[1152]{0:T(1024)S(1)} %get-tuple-element.319), kind=kLoop, calls=%fused_computation.59 | loop fusion | flops 80953344 | bytes 5317632 | tf_op jit(solution)/shard_map/cond/branch_1_fun/convert_element_type | solution.py:407
  371.7 12.1 %fusion.42 = (bf16[1024,1152]{1,0:T(8,128)(2,1)S(1)}, f32[1024,1152]{1,0:T(8,128)}) fusion(f32[1024,1152]{1,0:T(8,128)} %fusion.112, bf16[1024,2304]{1,0:T(8,128)(2,1)} %get-tuple-element.204, bf16[2304,1152]{1,0:T(8,128)(2,1)} %get-tuple-element.209), kind=kOutput, calls=%fused_computation.203 | convolution fusion | flops 5447614464 | bytes 21823488 | tf_op jit(solution)/shard_map/dot_general | solution.py:103
  383.8 13.2 %conditional.19 = (bf16[2304,1152]{1,0:T(8,128)(2,1)}) conditional(s32[]{:T(128)} %bitcast.71, () %tuple.157, bf16[2,8,72,1152]{3,2,1,0:T(8,128)(2,1)} %bitcast.90), branch_computations={%region_20.21_spmd, %region_21.22_spmd} | conditional | flops 6 | bytes 23887990 | solution.py:165
  397.1 9.0 fusion.113
  406.1 47.8 %conditional.20 = (f32[128,2304]{1,0:T(8,128)S(1)}, f32[128]{0:T(128)}, f32[128,1]{0,1:T(1,128)S(1)}) conditional(s32[]{:T(128)} %bitcast.71, () %tuple.150, bf16[1024,2304]{1,0:T(8,128)(2,1)S(1)} %fusion.113), branch_computations={%region_22.23_spmd, %region_23.25_spmd} | conditional | flops 6487936 | bytes 45418368 | solution.py:165
  408.3 7.8 collective-permute-start.47
  416.8 9.4 %collective-permute-done.50 = bf16[2,1,2,128,768]{4,3,2,1,0:T(8,128)(2,1)S(1)} collective-permute-done((bf16[2,1,2,128,768]{4,3,2,1,0:T(8,128)(2,1)S(1)}, bf16[2,1,2,128,768]{4,3,2,1,0:T(8,128)(2,1)S(1)}, u32[]{:S(2)}, u32[]{:S(2)}) %collective-permute-start.50) | collective-permute-done | bytes 786464 | tf_op jit(solution)/shard_map/cond/branch_1_fun/ppermute | solution.py:112
  426.4 7.8 collective-permute-start.51
  456.9 45.9 %conditional.21 = (bf16[1024,2304]{1,0:T(8,128)(2,1)}, f32[2,2,2,3328]{3,2,1,0:T(2,128)}) conditional(s32[]{:T(128)} %bitcast.71, () %tuple.162, (bf16[128,2304]{1,0:T(8,128)(2,1)S(1)}, bf16[2,256]{1,0:T(2,128)(2,1)S(1)}, bf16[1152]{0:T(1024)(128)(2,1)S(1)}, bf16[1152]{0:T(1024)(128)(2,1)}) %tuple.272), branch_computations={%region_26.27_spmd, %region_27.28_spmd} | conditional | flops 44421632 | bytes 35671760 | solution.py:165
  485.9 13.4 %collective-permute-done.33 = bf16[2,1,2,128,768]{4,3,2,1,0:T(8,128)(2,1)S(1)} collective-permute-done((bf16[2,1,2,128,768]{4,3,2,1,0:T(8,128)(2,1)S(1)}, bf16[2,1,2,128,768]{4,3,2,1,0:T(8,128)(2,1)S(1)}, u32[]{:S(2)}, u32[]{:S(2)}) %collective-permute-start.33) | collective-permute-done | bytes 786464 | tf_op jit(solution)/shard_map/cond/branch_1_fun/ppermute | solution.py:112
  502.8 33.6 %conditional.22 = (bf16[2,8,72,1152]{3,2,1,0:T(8,128)(2,1)}, bf16[1024,1152]{1,0:T(8,128)(2,1)}, bf16[1024,1152]{1,0:T(8,128)(2,1)}) conditional(s32[]{:T(128)} %bitcast.71, () %tuple.161, (bf16[1024,2304]{1,0:T(8,128)(2,1)}, bf16[1024,1152]{1,0:T(8,128)(2,1)}, bf16[2304,1152]{1,0:T(8,128)(2,1)}, f32[1024,1152]{1,0:T(8,128)}, ...), branch_computations={%region_28.29_spmd, %region_29.30_spmd} | conditional | flops 10905255936 | bytes 81690824 | solution.py:165
  502.8 10.4 %fusion.105 = bf16[2304,1152]{1,0:T(8,128)(2,1)} fusion(bf16[1024,2304]{1,0:T(8,128)(2,1)} %get-tuple-element.126, bf16[1024,1152]{1,0:T(8,128)(2,1)} %get-tuple-element.125), kind=kOutput, calls=%fused_computation.352 | convolution fusion | flops 5435817984 | bytes 12386304 | tf_op jit(solution)/shard_map/cond/branch_1_fun/dot_general | solution.py:103
  516.7 15.8 %multiply_convert_fusion.3 = (bf16[1024,1152]{1,0:T(8,128)(2,1)}, bf16[1024,1152]{1,0:T(8,128)(2,1)}) fusion(f32[1024,1152]{1,0:T(8,128)} %get-tuple-element.129, f32[1024,1152]{1,0:T(8,128)} %get-tuple-element.128, bf16[1024,2304]{1,0:T(8,128)(2,1)} %get-tuple-element.126, bf16[2304,1152]{1,0:T(8,128)(2,1)} %get-tuple-element.127), kind=kOutput, calls=%fused_computation.124 | convolution fusion | flops 5464129536 | bytes 24182784 | tf_op jit(solution)/shard_map/cond/branch_1_fun/dot_general | solution.py:103
  547.5 9.5 %fusion.114 = f32[1024,2304]{1,0:T(8,128)S(1)} fusion(bf16[1024,1152]{1,0:T(8,128)(2,1)} %get-tuple-element.219, bf16[2304,1152]{1,0:T(8,128)(2,1)} %get-tuple-element.205), kind=kOutput, calls=%fused_computation.361 | convolution fusion | flops 5435817984 | bytes 17104896 | tf_op jit(solution)/shard_map/dot_general | solution.py:103
  557.1 9.5 %add_convert_fusion.2 = bf16[1024,2304]{1,0:T(8,128)(2,1)S(1)} fusion(f32[1024,2304]{1,0:T(8,128)S(1)} %fusion.114, bf16[1024,1152]{1,0:T(8,128)(2,1)} %get-tuple-element.220, bf16[2304,1152]{1,0:T(8,128)(2,1)} %get-tuple-element.209), kind=kOutput, calls=%fused_computation.185 | convolution fusion | flops 5440536576 | bytes 21823488 | tf_op jit(solution)/shard_map/dot_general | solution.py:103
  566.6 71.4 %conditional.23 = (f32[128,2304]{1,0:T(8,128)S(1)}, bf16[16,72,1152]{2,1,0:T(8,128)(2,1)}, bf16[16,72,1152]{2,1,0:T(8,128)(2,1)}) conditional(s32[]{:T(128)} %bitcast.71, () %tuple.160, (bf16[1024,2304]{1,0:T(8,128)(2,1)S(1)}, bf16[2304,1024]{1,0:T(8,128)(2,1)}, bf16[1024,1152]{1,0:T(8,128)(2,1)}, bf16[1024,1152]{1,0:T(8,128)(2,1)}) %tuple.269), branch_computations={%region_30.31_spmd, %region_31.32_spmd} | conditional | flops 10888151040 | bytes 189924064 | solution.py:165
  573.6 10.3 %fusion.106 = bf16[2304,1152]{1,0:T(8,128)(2,1)} fusion(bf16[2304,1024]{1,0:T(8,128)(2,1)} %get-tuple-element.131, bf16[1024,1152]{1,0:T(8,128)(2,1)} %get-tuple-element.132), kind=kOutput, calls=%fused_computation.353 | convolution fusion | flops 5435817984 | bytes 12386304 | tf_op jit(solution)/shard_map/cond/branch_1_fun/dot_general | solution.py:103
  587.4 8.9 fusion.107
  649.6 53.5 %conditional.24 = (bf16[1024,2304]{1,0:T(8,128)(2,1)}) conditional(s32[]{:T(128)} %bitcast.71, () %tuple.167, bf16[128,2304]{1,0:T(8,128)(2,1)S(1)} %fusion.52), branch_computations={%region_34.35_spmd, %region_35.36_spmd} | conditional | flops 30081024 | bytes 34210040 | solution.py:165
  659.7 14.2 %collective-permute-done.38 = bf16[1,1,1,128,1152]{4,3,2,1,0:T(8,128)(2,1)S(1)} collective-permute-done((bf16[1,1,1,128,1152]{4,3,2,1,0:T(8,128)(2,1)S(1)}, bf16[1,1,1,128,1152]{4,3,2,1,0:T(8,128)(2,1)S(1)}, u32[]{:S(2)}, u32[]{:S(2)}) %collective-permute-start.38) | collective-permute-done | bytes 294944 | tf_op jit(solution)/shard_map/cond/branch_1_fun/ppermute | solution.py:112
  675.5 10.9 %collective-permute-done.42 = bf16[1,1,2,128,1152]{4,3,2,1,0:T(8,128)(2,1)S(1)} collective-permute-done((bf16[1,1,2,128,1152]{4,3,2,1,0:T(8,128)(2,1)S(1)}, bf16[1,1,2,128,1152]{4,3,2,1,0:T(8,128)(2,1)S(1)}, u32[]{:S(2)}, u32[]{:S(2)}) %collective-permute-start.42) | collective-permute-done | bytes 589856 | tf_op jit(solution)/shard_map/cond/branch_1_fun/ppermute | solution.py:112
  686.6 9.5 %collective-permute-done.39 = bf16[1,2,1,128,1152]{4,3,2,1,0:T(8,128)(2,1)S(1)} collective-permute-done((bf16[1,2,1,128,1152]{4,3,2,1,0:T(8,128)(2,1)S(1)}, bf16[1,2,1,128,1152]{4,3,2,1,0:T(8,128)(2,1)S(1)}, u32[]{:S(2)}, u32[]{:S(2)}) %collective-permute-start.39) | collective-permute-done | bytes 589856 | tf_op jit(solution)/shard_map/cond/branch_1_fun/ppermute | solution.py:112
  715.8 25.1 %shard_map.170 = (bf16[1024,256]{1,0:T(8,128)(2,1)}, f32[3072,256]{1,0:T(8,128)S(1)}, f32[3072,256]{1,0:T(8,128)}) custom-call(bf16[1024,256]{1,0:T(8,128)(2,1)} %get-tuple-element.302.q_ref, bf16[3072,256]{1,0:T(8,128)(2,1)} %get-tuple-element.197.k_ref, bf16[3072,256]{1,0:T(8,128)(2,1)} %get-tuple-element.198.v_ref, s32[1024,1]{1,0:T(8,128)} %add_maximum_fusion.low_ref, ...), custom_call_target="tpu_custom_call" | custom-call | flops 1 | bytes 1 | tf_op jit(solution)/shard_map/pallas_call | solution.py:285
  745.2 56.3 %conditional.25 = (bf16[2304,1024]{0,1:T(8,128)(2,1)}, f32[1024,256]{1,0:T(8,128)}, f32[1024,128]{1,0:T(8,128)S(1)}, f32[1024,128]{1,0:T(8,128)S(1)}, bf16[32,1,72,256]{3,2,0,1:T(8,128)(2,1)}) conditional(s32[]{:T(128)} %bitcast.71, () %tuple.168, (bf16[1024,2304]{1,0:T(8,128)(2,1)}, s32[]{:T(128)}, f32[3072,256]{1,0:T(8,128)S(1)}, ...), branch_computations={%region_36.37_spmd, %region_37.38_spmd} | conditional | flops 1216086016 | bytes 85066000 | solution.py:165
  755.3 19.3 %collective-permute-done.81 = bf16[1024,256]{1,0:T(8,128)(2,1)S(1)} collective-permute-done((bf16[1024,256]{1,0:T(8,128)(2,1)S(1)}, bf16[1024,256]{1,0:T(8,128)(2,1)S(1)}, u32[]{:S(2)}, u32[]{:S(2)}) %collective-permute-start.81) | collective-permute-done | bytes 524320 | tf_op jit(solution)/shard_map/cond/branch_1_fun/ppermute | solution.py:202
  776.1 22.6 %collective-permute-done.82 = bf16[1024,256]{1,0:T(8,128)(2,1)S(1)} collective-permute-done((bf16[1024,256]{1,0:T(8,128)(2,1)S(1)}, bf16[1024,256]{1,0:T(8,128)(2,1)S(1)}, u32[]{:S(2)}, u32[]{:S(2)}) %collective-permute-start.82) | collective-permute-done | bytes 524320 | tf_op jit(solution)/shard_map/cond/branch_1_fun/ppermute | solution.py:202
  824.8 53.5 %conditional.26 = (f32[128,2304]{1,0:T(8,128)S(1)}) conditional(s32[]{:T(128)} %bitcast.71, () %tuple.166, bf16[1024,2304]{1,0:T(8,128)(2,1)} %add_convert_fusion.1), branch_computations={%region_38.39_spmd, %region_39.40_spmd} | conditional | flops 5603328 | bytes 64291092 | solution.py:165
  835.2 29.0 %collective-permute-done.57 = bf16[1,1,2,128,1152]{4,3,2,1,0:T(8,128)(2,1)S(1)} collective-permute-done((bf16[1,1,2,128,1152]{4,3,2,1,0:T(8,128)(2,1)S(1)}, bf16[1,1,2,128,1152]{4,3,2,1,0:T(8,128)(2,1)S(1)}, u32[]{:S(2)}, u32[]{:S(2)}) %collective-permute-start.57) | collective-permute-done | bytes 589856 | tf_op jit(solution)/shard_map/cond/branch_1_fun/ppermute | solution.py:112
  879.0 20.6 %conditional.27 = (f32[4,2304]{1,0:T(4,128)S(1)}) conditional(s32[]{:T(128)} %bitcast.71, () %tuple.173, f32[4,2304]{1,0:T(4,128)S(1)} %pad_maximum_fusion.33), branch_computations={%region_49.50_spmd, %region_50.51_spmd} | conditional | flops 46080 | bytes 1290448 | solution.py:165
  (591 shorter events, 463.7 us)
Async XLA Ops:
  3.7 70.9 %all-to-all-start = ((bf16[32,2,72,256]{3,2,1,0:T(8,128)(2,1)}), bf16[32,2,72,256]{3,2,1,0:T(8,128)(2,1)S(1)}, u32[]{:S(2)}, u32[]{:S(2)}) async-start(bf16[32,2,72,256]{3,2,1,0:T(8,128)(2,1)} %bitcast.279), calls=%async_computation | async-start | bytes 4718592 | tf_op jit(solution)/shard_map/all_to_all | solution.py:299
  17.8 23.6 %collective-permute-start.8 = (bf16[1,1,1,128,1152]{4,3,2,1,0:T(8,128)(2,1)S(1)}, bf16[1,1,1,128,1152]{4,3,2,1,0:T(8,128)(2,1)S(1)}, u32[]{:S(2)}, u32[]{:S(2)}) collective-permute-start(bf16[1,1,1,128,1152]{4,3,2,1,0:T(8,128)(2,1)S(1)} %get-tuple-element.327), channel_id=1, source_target_pairs={{0,2},{2,0},{1,3},{3,1},{4,6},{6,4},{5,7},{7,5},{8,10},{10,8},{9,1... | collective-permute-start | bytes 884744 | tf_op jit(solution)/shard_map/cond/branch_1_fun/ppermute | solution.py:112
  19.7 23.7 %collective-permute-start.5 = (bf16[1,1,1,128,1152]{4,3,2,1,0:T(8,128)(2,1)S(1)}, bf16[1,1,1,128,1152]{4,3,2,1,0:T(8,128)(2,1)S(1)}, u32[]{:S(2)}, u32[]{:S(2)}) collective-permute-start(bf16[1,1,1,128,1152]{4,3,2,1,0:T(8,128)(2,1)S(1)} %get-tuple-element.326), channel_id=1, source_target_pairs={{0,4},{4,0},{1,5},{5,1},{2,6},{6,2},{3,7},{7,3},{8,12},{12,8},{9,1... | collective-permute-start | bytes 884744 | tf_op jit(solution)/shard_map/cond/branch_1_fun/ppermute | solution.py:112
  41.5 18.6 %collective-permute-start.9 = (bf16[1,1,2,128,1152]{4,3,2,1,0:T(8,128)(2,1)S(1)}, bf16[1,1,2,128,1152]{4,3,2,1,0:T(8,128)(2,1)S(1)}, u32[]{:S(2)}, u32[]{:S(2)}) collective-permute-start(bf16[1,1,2,128,1152]{4,3,2,1,0:T(8,128)(2,1)S(1)} %pad_maximum_fusion.3), channel_id=1, source_target_pairs={{0,4},{4,0},{1,5},{5,1},{2,6},{6,2},{3,7},{7,3},{8,12},{12,8},{9,1... | collective-permute-start | bytes 1769480 | tf_op jit(solution)/shard_map/cond/branch_1_fun/ppermute | solution.py:112
  43.4 19.0 %collective-permute-start.6 = (bf16[1,2,1,128,1152]{4,3,2,1,0:T(8,128)(2,1)S(1)}, bf16[1,2,1,128,1152]{4,3,2,1,0:T(8,128)(2,1)S(1)}, u32[]{:S(2)}, u32[]{:S(2)}) collective-permute-start(bf16[1,2,1,128,1152]{4,3,2,1,0:T(8,128)(2,1)S(1)} %pad_maximum_fusion.2), channel_id=1, source_target_pairs={{0,2},{2,0},{1,3},{3,1},{4,6},{6,4},{5,7},{7,5},{8,10},{10,8},{9,1... | collective-permute-start | bytes 1769480 | tf_op jit(solution)/shard_map/cond/branch_1_fun/ppermute | solution.py:112
  76.0 68.3 %all-to-all-start.1 = ((bf16[32,72,256]{2,1,0:T(8,128)(2,1)}), bf16[32,72,256]{2,1,0:T(8,128)(2,1)}, u32[]{:S(2)}, u32[]{:S(2)}) async-start(bf16[32,72,256]{2,1,0:T(8,128)(2,1)} %bitcast.315), calls=%async_computation.1 | async-start | bytes 2359296 | tf_op jit(solution)/shard_map/all_to_all | solution.py:299
  95.8 15.4 %collective-permute-start.65 = (bf16[1024,256]{1,0:T(8,128)(2,1)}, bf16[1024,256]{1,0:T(8,128)(2,1)}, u32[]{:S(2)}, u32[]{:S(2)}) collective-permute-start(bf16[1024,256]{1,0:T(8,128)(2,1)} %get-tuple-element.101), channel_id=1, source_target_pairs={{0,8},{8,16},{16,24},{1,9},{9,17},{17,25},{2,10},{10,18},{18,26},{... | collective-permute-start | bytes 1572872 | tf_op jit(solution)/shard_map/cond/branch_1_fun/ppermute | solution.py:202
  111.4 20.6 %collective-permute-start.66 = (bf16[1024,256]{1,0:T(8,128)(2,1)}, bf16[1024,256]{1,0:T(8,128)(2,1)S(1)}, u32[]{:S(2)}, u32[]{:S(2)}) collective-permute-start(bf16[1024,256]{1,0:T(8,128)(2,1)} %collective-permute-done.65), channel_id=1, source_target_pairs={{0,8},{8,16},{16,24},{1,9},{9,17},{17,25},{2,10},{10,18},{18,26},{... | collective-permute-start | bytes 1572872 | tf_op jit(solution)/shard_map/cond/branch_1_fun/ppermute | solution.py:202
  145.8 79.3 %all-to-all-start.2 = ((bf16[16,72,1152]{2,1,0:T(8,128)(2,1)}), bf16[16,72,1152]{2,1,0:T(8,128)(2,1)S(1)}, u32[]{:S(2)}, u32[]{:S(2)}) async-start(bf16[16,72,1152]{2,1,0:T(8,128)(2,1)} %copy-done.6), calls=%async_computation.2 | async-start | bytes 5308416 | tf_op jit(solution)/shard_map/all_to_all | solution.py:299
  182.6 23.2 %collective-permute-start.63 = (bf16[1,1,2,128,1152]{4,3,2,1,0:T(8,128)(2,1)S(1)}, bf16[1,1,2,128,1152]{4,3,2,1,0:T(8,128)(2,1)S(1)}, u32[]{:S(2)}, u32[]{:S(2)}) collective-permute-start(bf16[1,1,2,128,1152]{4,3,2,1,0:T(8,128)(2,1)S(1)} %slice.563), channel_id=1, source_target_pairs={{0,4},{4,0},{1,5},{5,1},{2,6},{6,2},{3,7},{7,3},{8,12},{12,8},{9,1... | collective-permute-start | bytes 1769480 | tf_op jit(solution)/shard_map/cond/branch_1_fun/ppermute | solution.py:112
  184.7 24.6 %collective-permute-start.60 = (bf16[1,2,1,128,1152]{4,3,2,1,0:T(8,128)(2,1)S(1)}, bf16[1,2,1,128,1152]{4,3,2,1,0:T(8,128)(2,1)S(1)}, u32[]{:S(2)}, u32[]{:S(2)}) collective-permute-start(bf16[1,2,1,128,1152]{4,3,2,1,0:T(8,128)(2,1)S(1)} %slice.564), channel_id=1, source_target_pairs={{0,2},{2,0},{1,3},{3,1},{4,6},{6,4},{5,7},{7,5},{8,10},{10,8},{9,1... | collective-permute-start | bytes 1769480 | tf_op jit(solution)/shard_map/cond/branch_1_fun/ppermute | solution.py:112
  209.4 14.5 %collective-permute-start.61 = (bf16[1,1,1,128,1152]{4,3,2,1,0:T(8,128)(2,1)S(1)}, bf16[1,1,1,128,1152]{4,3,2,1,0:T(8,128)(2,1)S(1)}, u32[]{:S(2)}, u32[]{:S(2)}) collective-permute-start(bf16[1,1,1,128,1152]{4,3,2,1,0:T(8,128)(2,1)S(1)} %slice.566), channel_id=1, source_target_pairs={{0,4},{4,0},{1,5},{5,1},{2,6},{6,2},{3,7},{7,3},{8,12},{12,8},{9,1... | collective-permute-start | bytes 884744 | tf_op jit(solution)/shard_map/cond/branch_1_fun/ppermute | solution.py:112
  225.1 98.2 %all-to-all-start.3 = ((bf16[16,72,1152]{2,1,0:T(8,128)(2,1)}), bf16[16,72,1152]{2,1,0:T(8,128)(2,1)}, u32[]{:S(2)}, u32[]{:S(2)}) async-start(bf16[16,72,1152]{2,1,0:T(8,128)(2,1)} %get-tuple-element.207), calls=%async_computation.3 | async-start | bytes 5308416 | tf_op jit(solution)/shard_map/all_to_all | solution.py:299
  238.6 22.5 %collective-permute-start.18 = (bf16[1,1,1,128,768]{4,3,2,1,0:T(8,128)(2,1)S(1)}, bf16[1,1,1,128,768]{4,3,2,1,0:T(8,128)(2,1)S(1)}, u32[]{:S(2)}, u32[]{:S(2)}) collective-permute-start(bf16[1,1,1,128,768]{4,3,2,1,0:T(8,128)(2,1)S(1)} %get-tuple-element.335), channel_id=1, source_target_pairs={{0,2},{2,0},{1,3},{3,1},{4,6},{6,4},{5,7},{7,5},{8,10},{10,8},{9,1... | collective-permute-start | bytes 589832 | tf_op jit(solution)/shard_map/cond/branch_1_fun/ppermute | solution.py:112
  240.9 22.5 %collective-permute-start.15 = (bf16[1,1,1,128,768]{4,3,2,1,0:T(8,128)(2,1)S(1)}, bf16[1,1,1,128,768]{4,3,2,1,0:T(8,128)(2,1)S(1)}, u32[]{:S(2)}, u32[]{:S(2)}) collective-permute-start(bf16[1,1,1,128,768]{4,3,2,1,0:T(8,128)(2,1)S(1)} %get-tuple-element.336), channel_id=1, source_target_pairs={{0,4},{4,0},{1,5},{5,1},{2,6},{6,2},{3,7},{7,3},{8,12},{12,8},{9,1... | collective-permute-start | bytes 589832 | tf_op jit(solution)/shard_map/cond/branch_1_fun/ppermute | solution.py:112
  242.4 39.6 %collective-permute-start.11 = (bf16[1,1,1,128,768]{4,3,2,1,0:T(8,128)(2,1)S(1)}, bf16[1,1,1,128,768]{4,3,2,1,0:T(8,128)(2,1)S(1)}, u32[]{:S(2)}, u32[]{:S(2)}) collective-permute-start(bf16[1,1,1,128,768]{4,3,2,1,0:T(8,128)(2,1)S(1)} %get-tuple-element.334), channel_id=1, source_target_pairs={{0,8},{8,0},{1,9},{9,1},{2,10},{10,2},{3,11},{11,3},{4,12},{12,4},... | collective-permute-start | bytes 589832 | tf_op jit(solution)/shard_map/cond/branch_1_fun/ppermute | solution.py:112
  261.1 54.3 %collective-permute-start.21 = (bf16[2,8,72,1152]{3,2,1,0:T(8,128)(2,1)}, bf16[2,8,72,1152]{3,2,1,0:T(8,128)(2,1)}, u32[]{:S(2)}, u32[]{:S(2)}) collective-permute-start(bf16[2,8,72,1152]{3,2,1,0:T(8,128)(2,1)} %multiply_convert_fusion), channel_id=1, source_target_pairs={{0,1},{1,0},{2,3},{3,2},{4,5},{5,4},{6,7},{7,6},{8,9},{9,8},{10,11... | collective-permute-start | bytes 7962632 | tf_op jit(solution)/shard_map/cond/branch_1_fun/ppermute | solution.py:112
  262.8 29.2 %collective-permute-start.19 = (bf16[1,1,2,128,768]{4,3,2,1,0:T(8,128)(2,1)S(1)}, bf16[1,1,2,128,768]{4,3,2,1,0:T(8,128)(2,1)S(1)}, u32[]{:S(2)}, u32[]{:S(2)}) collective-permute-start(bf16[1,1,2,128,768]{4,3,2,1,0:T(8,128)(2,1)S(1)} %pad_maximum_fusion.10), channel_id=1, source_target_pairs={{0,8},{8,0},{1,9},{9,1},{2,10},{10,2},{3,11},{11,3},{4,12},{12,4},... | collective-permute-start | bytes 1179656 | tf_op jit(solution)/shard_map/cond/branch_1_fun/ppermute | solution.py:112
  263.4 29.8 %collective-permute-start.16 = (bf16[1,2,1,128,768]{4,3,2,1,0:T(8,128)(2,1)S(1)}, bf16[1,2,1,128,768]{4,3,2,1,0:T(8,128)(2,1)S(1)}, u32[]{:S(2)}, u32[]{:S(2)}) collective-permute-start(bf16[1,2,1,128,768]{4,3,2,1,0:T(8,128)(2,1)S(1)} %pad_maximum_fusion.9), channel_id=1, source_target_pairs={{0,2},{2,0},{1,3},{3,1},{4,6},{6,4},{5,7},{7,5},{8,10},{10,8},{9,1... | collective-permute-start | bytes 1179656 | tf_op jit(solution)/shard_map/cond/branch_1_fun/ppermute | solution.py:112
  292.0 18.7 %collective-permute-start.20 = (bf16[2,1,2,128,768]{4,3,2,1,0:T(8,128)(2,1)S(1)}, bf16[2,1,2,128,768]{4,3,2,1,0:T(8,128)(2,1)}, u32[]{:S(2)}, u32[]{:S(2)}) collective-permute-start(bf16[2,1,2,128,768]{4,3,2,1,0:T(8,128)(2,1)S(1)} %constant_dynamic-update-slice_fusion.4), channel_id=1, source_target_pairs={{0,4},{4,0},{1,5},{5,1},{2,6},{6,2},{3,7},{7,3},{8,12},{12,8},{9,1... | collective-permute-start | bytes 2359304 | tf_op jit(solution)/shard_map/cond/branch_1_fun/ppermute | solution.py:112
  293.3 18.4 %collective-permute-start.17 = (bf16[1,2,2,128,768]{4,3,2,1,0:T(8,128)(2,1)S(1)}, bf16[1,2,2,128,768]{4,3,2,1,0:T(8,128)(2,1)}, u32[]{:S(2)}, u32[]{:S(2)}) collective-permute-start(bf16[1,2,2,128,768]{4,3,2,1,0:T(8,128)(2,1)S(1)} %constant_dynamic-update-slice_fusion.2), channel_id=1, source_target_pairs={{0,8},{8,0},{1,9},{9,1},{2,10},{10,2},{3,11},{11,3},{4,12},{12,4},... | collective-permute-start | bytes 2359304 | tf_op jit(solution)/shard_map/cond/branch_1_fun/ppermute | solution.py:112
  293.4 18.4 %collective-permute-start.14 = (bf16[2,2,1,128,768]{4,3,2,1,0:T(8,128)(2,1)S(1)}, bf16[2,2,1,128,768]{4,3,2,1,0:T(8,128)(2,1)}, u32[]{:S(2)}, u32[]{:S(2)}) collective-permute-start(bf16[2,2,1,128,768]{4,3,2,1,0:T(8,128)(2,1)S(1)} %constant_dynamic-update-slice_fusion), channel_id=1, source_target_pairs={{0,2},{2,0},{1,3},{3,1},{4,6},{6,4},{5,7},{7,5},{8,10},{10,8},{9,1... | collective-permute-start | bytes 2359304 | tf_op jit(solution)/shard_map/cond/branch_1_fun/ppermute | solution.py:112
  323.4 60.5 %all-to-all-start.4 = ((bf16[16,72,1152]{2,1,0:T(8,128)(2,1)}), bf16[16,72,1152]{2,1,0:T(8,128)(2,1)}, u32[]{:S(2)}, u32[]{:S(2)}) async-start(bf16[16,72,1152]{2,1,0:T(8,128)(2,1)} %get-tuple-element.211), calls=%async_computation.4 | async-start | bytes 5308416 | tf_op jit(solution)/shard_map/all_to_all | solution.py:299
  406.2 20.0 %collective-permute-start.50 = (bf16[2,1,2,128,768]{4,3,2,1,0:T(8,128)(2,1)S(1)}, bf16[2,1,2,128,768]{4,3,2,1,0:T(8,128)(2,1)S(1)}, u32[]{:S(2)}, u32[]{:S(2)}) collective-permute-start(bf16[2,1,2,128,768]{4,3,2,1,0:T(8,128)(2,1)S(1)} %slice.399), channel_id=1, source_target_pairs={{0,4},{4,0},{1,5},{5,1},{2,6},{6,2},{3,7},{7,3},{8,12},{12,8},{9,1... | collective-permute-start | bytes 2359304 | tf_op jit(solution)/shard_map/cond/branch_1_fun/ppermute | solution.py:112
  408.3 25.9 %collective-permute-start.47 = (bf16[1,2,2,128,768]{4,3,2,1,0:T(8,128)(2,1)S(1)}, bf16[1,2,2,128,768]{4,3,2,1,0:T(8,128)(2,1)S(1)}, u32[]{:S(2)}, u32[]{:S(2)}) collective-permute-start(bf16[1,2,2,128,768]{4,3,2,1,0:T(8,128)(2,1)S(1)} %slice.393), channel_id=1, source_target_pairs={{0,8},{8,0},{1,9},{9,1},{2,10},{10,2},{3,11},{11,3},{4,12},{12,4},... | collective-permute-start | bytes 2359304 | tf_op jit(solution)/shard_map/cond/branch_1_fun/ppermute | solution.py:112
  416.2 19.2 %collective-permute-start.44 = (bf16[2,2,1,128,768]{4,3,2,1,0:T(8,128)(2,1)S(1)}, bf16[2,2,1,128,768]{4,3,2,1,0:T(8,128)(2,1)S(1)}, u32[]{:S(2)}, u32[]{:S(2)}) collective-permute-start(bf16[2,2,1,128,768]{4,3,2,1,0:T(8,128)(2,1)S(1)} %slice.387), channel_id=1, source_target_pairs={{0,2},{2,0},{1,3},{3,1},{4,6},{6,4},{5,7},{7,5},{8,10},{10,8},{9,1... | collective-permute-start | bytes 2359304 | tf_op jit(solution)/shard_map/cond/branch_1_fun/ppermute | solution.py:112
  426.4 16.8 %collective-permute-start.51 = (bf16[1,1,2,128,768]{4,3,2,1,0:T(8,128)(2,1)S(1)}, bf16[1,1,2,128,768]{4,3,2,1,0:T(8,128)(2,1)S(1)}, u32[]{:S(2)}, u32[]{:S(2)}) collective-permute-start(bf16[1,1,2,128,768]{4,3,2,1,0:T(8,128)(2,1)S(1)} %slice.567), channel_id=1, source_target_pairs={{0,8},{8,0},{1,9},{9,1},{2,10},{10,2},{3,11},{11,3},{4,12},{12,4},... | collective-permute-start | bytes 1179656 | tf_op jit(solution)/shard_map/cond/branch_1_fun/ppermute | solution.py:112
  480.7 18.7 %collective-permute-start.33 = (bf16[2,1,2,128,768]{4,3,2,1,0:T(8,128)(2,1)S(1)}, bf16[2,1,2,128,768]{4,3,2,1,0:T(8,128)(2,1)S(1)}, u32[]{:S(2)}, u32[]{:S(2)}) collective-permute-start(bf16[2,1,2,128,768]{4,3,2,1,0:T(8,128)(2,1)S(1)} %pad_maximum_fusion.14), channel_id=1, source_target_pairs={{0,4},{4,0},{1,5},{5,1},{2,6},{6,2},{3,7},{7,3},{8,12},{12,8},{9,1... | collective-permute-start | bytes 2359304 | tf_op jit(solution)/shard_map/cond/branch_1_fun/ppermute | solution.py:112
  482.2 17.3 %collective-permute-start.30 = (bf16[1,2,2,128,768]{4,3,2,1,0:T(8,128)(2,1)S(1)}, bf16[1,2,2,128,768]{4,3,2,1,0:T(8,128)(2,1)S(1)}, u32[]{:S(2)}, u32[]{:S(2)}) collective-permute-start(bf16[1,2,2,128,768]{4,3,2,1,0:T(8,128)(2,1)S(1)} %pad_maximum_fusion.13), channel_id=1, source_target_pairs={{0,8},{8,0},{1,9},{9,1},{2,10},{10,2},{3,11},{11,3},{4,12},{12,4},... | collective-permute-start | bytes 2359304 | tf_op jit(solution)/shard_map/cond/branch_1_fun/ppermute | solution.py:112
  483.6 16.4 %collective-permute-start.27 = (bf16[2,2,1,128,768]{4,3,2,1,0:T(8,128)(2,1)S(1)}, bf16[2,2,1,128,768]{4,3,2,1,0:T(8,128)(2,1)S(1)}, u32[]{:S(2)}, u32[]{:S(2)}) collective-permute-start(bf16[2,2,1,128,768]{4,3,2,1,0:T(8,128)(2,1)S(1)} %pad_maximum_fusion.12), channel_id=1, source_target_pairs={{0,2},{2,0},{1,3},{3,1},{4,6},{6,4},{5,7},{7,5},{8,10},{10,8},{9,1... | collective-permute-start | bytes 2359304 | tf_op jit(solution)/shard_map/cond/branch_1_fun/ppermute | solution.py:112
  516.7 15.8 %collective-permute-start.68 = (bf16[2,8,72,1152]{3,2,1,0:T(8,128)(2,1)}, bf16[2,8,72,1152]{3,2,1,0:T(8,128)(2,1)}, u32[]{:S(2)}, u32[]{:S(2)}) collective-permute-start(bf16[2,8,72,1152]{3,2,1,0:T(8,128)(2,1)} %dynamic-slice_bitcast_fusion), channel_id=1, source_target_pairs={{0,1},{1,0},{2,3},{3,2},{4,5},{5,4},{6,7},{7,6},{8,9},{9,8},{10,11... | collective-permute-start | bytes 7962632 | tf_op jit(solution)/shard_map/cond/branch_1_fun/ppermute | solution.py:112
  536.4 101.5 %all-to-all-start.5 = ((bf16[16,72,1152]{2,1,0:T(8,128)(2,1)}), bf16[16,72,1152]{2,1,0:T(8,128)(2,1)}, u32[]{:S(2)}, u32[]{:S(2)}) async-start(bf16[16,72,1152]{2,1,0:T(8,128)(2,1)} %bitcast.98), calls=%async_computation.5 | async-start | bytes 5308416 | tf_op jit(solution)/shard_map/all_to_all | solution.py:299
  567.8 33.0 %collective-permute-start.75 = (bf16[2,1,2,128,768]{4,3,2,1,0:T(8,128)(2,1)}, bf16[2,1,2,128,768]{4,3,2,1,0:T(8,128)(2,1)}, u32[]{:S(2)}, u32[]{:S(2)}) collective-permute-start(bf16[2,1,2,128,768]{4,3,2,1,0:T(8,128)(2,1)} %slice.417), channel_id=1, source_target_pairs={{0,4},{4,0},{1,5},{5,1},{2,6},{6,2},{3,7},{7,3},{8,12},{12,8},{9,1... | collective-permute-start | bytes 2359304 | tf_op jit(solution)/shard_map/cond/branch_1_fun/ppermute | solution.py:112
  570.5 36.8 %collective-permute-start.72 = (bf16[1,2,2,128,768]{4,3,2,1,0:T(8,128)(2,1)}, bf16[1,2,2,128,768]{4,3,2,1,0:T(8,128)(2,1)}, u32[]{:S(2)}, u32[]{:S(2)}) collective-permute-start(bf16[1,2,2,128,768]{4,3,2,1,0:T(8,128)(2,1)} %slice.411), channel_id=1, source_target_pairs={{0,8},{8,0},{1,9},{9,1},{2,10},{10,2},{3,11},{11,3},{4,12},{12,4},... | collective-permute-start | bytes 2359304 | tf_op jit(solution)/shard_map/cond/branch_1_fun/ppermute | solution.py:112
  572.0 38.4 %collective-permute-start.69 = (bf16[2,2,1,128,768]{4,3,2,1,0:T(8,128)(2,1)S(1)}, bf16[2,2,1,128,768]{4,3,2,1,0:T(8,128)(2,1)}, u32[]{:S(2)}, u32[]{:S(2)}) collective-permute-start(bf16[2,2,1,128,768]{4,3,2,1,0:T(8,128)(2,1)S(1)} %slice.405), channel_id=1, source_target_pairs={{0,2},{2,0},{1,3},{3,1},{4,6},{6,4},{5,7},{7,5},{8,10},{10,8},{9,1... | collective-permute-start | bytes 2359304 | tf_op jit(solution)/shard_map/cond/branch_1_fun/ppermute | solution.py:112
  587.4 42.4 %collective-permute-start.78 = (bf16[2,8,72,1152]{3,2,1,0:T(8,128)(2,1)}, bf16[2,8,72,1152]{3,2,1,0:T(8,128)(2,1)}, u32[]{:S(2)}, u32[]{:S(2)}) collective-permute-start(bf16[2,8,72,1152]{3,2,1,0:T(8,128)(2,1)} %dynamic-slice_bitcast_fusion.2), channel_id=1, source_target_pairs={{0,1},{1,0},{2,3},{3,2},{4,5},{5,4},{6,7},{7,6},{8,9},{9,8},{10,11... | collective-permute-start | bytes 7962632 | tf_op jit(solution)/shard_map/cond/branch_1_fun/ppermute | solution.py:112
  600.2 33.7 %collective-permute-start.79 = (bf16[2,8,72,1152]{3,2,1,0:T(8,128)(2,1)}, bf16[2,8,72,1152]{3,2,1,0:T(8,128)(2,1)}, u32[]{:S(2)}, u32[]{:S(2)}) collective-permute-start(bf16[2,8,72,1152]{3,2,1,0:T(8,128)(2,1)} %dynamic-slice_bitcast_fusion.1), channel_id=1, source_target_pairs={{0,1},{1,0},{2,3},{3,2},{4,5},{5,4},{6,7},{7,6},{8,9},{9,8},{10,11... | collective-permute-start | bytes 7962632 | tf_op jit(solution)/shard_map/cond/branch_1_fun/ppermute | solution.py:112
  602.3 12.9 %collective-permute-start.76 = (bf16[1,1,2,128,768]{4,3,2,1,0:T(8,128)(2,1)S(1)}, bf16[1,1,2,128,768]{4,3,2,1,0:T(8,128)(2,1)S(1)}, u32[]{:S(2)}, u32[]{:S(2)}) collective-permute-start(bf16[1,1,2,128,768]{4,3,2,1,0:T(8,128)(2,1)S(1)} %slice.573), channel_id=1, source_target_pairs={{0,8},{8,0},{1,9},{9,1},{2,10},{10,2},{3,11},{11,3},{4,12},{12,4},... | collective-permute-start | bytes 1179656 | tf_op jit(solution)/shard_map/cond/branch_1_fun/ppermute | solution.py:112
  638.0 65.1 %all-to-all-start.6 = ((bf16[16,72,1152]{2,1,0:T(8,128)(2,1)}), bf16[16,72,1152]{2,1,0:T(8,128)(2,1)}, u32[]{:S(2)}, u32[]{:S(2)}) async-start(bf16[16,72,1152]{2,1,0:T(8,128)(2,1)} %get-tuple-element.234), calls=%async_computation.6 | async-start | bytes 5308416 | tf_op jit(solution)/shard_map/all_to_all | solution.py:299
  651.8 22.1 %collective-permute-start.38 = (bf16[1,1,1,128,1152]{4,3,2,1,0:T(8,128)(2,1)S(1)}, bf16[1,1,1,128,1152]{4,3,2,1,0:T(8,128)(2,1)S(1)}, u32[]{:S(2)}, u32[]{:S(2)}) collective-permute-start(bf16[1,1,1,128,1152]{4,3,2,1,0:T(8,128)(2,1)S(1)} %get-tuple-element.352), channel_id=1, source_target_pairs={{0,4},{4,0},{1,5},{5,1},{2,6},{6,2},{3,7},{7,3},{8,12},{12,8},{9,1... | collective-permute-start | bytes 884744 | tf_op jit(solution)/shard_map/cond/branch_1_fun/ppermute | solution.py:112
  659.4 27.1 %collective-permute-start.42 = (bf16[1,1,2,128,1152]{4,3,2,1,0:T(8,128)(2,1)S(1)}, bf16[1,1,2,128,1152]{4,3,2,1,0:T(8,128)(2,1)S(1)}, u32[]{:S(2)}, u32[]{:S(2)}) collective-permute-start(bf16[1,1,2,128,1152]{4,3,2,1,0:T(8,128)(2,1)S(1)} %pad_maximum_fusion.24), channel_id=1, source_target_pairs={{0,4},{4,0},{1,5},{5,1},{2,6},{6,2},{3,7},{7,3},{8,12},{12,8},{9,1... | collective-permute-start | bytes 1769480 | tf_op jit(solution)/shard_map/cond/branch_1_fun/ppermute | solution.py:112
  674.0 22.1 %collective-permute-start.39 = (bf16[1,2,1,128,1152]{4,3,2,1,0:T(8,128)(2,1)S(1)}, bf16[1,2,1,128,1152]{4,3,2,1,0:T(8,128)(2,1)S(1)}, u32[]{:S(2)}, u32[]{:S(2)}) collective-permute-start(bf16[1,2,1,128,1152]{4,3,2,1,0:T(8,128)(2,1)S(1)} %pad_maximum_fusion.23), channel_id=1, source_target_pairs={{0,2},{2,0},{1,3},{3,1},{4,6},{6,4},{5,7},{7,5},{8,10},{10,8},{9,1... | collective-permute-start | bytes 1769480 | tf_op jit(solution)/shard_map/cond/branch_1_fun/ppermute | solution.py:112
  703.0 111.2 %all-to-all-start.7 = ((bf16[16,72,1152]{2,1,0:T(8,128)(2,1)}), bf16[16,72,1152]{2,1,0:T(8,128)(2,1)}, u32[]{:S(2)}, u32[]{:S(2)}) async-start(bf16[16,72,1152]{2,1,0:T(8,128)(2,1)} %get-tuple-element.235), calls=%async_computation.7 | async-start | bytes 5308416 | tf_op jit(solution)/shard_map/all_to_all | solution.py:299
  751.5 23.1 %collective-permute-start.81 = (bf16[1024,256]{1,0:T(8,128)(2,1)S(1)}, bf16[1024,256]{1,0:T(8,128)(2,1)S(1)}, u32[]{:S(2)}, u32[]{:S(2)}) collective-permute-start(bf16[1024,256]{1,0:T(8,128)(2,1)S(1)} %fusion.31), channel_id=1, source_target_pairs={{8,0},{16,8},{24,16},{9,1},{17,9},{25,17},{10,2},{18,10},{26,18},{... | collective-permute-start | bytes 1572872 | tf_op jit(solution)/shard_map/cond/branch_1_fun/ppermute | solution.py:202
  774.8 23.9 %collective-permute-start.82 = (bf16[1024,256]{1,0:T(8,128)(2,1)S(1)}, bf16[1024,256]{1,0:T(8,128)(2,1)S(1)}, u32[]{:S(2)}, u32[]{:S(2)}) collective-permute-start(bf16[1024,256]{1,0:T(8,128)(2,1)S(1)} %fusion.27), channel_id=1, source_target_pairs={{8,0},{16,8},{24,16},{9,1},{17,9},{25,17},{10,2},{18,10},{26,18},{... | collective-permute-start | bytes 1572872 | tf_op jit(solution)/shard_map/cond/branch_1_fun/ppermute | solution.py:202
  814.2 99.7 %all-to-all-start.8 = ((bf16[32,3,72,256]{3,2,1,0:T(8,128)(2,1)}), bf16[32,3,72,256]{3,2,1,0:T(8,128)(2,1)}, u32[]{:S(2)}, u32[]{:S(2)}) async-start(bf16[32,3,72,256]{3,2,1,0:T(8,128)(2,1)} %pad_maximum_fusion.28), calls=%async_computation.8 | async-start | bytes 7077888 | tf_op jit(solution)/shard_map/all_to_all | solution.py:299
  831.9 32.2 %collective-permute-start.57 = (bf16[1,1,2,128,1152]{4,3,2,1,0:T(8,128)(2,1)S(1)}, bf16[1,1,2,128,1152]{4,3,2,1,0:T(8,128)(2,1)S(1)}, u32[]{:S(2)}, u32[]{:S(2)}) collective-permute-start(bf16[1,1,2,128,1152]{4,3,2,1,0:T(8,128)(2,1)S(1)} %slice.579), channel_id=1, source_target_pairs={{0,4},{4,0},{1,5},{5,1},{2,6},{6,2},{3,7},{7,3},{8,12},{12,8},{9,1... | collective-permute-start | bytes 1769480 | tf_op jit(solution)/shard_map/cond/branch_1_fun/ppermute | solution.py:112
  833.6 32.7 %collective-permute-start.54 = (bf16[1,2,1,128,1152]{4,3,2,1,0:T(8,128)(2,1)S(1)}, bf16[1,2,1,128,1152]{4,3,2,1,0:T(8,128)(2,1)S(1)}, u32[]{:S(2)}, u32[]{:S(2)}) collective-permute-start(bf16[1,2,1,128,1152]{4,3,2,1,0:T(8,128)(2,1)S(1)} %slice.580), channel_id=1, source_target_pairs={{0,2},{2,0},{1,3},{3,1},{4,6},{6,4},{5,7},{7,5},{8,10},{10,8},{9,1... | collective-permute-start | bytes 1769480 | tf_op jit(solution)/shard_map/cond/branch_1_fun/ppermute | solution.py:112
  (127 other events, 1532.2 us)

commit v6 on v5

--- a/solution.py
+++ b/solution.py
@@ -209,9 +209,6 @@
     return full.reshape(-1, part.shape[-1])
 
 
-Q_ROWS = 128
-
-
 def scores(q_ref, k_ref, low_ref, place_ref, k_place_ref):
     raw = dot(q_ref[...], k_ref[...], ROWS) * (1.0 / (math.sqrt(HD) * SOFTCAP))
     places = k_place_ref[...]
@@ -250,12 +247,13 @@
 
 
 def attention_specs(rows, keys):
-    q_spec = pl.BlockSpec((Q_ROWS, HD), lambda i: (i, 0))
+    q_rows = 256 if keys <= 4096 else 128
+    q_spec = pl.BlockSpec((q_rows, HD), lambda i: (i, 0))
     k_spec = pl.BlockSpec((keys, HD), lambda i: (0, 0))
-    row_spec = pl.BlockSpec((Q_ROWS, 1), lambda i: (i, 0))
+    row_spec = pl.BlockSpec((q_rows, 1), lambda i: (i, 0))
     place_spec = pl.BlockSpec((1, keys), lambda i: (0, 0))
     common = dict(
-        grid=(rows // Q_ROWS,),
+        grid=(rows // q_rows,),
         compiler_params=pltpu.CompilerParams(
             dimension_semantics=("arbitrary",), vmem_limit_bytes=56 * 2**20
         ),

time: 929 us -> 927 us (level)
  Pallas kernels: 41 us -> 31 us
  transfers between devices with their start and end apart: 92 -> 92, of which waited for: 61 -> 61; matrix products, arithmetic and copies ran while one was open for 32% -> 32% of each run, Pallas kernels for 4% -> 3%
where the time goes in v6:
time: 927 us; the launch traced here: 917 us
  waiting for transfers between devices  360 us (39%)
  starting transfers between devices  168 us (18%)
  other arithmetic  141 us (15%)
  matrix products  127 us (14%)
  local copies, waits for them, and re-layouts  84.3 us (9%)
  Pallas kernels  31 us (3%)
    ppermute x79, waiting for transfers between devices, swap(): return lax.ppermute(value, axis, SWAP)  298 us
    dot_general x18, matrix products, dot(): lax.dot_general(left, right, (dims, ((), ())), preferred_element_type=out)  127 us
    ppermute x79, starting transfers between devices, swap(): return lax.ppermute(value, axis, SWAP)  94.7 us
    ppermute x4, waiting for transfers between devices, shift(): lax.ppermute(value, LINE, [(i, i + step) for i in range(count) if 0 <= i...  62.2 us
    all_to_all x9, starting transfers between devices, exchange(): return lax.all_to_all(value, axes, split_axis=0, concat_axis=0, tiled=True)  56.8 us
    convert_element_type x2, other arithmetic, quantize(): nested(lat.astype(f32), top.astype(f32) + EPSILON).astype(bf16)  23.7 us
  transfers between devices with their start and end apart: 92, of which 61 were waited for; matrix products, arithmetic and copies ran while one was open for 32% of the time, Pallas kernels for 3%

profile of v6, /device:TPU:0, one launch (start us, length us, event | category | flops | bytes accessed | tf_op | source)
XLA Modules:
  0.0 916.9 jit_solution(4523641596559642521)
XLA Ops:
  16.7 52.8 %conditional.14 = (bf16[1024,2304]{1,0:T(8,128)(2,1)}) conditional(s32[]{:T(128)} %bitcast.71, () %tuple.146, bf16[128,2304]{1,0:T(8,128)(2,1)} %fusion.47), branch_computations={%region_1.0_spmd, %region_2.0_spmd} | conditional | flops 30081024 | bytes 34210040 | solution.py:165
  21.1 20.3 %collective-permute-done.8 = bf16[1,1,1,128,1152]{4,3,2,1,0:T(8,128)(2,1)S(1)} collective-permute-done((bf16[1,1,1,128,1152]{4,3,2,1,0:T(8,128)(2,1)S(1)}, bf16[1,1,1,128,1152]{4,3,2,1,0:T(8,128)(2,1)S(1)}, u32[]{:S(2)}, u32[]{:S(2)}) %collective-permute-start.8) | collective-permute-done | bytes 294944 | tf_op jit(solution)/shard_map/cond/branch_1_fun/ppermute | solution.py:112
  43.5 16.6 %collective-permute-done.9 = bf16[1,1,2,128,1152]{4,3,2,1,0:T(8,128)(2,1)S(1)} collective-permute-done((bf16[1,1,2,128,1152]{4,3,2,1,0:T(8,128)(2,1)S(1)}, bf16[1,1,2,128,1152]{4,3,2,1,0:T(8,128)(2,1)S(1)}, u32[]{:S(2)}, u32[]{:S(2)}) %collective-permute-start.9) | collective-permute-done | bytes 589856 | tf_op jit(solution)/shard_map/cond/branch_1_fun/ppermute | solution.py:112
  79.5 9.4 %multiply_convert_fusion.4 = bf16[4,8,2,72,256]{4,3,2,1,0:T(8,128)(2,1)S(1)} fusion(bf16[4,8,2,72,256]{4,3,2,1,0:T(8,128)(2,1)S(1)} %bitcast.264, f32[2,256]{1,0:T(2,128)S(1)} %get-tuple-element.379, f32[2,256]{1,0:T(2,128)S(1)} %get-tuple-element.378), kind=kLoop, calls=%fused_computation.204 | loop fusion | flops 71958528 | bytes 4722688 | tf_op jit(solution)/shard_map/convert_element_type | solution.py:363
  95.8 48.5 %conditional.15 = (bf16[3072,256]{1,0:T(8,128)(2,1)}, bf16[3072,256]{1,0:T(8,128)(2,1)}, bf16[16,72,1152]{2,1,0:T(8,128)(2,1)S(1)}, bf16[1024,256]{1,0:T(8,128)(2,1)}) conditional(s32[]{:T(128)} %bitcast.71, () %tuple.145, (s32[]{:T(128)}, bf16[1024,256]{1,0:T(8,128)(2,1)}, bf16[1024,2304]{1,0:T(8,128)(2,1)S(1)}, bf16[2304,256]{1,0:T(8,128)(2,1)S(1)}, ...), branch_computations={%region_6.7_spmd, %region_7.8_spmd} | conditional | flops 1221066752 | bytes 71975240 | solution.py:165
  111.4 9.0 collective-permute-start.66
  120.5 11.6 %collective-permute-done.66 = bf16[1024,256]{1,0:T(8,128)(2,1)S(1)} collective-permute-done((bf16[1024,256]{1,0:T(8,128)(2,1)}, bf16[1024,256]{1,0:T(8,128)(2,1)S(1)}, u32[]{:S(2)}, u32[]{:S(2)}) %collective-permute-start.66) | collective-permute-done | bytes 524320 | tf_op jit(solution)/shard_map/cond/branch_1_fun/ppermute | solution.py:202
  145.8 7.9 all-to-all-start.2
  158.4 13.0 %shard_map.169 = (bf16[1024,256]{1,0:T(8,128)(2,1)S(1)}, f32[1024,1]{1,0:T(8,128)}) custom-call(bf16[1024,256]{1,0:T(8,128)(2,1)} %get-tuple-element.302.q_ref, bf16[3072,256]{1,0:T(8,128)(2,1)} %get-tuple-element.197.k_ref, bf16[3072,256]{1,0:T(8,128)(2,1)} %get-tuple-element.198.v_ref, s32[1024,1]{1,0:T(8,128)} %add_maximum_fusion.low_ref, ...), custom_call_target="tpu_custom_call" | custom-call | flops 1 | bytes 1 | tf_op jit(solution)/shard_map/pallas_call | solution.py:268
  174.4 49.8 %conditional.16 = (f32[128,2304]{1,0:T(8,128)}, bf16[16,72,1152]{2,1,0:T(8,128)(2,1)}, f32[128]{0:T(128)S(1)}) conditional(s32[]{:T(128)} %bitcast.71, () %tuple.144, (bf16[1024,2304]{1,0:T(8,128)(2,1)S(1)}, bf16[72,18432]{1,0:T(8,128)(2,1)S(1)}) %tuple.270), branch_computations={%region_9.10_spmd, %region_10.11_spmd} | conditional | flops 6193024 | bytes 57361160 | solution.py:165
  183.3 18.4 %collective-permute-done.63 = bf16[1,1,2,128,1152]{4,3,2,1,0:T(8,128)(2,1)S(1)} collective-permute-done((bf16[1,1,2,128,1152]{4,3,2,1,0:T(8,128)(2,1)S(1)}, bf16[1,1,2,128,1152]{4,3,2,1,0:T(8,128)(2,1)S(1)}, u32[]{:S(2)}, u32[]{:S(2)}) %collective-permute-start.63) | collective-permute-done | bytes 589856 | tf_op jit(solution)/shard_map/cond/branch_1_fun/ppermute | solution.py:112
  224.2 8.3 all-to-all-start.3
  236.8 83.9 %conditional.17 = (bf16[1024,2304]{1,0:T(8,128)(2,1)}, bf16[1152]{0:T(1024)(128)(2,1)S(1)}, bf16[2304,1152]{1,0:T(8,128)(2,1)}, bf16[16,72,1152]{2,1,0:T(8,128)(2,1)}) conditional(s32[]{:T(128)} %bitcast.71, () %tuple.151, (bf16[128,2304]{1,0:T(8,128)(2,1)S(1)}, bf16[2,8,72,1152]{3,2,1,0:T(8,128)(2,1)S(1)}, f32[72]{0:T(128)S(1)}, ...), branch_computations={%region_14.15_spmd, %region_15.17_spmd} | conditional | flops 152992736 | bytes 78063856 | solution.py:165
  248.4 11.3 %multiply_convert_fusion = bf16[2,8,72,1152]{3,2,1,0:T(8,128)(2,1)} fusion(bf16[2,8,72,1152]{3,2,1,0:T(8,128)(2,1)S(1)} %get-tuple-element.114, f32[1152]{0:T(1024)S(1)} %fusion.2, f32[1152]{0:T(1024)S(1)} %get-tuple-element.317), kind=kLoop, calls=%fused_computation.31 | loop fusion | flops 80953344 | bytes 5317632 | tf_op jit(solution)/shard_map/cond/branch_1_fun/convert_element_type | solution.py:405
  262.7 17.9 %collective-permute-done.11 = bf16[1,1,1,128,768]{4,3,2,1,0:T(8,128)(2,1)S(1)} collective-permute-done((bf16[1,1,1,128,768]{4,3,2,1,0:T(8,128)(2,1)S(1)}, bf16[1,1,1,128,768]{4,3,2,1,0:T(8,128)(2,1)S(1)}, u32[]{:S(2)}, u32[]{:S(2)}) %collective-permute-start.11) | collective-permute-done | bytes 196640 | tf_op jit(solution)/shard_map/cond/branch_1_fun/ppermute | solution.py:112
  292.1 16.7 %collective-permute-done.20 = bf16[2,1,2,128,768]{4,3,2,1,0:T(8,128)(2,1)} collective-permute-done((bf16[2,1,2,128,768]{4,3,2,1,0:T(8,128)(2,1)S(1)}, bf16[2,1,2,128,768]{4,3,2,1,0:T(8,128)(2,1)}, u32[]{:S(2)}, u32[]{:S(2)}) %collective-permute-start.20) | collective-permute-done | bytes 786464 | tf_op jit(solution)/shard_map/cond/branch_1_fun/ppermute | solution.py:112
  327.9 11.1 %fusion.112 = f32[1024,1152]{1,0:T(8,128)} fusion(bf16[1024,2304]{1,0:T(8,128)(2,1)} %get-tuple-element.204, bf16[2304,1152]{1,0:T(8,128)(2,1)} %get-tuple-element.205), kind=kOutput, calls=%fused_computation.359 | convolution fusion | flops 5435817984 | bytes 14745600 | tf_op jit(solution)/shard_map/dot_general | solution.py:103
  339.0 30.4 %conditional.18 = (bf16[1152]{0:T(1024)(128)(2,1)}, bf16[2304,1152]{1,0:T(8,128)(2,1)}) conditional(s32[]{:T(128)} %bitcast.71, () %tuple.154, bf16[2,8,72,1152]{3,2,1,0:T(8,128)(2,1)} %bitcast.89), branch_computations={%region_17.18_spmd, %region_18.20_spmd} | conditional | flops 83614464 | bytes 31889830 | solution.py:165
  343.7 12.3 %multiply_convert_fusion.2 = bf16[2,8,72,1152]{3,2,1,0:T(8,128)(2,1)} fusion(bf16[2,8,72,1152]{3,2,1,0:T(8,128)(2,1)} %param.9, f32[1152]{0:T(1024)S(1)} %fusion.4, f32[1152]{0:T(1024)S(1)} %get-tuple-element.319), kind=kLoop, calls=%fused_computation.59 | loop fusion | flops 80953344 | bytes 5317632 | tf_op jit(solution)/shard_map/cond/branch_1_fun/convert_element_type | solution.py:405
  369.4 12.1 %fusion.42 = (bf16[1024,1152]{1,0:T(8,128)(2,1)S(1)}, f32[1024,1152]{1,0:T(8,128)}) fusion(f32[1024,1152]{1,0:T(8,128)} %fusion.112, bf16[1024,2304]{1,0:T(8,128)(2,1)} %get-tuple-element.204, bf16[2304,1152]{1,0:T(8,128)(2,1)} %get-tuple-element.209), kind=kOutput, calls=%fused_computation.203 | convolution fusion | flops 5447614464 | bytes 21823488 | tf_op jit(solution)/shard_map/dot_general | solution.py:103
  381.5 13.2 %conditional.19 = (bf16[2304,1152]{1,0:T(8,128)(2,1)}) conditional(s32[]{:T(128)} %bitcast.71, () %tuple.157, bf16[2,8,72,1152]{3,2,1,0:T(8,128)(2,1)} %bitcast.90), branch_computations={%region_20.21_spmd, %region_21.22_spmd} | conditional | flops 6 | bytes 23887990 | solution.py:165
  394.8 9.0 fusion.113
  403.8 47.8 %conditional.20 = (f32[128,2304]{1,0:T(8,128)S(1)}, f32[128]{0:T(128)}, f32[128,1]{0,1:T(1,128)S(1)}) conditional(s32[]{:T(128)} %bitcast.71, () %tuple.150, bf16[1024,2304]{1,0:T(8,128)(2,1)S(1)} %fusion.113), branch_computations={%region_22.23_spmd, %region_23.25_spmd} | conditional | flops 6487936 | bytes 45418368 | solution.py:165
  406.0 7.8 collective-permute-start.47
  414.5 9.4 %collective-permute-done.50 = bf16[2,1,2,128,768]{4,3,2,1,0:T(8,128)(2,1)S(1)} collective-permute-done((bf16[2,1,2,128,768]{4,3,2,1,0:T(8,128)(2,1)S(1)}, bf16[2,1,2,128,768]{4,3,2,1,0:T(8,128)(2,1)S(1)}, u32[]{:S(2)}, u32[]{:S(2)}) %collective-permute-start.50) | collective-permute-done | bytes 786464 | tf_op jit(solution)/shard_map/cond/branch_1_fun/ppermute | solution.py:112
  424.1 7.8 collective-permute-start.51
  454.6 45.9 %conditional.21 = (bf16[1024,2304]{1,0:T(8,128)(2,1)}, f32[2,2,2,3328]{3,2,1,0:T(2,128)}) conditional(s32[]{:T(128)} %bitcast.71, () %tuple.162, (bf16[128,2304]{1,0:T(8,128)(2,1)S(1)}, bf16[2,256]{1,0:T(2,128)(2,1)S(1)}, bf16[1152]{0:T(1024)(128)(2,1)S(1)}, bf16[1152]{0:T(1024)(128)(2,1)}) %tuple.272), branch_computations={%region_26.27_spmd, %region_27.28_spmd} | conditional | flops 44421632 | bytes 35671760 | solution.py:165
  483.6 13.4 %collective-permute-done.33 = bf16[2,1,2,128,768]{4,3,2,1,0:T(8,128)(2,1)S(1)} collective-permute-done((bf16[2,1,2,128,768]{4,3,2,1,0:T(8,128)(2,1)S(1)}, bf16[2,1,2,128,768]{4,3,2,1,0:T(8,128)(2,1)S(1)}, u32[]{:S(2)}, u32[]{:S(2)}) %collective-permute-start.33) | collective-permute-done | bytes 786464 | tf_op jit(solution)/shard_map/cond/branch_1_fun/ppermute | solution.py:112
  500.6 33.6 %conditional.22 = (bf16[2,8,72,1152]{3,2,1,0:T(8,128)(2,1)}, bf16[1024,1152]{1,0:T(8,128)(2,1)}, bf16[1024,1152]{1,0:T(8,128)(2,1)}) conditional(s32[]{:T(128)} %bitcast.71, () %tuple.161, (bf16[1024,2304]{1,0:T(8,128)(2,1)}, bf16[1024,1152]{1,0:T(8,128)(2,1)}, bf16[2304,1152]{1,0:T(8,128)(2,1)}, f32[1024,1152]{1,0:T(8,128)}, ...), branch_computations={%region_28.29_spmd, %region_29.30_spmd} | conditional | flops 10905255936 | bytes 81690824 | solution.py:165
  500.6 10.4 %fusion.105 = bf16[2304,1152]{1,0:T(8,128)(2,1)} fusion(bf16[1024,2304]{1,0:T(8,128)(2,1)} %get-tuple-element.126, bf16[1024,1152]{1,0:T(8,128)(2,1)} %get-tuple-element.125), kind=kOutput, calls=%fused_computation.352 | convolution fusion | flops 5435817984 | bytes 12386304 | tf_op jit(solution)/shard_map/cond/branch_1_fun/dot_general | solution.py:103
  514.4 15.8 %multiply_convert_fusion.3 = (bf16[1024,1152]{1,0:T(8,128)(2,1)}, bf16[1024,1152]{1,0:T(8,128)(2,1)}) fusion(f32[1024,1152]{1,0:T(8,128)} %get-tuple-element.129, f32[1024,1152]{1,0:T(8,128)} %get-tuple-element.128, bf16[1024,2304]{1,0:T(8,128)(2,1)} %get-tuple-element.126, bf16[2304,1152]{1,0:T(8,128)(2,1)} %get-tuple-element.127), kind=kOutput, calls=%fused_computation.124 | convolution fusion | flops 5464129536 | bytes 24182784 | tf_op jit(solution)/shard_map/cond/branch_1_fun/dot_general | solution.py:103
  545.3 9.5 %fusion.114 = f32[1024,2304]{1,0:T(8,128)S(1)} fusion(bf16[1024,1152]{1,0:T(8,128)(2,1)} %get-tuple-element.219, bf16[2304,1152]{1,0:T(8,128)(2,1)} %get-tuple-element.205), kind=kOutput, calls=%fused_computation.361 | convolution fusion | flops 5435817984 | bytes 17104896 | tf_op jit(solution)/shard_map/dot_general | solution.py:103
  554.8 9.5 %add_convert_fusion.2 = bf16[1024,2304]{1,0:T(8,128)(2,1)S(1)} fusion(f32[1024,2304]{1,0:T(8,128)S(1)} %fusion.114, bf16[1024,1152]{1,0:T(8,128)(2,1)} %get-tuple-element.220, bf16[2304,1152]{1,0:T(8,128)(2,1)} %get-tuple-element.209), kind=kOutput, calls=%fused_computation.185 | convolution fusion | flops 5440536576 | bytes 21823488 | tf_op jit(solution)/shard_map/dot_general | solution.py:103
  564.3 71.4 %conditional.23 = (f32[128,2304]{1,0:T(8,128)S(1)}, bf16[16,72,1152]{2,1,0:T(8,128)(2,1)}, bf16[16,72,1152]{2,1,0:T(8,128)(2,1)}) conditional(s32[]{:T(128)} %bitcast.71, () %tuple.160, (bf16[1024,2304]{1,0:T(8,128)(2,1)S(1)}, bf16[2304,1024]{1,0:T(8,128)(2,1)}, bf16[1024,1152]{1,0:T(8,128)(2,1)}, bf16[1024,1152]{1,0:T(8,128)(2,1)}) %tuple.269), branch_computations={%region_30.31_spmd, %region_31.32_spmd} | conditional | flops 10888151040 | bytes 189924064 | solution.py:165
  571.3 10.3 %fusion.106 = bf16[2304,1152]{1,0:T(8,128)(2,1)} fusion(bf16[2304,1024]{1,0:T(8,128)(2,1)} %get-tuple-element.131, bf16[1024,1152]{1,0:T(8,128)(2,1)} %get-tuple-element.132), kind=kOutput, calls=%fused_computation.353 | convolution fusion | flops 5435817984 | bytes 12386304 | tf_op jit(solution)/shard_map/cond/branch_1_fun/dot_general | solution.py:103
  585.1 8.9 fusion.107
  647.3 53.4 %conditional.24 = (bf16[1024,2304]{1,0:T(8,128)(2,1)}) conditional(s32[]{:T(128)} %bitcast.71, () %tuple.167, bf16[128,2304]{1,0:T(8,128)(2,1)S(1)} %fusion.52), branch_computations={%region_34.35_spmd, %region_35.36_spmd} | conditional | flops 30081024 | bytes 34210040 | solution.py:165
  657.4 14.2 %collective-permute-done.38 = bf16[1,1,1,128,1152]{4,3,2,1,0:T(8,128)(2,1)S(1)} collective-permute-done((bf16[1,1,1,128,1152]{4,3,2,1,0:T(8,128)(2,1)S(1)}, bf16[1,1,1,128,1152]{4,3,2,1,0:T(8,128)(2,1)S(1)}, u32[]{:S(2)}, u32[]{:S(2)}) %collective-permute-start.38) | collective-permute-done | bytes 294944 | tf_op jit(solution)/shard_map/cond/branch_1_fun/ppermute | solution.py:112
  673.2 10.9 %collective-permute-done.42 = bf16[1,1,2,128,1152]{4,3,2,1,0:T(8,128)(2,1)S(1)} collective-permute-done((bf16[1,1,2,128,1152]{4,3,2,1,0:T(8,128)(2,1)S(1)}, bf16[1,1,2,128,1152]{4,3,2,1,0:T(8,128)(2,1)S(1)}, u32[]{:S(2)}, u32[]{:S(2)}) %collective-permute-start.42) | collective-permute-done | bytes 589856 | tf_op jit(solution)/shard_map/cond/branch_1_fun/ppermute | solution.py:112
  684.3 9.5 %collective-permute-done.39 = bf16[1,2,1,128,1152]{4,3,2,1,0:T(8,128)(2,1)S(1)} collective-permute-done((bf16[1,2,1,128,1152]{4,3,2,1,0:T(8,128)(2,1)S(1)}, bf16[1,2,1,128,1152]{4,3,2,1,0:T(8,128)(2,1)S(1)}, u32[]{:S(2)}, u32[]{:S(2)}) %collective-permute-start.39) | collective-permute-done | bytes 589856 | tf_op jit(solution)/shard_map/cond/branch_1_fun/ppermute | solution.py:112
  700.7 7.8 all-to-all-start.7
  713.5 18.0 %shard_map.170 = (bf16[1024,256]{1,0:T(8,128)(2,1)}, f32[3072,256]{1,0:T(8,128)S(1)}, f32[3072,256]{1,0:T(8,128)}) custom-call(bf16[1024,256]{1,0:T(8,128)(2,1)} %get-tuple-element.302.q_ref, bf16[3072,256]{1,0:T(8,128)(2,1)} %get-tuple-element.197.k_ref, bf16[3072,256]{1,0:T(8,128)(2,1)} %get-tuple-element.198.v_ref, s32[1024,1]{1,0:T(8,128)} %add_maximum_fusion.low_ref, ...), custom_call_target="tpu_custom_call" | custom-call | flops 1 | bytes 1 | tf_op jit(solution)/shard_map/pallas_call | solution.py:283
  735.8 63.4 %conditional.25 = (bf16[2304,1024]{0,1:T(8,128)(2,1)}, f32[1024,256]{1,0:T(8,128)}, f32[1024,128]{1,0:T(8,128)S(1)}, f32[1024,128]{1,0:T(8,128)S(1)}, bf16[32,1,72,256]{3,2,0,1:T(8,128)(2,1)}) conditional(s32[]{:T(128)} %bitcast.71, () %tuple.168, (bf16[1024,2304]{1,0:T(8,128)(2,1)}, s32[]{:T(128)}, f32[3072,256]{1,0:T(8,128)S(1)}, ...), branch_computations={%region_36.37_spmd, %region_37.38_spmd} | conditional | flops 1216086016 | bytes 85066000 | solution.py:165
  745.9 21.5 %collective-permute-done.81 = bf16[1024,256]{1,0:T(8,128)(2,1)S(1)} collective-permute-done((bf16[1024,256]{1,0:T(8,128)(2,1)S(1)}, bf16[1024,256]{1,0:T(8,128)(2,1)S(1)}, u32[]{:S(2)}, u32[]{:S(2)}) %collective-permute-start.81) | collective-permute-done | bytes 524320 | tf_op jit(solution)/shard_map/cond/branch_1_fun/ppermute | solution.py:202
  768.9 27.6 %collective-permute-done.82 = bf16[1024,256]{1,0:T(8,128)(2,1)S(1)} collective-permute-done((bf16[1024,256]{1,0:T(8,128)(2,1)S(1)}, bf16[1024,256]{1,0:T(8,128)(2,1)S(1)}, u32[]{:S(2)}, u32[]{:S(2)}) %collective-permute-start.82) | collective-permute-done | bytes 524320 | tf_op jit(solution)/shard_map/cond/branch_1_fun/ppermute | solution.py:202
  822.5 53.5 %conditional.26 = (f32[128,2304]{1,0:T(8,128)S(1)}) conditional(s32[]{:T(128)} %bitcast.71, () %tuple.166, bf16[1024,2304]{1,0:T(8,128)(2,1)} %add_convert_fusion.1), branch_computations={%region_38.39_spmd, %region_39.40_spmd} | conditional | flops 5603328 | bytes 64291092 | solution.py:165
  833.0 28.9 %collective-permute-done.57 = bf16[1,1,2,128,1152]{4,3,2,1,0:T(8,128)(2,1)S(1)} collective-permute-done((bf16[1,1,2,128,1152]{4,3,2,1,0:T(8,128)(2,1)S(1)}, bf16[1,1,2,128,1152]{4,3,2,1,0:T(8,128)(2,1)S(1)}, u32[]{:S(2)}, u32[]{:S(2)}) %collective-permute-start.57) | collective-permute-done | bytes 589856 | tf_op jit(solution)/shard_map/cond/branch_1_fun/ppermute | solution.py:112
  876.8 20.6 %conditional.27 = (f32[4,2304]{1,0:T(4,128)S(1)}) conditional(s32[]{:T(128)} %bitcast.71, () %tuple.173, f32[4,2304]{1,0:T(4,128)S(1)} %pad_maximum_fusion.33), branch_computations={%region_49.50_spmd, %region_50.51_spmd} | conditional | flops 46080 | bytes 1290448 | solution.py:165
  (591 shorter events, 465.1 us)
Async XLA Ops:
  3.7 70.9 %all-to-all-start = ((bf16[32,2,72,256]{3,2,1,0:T(8,128)(2,1)}), bf16[32,2,72,256]{3,2,1,0:T(8,128)(2,1)S(1)}, u32[]{:S(2)}, u32[]{:S(2)}) async-start(bf16[32,2,72,256]{3,2,1,0:T(8,128)(2,1)} %bitcast.279), calls=%async_computation | async-start | bytes 4718592 | tf_op jit(solution)/shard_map/all_to_all | solution.py:297
  17.8 23.6 %collective-permute-start.8 = (bf16[1,1,1,128,1152]{4,3,2,1,0:T(8,128)(2,1)S(1)}, bf16[1,1,1,128,1152]{4,3,2,1,0:T(8,128)(2,1)S(1)}, u32[]{:S(2)}, u32[]{:S(2)}) collective-permute-start(bf16[1,1,1,128,1152]{4,3,2,1,0:T(8,128)(2,1)S(1)} %get-tuple-element.327), channel_id=1, source_target_pairs={{0,2},{2,0},{1,3},{3,1},{4,6},{6,4},{5,7},{7,5},{8,10},{10,8},{9,1... | collective-permute-start | bytes 884744 | tf_op jit(solution)/shard_map/cond/branch_1_fun/ppermute | solution.py:112
  19.7 23.7 %collective-permute-start.5 = (bf16[1,1,1,128,1152]{4,3,2,1,0:T(8,128)(2,1)S(1)}, bf16[1,1,1,128,1152]{4,3,2,1,0:T(8,128)(2,1)S(1)}, u32[]{:S(2)}, u32[]{:S(2)}) collective-permute-start(bf16[1,1,1,128,1152]{4,3,2,1,0:T(8,128)(2,1)S(1)} %get-tuple-element.326), channel_id=1, source_target_pairs={{0,4},{4,0},{1,5},{5,1},{2,6},{6,2},{3,7},{7,3},{8,12},{12,8},{9,1... | collective-permute-start | bytes 884744 | tf_op jit(solution)/shard_map/cond/branch_1_fun/ppermute | solution.py:112
  41.5 18.6 %collective-permute-start.9 = (bf16[1,1,2,128,1152]{4,3,2,1,0:T(8,128)(2,1)S(1)}, bf16[1,1,2,128,1152]{4,3,2,1,0:T(8,128)(2,1)S(1)}, u32[]{:S(2)}, u32[]{:S(2)}) collective-permute-start(bf16[1,1,2,128,1152]{4,3,2,1,0:T(8,128)(2,1)S(1)} %pad_maximum_fusion.3), channel_id=1, source_target_pairs={{0,4},{4,0},{1,5},{5,1},{2,6},{6,2},{3,7},{7,3},{8,12},{12,8},{9,1... | collective-permute-start | bytes 1769480 | tf_op jit(solution)/shard_map/cond/branch_1_fun/ppermute | solution.py:112
  43.4 19.0 %collective-permute-start.6 = (bf16[1,2,1,128,1152]{4,3,2,1,0:T(8,128)(2,1)S(1)}, bf16[1,2,1,128,1152]{4,3,2,1,0:T(8,128)(2,1)S(1)}, u32[]{:S(2)}, u32[]{:S(2)}) collective-permute-start(bf16[1,2,1,128,1152]{4,3,2,1,0:T(8,128)(2,1)S(1)} %pad_maximum_fusion.2), channel_id=1, source_target_pairs={{0,2},{2,0},{1,3},{3,1},{4,6},{6,4},{5,7},{7,5},{8,10},{10,8},{9,1... | collective-permute-start | bytes 1769480 | tf_op jit(solution)/shard_map/cond/branch_1_fun/ppermute | solution.py:112
  76.0 68.3 %all-to-all-start.1 = ((bf16[32,72,256]{2,1,0:T(8,128)(2,1)}), bf16[32,72,256]{2,1,0:T(8,128)(2,1)}, u32[]{:S(2)}, u32[]{:S(2)}) async-start(bf16[32,72,256]{2,1,0:T(8,128)(2,1)} %bitcast.315), calls=%async_computation.1 | async-start | bytes 2359296 | tf_op jit(solution)/shard_map/all_to_all | solution.py:297
  95.8 15.4 %collective-permute-start.65 = (bf16[1024,256]{1,0:T(8,128)(2,1)}, bf16[1024,256]{1,0:T(8,128)(2,1)}, u32[]{:S(2)}, u32[]{:S(2)}) collective-permute-start(bf16[1024,256]{1,0:T(8,128)(2,1)} %get-tuple-element.101), channel_id=1, source_target_pairs={{0,8},{8,16},{16,24},{1,9},{9,17},{17,25},{2,10},{10,18},{18,26},{... | collective-permute-start | bytes 1572872 | tf_op jit(solution)/shard_map/cond/branch_1_fun/ppermute | solution.py:202
  111.4 20.6 %collective-permute-start.66 = (bf16[1024,256]{1,0:T(8,128)(2,1)}, bf16[1024,256]{1,0:T(8,128)(2,1)S(1)}, u32[]{:S(2)}, u32[]{:S(2)}) collective-permute-start(bf16[1024,256]{1,0:T(8,128)(2,1)} %collective-permute-done.65), channel_id=1, source_target_pairs={{0,8},{8,16},{16,24},{1,9},{9,17},{17,25},{2,10},{10,18},{18,26},{... | collective-permute-start | bytes 1572872 | tf_op jit(solution)/shard_map/cond/branch_1_fun/ppermute | solution.py:202
  145.8 78.4 %all-to-all-start.2 = ((bf16[16,72,1152]{2,1,0:T(8,128)(2,1)}), bf16[16,72,1152]{2,1,0:T(8,128)(2,1)S(1)}, u32[]{:S(2)}, u32[]{:S(2)}) async-start(bf16[16,72,1152]{2,1,0:T(8,128)(2,1)} %copy-done.6), calls=%async_computation.2 | async-start | bytes 5308416 | tf_op jit(solution)/shard_map/all_to_all | solution.py:297
  179.7 22.0 %collective-permute-start.63 = (bf16[1,1,2,128,1152]{4,3,2,1,0:T(8,128)(2,1)S(1)}, bf16[1,1,2,128,1152]{4,3,2,1,0:T(8,128)(2,1)S(1)}, u32[]{:S(2)}, u32[]{:S(2)}) collective-permute-start(bf16[1,1,2,128,1152]{4,3,2,1,0:T(8,128)(2,1)S(1)} %slice.563), channel_id=1, source_target_pairs={{0,4},{4,0},{1,5},{5,1},{2,6},{6,2},{3,7},{7,3},{8,12},{12,8},{9,1... | collective-permute-start | bytes 1769480 | tf_op jit(solution)/shard_map/cond/branch_1_fun/ppermute | solution.py:112
  181.8 27.0 %collective-permute-start.60 = (bf16[1,2,1,128,1152]{4,3,2,1,0:T(8,128)(2,1)S(1)}, bf16[1,2,1,128,1152]{4,3,2,1,0:T(8,128)(2,1)S(1)}, u32[]{:S(2)}, u32[]{:S(2)}) collective-permute-start(bf16[1,2,1,128,1152]{4,3,2,1,0:T(8,128)(2,1)S(1)} %slice.564), channel_id=1, source_target_pairs={{0,2},{2,0},{1,3},{3,1},{4,6},{6,4},{5,7},{7,5},{8,10},{10,8},{9,1... | collective-permute-start | bytes 1769480 | tf_op jit(solution)/shard_map/cond/branch_1_fun/ppermute | solution.py:112
  201.9 14.8 %collective-permute-start.64 = (bf16[1,1,1,128,1152]{4,3,2,1,0:T(8,128)(2,1)S(1)}, bf16[1,1,1,128,1152]{4,3,2,1,0:T(8,128)(2,1)S(1)}, u32[]{:S(2)}, u32[]{:S(2)}) collective-permute-start(bf16[1,1,1,128,1152]{4,3,2,1,0:T(8,128)(2,1)S(1)} %slice.565), channel_id=1, source_target_pairs={{0,2},{2,0},{1,3},{3,1},{4,6},{6,4},{5,7},{7,5},{8,10},{10,8},{9,1... | collective-permute-start | bytes 884744 | tf_op jit(solution)/shard_map/cond/branch_1_fun/ppermute | solution.py:112
  208.9 14.1 %collective-permute-start.61 = (bf16[1,1,1,128,1152]{4,3,2,1,0:T(8,128)(2,1)S(1)}, bf16[1,1,1,128,1152]{4,3,2,1,0:T(8,128)(2,1)S(1)}, u32[]{:S(2)}, u32[]{:S(2)}) collective-permute-start(bf16[1,1,1,128,1152]{4,3,2,1,0:T(8,128)(2,1)S(1)} %slice.566), channel_id=1, source_target_pairs={{0,4},{4,0},{1,5},{5,1},{2,6},{6,2},{3,7},{7,3},{8,12},{12,8},{9,1... | collective-permute-start | bytes 884744 | tf_op jit(solution)/shard_map/cond/branch_1_fun/ppermute | solution.py:112
  224.2 96.5 %all-to-all-start.3 = ((bf16[16,72,1152]{2,1,0:T(8,128)(2,1)}), bf16[16,72,1152]{2,1,0:T(8,128)(2,1)}, u32[]{:S(2)}, u32[]{:S(2)}) async-start(bf16[16,72,1152]{2,1,0:T(8,128)(2,1)} %get-tuple-element.207), calls=%async_computation.3 | async-start | bytes 5308416 | tf_op jit(solution)/shard_map/all_to_all | solution.py:297
  237.3 22.5 %collective-permute-start.18 = (bf16[1,1,1,128,768]{4,3,2,1,0:T(8,128)(2,1)S(1)}, bf16[1,1,1,128,768]{4,3,2,1,0:T(8,128)(2,1)S(1)}, u32[]{:S(2)}, u32[]{:S(2)}) collective-permute-start(bf16[1,1,1,128,768]{4,3,2,1,0:T(8,128)(2,1)S(1)} %get-tuple-element.335), channel_id=1, source_target_pairs={{0,2},{2,0},{1,3},{3,1},{4,6},{6,4},{5,7},{7,5},{8,10},{10,8},{9,1... | collective-permute-start | bytes 589832 | tf_op jit(solution)/shard_map/cond/branch_1_fun/ppermute | solution.py:112
  239.6 22.5 %collective-permute-start.15 = (bf16[1,1,1,128,768]{4,3,2,1,0:T(8,128)(2,1)S(1)}, bf16[1,1,1,128,768]{4,3,2,1,0:T(8,128)(2,1)S(1)}, u32[]{:S(2)}, u32[]{:S(2)}) collective-permute-start(bf16[1,1,1,128,768]{4,3,2,1,0:T(8,128)(2,1)S(1)} %get-tuple-element.336), channel_id=1, source_target_pairs={{0,4},{4,0},{1,5},{5,1},{2,6},{6,2},{3,7},{7,3},{8,12},{12,8},{9,1... | collective-permute-start | bytes 589832 | tf_op jit(solution)/shard_map/cond/branch_1_fun/ppermute | solution.py:112
  241.1 39.6 %collective-permute-start.11 = (bf16[1,1,1,128,768]{4,3,2,1,0:T(8,128)(2,1)S(1)}, bf16[1,1,1,128,768]{4,3,2,1,0:T(8,128)(2,1)S(1)}, u32[]{:S(2)}, u32[]{:S(2)}) collective-permute-start(bf16[1,1,1,128,768]{4,3,2,1,0:T(8,128)(2,1)S(1)} %get-tuple-element.334), channel_id=1, source_target_pairs={{0,8},{8,0},{1,9},{9,1},{2,10},{10,2},{3,11},{11,3},{4,12},{12,4},... | collective-permute-start | bytes 589832 | tf_op jit(solution)/shard_map/cond/branch_1_fun/ppermute | solution.py:112
  259.7 52.9 %collective-permute-start.21 = (bf16[2,8,72,1152]{3,2,1,0:T(8,128)(2,1)}, bf16[2,8,72,1152]{3,2,1,0:T(8,128)(2,1)}, u32[]{:S(2)}, u32[]{:S(2)}) collective-permute-start(bf16[2,8,72,1152]{3,2,1,0:T(8,128)(2,1)} %multiply_convert_fusion), channel_id=1, source_target_pairs={{0,1},{1,0},{2,3},{3,2},{4,5},{5,4},{6,7},{7,6},{8,9},{9,8},{10,11... | collective-permute-start | bytes 7962632 | tf_op jit(solution)/shard_map/cond/branch_1_fun/ppermute | solution.py:112
  261.5 28.7 %collective-permute-start.19 = (bf16[1,1,2,128,768]{4,3,2,1,0:T(8,128)(2,1)S(1)}, bf16[1,1,2,128,768]{4,3,2,1,0:T(8,128)(2,1)S(1)}, u32[]{:S(2)}, u32[]{:S(2)}) collective-permute-start(bf16[1,1,2,128,768]{4,3,2,1,0:T(8,128)(2,1)S(1)} %pad_maximum_fusion.10), channel_id=1, source_target_pairs={{0,8},{8,0},{1,9},{9,1},{2,10},{10,2},{3,11},{11,3},{4,12},{12,4},... | collective-permute-start | bytes 1179656 | tf_op jit(solution)/shard_map/cond/branch_1_fun/ppermute | solution.py:112
  262.1 28.2 %collective-permute-start.16 = (bf16[1,2,1,128,768]{4,3,2,1,0:T(8,128)(2,1)S(1)}, bf16[1,2,1,128,768]{4,3,2,1,0:T(8,128)(2,1)S(1)}, u32[]{:S(2)}, u32[]{:S(2)}) collective-permute-start(bf16[1,2,1,128,768]{4,3,2,1,0:T(8,128)(2,1)S(1)} %pad_maximum_fusion.9), channel_id=1, source_target_pairs={{0,2},{2,0},{1,3},{3,1},{4,6},{6,4},{5,7},{7,5},{8,10},{10,8},{9,1... | collective-permute-start | bytes 1179656 | tf_op jit(solution)/shard_map/cond/branch_1_fun/ppermute | solution.py:112
  290.2 18.7 %collective-permute-start.20 = (bf16[2,1,2,128,768]{4,3,2,1,0:T(8,128)(2,1)S(1)}, bf16[2,1,2,128,768]{4,3,2,1,0:T(8,128)(2,1)}, u32[]{:S(2)}, u32[]{:S(2)}) collective-permute-start(bf16[2,1,2,128,768]{4,3,2,1,0:T(8,128)(2,1)S(1)} %constant_dynamic-update-slice_fusion.4), channel_id=1, source_target_pairs={{0,4},{4,0},{1,5},{5,1},{2,6},{6,2},{3,7},{7,3},{8,12},{12,8},{9,1... | collective-permute-start | bytes 2359304 | tf_op jit(solution)/shard_map/cond/branch_1_fun/ppermute | solution.py:112
  290.3 18.7 %collective-permute-start.17 = (bf16[1,2,2,128,768]{4,3,2,1,0:T(8,128)(2,1)S(1)}, bf16[1,2,2,128,768]{4,3,2,1,0:T(8,128)(2,1)}, u32[]{:S(2)}, u32[]{:S(2)}) collective-permute-start(bf16[1,2,2,128,768]{4,3,2,1,0:T(8,128)(2,1)S(1)} %constant_dynamic-update-slice_fusion.2), channel_id=1, source_target_pairs={{0,8},{8,0},{1,9},{9,1},{2,10},{10,2},{3,11},{11,3},{4,12},{12,4},... | collective-permute-start | bytes 2359304 | tf_op jit(solution)/shard_map/cond/branch_1_fun/ppermute | solution.py:112
  290.6 18.5 %collective-permute-start.14 = (bf16[2,2,1,128,768]{4,3,2,1,0:T(8,128)(2,1)S(1)}, bf16[2,2,1,128,768]{4,3,2,1,0:T(8,128)(2,1)}, u32[]{:S(2)}, u32[]{:S(2)}) collective-permute-start(bf16[2,2,1,128,768]{4,3,2,1,0:T(8,128)(2,1)S(1)} %constant_dynamic-update-slice_fusion), channel_id=1, source_target_pairs={{0,2},{2,0},{1,3},{3,1},{4,6},{6,4},{5,7},{7,5},{8,10},{10,8},{9,1... | collective-permute-start | bytes 2359304 | tf_op jit(solution)/shard_map/cond/branch_1_fun/ppermute | solution.py:112
  320.7 60.9 %all-to-all-start.4 = ((bf16[16,72,1152]{2,1,0:T(8,128)(2,1)}), bf16[16,72,1152]{2,1,0:T(8,128)(2,1)}, u32[]{:S(2)}, u32[]{:S(2)}) async-start(bf16[16,72,1152]{2,1,0:T(8,128)(2,1)} %get-tuple-element.211), calls=%async_computation.4 | async-start | bytes 5308416 | tf_op jit(solution)/shard_map/all_to_all | solution.py:297
  403.9 20.0 %collective-permute-start.50 = (bf16[2,1,2,128,768]{4,3,2,1,0:T(8,128)(2,1)S(1)}, bf16[2,1,2,128,768]{4,3,2,1,0:T(8,128)(2,1)S(1)}, u32[]{:S(2)}, u32[]{:S(2)}) collective-permute-start(bf16[2,1,2,128,768]{4,3,2,1,0:T(8,128)(2,1)S(1)} %slice.399), channel_id=1, source_target_pairs={{0,4},{4,0},{1,5},{5,1},{2,6},{6,2},{3,7},{7,3},{8,12},{12,8},{9,1... | collective-permute-start | bytes 2359304 | tf_op jit(solution)/shard_map/cond/branch_1_fun/ppermute | solution.py:112
  406.0 25.9 %collective-permute-start.47 = (bf16[1,2,2,128,768]{4,3,2,1,0:T(8,128)(2,1)S(1)}, bf16[1,2,2,128,768]{4,3,2,1,0:T(8,128)(2,1)S(1)}, u32[]{:S(2)}, u32[]{:S(2)}) collective-permute-start(bf16[1,2,2,128,768]{4,3,2,1,0:T(8,128)(2,1)S(1)} %slice.393), channel_id=1, source_target_pairs={{0,8},{8,0},{1,9},{9,1},{2,10},{10,2},{3,11},{11,3},{4,12},{12,4},... | collective-permute-start | bytes 2359304 | tf_op jit(solution)/shard_map/cond/branch_1_fun/ppermute | solution.py:112
  413.9 19.2 %collective-permute-start.44 = (bf16[2,2,1,128,768]{4,3,2,1,0:T(8,128)(2,1)S(1)}, bf16[2,2,1,128,768]{4,3,2,1,0:T(8,128)(2,1)S(1)}, u32[]{:S(2)}, u32[]{:S(2)}) collective-permute-start(bf16[2,2,1,128,768]{4,3,2,1,0:T(8,128)(2,1)S(1)} %slice.387), channel_id=1, source_target_pairs={{0,2},{2,0},{1,3},{3,1},{4,6},{6,4},{5,7},{7,5},{8,10},{10,8},{9,1... | collective-permute-start | bytes 2359304 | tf_op jit(solution)/shard_map/cond/branch_1_fun/ppermute | solution.py:112
  424.1 16.8 %collective-permute-start.51 = (bf16[1,1,2,128,768]{4,3,2,1,0:T(8,128)(2,1)S(1)}, bf16[1,1,2,128,768]{4,3,2,1,0:T(8,128)(2,1)S(1)}, u32[]{:S(2)}, u32[]{:S(2)}) collective-permute-start(bf16[1,1,2,128,768]{4,3,2,1,0:T(8,128)(2,1)S(1)} %slice.567), channel_id=1, source_target_pairs={{0,8},{8,0},{1,9},{9,1},{2,10},{10,2},{3,11},{11,3},{4,12},{12,4},... | collective-permute-start | bytes 1179656 | tf_op jit(solution)/shard_map/cond/branch_1_fun/ppermute | solution.py:112
  478.4 18.6 %collective-permute-start.33 = (bf16[2,1,2,128,768]{4,3,2,1,0:T(8,128)(2,1)S(1)}, bf16[2,1,2,128,768]{4,3,2,1,0:T(8,128)(2,1)S(1)}, u32[]{:S(2)}, u32[]{:S(2)}) collective-permute-start(bf16[2,1,2,128,768]{4,3,2,1,0:T(8,128)(2,1)S(1)} %pad_maximum_fusion.14), channel_id=1, source_target_pairs={{0,4},{4,0},{1,5},{5,1},{2,6},{6,2},{3,7},{7,3},{8,12},{12,8},{9,1... | collective-permute-start | bytes 2359304 | tf_op jit(solution)/shard_map/cond/branch_1_fun/ppermute | solution.py:112
  480.0 17.3 %collective-permute-start.30 = (bf16[1,2,2,128,768]{4,3,2,1,0:T(8,128)(2,1)S(1)}, bf16[1,2,2,128,768]{4,3,2,1,0:T(8,128)(2,1)S(1)}, u32[]{:S(2)}, u32[]{:S(2)}) collective-permute-start(bf16[1,2,2,128,768]{4,3,2,1,0:T(8,128)(2,1)S(1)} %pad_maximum_fusion.13), channel_id=1, source_target_pairs={{0,8},{8,0},{1,9},{9,1},{2,10},{10,2},{3,11},{11,3},{4,12},{12,4},... | collective-permute-start | bytes 2359304 | tf_op jit(solution)/shard_map/cond/branch_1_fun/ppermute | solution.py:112
  481.3 16.5 %collective-permute-start.27 = (bf16[2,2,1,128,768]{4,3,2,1,0:T(8,128)(2,1)S(1)}, bf16[2,2,1,128,768]{4,3,2,1,0:T(8,128)(2,1)S(1)}, u32[]{:S(2)}, u32[]{:S(2)}) collective-permute-start(bf16[2,2,1,128,768]{4,3,2,1,0:T(8,128)(2,1)S(1)} %pad_maximum_fusion.12), channel_id=1, source_target_pairs={{0,2},{2,0},{1,3},{3,1},{4,6},{6,4},{5,7},{7,5},{8,10},{10,8},{9,1... | collective-permute-start | bytes 2359304 | tf_op jit(solution)/shard_map/cond/branch_1_fun/ppermute | solution.py:112
  514.4 15.8 %collective-permute-start.68 = (bf16[2,8,72,1152]{3,2,1,0:T(8,128)(2,1)}, bf16[2,8,72,1152]{3,2,1,0:T(8,128)(2,1)}, u32[]{:S(2)}, u32[]{:S(2)}) collective-permute-start(bf16[2,8,72,1152]{3,2,1,0:T(8,128)(2,1)} %dynamic-slice_bitcast_fusion), channel_id=1, source_target_pairs={{0,1},{1,0},{2,3},{3,2},{4,5},{5,4},{6,7},{7,6},{8,9},{9,8},{10,11... | collective-permute-start | bytes 7962632 | tf_op jit(solution)/shard_map/cond/branch_1_fun/ppermute | solution.py:112
  534.1 101.5 %all-to-all-start.5 = ((bf16[16,72,1152]{2,1,0:T(8,128)(2,1)}), bf16[16,72,1152]{2,1,0:T(8,128)(2,1)}, u32[]{:S(2)}, u32[]{:S(2)}) async-start(bf16[16,72,1152]{2,1,0:T(8,128)(2,1)} %bitcast.98), calls=%async_computation.5 | async-start | bytes 5308416 | tf_op jit(solution)/shard_map/all_to_all | solution.py:297
  565.5 33.0 %collective-permute-start.75 = (bf16[2,1,2,128,768]{4,3,2,1,0:T(8,128)(2,1)}, bf16[2,1,2,128,768]{4,3,2,1,0:T(8,128)(2,1)}, u32[]{:S(2)}, u32[]{:S(2)}) collective-permute-start(bf16[2,1,2,128,768]{4,3,2,1,0:T(8,128)(2,1)} %slice.417), channel_id=1, source_target_pairs={{0,4},{4,0},{1,5},{5,1},{2,6},{6,2},{3,7},{7,3},{8,12},{12,8},{9,1... | collective-permute-start | bytes 2359304 | tf_op jit(solution)/shard_map/cond/branch_1_fun/ppermute | solution.py:112
  568.2 36.8 %collective-permute-start.72 = (bf16[1,2,2,128,768]{4,3,2,1,0:T(8,128)(2,1)}, bf16[1,2,2,128,768]{4,3,2,1,0:T(8,128)(2,1)}, u32[]{:S(2)}, u32[]{:S(2)}) collective-permute-start(bf16[1,2,2,128,768]{4,3,2,1,0:T(8,128)(2,1)} %slice.411), channel_id=1, source_target_pairs={{0,8},{8,0},{1,9},{9,1},{2,10},{10,2},{3,11},{11,3},{4,12},{12,4},... | collective-permute-start | bytes 2359304 | tf_op jit(solution)/shard_map/cond/branch_1_fun/ppermute | solution.py:112
  569.7 38.4 %collective-permute-start.69 = (bf16[2,2,1,128,768]{4,3,2,1,0:T(8,128)(2,1)S(1)}, bf16[2,2,1,128,768]{4,3,2,1,0:T(8,128)(2,1)}, u32[]{:S(2)}, u32[]{:S(2)}) collective-permute-start(bf16[2,2,1,128,768]{4,3,2,1,0:T(8,128)(2,1)S(1)} %slice.405), channel_id=1, source_target_pairs={{0,2},{2,0},{1,3},{3,1},{4,6},{6,4},{5,7},{7,5},{8,10},{10,8},{9,1... | collective-permute-start | bytes 2359304 | tf_op jit(solution)/shard_map/cond/branch_1_fun/ppermute | solution.py:112
  585.1 42.4 %collective-permute-start.78 = (bf16[2,8,72,1152]{3,2,1,0:T(8,128)(2,1)}, bf16[2,8,72,1152]{3,2,1,0:T(8,128)(2,1)}, u32[]{:S(2)}, u32[]{:S(2)}) collective-permute-start(bf16[2,8,72,1152]{3,2,1,0:T(8,128)(2,1)} %dynamic-slice_bitcast_fusion.2), channel_id=1, source_target_pairs={{0,1},{1,0},{2,3},{3,2},{4,5},{5,4},{6,7},{7,6},{8,9},{9,8},{10,11... | collective-permute-start | bytes 7962632 | tf_op jit(solution)/shard_map/cond/branch_1_fun/ppermute | solution.py:112
  598.0 33.7 %collective-permute-start.79 = (bf16[2,8,72,1152]{3,2,1,0:T(8,128)(2,1)}, bf16[2,8,72,1152]{3,2,1,0:T(8,128)(2,1)}, u32[]{:S(2)}, u32[]{:S(2)}) collective-permute-start(bf16[2,8,72,1152]{3,2,1,0:T(8,128)(2,1)} %dynamic-slice_bitcast_fusion.1), channel_id=1, source_target_pairs={{0,1},{1,0},{2,3},{3,2},{4,5},{5,4},{6,7},{7,6},{8,9},{9,8},{10,11... | collective-permute-start | bytes 7962632 | tf_op jit(solution)/shard_map/cond/branch_1_fun/ppermute | solution.py:112
  635.7 65.0 %all-to-all-start.6 = ((bf16[16,72,1152]{2,1,0:T(8,128)(2,1)}), bf16[16,72,1152]{2,1,0:T(8,128)(2,1)}, u32[]{:S(2)}, u32[]{:S(2)}) async-start(bf16[16,72,1152]{2,1,0:T(8,128)(2,1)} %get-tuple-element.234), calls=%async_computation.6 | async-start | bytes 5308416 | tf_op jit(solution)/shard_map/all_to_all | solution.py:297
  649.5 22.1 %collective-permute-start.38 = (bf16[1,1,1,128,1152]{4,3,2,1,0:T(8,128)(2,1)S(1)}, bf16[1,1,1,128,1152]{4,3,2,1,0:T(8,128)(2,1)S(1)}, u32[]{:S(2)}, u32[]{:S(2)}) collective-permute-start(bf16[1,1,1,128,1152]{4,3,2,1,0:T(8,128)(2,1)S(1)} %get-tuple-element.352), channel_id=1, source_target_pairs={{0,4},{4,0},{1,5},{5,1},{2,6},{6,2},{3,7},{7,3},{8,12},{12,8},{9,1... | collective-permute-start | bytes 884744 | tf_op jit(solution)/shard_map/cond/branch_1_fun/ppermute | solution.py:112
  657.1 27.0 %collective-permute-start.42 = (bf16[1,1,2,128,1152]{4,3,2,1,0:T(8,128)(2,1)S(1)}, bf16[1,1,2,128,1152]{4,3,2,1,0:T(8,128)(2,1)S(1)}, u32[]{:S(2)}, u32[]{:S(2)}) collective-permute-start(bf16[1,1,2,128,1152]{4,3,2,1,0:T(8,128)(2,1)S(1)} %pad_maximum_fusion.24), channel_id=1, source_target_pairs={{0,4},{4,0},{1,5},{5,1},{2,6},{6,2},{3,7},{7,3},{8,12},{12,8},{9,1... | collective-permute-start | bytes 1769480 | tf_op jit(solution)/shard_map/cond/branch_1_fun/ppermute | solution.py:112
  671.7 22.1 %collective-permute-start.39 = (bf16[1,2,1,128,1152]{4,3,2,1,0:T(8,128)(2,1)S(1)}, bf16[1,2,1,128,1152]{4,3,2,1,0:T(8,128)(2,1)S(1)}, u32[]{:S(2)}, u32[]{:S(2)}) collective-permute-start(bf16[1,2,1,128,1152]{4,3,2,1,0:T(8,128)(2,1)S(1)} %pad_maximum_fusion.23), channel_id=1, source_target_pairs={{0,2},{2,0},{1,3},{3,1},{4,6},{6,4},{5,7},{7,5},{8,10},{10,8},{9,1... | collective-permute-start | bytes 1769480 | tf_op jit(solution)/shard_map/cond/branch_1_fun/ppermute | solution.py:112
  700.7 111.3 %all-to-all-start.7 = ((bf16[16,72,1152]{2,1,0:T(8,128)(2,1)}), bf16[16,72,1152]{2,1,0:T(8,128)(2,1)}, u32[]{:S(2)}, u32[]{:S(2)}) async-start(bf16[16,72,1152]{2,1,0:T(8,128)(2,1)} %get-tuple-element.235), calls=%async_computation.7 | async-start | bytes 5308416 | tf_op jit(solution)/shard_map/all_to_all | solution.py:297
  742.1 25.3 %collective-permute-start.81 = (bf16[1024,256]{1,0:T(8,128)(2,1)S(1)}, bf16[1024,256]{1,0:T(8,128)(2,1)S(1)}, u32[]{:S(2)}, u32[]{:S(2)}) collective-permute-start(bf16[1024,256]{1,0:T(8,128)(2,1)S(1)} %fusion.31), channel_id=1, source_target_pairs={{8,0},{16,8},{24,16},{9,1},{17,9},{25,17},{10,2},{18,10},{26,18},{... | collective-permute-start | bytes 1572872 | tf_op jit(solution)/shard_map/cond/branch_1_fun/ppermute | solution.py:202
  767.6 28.9 %collective-permute-start.82 = (bf16[1024,256]{1,0:T(8,128)(2,1)S(1)}, bf16[1024,256]{1,0:T(8,128)(2,1)S(1)}, u32[]{:S(2)}, u32[]{:S(2)}) collective-permute-start(bf16[1024,256]{1,0:T(8,128)(2,1)S(1)} %fusion.27), channel_id=1, source_target_pairs={{8,0},{16,8},{24,16},{9,1},{17,9},{25,17},{10,2},{18,10},{26,18},{... | collective-permute-start | bytes 1572872 | tf_op jit(solution)/shard_map/cond/branch_1_fun/ppermute | solution.py:202
  812.0 99.7 %all-to-all-start.8 = ((bf16[32,3,72,256]{3,2,1,0:T(8,128)(2,1)}), bf16[32,3,72,256]{3,2,1,0:T(8,128)(2,1)}, u32[]{:S(2)}, u32[]{:S(2)}) async-start(bf16[32,3,72,256]{3,2,1,0:T(8,128)(2,1)} %pad_maximum_fusion.28), calls=%async_computation.8 | async-start | bytes 7077888 | tf_op jit(solution)/shard_map/all_to_all | solution.py:297
  829.7 32.2 %collective-permute-start.57 = (bf16[1,1,2,128,1152]{4,3,2,1,0:T(8,128)(2,1)S(1)}, bf16[1,1,2,128,1152]{4,3,2,1,0:T(8,128)(2,1)S(1)}, u32[]{:S(2)}, u32[]{:S(2)}) collective-permute-start(bf16[1,1,2,128,1152]{4,3,2,1,0:T(8,128)(2,1)S(1)} %slice.579), channel_id=1, source_target_pairs={{0,4},{4,0},{1,5},{5,1},{2,6},{6,2},{3,7},{7,3},{8,12},{12,8},{9,1... | collective-permute-start | bytes 1769480 | tf_op jit(solution)/shard_map/cond/branch_1_fun/ppermute | solution.py:112
  831.4 32.7 %collective-permute-start.54 = (bf16[1,2,1,128,1152]{4,3,2,1,0:T(8,128)(2,1)S(1)}, bf16[1,2,1,128,1152]{4,3,2,1,0:T(8,128)(2,1)S(1)}, u32[]{:S(2)}, u32[]{:S(2)}) collective-permute-start(bf16[1,2,1,128,1152]{4,3,2,1,0:T(8,128)(2,1)S(1)} %slice.580), channel_id=1, source_target_pairs={{0,2},{2,0},{1,3},{3,1},{4,6},{6,4},{5,7},{7,5},{8,10},{10,8},{9,1... | collective-permute-start | bytes 1769480 | tf_op jit(solution)/shard_map/cond/branch_1_fun/ppermute | solution.py:112
  (127 other events, 1538.1 us)
